TPU v7x, 256 devices: a whole 4x4x8 slice. The times are simulated.
256 devices in a mesh: patch: 32 (over x_lo, z, core), tensor: 8 (over y, x_hi).
Axes of the slice: x: 4 (x_hi: 2, x_lo: 2; x = x_hi * 2 + x_lo), y: 4, z: 8, core: 2. Of those that a mesh axis runs over, the one named last changes fastest.
Arguments:
- latents: bfloat16 [8192, 3072], P('patch'), may hold values from -6 to 6
- token_rows: int32 [8192], P('patch'), may hold values from 0 to 8191, each once
- mod_shift: float32 [3072], replicated, may hold values from -3 to 3
- mod_scale: float32 [3072], replicated, may hold values from -2 to 2
- mod_gate: float32 [3072], replicated, may hold values from 0.5 to 2
- w_qkv: bfloat16 [3072, 3, 3072], P(None, None, 'tensor'), may hold values from -0.109375 to 0.109375
- q_gain: float32 [128], replicated, may hold values from 0.5 to 2
- k_gain: float32 [128], replicated, may hold values from 0.5 to 2
- stale_kv: bfloat16 [8192, 2, 3072], P('patch', None, 'tensor'), may hold values from -84 to 84
- text_kv: bfloat16 [512, 2, 3072], P(None, None, 'tensor'), may hold values from -6 to 6
- w_out: bfloat16 [3072, 3072], P('tensor'), may hold values from -0.109375 to 0.109375
- b_out: float32 [3072], replicated, may hold values from -3 to 3
Outputs:
- block_out: bfloat16 [8192, 3072], P('patch')
- fresh_kv: bfloat16 [8192, 2, 3072], P('patch', None, 'tensor')
Inputs may be any that keep to these rules, and one draw needn't show every extreme that they name: `token_rows`: each position of the image of 8192 tokens appears once.
All inputs are finite; a program needn't handle non-finite values.
Results may differ from a plain program's by a relative error of at most 0.008.
Values may be sent and summed in bfloat16 or wider, within the bound.
No kernel may reach another device: no remote copies, remote signals or barrier semaphores. Data moves between devices by JAX's collectives and lax.ppermute only.
A program may use at most 192 MiB of HBM per device.

v0:
```python
import jax
import jax.numpy as jnp
from jax import lax
from jax.sharding import PartitionSpec as P

WIDTH_TOK = 256


def rope_tables(rows):
    row_pos = (rows // WIDTH_TOK).astype(jnp.float32)
    col_pos = (rows % WIDTH_TOK).astype(jnp.float32)
    steps = jnp.arange(28).astype(jnp.float32)
    omega = 10000.0 ** (-2.0 * steps / 56.0)
    angles = jnp.concatenate(
        [
            jnp.zeros((rows.shape[0], 8), jnp.float32),
            row_pos[:, None] * omega[None, :],
            col_pos[:, None] * omega[None, :],
        ],
        axis=1,
    )
    return (jnp.cos(angles), jnp.sin(angles))


def rotate(values, cosine, sine):
    count, heads, size = values.shape
    pairs = values.reshape(count, heads, size // 2, 2)
    first = pairs[..., 0]
    second = pairs[..., 1]
    cosine = cosine[:, None, :]
    sine = sine[:, None, :]
    out_first = first * cosine - second * sine
    out_second = first * sine + second * cosine
    return jnp.stack([out_first, out_second], axis=-1).reshape(count, heads, size)


def norm_head(values, gain):
    return values * lax.rsqrt(jnp.mean(values * values, axis=-1, keepdims=True) + 1e-06) * gain


def prepare(latents, rows, mod_shift, mod_scale, w_qkv, q_gain, k_gain):
    inputs = latents.astype(jnp.float32)
    centred = inputs - jnp.mean(inputs, axis=-1, keepdims=True)
    spread = jnp.mean(centred * centred, axis=-1, keepdims=True)
    normed = (centred * lax.rsqrt(spread + 1e-06) * (1.0 + mod_scale) + mod_shift).astype(
        jnp.bfloat16
    )
    count = inputs.shape[0]
    width = w_qkv.shape[2]
    heads = width // 128
    qkv = jnp.dot(
        normed, w_qkv.reshape(w_qkv.shape[0], 3 * width), preferred_element_type=jnp.float32
    )
    qkv = qkv.reshape(count, 3, heads, 128)
    cosine, sine = rope_tables(rows)
    query = (
        rotate(norm_head(qkv[:, 0], q_gain), cosine, sine)
        .astype(jnp.bfloat16)
        .reshape(count, width)
    )
    keys = (
        rotate(norm_head(qkv[:, 1], k_gain), cosine, sine)
        .astype(jnp.bfloat16)
        .reshape(count, width)
    )
    values = qkv[:, 2].astype(jnp.bfloat16).reshape(count, width)
    return (inputs, query, keys, values)


def scores(left, right):
    return lax.dot_general(
        left, right, (((1,), (1,)), ((), ())), preferred_element_type=jnp.float32
    )


def head_cols(matrix, head):
    return lax.dynamic_slice_in_dim(matrix, head * 128, 128, 1)


def shards(
    latents,
    token_rows,
    mod_shift,
    mod_scale,
    mod_gate,
    w_qkv,
    q_gain,
    k_gain,
    stale_kv,
    text_kv,
    w_out,
    b_out,
):
    inputs, query, keys, values = prepare(
        latents, token_rows, mod_shift, mod_scale, w_qkv, q_gain, k_gain
    )
    fresh_kv = jnp.stack([keys, values], axis=1)
    count = inputs.shape[0]
    width = query.shape[1]
    local_heads = width // 128
    factor = 1.0 / 128**0.5
    own_start = lax.axis_index("patch") * count
    text_k = text_kv[:, 0]
    text_v = text_kv[:, 1]
    head_ids = jnp.arange(local_heads)
    gathered = lax.all_gather(stale_kv, "patch", axis=0, tiled=True)
    anchor = (own_start, own_start * 0)
    every_k = lax.dynamic_update_slice(gathered[:, 0], keys, anchor)
    every_v = lax.dynamic_update_slice(gathered[:, 1], values, anchor)
    all_k = jnp.concatenate([text_k, every_k], axis=0)
    all_v = jnp.concatenate([text_v, every_v], axis=0)

    def head_out(head):
        logits = scores(head_cols(query, head), head_cols(all_k, head)) * factor
        largest = jnp.max(logits, axis=1, keepdims=True)
        weights = jnp.exp(logits - largest)
        total = jnp.sum(weights, axis=1, keepdims=True)
        weighted = jnp.dot(
            weights.astype(jnp.bfloat16), head_cols(all_v, head), preferred_element_type=jnp.float32
        )
        return weighted / total

    heads_out = lax.map(head_out, head_ids)
    attn = jnp.transpose(heads_out, (1, 0, 2)).reshape(count, width).astype(jnp.bfloat16)
    projected = jnp.dot(attn, w_out, preferred_element_type=jnp.float32)
    summed = lax.psum(projected.astype(jnp.bfloat16), "tensor").astype(jnp.float32)
    block_out = (inputs + mod_gate * (summed + b_out)).astype(jnp.bfloat16)
    return (block_out, fresh_kv)


def solution(mesh):
    return jax.shard_map(
        shards,
        mesh=mesh,
        in_specs=(
            P("patch", None),
            P("patch"),
            P(),
            P(),
            P(),
            P(None, None, "tensor"),
            P(),
            P(),
            P("patch", None, "tensor"),
            P(None, None, "tensor"),
            P("tensor", None),
            P(),
        ),
        out_specs=(P("patch", None), P("patch", None, "tensor")),
        check_vma=False,
    )
```

profile of v0, /device:TPU:6, one launch (start us, length us, event | category | flops | bytes accessed | tf_op | source)
XLA Modules:
  0.0 247.6 jit_solution(682027710139722250)
XLA Ops:
  7.2 2.0 copy.24
  9.3 1.4 mul.192
  11.5 10.1 %copy.22 = bf16[3072,3,384]{0,2,1:T(8,128)(2,1)} copy(bf16[3072,3,384]{2,0,1:T(8,128)(2,1)} %param.19) | data formatting | bytes 14155776 | tf_op args[5]
  21.6 1.7 convert_reduce_fusion
  23.3 2.0 fusion.22
  25.4 5.7 %fusion.28 = f32[256,3,3,128]{0,3,2,1:T(8,128)S(1)} fusion(bf16[3,3,128,3072]{3,2,1,0:T(8,128)(2,1)} %bitcast.47, bf16[256,3072]{1,0:T(8,128)(2,1)} %param.14, f32[3072]{0:T(1024)S(1)} %copy-done.12, f32[3072]{0:T(1024)S(1)} %broadcast_add_fusion, f32[256]{0:T(256)S(1)} %add_rsqrt_fusion.2, f32[256]{0:T(256)S(1)} %broadcast_multiply_fusion.2), kind=kOutput, calls=%fused_computation.30 | convolution fusion | flops 1816657920 | bytes 9857024 | tf_op jit(solution)/shard_map/dot_general | solution.py:51
  33.0 2.1 multiply_reduce_fusion
  35.1 2.0 squeeze.28
  37.6 1.3 multiply_multiply_fusion
  40.6 1.8 copy.25
  42.3 2.0 squeeze.25
  44.3 1.2 multiply_multiply_fusion.1
  45.6 1.4 subtract_convert_fusion
  47.0 1.1 pad_maximum_fusion.3
  48.1 1.7 convert_element_type.86
  51.0 41.5 %all-gather.2.cloned.1.call-done = bf16[8192,2,384]{2,0,1:T(8,128)(2,1)} async-done(((bf16[256,2,384]{2,0,1:T(8,128)(2,1)}), bf16[8192,2,384]{2,0,1:T(8,128)(2,1)}) %all-gather.2.cloned.1.call-update) | async-done | bytes 12582928 | tf_op jit(solution)/shard_map/all_gather | solution.py:106
  92.6 6.1 %slice_bitcast_fusion = (bf16[8192,384]{1,0:T(8,128)(2,1)S(1)}, bf16[8192,384]{1,0:T(8,128)(2,1)S(1)}) fusion(bf16[8192,2,384]{2,0,1:T(8,128)(2,1)} %all-gather.2.cloned.1.call-done), kind=kLoop, calls=%fused_computation.16 | loop fusion | bytes 25165824 | tf_op jit(solution)/shard_map/squeeze | solution.py:109
  98.7 4.6 %pad_maximum_fusion.1 = bf16[8704,384]{1,0:T(8,128)(2,1)} fusion(bf16[8192,384]{1,0:T(8,128)(2,1)S(1)} %constant_dynamic-update-slice_fusion.1, bf16[512,384]{1,0:T(8,128)(2,1)S(1)} %get-tuple-element.77), kind=kLoop, calls=%fused_computation.15 | loop fusion | flops 13369344 | bytes 13369344 | tf_op jit(solution)/shard_map/concatenate | solution.py:111
  103.4 4.8 %pad_maximum_fusion = bf16[8704,384]{1,0:T(8,128)(2,1)} fusion(bf16[8192,384]{1,0:T(8,128)(2,1)S(1)} %constant_dynamic-update-slice_fusion.2, bf16[512,384]{1,0:T(8,128)(2,1)S(1)} %get-tuple-element.78), kind=kLoop, calls=%fused_computation.14 | loop fusion | flops 13369344 | bytes 13369344 | tf_op jit(solution)/shard_map/concatenate | solution.py:110
  108.1 27.6 %while.10 = (s32[]{:T(128)}, bf16[3,256,128]{1,2,0:T(8,128)(2,1)S(1)}, s32[3]{0:T(128)S(1)}, bf16[256,384]{0,1:T(8,128)(2,1)}, bf16[8704,384]{1,0:T(8,128)(2,1)}...) while((s32[]{:T(128)}, bf16[3,256,128]{1,2,0:T(8,128)(2,1)S(1)}, ...), condition=%wide.region_7.8_spmd, body=%wide.region_4.7_spmd.sunk | while | flops 1154285056 | bytes 31594672 | solution.py:123
  109.4 3.1 %fusion.50 = (f32[256]{0:T(256)S(1)}, f32[256,8704]{1,0:T(8,128)S(1)}) fusion(bf16[8704,384]{1,0:T(8,128)(2,1)} %get-tuple-element.144, s32[]{:T(128)S(6)} %select_n.31, bf16[256,384]{0,1:T(8,128)(2,1)} %get-tuple-element.143), kind=kOutput, calls=%fused_computation.71.clone.1 | convolution fusion | flops 574881536 | bytes 11208704 | tf_op jit(solution)/shard_map/while/body/eval_jaxpr/dot_general | solution.py:71
  112.5 1.4 fusion.51
  113.9 3.3 %fusion.52 = bf16[1,256,128]{2,1,0:T(8,128)(2,1)S(1)} fusion(bf16[8704,384]{1,0:T(8,128)(2,1)} %get-tuple-element.145, s32[]{:T(128)S(6)} %select_n.31, f32[256,8704]{1,0:T(8,128)S(1)} %get-tuple-element.118, f32[256]{0:T(256)S(1)} %get-tuple-element.119, f32[256]{0:T(256)S(1)} %fusion.51), kind=kOutput, calls=%fused_computation.9.clone.1 | convolution fusion | flops 574947328 | bytes 11208708 | tf_op jit(solution)/shard_map/while/body/eval_jaxpr/dot_general | solution.py:118
  118.6 3.1 %fusion.50 = (f32[256]{0:T(256)S(1)}, f32[256,8704]{1,0:T(8,128)S(1)}) fusion(bf16[8704,384]{1,0:T(8,128)(2,1)} %get-tuple-element.144, s32[]{:T(128)S(6)} %select_n.31, bf16[256,384]{0,1:T(8,128)(2,1)} %get-tuple-element.143), kind=kOutput, calls=%fused_computation.71.clone.1 | convolution fusion | flops 574881536 | bytes 11208704 | tf_op jit(solution)/shard_map/while/body/eval_jaxpr/dot_general | solution.py:71
  121.7 1.4 fusion.51
  123.1 3.3 %fusion.52 = bf16[1,256,128]{2,1,0:T(8,128)(2,1)S(1)} fusion(bf16[8704,384]{1,0:T(8,128)(2,1)} %get-tuple-element.145, s32[]{:T(128)S(6)} %select_n.31, f32[256,8704]{1,0:T(8,128)S(1)} %get-tuple-element.118, f32[256]{0:T(256)S(1)} %get-tuple-element.119, f32[256]{0:T(256)S(1)} %fusion.51), kind=kOutput, calls=%fused_computation.9.clone.1 | convolution fusion | flops 574947328 | bytes 11208708 | tf_op jit(solution)/shard_map/while/body/eval_jaxpr/dot_general | solution.py:118
  127.8 3.1 %fusion.50 = (f32[256]{0:T(256)S(1)}, f32[256,8704]{1,0:T(8,128)S(1)}) fusion(bf16[8704,384]{1,0:T(8,128)(2,1)} %get-tuple-element.144, s32[]{:T(128)S(6)} %select_n.31, bf16[256,384]{0,1:T(8,128)(2,1)} %get-tuple-element.143), kind=kOutput, calls=%fused_computation.71.clone.1 | convolution fusion | flops 574881536 | bytes 11208704 | tf_op jit(solution)/shard_map/while/body/eval_jaxpr/dot_general | solution.py:71
  130.9 1.4 fusion.51
  132.3 3.3 %fusion.52 = bf16[1,256,128]{2,1,0:T(8,128)(2,1)S(1)} fusion(bf16[8704,384]{1,0:T(8,128)(2,1)} %get-tuple-element.145, s32[]{:T(128)S(6)} %select_n.31, f32[256,8704]{1,0:T(8,128)S(1)} %get-tuple-element.118, f32[256]{0:T(256)S(1)} %get-tuple-element.119, f32[256]{0:T(256)S(1)} %fusion.51), kind=kOutput, calls=%fused_computation.9.clone.1 | convolution fusion | flops 574947328 | bytes 11208708 | tf_op jit(solution)/shard_map/while/body/eval_jaxpr/dot_general | solution.py:118
  135.8 2.1 convolution_convert_fusion
  139.2 97.9 %all-reduce.2.cloned.1.call-done = bf16[256,3072]{1,0:T(8,128)(2,1)} async-done(((bf16[256,3072]{1,0:T(8,128)(2,1)}), bf16[256,3072]{1,0:T(8,128)(2,1)}) %all-reduce.2.cloned.1.call-update) | async-done | bytes 1572880 | tf_op jit(solution)/shard_map/psum | solution.py:126
  237.1 3.6 %fusion.26 = bf16[256,3072]{1,0:T(8,128)(2,1)} fusion(bf16[256,3072]{1,0:T(8,128)(2,1)} %param.14, bf16[256,3072]{1,0:T(8,128)(2,1)} %all-reduce.2.cloned.1.call-done, f32[3072]{0:T(1024)S(1)} %copy-done.8, f32[3072]{0:T(1024)S(1)} %copy-done.9), kind=kLoop, calls=%fused_computation.28 | loop fusion | flops 4718592 | bytes 4743168 | tf_op jit(solution)/shard_map/convert_element_type | solution.py:127
  (64 shorter events, 9.6 us)
Async XLA Ops:
  7.2 128.6 %copy-start = (bf16[384,3072]{1,0:T(8,128)(2,1)S(1)}, bf16[384,3072]{1,0:T(8,128)(2,1)}, u32[]{:S(2)}) copy-start(bf16[384,3072]{1,0:T(8,128)(2,1)} %param.24) | copy-start | bytes 7077892
  7.2 85.4 %all-gather.2.cloned.1.call-start = ((), (), s32[]{:S(2)}) async-start(), calls=%async_computation | async-start | bytes 12976128 | tf_op jit(solution)/shard_map/all_gather | solution.py:106
  9.2 227.9 %all-reduce.2.cloned.1.call-start = ((), (), s32[]{:S(2)}) async-start(), calls=%async_computation.1 | async-start | bytes 3145728 | tf_op jit(solution)/shard_map/psum | solution.py:126
  11.5 13.8 %copy-start.10 = (f32[3072]{0:T(1024)S(1)}, f32[3072]{0:T(1024)}, u32[]{:S(2)}) copy-start(f32[3072]{0:T(1024)} %param.17) | copy-start | bytes 36868
  11.5 13.9 %copy-start.12 = (f32[3072]{0:T(1024)S(1)}, f32[3072]{0:T(1024)}, u32[]{:S(2)}) copy-start(f32[3072]{0:T(1024)} %param.16) | copy-start | bytes 36868
  25.3 11.8 %copy-start.11 = (s32[256]{0:T(256)S(1)}, s32[256]{0:T(256)}, u32[]{:S(2)}) copy-start(s32[256]{0:T(256)} %param.15) | copy-start | bytes 3076
  31.1 1.0 copy-start.2
  32.1 17.7 %copy-start.1 = (bf16[512,2,384]{2,1,0:T(2,128)(2,1)S(1)}, bf16[512,2,384]{2,1,0:T(2,128)(2,1)}, u32[]{:S(2)}) copy-start(bf16[512,2,384]{2,1,0:T(2,128)(2,1)} %param.23) | copy-start | bytes 2359300
  37.5 1.8 copy-start.5
  37.5 1.8 copy-start.6
  92.6 6.1 %copy-start.3 = (bf16[256,384]{1,0:T(8,128)(2,1)S(1)}, bf16[256,384]{1,0:T(8,128)(2,1)}, u32[]{:S(2)}) copy-start(bf16[256,384]{1,0:T(8,128)(2,1)} %copy.27) | copy-start | bytes 589828
  98.7 4.7 %copy-start.4 = (bf16[256,384]{1,0:T(8,128)(2,1)S(1)}, bf16[256,384]{1,0:T(8,128)(2,1)}, u32[]{:S(2)}) copy-start(bf16[256,384]{1,0:T(8,128)(2,1)} %copy.25) | copy-start | bytes 589828
  103.4 4.8 %copy-start.7 = (bf16[3,256,128]{1,2,0:T(8,128)(2,1)S(1)}, bf16[3,256,128]{1,2,0:T(8,128)(2,1)}, u32[]{:S(2)}) copy-start(bf16[3,256,128]{1,2,0:T(8,128)(2,1)} %custom-call) | copy-start | bytes 589828
  135.7 101.4 %copy-start.8 = (f32[3072]{0:T(1024)S(1)}, f32[3072]{0:T(1024)}, u32[]{:S(2)}) copy-start(f32[3072]{0:T(1024)} %param.25) | copy-start | bytes 36868
  135.8 101.4 %copy-start.9 = (f32[3072]{0:T(1024)S(1)}, f32[3072]{0:T(1024)}, u32[]{:S(2)}) copy-start(f32[3072]{0:T(1024)} %param.18) | copy-start | bytes 36868
Sparse Core Ops, SparseCore 0:
  9.8 82.6 all-gather.1
  138.1 98.9 all-reduce.1
where the time goes:
time: 251 us; the launch traced here: 248 us
  waiting for transfers between devices  139 us (55%)
  local copies, waits for them, and re-layouts  35.1 us (14%)
  other arithmetic  29.5 us (12%)
  matrix products  27 us (11%)
  between operations  14.3 us (6%)
    psum x1, waiting for transfers between devices, shards(): lax.psum(projected.astype(jnp.bfloat16), 'tensor').astype(jnp.float32)  97.9 us
    all_gather x1, waiting for transfers between devices, shards(): gathered = lax.all_gather(stale_kv, 'patch', axis=0, tiled=True)  41.5 us
    unnamed x29, local copies, waits for them, and re-layouts  14.3 us
    dot_general x3, matrix products, head_out(): jnp.dot(weights.astype(jnp.bfloat16), head_cols(all_v, head), preferred_e...  9.8 us
    dot_general x3, matrix products, scores(): lax.dot_general(left, right, (((1,), (1,)), ((), ())), preferred_element_...  9.3 us
    squeeze x1, local copies, waits for them, and re-layouts, shards(): every_v = lax.dynamic_update_slice(gathered[:, 1], values, anchor)  6.07 us
    dot_general x1, matrix products, prepare(): jnp.dot(normed, w_qkv.reshape(w_qkv.shape[0], 3 * width), preferred_eleme...  5.74 us
  transfers between devices with their start and end apart: 2, of which 2 were waited for; matrix products, arithmetic and copies ran while one was open for 17% of the time, Pallas kernels for 0%

commit v1 on v0

v1 whole, which is shorter than its diff:
```python
import jax
import jax.numpy as jnp
import numpy as np
from jax import lax
from jax.experimental import pallas as pl
from jax.experimental.pallas import tpu as pltpu
from jax.sharding import Mesh
from jax.sharding import PartitionSpec as P

WIDTH_TOK = 256
HEAD = 128
LOCAL_HEADS = 3
WIDTH = HEAD * LOCAL_HEADS
COUNT = 256
TEXT = 512
MODEL = 3072
ROWS = COUNT // 8
AXES = ("x_lo", "z", "core", "y", "x_hi")
SIZES = (2, 8, 2, 4, 2)
PATCH = ("x_lo", "z", "core")
TENSOR = ("y", "x_hi")
SCALE = float(np.log2(np.e) / np.sqrt(128.0))
MIB = 1024 * 1024
HOPS = [(0, 0), (2, 1), (2, 0), (1, 1), (3, 1), (1, 0), (3, 0), (0, 1)]
FULL = pl.BlockSpec(memory_space=pltpu.VMEM)
SMEM = pl.BlockSpec(memory_space=pltpu.SMEM)


def params(mib=48):
    return pltpu.CompilerParams(vmem_limit_bytes=mib * MIB)


def cost(flops, nbytes, exps=0):
    return pl.CostEstimate(flops=flops, bytes_accessed=nbytes, transcendentals=exps)


def head_of(head):
    return slice(head * HEAD, (head + 1) * HEAD)


def qkv_kernel(lat, shift, scale, w, q_gain, k_gain, cosine, sine, q, k, v, normed):
    part = pl.program_id(0)

    @pl.when(part == 0)
    def _():
        x = lat[...].astype(jnp.float32)
        centred = x - jnp.mean(x, axis=-1, keepdims=True)
        spread = jnp.mean(centred * centred, axis=-1, keepdims=True)
        y = centred * lax.rsqrt(spread + 1e-06) * (1.0 + scale[...]) + shift[...]
        normed[...] = y.astype(jnp.bfloat16)

    out = jnp.dot(normed[...], w[0], preferred_element_type=jnp.float32)

    def rotated(gain):
        even = lax.broadcasted_iota(jnp.int32, (COUNT, HEAD), 1) % 2 == 0
        heads = []
        for head in range(LOCAL_HEADS):
            x = out[:, head_of(head)]
            x = x * lax.rsqrt(jnp.mean(x * x, axis=-1, keepdims=True) + 1e-06) * gain[...]
            other = jnp.where(even, pltpu.roll(x, HEAD - 1, 1), pltpu.roll(x, 1, 1))
            heads.append((x * cosine[...] + other * sine[...]).astype(jnp.bfloat16))
        return jnp.concatenate(heads, axis=1)

    @pl.when(part == 0)
    def _():
        q[...] = rotated(q_gain)

    @pl.when(part == 1)
    def _():
        k[...] = rotated(k_gain)

    @pl.when(part == 2)
    def _():
        v[...] = out.astype(jnp.bfloat16)


def qkv_call(latents, shift, scale, w, q_gain, k_gain, cosine, sine):
    whole = lambda shape: pl.BlockSpec(shape, lambda i: (0,) * len(shape))
    piece = jax.ShapeDtypeStruct((COUNT, WIDTH), jnp.bfloat16)
    return pl.pallas_call(
        qkv_kernel,
        grid=(3,),
        in_specs=[
            whole((COUNT, MODEL)),
            whole((1, MODEL)),
            whole((1, MODEL)),
            pl.BlockSpec((1, MODEL, WIDTH), lambda i: (i, 0, 0)),
            whole((1, HEAD)),
            whole((1, HEAD)),
            whole((COUNT, HEAD)),
            whole((COUNT, HEAD)),
        ],
        out_specs=[whole((COUNT, WIDTH))] * 3,
        out_shape=[piece] * 3,
        scratch_shapes=[pltpu.VMEM((COUNT, MODEL), jnp.bfloat16)],
        compiler_params=params(),
        cost_estimate=cost(2 * COUNT * MODEL * WIDTH * 3, 10 * MIB),
    )(
        latents,
        shift.reshape(1, MODEL),
        scale.reshape(1, MODEL),
        w,
        q_gain.reshape(1, HEAD),
        k_gain.reshape(1, HEAD),
        cosine,
        sine,
    )


def pick(values):
    rows = values[0].shape[0]
    lane = lax.broadcasted_iota(jnp.int32, (rows, HEAD), 1)
    out = jnp.zeros((rows, HEAD), jnp.float32)
    for at, value in enumerate(values):
        out = jnp.where(lane == at, value, out)
    return out


def attend(q, pairs, state):
    scores = [
        lax.dot_general(q, k, (((1,), (1,)), ((), ())), preferred_element_type=jnp.float32) * SCALE
        for k, _ in pairs
    ]
    most = scores[0]
    for s in scores[1:]:
        most = jnp.maximum(most, s)
    top = jnp.max(most, axis=1, keepdims=True)
    if state is not None:
        top = jnp.maximum(top, state[1])
    total = None
    for s, (_, v) in zip(scores, pairs):
        p = jnp.exp2(s - top).astype(jnp.bfloat16)
        wide = jnp.concatenate([v, jnp.ones_like(v)], axis=1)
        part = jnp.dot(p, wide, preferred_element_type=jnp.float32)
        total = part if total is None else total + part
    num, den = total[:, :HEAD], total[:, HEAD : HEAD + 1]
    if state is not None:
        keep = jnp.exp2(state[1] - top)
        num, den = num + keep * state[0], den + keep * state[2]
    return num, top, den


def store_state(num, ml, results):
    for head, result in enumerate(results):
        num[0, :, head_of(head)] = result[0]
    ml[0] = pick([r[1] for r in results] + [r[2] for r in results])


def load_state(num, ml):
    stats = ml[0]
    return [
        (num[0, :, head_of(h)], stats[:, h : h + 1], stats[:, LOCAL_HEADS + h : LOCAL_HEADS + h + 1])
        for h in range(LOCAL_HEADS)
    ]


def first_kernel(q, k, v, text, own, num, ml):
    def run(pairs_of):
        results = []
        for head in range(LOCAL_HEADS):
            cols = head_of(head)
            results.append(attend(q[0, :, cols], pairs_of(cols), None))
        store_state(num, ml, results)

    @pl.when(pl.program_id(0) == 0)
    def _():
        run(
            lambda c: [
                (k[:, c], v[:, c]),
                (text[0, :COUNT, c], text[1, :COUNT, c]),
                (text[0, COUNT:, c], text[1, COUNT:, c]),
            ]
        )

    @pl.when(pl.program_id(0) != 0)
    def _():
        run(lambda c: [(own[0, :, c], own[1, :, c])])


def whole_spec(shape):
    return pl.BlockSpec(shape, lambda i: (0,) * len(shape))


def at_spec(shape, offset=0):
    return pl.BlockSpec((1, *shape), lambda i: (i + offset, 0, 0))


def state_shapes(blocks):
    return [
        jax.ShapeDtypeStruct((blocks, COUNT, WIDTH), jnp.float32),
        jax.ShapeDtypeStruct((blocks, COUNT, HEAD), jnp.float32),
    ]


def attend_cost(blocks):
    return cost(blocks * COUNT * COUNT * WIDTH * 4, 6 * MIB, blocks * COUNT * COUNT * LOCAL_HEADS)


def first_call(qs, k, v, text, own):
    return pl.pallas_call(
        first_kernel,
        grid=(4,),
        in_specs=[
            at_spec((COUNT, WIDTH)),
            whole_spec((COUNT, WIDTH)),
            whole_spec((COUNT, WIDTH)),
            whole_spec((2, TEXT, WIDTH)),
            whole_spec((2, COUNT, WIDTH)),
        ],
        out_specs=[at_spec((COUNT, WIDTH)), at_spec((COUNT, HEAD))],
        out_shape=state_shapes(4),
        compiler_params=params(),
        cost_estimate=attend_cost(6),
    )(qs, k, v, text, own)


def next_kernel(q, left, right, num_in, ml_in, num, ml):
    states = load_state(num_in, ml_in)
    results = []
    for head in range(LOCAL_HEADS):
        c = head_of(head)
        pairs = [(left[0, :, c], left[1, :, c]), (right[0, :, c], right[1, :, c])]
        results.append(attend(q[0, :, c], pairs, states[head]))
    store_state(num, ml, results)


def next_call(qs, left, right, num, ml):
    return pl.pallas_call(
        next_kernel,
        grid=(4,),
        in_specs=[
            at_spec((COUNT, WIDTH)),
            whole_spec((2, COUNT, WIDTH)),
            whole_spec((2, COUNT, WIDTH)),
            at_spec((COUNT, WIDTH)),
            at_spec((COUNT, HEAD)),
        ],
        out_specs=[at_spec((COUNT, WIDTH)), at_spec((COUNT, HEAD))],
        out_shape=state_shapes(4),
        compiler_params=params(),
        cost_estimate=attend_cost(8),
    )(qs, left, right, num, ml)


def pack_message(message, results):
    logs = []
    for head, (num, top, den) in enumerate(results):
        message[:, head_of(head)] = (num / den).astype(jnp.bfloat16)
        logs.append(top + jnp.log2(den))
    parts = []
    for _ in range(3):
        rounded = [x.astype(jnp.bfloat16).astype(jnp.float32) for x in logs]
        parts += rounded
        logs = [x - r for x, r in zip(logs, rounded)]
    message[:, WIDTH:] = pick(parts).astype(jnp.bfloat16)


def open_message(message):
    stats = message[:, WIDTH:].astype(jnp.float32)
    out = []
    for h in range(LOCAL_HEADS):
        log = sum(
            stats[:, n * LOCAL_HEADS + h : n * LOCAL_HEADS + h + 1] for n in (1, 2)
        ) + stats[:, h : h + 1]
        out.append((message[:, head_of(h)].astype(jnp.float32), log, 1.0))
    return out


def merge(states):
    top = states[0][1]
    for s in states[1:]:
        top = jnp.maximum(top, s[1])
    num, den = 0.0, 0.0
    for n, m, d in states:
        keep = jnp.exp2(m - top)
        num, den = num + keep * n, den + keep * d
    return num, top, den


def last_kernel(q, keys, values, num_in, ml_in, num, ml, message):
    states = load_state(num_in, ml_in)
    results = []
    for head in range(LOCAL_HEADS):
        c = head_of(head)
        results.append(attend(q[0, :, c], [(keys[:, c], values[:, c])], states[head]))

    @pl.when(pl.program_id(0) == 0)
    def _():
        store_state(num, ml, results)

    @pl.when(pl.program_id(0) == 1)
    def _():
        pack_message(message, results)


def last_call(qs, keys, values, num, ml, offset):
    return pl.pallas_call(
        last_kernel,
        grid=(2,),
        in_specs=[
            at_spec((COUNT, WIDTH), offset),
            whole_spec((COUNT, WIDTH)),
            whole_spec((COUNT, WIDTH)),
            at_spec((COUNT, WIDTH), offset),
            at_spec((COUNT, HEAD), offset),
        ],
        out_specs=[
            whole_spec((1, COUNT, WIDTH)),
            whole_spec((1, COUNT, HEAD)),
            whole_spec((COUNT, WIDTH + HEAD)),
        ],
        out_shape=state_shapes(1) + [jax.ShapeDtypeStruct((COUNT, WIDTH + HEAD), jnp.bfloat16)],
        compiler_params=params(),
        cost_estimate=attend_cost(2),
    )(qs, keys, values, num, ml)


def merge_kernel(num, ml, message, out):
    mine, other = load_state(num, ml), open_message(message)
    pack_message(out, [merge([a, b]) for a, b in zip(mine, other)])


def merge_call(num, ml, message):
    return pl.pallas_call(
        merge_kernel,
        in_specs=[FULL] * 3,
        out_specs=FULL,
        out_shape=jax.ShapeDtypeStruct((COUNT, WIDTH + HEAD), jnp.bfloat16),
        compiler_params=params(),
        cost_estimate=cost(0, 2 * MIB),
    )(num, ml, message)


def project_kernel(place, num, ml, near, far, w, *rest):
    outs, attn, full = rest[:8], rest[8], rest[9]
    triples = zip(load_state(num, ml), open_message(near), open_message(far))
    for head, states in enumerate(triples):
        total, _, den = merge(states)
        attn[:, head_of(head)] = (total / den).astype(jnp.bfloat16)
    for at in range(0, MODEL, 768):
        full[:, at : at + 768] = jnp.dot(
            attn[...], w[:, at : at + 768], preferred_element_type=jnp.float32
        ).astype(jnp.bfloat16)
    for n in range(8):
        outs[n][...] = full[pl.ds(pl.multiple_of(place[n] * ROWS, ROWS), ROWS), :]


def project_call(place, num, ml, near, far, w):
    return pl.pallas_call(
        project_kernel,
        in_specs=[SMEM] + [FULL] * 5,
        out_specs=[FULL] * 8,
        out_shape=[jax.ShapeDtypeStruct((ROWS, MODEL), jnp.bfloat16)] * 8,
        scratch_shapes=[
            pltpu.VMEM((COUNT, WIDTH), jnp.bfloat16),
            pltpu.VMEM((COUNT, MODEL), jnp.bfloat16),
        ],
        compiler_params=params(),
        cost_estimate=cost(2 * COUNT * WIDTH * MODEL, 5 * MIB),
    )(place, num, ml, near, far, w)


def gather_kernel(place, *refs):
    out = refs[8]
    for n in range(8):
        out[pl.ds(pl.multiple_of(place[n] * ROWS, ROWS), ROWS), :] = refs[n][...]


def gather_call(place, pieces):
    return pl.pallas_call(
        gather_kernel,
        in_specs=[SMEM] + [FULL] * 8,
        out_specs=FULL,
        out_shape=jax.ShapeDtypeStruct((COUNT, MODEL), jnp.bfloat16),
        compiler_params=params(),
        cost_estimate=cost(0, 4 * MIB),
    )(place, *pieces)


def ring(value, axis, step):
    size = SIZES[AXES.index(axis)]
    return lax.ppermute(value, axis, [(i, (i + step) % size) for i in range(size)])


def across(value, dy, dx):
    pairs = [(y * 2 + x, (y + dy) % 4 * 2 + (x ^ dx)) for y in range(4) for x in range(2)]
    return lax.ppermute(value, TENSOR, pairs)


def tables(rows):
    row_pos = (rows // WIDTH_TOK).astype(jnp.float32)
    col_pos = (rows % WIDTH_TOK).astype(jnp.float32)
    omega = 10000.0 ** (-2.0 * np.arange(28) / 56.0)
    by_row = np.repeat(np.concatenate([np.zeros(8), omega, np.zeros(28)]), 2).astype(np.float32)
    by_col = np.repeat(np.concatenate([np.zeros(36), omega]), 2).astype(np.float32)
    angles = row_pos[:, None] * by_row[None, :] + col_pos[:, None] * by_col[None, :]
    sign = np.tile(np.array([-1.0, 1.0], np.float32), HEAD // 2)
    return jnp.cos(angles), jnp.sin(angles) * sign[None, :]


def shards(
    latents,
    token_rows,
    mod_shift,
    mod_scale,
    mod_gate,
    w_qkv,
    q_gain,
    k_gain,
    stale_kv,
    text_kv,
    w_out,
    b_out,
):
    own = jnp.transpose(stale_kv, (1, 0, 2))
    right, left = [ring(own, "z", 1)], [ring(own, "z", -1)]
    cosine, sine = tables(token_rows)
    q, k, v = qkv_call(
        latents, mod_shift, mod_scale, jnp.transpose(w_qkv, (1, 0, 2)), q_gain, k_gain, cosine, sine
    )
    q_core = ring(q, "core", 1)
    q_x = ring(q, "x_lo", 1)
    q_both = lax.ppermute(q, ("x_lo", "core"), [(0, 3), (1, 2), (2, 1), (3, 0)])
    fresh_kv = jnp.stack([k, v], axis=1)
    text = jnp.transpose(text_kv, (1, 0, 2))
    qs = jnp.stack([q, q_core, q_x, q_both])
    for _ in range(2):
        right.append(ring(right[-1], "z", 1))
        left.append(ring(left[-1], "z", -1))
    far_k = ring(right[-1][0], "z", 1)
    far_v = ring(left[-1][1], "z", -1)

    num, ml = first_call(qs, k, v, text, own)
    for r, l in zip(right, left):
        num, ml = next_call(qs, r, l, num, ml)

    x_num, x_ml, x_msg = last_call(qs, far_k, far_v, num, ml, 2)
    x_msg = ring(x_msg, "core", 1)
    x_out = ring(merge_call(x_num, x_ml, x_msg), "x_lo", 1)
    o_num, o_ml, o_msg = last_call(qs, far_k, far_v, num, ml, 0)
    o_msg = ring(o_msg, "core", 1)

    y, x = lax.axis_index("y"), lax.axis_index("x_hi")
    to = jnp.stack([(y + dy) % 4 * 2 + (x + dx) % 2 for dy, dx in HOPS]).astype(jnp.int32)
    come = jnp.stack([(y - dy) % 4 * 2 + (x + dx) % 2 for dy, dx in HOPS]).astype(jnp.int32)
    parts = project_call(to, o_num, o_ml, o_msg, x_out, w_out)
    parts = [parts[0]] + [across(p, dy, dx) for p, (dy, dx) in zip(parts[1:], HOPS[1:])]
    mine = lax.dynamic_slice_in_dim(latents, to[0] * ROWS, ROWS, 0).astype(jnp.float32)
    total = parts[0].astype(jnp.float32)
    for p in parts[1:]:
        total = total + p.astype(jnp.float32)
    piece = (mine + mod_gate * (total + b_out)).astype(jnp.bfloat16)
    pieces = [piece] + [across(piece, dy, dx) for dy, dx in HOPS[1:]]
    return (gather_call(come, pieces), fresh_kv)


def solution(mesh):
    fine = Mesh(mesh.devices.reshape(SIZES), AXES)
    return jax.shard_map(
        shards,
        mesh=fine,
        in_specs=(
            P(PATCH, None),
            P(PATCH),
            P(),
            P(),
            P(),
            P(None, None, TENSOR),
            P(),
            P(),
            P(PATCH, None, TENSOR),
            P(None, None, TENSOR),
            P(TENSOR, None),
            P(),
        ),
        out_specs=(P(PATCH, None), P(PATCH, None, TENSOR)),
        check_vma=False,
    )
```

time: 251 us -> 154 us (0.61)
  waiting for transfers between devices: 139 us -> 53.4 us
  starting transfers between devices: 0.08 us -> 47.5 us
  Pallas kernels: 0 us -> 40 us
  local copies, waits for them, and re-layouts: 35.1 us -> 7.32 us
  matrix products: 27 us -> 0 us
  other arithmetic: 29.5 us -> 3.42 us
  between operations: 14.3 us -> 0.84 us
    psum x1 -> x0, waiting for transfers between devices: 97.9 us -> none  [shards(): lax.psum(projected.astype(jnp.bfloat16), 'tensor').astype(jnp.float32)]
    ppermute x0 -> x28, waiting for transfers between devices: none -> 53.4 us  [the longest x13 27.2 us: ring(): lax.ppermute(value, axis, [(i, (i + step) % size) for i in range(size)])]
    ppermute x0 -> x28, starting transfers between devices: none -> 47.5 us  [the longest x14 28.3 us: across(): return lax.ppermute(value, TENSOR, pairs)]
    all_gather x1 -> x0, waiting for transfers between devices: 41.5 us -> none  [shards(): gathered = lax.all_gather(stale_kv, 'patch', axis=0, tiled=True)]
    pallas_call x0 -> x10, Pallas kernels: none -> 40 us  [the longest x3 15.2 us: next_call(): pl.pallas_call(next_kernel, grid=(4,), in_specs=[at_spec((COUNT, WIDTH)),...]
    dot_general x8 -> x0, matrix products: 27 us -> none  [the longest x3 9.8 us: head_out(): jnp.dot(weights.astype(jnp.bfloat16), head_cols(all_v, head), preferred_e...]
    squeeze x4 -> x2, local copies, waits for them, and re-layouts: 10.2 us -> 0.04 us  [the longest x1 0.02 us: shards(): far_v = ring(left[-1][1], 'z', -1)]
    reduce_sum x6 -> x0, other arithmetic: 10.1 us -> none  [the longest x3 4.31 us: head_out(): total = jnp.sum(weights, axis=1, keepdims=True)]
  transfers between devices with their start and end apart: 2 -> 28, of which waited for: 2 -> 12; matrix products, arithmetic and copies ran while one was open for 17% -> 2% of each run, Pallas kernels for 0% -> 20%
where the time goes in v1:
time: 154 us; the launch traced here: 152 us
  waiting for transfers between devices  53.4 us (35%)
  starting transfers between devices  47.5 us (31%)
  Pallas kernels  40 us (26%)
  local copies, waits for them, and re-layouts  7.32 us (5%)
  other arithmetic  3.42 us (2%)
    ppermute x14, starting transfers between devices, across(): return lax.ppermute(value, TENSOR, pairs)  28.3 us
    ppermute x13, waiting for transfers between devices, ring(): lax.ppermute(value, axis, [(i, (i + step) % size) for i in range(size)])  27.2 us
    ppermute x14, waiting for transfers between devices, across(): return lax.ppermute(value, TENSOR, pairs)  23 us
    ppermute x13, starting transfers between devices, ring(): lax.ppermute(value, axis, [(i, (i + step) % size) for i in range(size)])  18.3 us
    pallas_call x3, Pallas kernels, next_call(): pl.pallas_call(next_kernel, grid=(4,), in_specs=[at_spec((COUNT, WIDTH)),...  15.2 us
    pallas_call x2, Pallas kernels, last_call(): pl.pallas_call(last_kernel, grid=(2,), in_specs=[at_spec((COUNT, WIDTH),...  7.17 us
    pallas_call x1, Pallas kernels, qkv_call(): pl.pallas_call(qkv_kernel, grid=(3,), in_specs=[whole((COUNT, MODEL)), wh...  7.15 us
    unnamed x21, local copies, waits for them, and re-layouts  7.11 us
  transfers between devices with their start and end apart: 28, of which 12 were waited for; matrix products, arithmetic and copies ran while one was open for 2% of the time, Pallas kernels for 20%

profile of v1, /device:TPU:6, one launch (start us, length us, event | category | flops | bytes accessed | tf_op | source)
XLA Modules:
  0.0 152.4 jit_solution(1225735882610196131)
XLA Ops:
  1.7 5.9 %collective-permute-start.7 = (bf16[2,256,384]{2,1,0:T(8,128)(2,1)S(1)}, bf16[2,256,384]{2,1,0:T(8,128)(2,1)S(1)}, u32[]{:S(2)}, u32[]{:S(2)}) collective-permute-start(bf16[2,256,384]{2,1,0:T(8,128)(2,1)S(1)} %bitcast.36), channel_id=1, source_target_pairs={{0,112},{16,0},{32,16},{48,32},{64,48},{80,64},{96,80},{112,96},{1... | collective-permute-start | bytes 1179656 | tf_op jit(solution)/shard_map/ppermute | solution.py:382
  7.6 8.4 %collective-permute-done.7.right = bf16[2,256,384]{2,1,0:T(8,128)(2,1)S(1)} collective-permute-done((bf16[2,256,384]{2,1,0:T(8,128)(2,1)S(1)}, bf16[2,256,384]{2,1,0:T(8,128)(2,1)S(1)}, u32[]{:S(2)}, u32[]{:S(2)}) %collective-permute-start.7) | collective-permute-done | bytes 393248 | tf_op jit(solution)/shard_map/ppermute | solution.py:382
  16.0 3.7 %collective-permute-start.8 = (bf16[2,256,384]{2,1,0:T(8,128)(2,1)S(1)}, bf16[2,256,384]{2,1,0:T(8,128)(2,1)S(1)}, u32[]{:S(2)}, u32[]{:S(2)}) collective-permute-start(bf16[2,256,384]{2,1,0:T(8,128)(2,1)S(1)} %collective-permute-done.7.right), channel_id=1, source_target_pairs={{0,112},{16,0},{32,16},{48,32},{64,48},{80,64},{96,80},{112,96},{1... | collective-permute-start | bytes 1179656 | tf_op jit(solution)/shard_map/ppermute | solution.py:382
  21.7 5.4 %collective-permute-done.8.right = bf16[2,256,384]{2,1,0:T(8,128)(2,1)S(1)} collective-permute-done((bf16[2,256,384]{2,1,0:T(8,128)(2,1)S(1)}, bf16[2,256,384]{2,1,0:T(8,128)(2,1)S(1)}, u32[]{:S(2)}, u32[]{:S(2)}) %collective-permute-start.8) | collective-permute-done | bytes 393248 | tf_op jit(solution)/shard_map/ppermute | solution.py:382
  27.2 3.7 %collective-permute-start.9 = (bf16[2,256,384]{2,1,0:T(8,128)(2,1)S(1)}, bf16[2,256,384]{2,1,0:T(8,128)(2,1)S(1)}, u32[]{:S(2)}, u32[]{:S(2)}) collective-permute-start(bf16[2,256,384]{2,1,0:T(8,128)(2,1)S(1)} %collective-permute-done.8.right), channel_id=1, source_target_pairs={{0,112},{16,0},{32,16},{48,32},{64,48},{80,64},{96,80},{112,96},{1... | collective-permute-start | bytes 1179656 | tf_op jit(solution)/shard_map/ppermute | solution.py:382
  35.0 7.1 %shard_map.158 = (bf16[256,384]{1,0:T(8,128)(2,1)S(1)}, bf16[256,384]{1,0:T(8,128)(2,1)S(1)}, bf16[256,384]{1,0:T(8,128)(2,1)S(1)}) custom-call(bf16[256,3072]{1,0:T(8,128)(2,1)S(1)} %copy-done.1, f32[1,3072]{1,0:T(1,128)S(1)} %bitcast.42, f32[1,3072]{1,0:T(1,128)S(1)} %bitcast.43, bf16[3,3072,384]{2,1,0:T(8,128)(2,1)} %bitcast.46, f32[1,128]{1,0:T(1,128)S(1)} %bitcast.44, ...), custom_call_target="tpu_custom_call" | custom-call | flops 1811939328 | bytes 10485760 | tf_op jit(solution)/shard_map/pallas_call | solution.py:80
  44.3 5.7 %collective-permute-done.1 = bf16[256,384]{1,0:T(8,128)(2,1)S(1)} collective-permute-done((bf16[256,384]{1,0:T(8,128)(2,1)S(1)}, bf16[256,384]{1,0:T(8,128)(2,1)S(1)}, u32[]{:S(2)}, u32[]{:S(2)}) %collective-permute-start.1) | collective-permute-done | bytes 196640 | tf_op jit(solution)/shard_map/ppermute | solution.py:382
  50.1 3.3 %collective-permute-done.2 = bf16[256,384]{1,0:T(8,128)(2,1)S(1)} collective-permute-done((bf16[256,384]{1,0:T(8,128)(2,1)S(1)}, bf16[256,384]{1,0:T(8,128)(2,1)S(1)}, u32[]{:S(2)}, u32[]{:S(2)}) %collective-permute-start.2) | collective-permute-done | bytes 196640 | tf_op jit(solution)/shard_map/ppermute | solution.py:423
  53.4 3.3 %shard_map.159 = (f32[4,256,384]{2,1,0:T(8,128)S(1)}, f32[4,256,128]{2,1,0:T(8,128)S(1)}) custom-call(bf16[4,256,384]{2,1,0:T(8,128)(2,1)S(1)} %pad_maximum_fusion.q, bf16[256,384]{1,0:T(8,128)(2,1)S(1)} %get-tuple-element.28.k, bf16[256,384]{1,0:T(8,128)(2,1)S(1)} %get-tuple-element.29.v, bf16[2,512,384]{2,1,0:T(8,128)(2,1)S(1)} %bitcast.35, ...), custom_call_target="tpu_custom_call" | custom-call | flops 603979776 | bytes 6291456 | tf_op jit(solution)/shard_map/pallas_call | solution.py:200
  57.1 2.1 %collective-permute-start.6 = (bf16[256,384]{1,0:T(8,128)(2,1)S(1)}, bf16[256,384]{1,0:T(8,128)(2,1)S(1)}, u32[]{:S(2)}, u32[]{:S(2)}) collective-permute-start(bf16[256,384]{1,0:T(8,128)(2,1)S(1)} %slice_bitcast_fusion.1), channel_id=1, source_target_pairs={{0,16},{16,32},{32,48},{48,64},{64,80},{80,96},{96,112},{112,0},{1... | collective-permute-start | bytes 589832 | tf_op jit(solution)/shard_map/ppermute | solution.py:382
  59.1 5.1 %shard_map.160 = (f32[4,256,384]{2,1,0:T(8,128)S(1)}, f32[4,256,128]{2,1,0:T(8,128)S(1)}) custom-call(bf16[4,256,384]{2,1,0:T(8,128)(2,1)S(1)} %pad_maximum_fusion.q, bf16[2,256,384]{2,1,0:T(8,128)(2,1)S(1)} %collective-permute-done.3.left, bf16[2,256,384]{2,1,0:T(8,128)(2,1)S(1)} %collective-permute-done.7.right, ...), custom_call_target="tpu_custom_call" | custom-call | flops 805306368 | bytes 6291456 | tf_op jit(solution)/shard_map/pallas_call | solution.py:228
  64.2 5.1 %shard_map.161 = (f32[4,256,384]{2,1,0:T(8,128)S(1)}, f32[4,256,128]{2,1,0:T(8,128)S(1)}) custom-call(bf16[4,256,384]{2,1,0:T(8,128)(2,1)S(1)} %pad_maximum_fusion.q, bf16[2,256,384]{2,1,0:T(8,128)(2,1)S(1)} %collective-permute-done.4.left, bf16[2,256,384]{2,1,0:T(8,128)(2,1)S(1)} %collective-permute-done.8.right, ...), custom_call_target="tpu_custom_call" | custom-call | flops 805306368 | bytes 6291456 | tf_op jit(solution)/shard_map/pallas_call | solution.py:228
  69.3 5.1 %shard_map.162 = (f32[4,256,384]{2,1,0:T(8,128)S(1)}, f32[4,256,128]{2,1,0:T(8,128)S(1)}) custom-call(bf16[4,256,384]{2,1,0:T(8,128)(2,1)S(1)} %pad_maximum_fusion.q, bf16[2,256,384]{2,1,0:T(8,128)(2,1)S(1)} %collective-permute-done.5.left, bf16[2,256,384]{2,1,0:T(8,128)(2,1)S(1)} %collective-permute-done.9.right, ...), custom_call_target="tpu_custom_call" | custom-call | flops 805306368 | bytes 6291456 | tf_op jit(solution)/shard_map/pallas_call | solution.py:228
  74.4 3.2 %shard_map.164 = (f32[1,256,384]{2,1,0:T(8,128)S(1)}, f32[1,256,128]{2,1,0:T(8,128)S(1)}, bf16[256,512]{1,0:T(8,128)(2,1)S(1)}) custom-call(bf16[4,256,384]{2,1,0:T(8,128)(2,1)S(1)} %pad_maximum_fusion.q, bf16[256,384]{1,0:T(8,128)(2,1)S(1)} %collective-permute-done.6.keys, bf16[256,384]{1,0:T(8,128)(2,1)S(1)} %collective-permute-done.10.values, ...), custom_call_target="tpu_custom_call" | custom-call | flops 201326592 | bytes 6291456 | tf_op jit(solution)/shard_map/pallas_call | solution.py:297
  77.8 3.9 %shard_map.163 = (f32[1,256,384]{2,1,0:T(8,128)S(1)}, f32[1,256,128]{2,1,0:T(8,128)S(1)}, bf16[256,512]{1,0:T(8,128)(2,1)}) custom-call(bf16[4,256,384]{2,1,0:T(8,128)(2,1)S(1)} %pad_maximum_fusion.q, bf16[256,384]{1,0:T(8,128)(2,1)S(1)} %collective-permute-done.6.keys, bf16[256,384]{1,0:T(8,128)(2,1)S(1)} %collective-permute-done.10.values, ...), custom_call_target="tpu_custom_call" | custom-call | flops 201326592 | bytes 6291456 | tf_op jit(solution)/shard_map/pallas_call | solution.py:297
  84.6 7.6 %collective-permute-done.13.far = bf16[256,512]{1,0:T(8,128)(2,1)} collective-permute-done((bf16[256,512]{1,0:T(8,128)(2,1)}, bf16[256,512]{1,0:T(8,128)(2,1)}, u32[]{:S(2)}, u32[]{:S(2)}) %collective-permute-start.13) | collective-permute-done | bytes 262176 | tf_op jit(solution)/shard_map/ppermute | solution.py:382
  92.3 3.9 %shard_map.166 = (bf16[32,3072]{1,0:T(8,128)(2,1)S(1)}, bf16[32,3072]{1,0:T(8,128)(2,1)S(1)}, bf16[32,3072]{1,0:T(8,128)(2,1)S(1)}, bf16[32,3072]{1,0:T(8,128)(2...) custom-call(s32[8]{0:T(128)S(1)} %stack.89.place, ...), custom_call_target="tpu_custom_call" | custom-call | flops 603979776 | bytes 5242880 | tf_op jit(solution)/shard_map/pallas_call | solution.py:349
  96.8 4.0 %collective-permute-start.14 = (bf16[32,3072]{1,0:T(8,128)(2,1)S(1)}, bf16[32,3072]{1,0:T(8,128)(2,1)S(1)}, u32[]{:S(2)}, u32[]{:S(2)}) collective-permute-start(bf16[32,3072]{1,0:T(8,128)(2,1)S(1)} %get-tuple-element.45), channel_id=1, source_target_pairs={{0,5},{1,4},{2,7},{3,6},{4,1},{5,0},{6,3},{7,2},{8,13},{9,12},{10,... | collective-permute-start | bytes 589832 | tf_op jit(solution)/shard_map/ppermute | solution.py:387
  101.2 3.1 %collective-permute-start.16 = (bf16[32,3072]{1,0:T(8,128)(2,1)}, bf16[32,3072]{1,0:T(8,128)(2,1)S(1)}, u32[]{:S(2)}, u32[]{:S(2)}) collective-permute-start(bf16[32,3072]{1,0:T(8,128)(2,1)} %get-tuple-element.47), channel_id=1, source_target_pairs={{0,3},{1,2},{2,5},{3,4},{4,7},{5,6},{6,1},{7,0},{8,11},{9,10},{10,... | collective-permute-start | bytes 589832 | tf_op jit(solution)/shard_map/ppermute | solution.py:387
  104.3 2.5 %collective-permute-start.17 = (bf16[32,3072]{1,0:T(8,128)(2,1)}, bf16[32,3072]{1,0:T(8,128)(2,1)S(1)}, u32[]{:S(2)}, u32[]{:S(2)}) collective-permute-start(bf16[32,3072]{1,0:T(8,128)(2,1)} %get-tuple-element.48), channel_id=1, source_target_pairs={{0,7},{1,6},{2,1},{3,0},{4,3},{5,2},{6,5},{7,4},{8,15},{9,14},{10,... | collective-permute-start | bytes 589832 | tf_op jit(solution)/shard_map/ppermute | solution.py:387
  107.2 3.4 %collective-permute-start.19 = (bf16[32,3072]{1,0:T(8,128)(2,1)}, bf16[32,3072]{1,0:T(8,128)(2,1)S(1)}, u32[]{:S(2)}, u32[]{:S(2)}) collective-permute-start(bf16[32,3072]{1,0:T(8,128)(2,1)} %get-tuple-element.50), channel_id=1, source_target_pairs={{0,6},{1,7},{2,0},{3,1},{4,2},{5,3},{6,4},{7,5},{8,14},{9,15},{10,... | collective-permute-start | bytes 589832 | tf_op jit(solution)/shard_map/ppermute | solution.py:387
  110.6 4.7 %collective-permute-done.15 = bf16[32,3072]{1,0:T(8,128)(2,1)S(1)} collective-permute-done((bf16[32,3072]{1,0:T(8,128)(2,1)S(1)}, bf16[32,3072]{1,0:T(8,128)(2,1)S(1)}, u32[]{:S(2)}, u32[]{:S(2)}) %collective-permute-start.15) | collective-permute-done | bytes 196640 | tf_op jit(solution)/shard_map/ppermute | solution.py:387
  116.7 2.7 %collective-permute-done.18 = bf16[32,3072]{1,0:T(8,128)(2,1)S(1)} collective-permute-done((bf16[32,3072]{1,0:T(8,128)(2,1)}, bf16[32,3072]{1,0:T(8,128)(2,1)S(1)}, u32[]{:S(2)}, u32[]{:S(2)}) %collective-permute-start.18) | collective-permute-done | bytes 196640 | tf_op jit(solution)/shard_map/ppermute | solution.py:387
  119.3 4.4 %collective-permute-done.20 = bf16[32,3072]{1,0:T(8,128)(2,1)S(1)} collective-permute-done((bf16[32,3072]{1,0:T(8,128)(2,1)}, bf16[32,3072]{1,0:T(8,128)(2,1)S(1)}, u32[]{:S(2)}, u32[]{:S(2)}) %collective-permute-start.20) | collective-permute-done | bytes 196640 | tf_op jit(solution)/shard_map/ppermute | solution.py:387
  125.0 3.2 %collective-permute-start.21 = (bf16[32,3072]{1,0:T(8,128)(2,1)S(1)}, bf16[32,3072]{1,0:T(8,128)(2,1)S(1)}, u32[]{:S(2)}, u32[]{:S(2)}) collective-permute-start(bf16[32,3072]{1,0:T(8,128)(2,1)S(1)} %add_convert_fusion.refs_0_), channel_id=1, source_target_pairs={{0,5},{1,4},{2,7},{3,6},{4,1},{5,0},{6,3},{7,2},{8,13},{9,12},{10,... | collective-permute-start | bytes 589832 | tf_op jit(solution)/shard_map/ppermute | solution.py:387
  129.5 3.5 %collective-permute-start.23 = (bf16[32,3072]{1,0:T(8,128)(2,1)S(1)}, bf16[32,3072]{1,0:T(8,128)(2,1)S(1)}, u32[]{:S(2)}, u32[]{:S(2)}) collective-permute-start(bf16[32,3072]{1,0:T(8,128)(2,1)S(1)} %add_convert_fusion.refs_0_), channel_id=1, source_target_pairs={{0,3},{1,2},{2,5},{3,4},{4,7},{5,6},{6,1},{7,0},{8,11},{9,10},{10,... | collective-permute-start | bytes 589832 | tf_op jit(solution)/shard_map/ppermute | solution.py:387
  133.0 2.1 %collective-permute-start.24 = (bf16[32,3072]{1,0:T(8,128)(2,1)S(1)}, bf16[32,3072]{1,0:T(8,128)(2,1)S(1)}, u32[]{:S(2)}, u32[]{:S(2)}) collective-permute-start(bf16[32,3072]{1,0:T(8,128)(2,1)S(1)} %add_convert_fusion.refs_0_), channel_id=1, source_target_pairs={{0,7},{1,6},{2,1},{3,0},{4,3},{5,2},{6,5},{7,4},{8,15},{9,14},{10,... | collective-permute-start | bytes 589832 | tf_op jit(solution)/shard_map/ppermute | solution.py:387
  135.1 1.7 %collective-permute-done.21.refs_1_ = bf16[32,3072]{1,0:T(8,128)(2,1)S(1)} collective-permute-done((bf16[32,3072]{1,0:T(8,128)(2,1)S(1)}, bf16[32,3072]{1,0:T(8,128)(2,1)S(1)}, u32[]{:S(2)}, u32[]{:S(2)}) %collective-permute-start.21) | collective-permute-done | bytes 196640 | tf_op jit(solution)/shard_map/ppermute | solution.py:387
  136.8 1.6 %collective-permute-start.26 = (bf16[32,3072]{1,0:T(8,128)(2,1)S(1)}, bf16[32,3072]{1,0:T(8,128)(2,1)S(1)}, u32[]{:S(2)}, u32[]{:S(2)}) collective-permute-start(bf16[32,3072]{1,0:T(8,128)(2,1)S(1)} %add_convert_fusion.refs_0_), channel_id=1, source_target_pairs={{0,6},{1,7},{2,0},{3,1},{4,2},{5,3},{6,4},{7,5},{8,14},{9,15},{10,... | collective-permute-start | bytes 589832 | tf_op jit(solution)/shard_map/ppermute | solution.py:387
  138.4 5.1 %collective-permute-done.22.refs_2_ = bf16[32,3072]{1,0:T(8,128)(2,1)S(1)} collective-permute-done((bf16[32,3072]{1,0:T(8,128)(2,1)S(1)}, bf16[32,3072]{1,0:T(8,128)(2,1)S(1)}, u32[]{:S(2)}, u32[]{:S(2)}) %collective-permute-start.22) | collective-permute-done | bytes 196640 | tf_op jit(solution)/shard_map/ppermute | solution.py:387
  146.5 4.1 %collective-permute-done.27.refs_7_ = bf16[32,3072]{1,0:T(8,128)(2,1)S(1)} collective-permute-done((bf16[32,3072]{1,0:T(8,128)(2,1)S(1)}, bf16[32,3072]{1,0:T(8,128)(2,1)S(1)}, u32[]{:S(2)}, u32[]{:S(2)}) %collective-permute-start.27) | collective-permute-done | bytes 196640 | tf_op jit(solution)/shard_map/ppermute | solution.py:387
  150.6 1.8 %shard_map.167 = bf16[256,3072]{1,0:T(8,128)(2,1)} custom-call(s32[8]{0:T(128)S(1)} %stack.82.place, bf16[32,3072]{1,0:T(8,128)(2,1)S(1)} %add_convert_fusion.refs_0_, bf16[32,3072]{1,0:T(8,128)(2,1)S(1)} %collective-permute-done.21.refs_1_, bf16[32,3072]{1,0:T(8,128)(2,1)S(1)} %collective-permute-done.22.refs_2_, ...), custom_call_target="tpu_custom_call" | custom-call | bytes 4194304 | tf_op jit(solution)/shard_map/pallas_call | solution.py:370
  (64 shorter events, 21.3 us)
Async XLA Ops:
  1.7 14.3 %collective-permute-start.7 = (bf16[2,256,384]{2,1,0:T(8,128)(2,1)S(1)}, bf16[2,256,384]{2,1,0:T(8,128)(2,1)S(1)}, u32[]{:S(2)}, u32[]{:S(2)}) collective-permute-start(bf16[2,256,384]{2,1,0:T(8,128)(2,1)S(1)} %bitcast.36), channel_id=1, source_target_pairs={{0,112},{16,0},{32,16},{48,32},{64,48},{80,64},{96,80},{112,96},{1... | collective-permute-start | bytes 1179656 | tf_op jit(solution)/shard_map/ppermute | solution.py:382
  7.6 12.8 %collective-permute-start.3 = (bf16[2,256,384]{2,1,0:T(8,128)(2,1)S(1)}, bf16[2,256,384]{2,1,0:T(8,128)(2,1)S(1)}, u32[]{:S(2)}, u32[]{:S(2)}) collective-permute-start(bf16[2,256,384]{2,1,0:T(8,128)(2,1)S(1)} %bitcast.37), channel_id=1, source_target_pairs={{0,16},{16,32},{32,48},{48,64},{64,80},{80,96},{96,112},{112,0},{1... | collective-permute-start | bytes 1179656 | tf_op jit(solution)/shard_map/ppermute | solution.py:382
  16.0 11.2 %collective-permute-start.8 = (bf16[2,256,384]{2,1,0:T(8,128)(2,1)S(1)}, bf16[2,256,384]{2,1,0:T(8,128)(2,1)S(1)}, u32[]{:S(2)}, u32[]{:S(2)}) collective-permute-start(bf16[2,256,384]{2,1,0:T(8,128)(2,1)S(1)} %collective-permute-done.7.right), channel_id=1, source_target_pairs={{0,112},{16,0},{32,16},{48,32},{64,48},{80,64},{96,80},{112,96},{1... | collective-permute-start | bytes 1179656 | tf_op jit(solution)/shard_map/ppermute | solution.py:382
  20.4 23.9 %collective-permute-start.4 = (bf16[2,256,384]{2,1,0:T(8,128)(2,1)S(1)}, bf16[2,256,384]{2,1,0:T(8,128)(2,1)S(1)}, u32[]{:S(2)}, u32[]{:S(2)}) collective-permute-start(bf16[2,256,384]{2,1,0:T(8,128)(2,1)S(1)} %collective-permute-done.3.left), channel_id=1, source_target_pairs={{0,16},{16,32},{32,48},{48,64},{64,80},{80,96},{96,112},{112,0},{1... | collective-permute-start | bytes 1179656 | tf_op jit(solution)/shard_map/ppermute | solution.py:382
  27.2 29.5 %collective-permute-start.9 = (bf16[2,256,384]{2,1,0:T(8,128)(2,1)S(1)}, bf16[2,256,384]{2,1,0:T(8,128)(2,1)S(1)}, u32[]{:S(2)}, u32[]{:S(2)}) collective-permute-start(bf16[2,256,384]{2,1,0:T(8,128)(2,1)S(1)} %collective-permute-done.8.right), channel_id=1, source_target_pairs={{0,112},{16,0},{32,16},{48,32},{64,48},{80,64},{96,80},{112,96},{1... | collective-permute-start | bytes 1179656 | tf_op jit(solution)/shard_map/ppermute | solution.py:382
  30.9 1.4 copy-start.1
  35.0 9.1 %copy-start.7 = (bf16[512,2,384]{2,1,0:T(2,128)(2,1)S(1)}, bf16[512,2,384]{2,1,0:T(2,128)(2,1)}, u32[]{:S(2)}) copy-start(bf16[512,2,384]{2,1,0:T(2,128)(2,1)} %param.24) | copy-start | bytes 2359300
  42.2 2.2 %collective-permute-start = (bf16[256,384]{1,0:T(8,128)(2,1)S(1)}, bf16[256,384]{1,0:T(8,128)(2,1)S(1)}, u32[]{:S(2)}, u32[]{:S(2)}) collective-permute-start(bf16[256,384]{1,0:T(8,128)(2,1)S(1)} %get-tuple-element.27), channel_id=1, source_target_pairs={{0,8},{8,0},{1,9},{9,1},{2,10},{10,2},{3,11},{11,3},{4,12},{12,4},... | collective-permute-start | bytes 589832 | tf_op jit(solution)/shard_map/ppermute | solution.py:382
  42.3 7.8 %collective-permute-start.1 = (bf16[256,384]{1,0:T(8,128)(2,1)S(1)}, bf16[256,384]{1,0:T(8,128)(2,1)S(1)}, u32[]{:S(2)}, u32[]{:S(2)}) collective-permute-start(bf16[256,384]{1,0:T(8,128)(2,1)S(1)} %get-tuple-element.27), channel_id=1, source_target_pairs={{0,128},{128,0},{1,129},{129,1},{2,130},{130,2},{3,131},{131,3},{4... | collective-permute-start | bytes 589832 | tf_op jit(solution)/shard_map/ppermute | solution.py:382
  43.2 10.1 %collective-permute-start.2 = (bf16[256,384]{1,0:T(8,128)(2,1)S(1)}, bf16[256,384]{1,0:T(8,128)(2,1)S(1)}, u32[]{:S(2)}, u32[]{:S(2)}) collective-permute-start(bf16[256,384]{1,0:T(8,128)(2,1)S(1)} %get-tuple-element.27), channel_id=1, source_target_pairs={{0,136},{8,128},{128,8},{136,0},{1,137},{9,129},{129,9},{137,1},{2... | collective-permute-start | bytes 589832 | tf_op jit(solution)/shard_map/ppermute | solution.py:423
  44.2 12.8 %collective-permute-start.5 = (bf16[2,256,384]{2,1,0:T(8,128)(2,1)S(1)}, bf16[2,256,384]{2,1,0:T(8,128)(2,1)S(1)}, u32[]{:S(2)}, u32[]{:S(2)}) collective-permute-start(bf16[2,256,384]{2,1,0:T(8,128)(2,1)S(1)} %collective-permute-done.4.left), channel_id=1, source_target_pairs={{0,16},{16,32},{32,48},{48,64},{64,80},{80,96},{96,112},{112,0},{1... | collective-permute-start | bytes 1179656 | tf_op jit(solution)/shard_map/ppermute | solution.py:382
  56.8 17.6 %collective-permute-start.10 = (bf16[256,384]{1,0:T(8,128)(2,1)S(1)}, bf16[256,384]{1,0:T(8,128)(2,1)S(1)}, u32[]{:S(2)}, u32[]{:S(2)}) collective-permute-start(bf16[256,384]{1,0:T(8,128)(2,1)S(1)} %slice_bitcast_fusion), channel_id=1, source_target_pairs={{0,112},{16,0},{32,16},{48,32},{64,48},{80,64},{96,80},{112,96},{1... | collective-permute-start | bytes 589832 | tf_op jit(solution)/shard_map/ppermute | solution.py:382
  57.1 17.3 %collective-permute-start.6 = (bf16[256,384]{1,0:T(8,128)(2,1)S(1)}, bf16[256,384]{1,0:T(8,128)(2,1)S(1)}, u32[]{:S(2)}, u32[]{:S(2)}) collective-permute-start(bf16[256,384]{1,0:T(8,128)(2,1)S(1)} %slice_bitcast_fusion.1), channel_id=1, source_target_pairs={{0,16},{16,32},{32,48},{48,64},{64,80},{80,96},{96,112},{112,0},{1... | collective-permute-start | bytes 589832 | tf_op jit(solution)/shard_map/ppermute | solution.py:382
  77.7 14.6 %copy-start = (bf16[384,3072]{1,0:T(8,128)(2,1)S(1)}, bf16[384,3072]{1,0:T(8,128)(2,1)}, u32[]{:S(2)}) copy-start(bf16[384,3072]{1,0:T(8,128)(2,1)} %w.1) | copy-start | bytes 7077892
  77.7 4.5 %collective-permute-start.12 = (bf16[256,512]{1,0:T(8,128)(2,1)S(1)}, bf16[256,512]{1,0:T(8,128)(2,1)S(1)}, u32[]{:S(2)}, u32[]{:S(2)}) collective-permute-start(bf16[256,512]{1,0:T(8,128)(2,1)S(1)} %get-tuple-element.43), channel_id=1, source_target_pairs={{0,8},{8,0},{1,9},{9,1},{2,10},{10,2},{3,11},{11,3},{4,12},{12,4},... | collective-permute-start | bytes 786440 | tf_op jit(solution)/shard_map/ppermute | solution.py:382
  81.7 2.9 %collective-permute-start.11 = (bf16[256,512]{1,0:T(8,128)(2,1)}, bf16[256,512]{1,0:T(8,128)(2,1)S(1)}, u32[]{:S(2)}, u32[]{:S(2)}) collective-permute-start(bf16[256,512]{1,0:T(8,128)(2,1)} %get-tuple-element.40), channel_id=1, source_target_pairs={{0,8},{8,0},{1,9},{9,1},{2,10},{10,2},{3,11},{11,3},{4,12},{12,4},... | collective-permute-start | bytes 786440 | tf_op jit(solution)/shard_map/ppermute | solution.py:382
  83.7 8.6 %collective-permute-start.13 = (bf16[256,512]{1,0:T(8,128)(2,1)}, bf16[256,512]{1,0:T(8,128)(2,1)}, u32[]{:S(2)}, u32[]{:S(2)}) collective-permute-start(bf16[256,512]{1,0:T(8,128)(2,1)} %shard_map.165), channel_id=1, source_target_pairs={{0,128},{128,0},{1,129},{129,1},{2,130},{130,2},{3,131},{131,3},{4... | collective-permute-start | bytes 786440 | tf_op jit(solution)/shard_map/ppermute | solution.py:382
  92.3 31.4 %copy-start.8 = (f32[3072]{0:T(1024)S(1)}, f32[3072]{0:T(1024)}, u32[]{:S(2)}) copy-start(f32[3072]{0:T(1024)} %param.26) | copy-start | bytes 36868
  96.8 10.4 %collective-permute-start.14 = (bf16[32,3072]{1,0:T(8,128)(2,1)S(1)}, bf16[32,3072]{1,0:T(8,128)(2,1)S(1)}, u32[]{:S(2)}, u32[]{:S(2)}) collective-permute-start(bf16[32,3072]{1,0:T(8,128)(2,1)S(1)} %get-tuple-element.45), channel_id=1, source_target_pairs={{0,5},{1,4},{2,7},{3,6},{4,1},{5,0},{6,3},{7,2},{8,13},{9,12},{10,... | collective-permute-start | bytes 589832 | tf_op jit(solution)/shard_map/ppermute | solution.py:387
  100.8 14.4 %collective-permute-start.15 = (bf16[32,3072]{1,0:T(8,128)(2,1)S(1)}, bf16[32,3072]{1,0:T(8,128)(2,1)S(1)}, u32[]{:S(2)}, u32[]{:S(2)}) collective-permute-start(bf16[32,3072]{1,0:T(8,128)(2,1)S(1)} %get-tuple-element.46), channel_id=1, source_target_pairs={{0,4},{1,5},{2,6},{3,7},{4,0},{5,1},{6,2},{7,3},{8,12},{9,13},{10,... | collective-permute-start | bytes 589832 | tf_op jit(solution)/shard_map/ppermute | solution.py:387
  101.2 15.5 %collective-permute-start.16 = (bf16[32,3072]{1,0:T(8,128)(2,1)}, bf16[32,3072]{1,0:T(8,128)(2,1)S(1)}, u32[]{:S(2)}, u32[]{:S(2)}) collective-permute-start(bf16[32,3072]{1,0:T(8,128)(2,1)} %get-tuple-element.47), channel_id=1, source_target_pairs={{0,3},{1,2},{2,5},{3,4},{4,7},{5,6},{6,1},{7,0},{8,11},{9,10},{10,... | collective-permute-start | bytes 589832 | tf_op jit(solution)/shard_map/ppermute | solution.py:387
  104.3 12.3 %collective-permute-start.17 = (bf16[32,3072]{1,0:T(8,128)(2,1)}, bf16[32,3072]{1,0:T(8,128)(2,1)S(1)}, u32[]{:S(2)}, u32[]{:S(2)}) collective-permute-start(bf16[32,3072]{1,0:T(8,128)(2,1)} %get-tuple-element.48), channel_id=1, source_target_pairs={{0,7},{1,6},{2,1},{3,0},{4,3},{5,2},{6,5},{7,4},{8,15},{9,14},{10,... | collective-permute-start | bytes 589832 | tf_op jit(solution)/shard_map/ppermute | solution.py:387
  106.8 12.5 %collective-permute-start.18 = (bf16[32,3072]{1,0:T(8,128)(2,1)}, bf16[32,3072]{1,0:T(8,128)(2,1)S(1)}, u32[]{:S(2)}, u32[]{:S(2)}) collective-permute-start(bf16[32,3072]{1,0:T(8,128)(2,1)} %get-tuple-element.49), channel_id=1, source_target_pairs={{0,2},{1,3},{2,4},{3,5},{4,6},{5,7},{6,0},{7,1},{8,10},{9,11},{10,... | collective-permute-start | bytes 589832 | tf_op jit(solution)/shard_map/ppermute | solution.py:387
  107.2 12.1 %collective-permute-start.19 = (bf16[32,3072]{1,0:T(8,128)(2,1)}, bf16[32,3072]{1,0:T(8,128)(2,1)S(1)}, u32[]{:S(2)}, u32[]{:S(2)}) collective-permute-start(bf16[32,3072]{1,0:T(8,128)(2,1)} %get-tuple-element.50), channel_id=1, source_target_pairs={{0,6},{1,7},{2,0},{3,1},{4,2},{5,3},{6,4},{7,5},{8,14},{9,15},{10,... | collective-permute-start | bytes 589832 | tf_op jit(solution)/shard_map/ppermute | solution.py:387
  115.3 8.4 %collective-permute-start.20 = (bf16[32,3072]{1,0:T(8,128)(2,1)}, bf16[32,3072]{1,0:T(8,128)(2,1)S(1)}, u32[]{:S(2)}, u32[]{:S(2)}) collective-permute-start(bf16[32,3072]{1,0:T(8,128)(2,1)} %get-tuple-element.51), channel_id=1, source_target_pairs={{0,1},{1,0},{2,3},{3,2},{4,5},{5,4},{6,7},{7,6},{8,9},{9,8},{10,11... | collective-permute-start | bytes 589832 | tf_op jit(solution)/shard_map/ppermute | solution.py:387
  125.0 11.8 %collective-permute-start.21 = (bf16[32,3072]{1,0:T(8,128)(2,1)S(1)}, bf16[32,3072]{1,0:T(8,128)(2,1)S(1)}, u32[]{:S(2)}, u32[]{:S(2)}) collective-permute-start(bf16[32,3072]{1,0:T(8,128)(2,1)S(1)} %add_convert_fusion.refs_0_), channel_id=1, source_target_pairs={{0,5},{1,4},{2,7},{3,6},{4,1},{5,0},{6,3},{7,2},{8,13},{9,12},{10,... | collective-permute-start | bytes 589832 | tf_op jit(solution)/shard_map/ppermute | solution.py:387
  128.2 15.3 %collective-permute-start.22 = (bf16[32,3072]{1,0:T(8,128)(2,1)S(1)}, bf16[32,3072]{1,0:T(8,128)(2,1)S(1)}, u32[]{:S(2)}, u32[]{:S(2)}) collective-permute-start(bf16[32,3072]{1,0:T(8,128)(2,1)S(1)} %add_convert_fusion.refs_0_), channel_id=1, source_target_pairs={{0,4},{1,5},{2,6},{3,7},{4,0},{5,1},{6,2},{7,3},{8,12},{9,13},{10,... | collective-permute-start | bytes 589832 | tf_op jit(solution)/shard_map/ppermute | solution.py:387
  129.5 16.7 %collective-permute-start.23 = (bf16[32,3072]{1,0:T(8,128)(2,1)S(1)}, bf16[32,3072]{1,0:T(8,128)(2,1)S(1)}, u32[]{:S(2)}, u32[]{:S(2)}) collective-permute-start(bf16[32,3072]{1,0:T(8,128)(2,1)S(1)} %add_convert_fusion.refs_0_), channel_id=1, source_target_pairs={{0,3},{1,2},{2,5},{3,4},{4,7},{5,6},{6,1},{7,0},{8,11},{9,10},{10,... | collective-permute-start | bytes 589832 | tf_op jit(solution)/shard_map/ppermute | solution.py:387
  133.0 13.1 %collective-permute-start.24 = (bf16[32,3072]{1,0:T(8,128)(2,1)S(1)}, bf16[32,3072]{1,0:T(8,128)(2,1)S(1)}, u32[]{:S(2)}, u32[]{:S(2)}) collective-permute-start(bf16[32,3072]{1,0:T(8,128)(2,1)S(1)} %add_convert_fusion.refs_0_), channel_id=1, source_target_pairs={{0,7},{1,6},{2,1},{3,0},{4,3},{5,2},{6,5},{7,4},{8,15},{9,14},{10,... | collective-permute-start | bytes 589832 | tf_op jit(solution)/shard_map/ppermute | solution.py:387
  135.1 11.4 %collective-permute-start.25 = (bf16[32,3072]{1,0:T(8,128)(2,1)S(1)}, bf16[32,3072]{1,0:T(8,128)(2,1)S(1)}, u32[]{:S(2)}, u32[]{:S(2)}) collective-permute-start(bf16[32,3072]{1,0:T(8,128)(2,1)S(1)} %add_convert_fusion.refs_0_), channel_id=1, source_target_pairs={{0,2},{1,3},{2,4},{3,5},{4,6},{5,7},{6,0},{7,1},{8,10},{9,11},{10,... | collective-permute-start | bytes 589832 | tf_op jit(solution)/shard_map/ppermute | solution.py:387
  136.8 9.7 %collective-permute-start.26 = (bf16[32,3072]{1,0:T(8,128)(2,1)S(1)}, bf16[32,3072]{1,0:T(8,128)(2,1)S(1)}, u32[]{:S(2)}, u32[]{:S(2)}) collective-permute-start(bf16[32,3072]{1,0:T(8,128)(2,1)S(1)} %add_convert_fusion.refs_0_), channel_id=1, source_target_pairs={{0,6},{1,7},{2,0},{3,1},{4,2},{5,3},{6,4},{7,5},{8,14},{9,15},{10,... | collective-permute-start | bytes 589832 | tf_op jit(solution)/shard_map/ppermute | solution.py:387
  143.5 7.2 %collective-permute-start.27 = (bf16[32,3072]{1,0:T(8,128)(2,1)S(1)}, bf16[32,3072]{1,0:T(8,128)(2,1)S(1)}, u32[]{:S(2)}, u32[]{:S(2)}) collective-permute-start(bf16[32,3072]{1,0:T(8,128)(2,1)S(1)} %add_convert_fusion.refs_0_), channel_id=1, source_target_pairs={{0,1},{1,0},{2,3},{3,2},{4,5},{5,4},{6,7},{7,6},{8,9},{9,8},{10,11... | collective-permute-start | bytes 589832 | tf_op jit(solution)/shard_map/ppermute | solution.py:387
  (5 other events, 3.4 us)

commit v2 on v1

v2 whole, which is shorter than its diff:
```python
import jax
import jax.numpy as jnp
import numpy as np
from jax import lax
from jax.experimental import pallas as pl
from jax.experimental.pallas import tpu as pltpu
from jax.sharding import Mesh
from jax.sharding import PartitionSpec as P

WIDTH_TOK = 256
HEAD = 128
LOCAL_HEADS = 3
WIDTH = HEAD * LOCAL_HEADS
COUNT = 256
TEXT = 512
MODEL = 3072
ROWS = COUNT // 8
AXES = ("x_lo", "z", "core", "y", "x_hi")
SIZES = (2, 8, 2, 4, 2)
PATCH = ("x_lo", "z", "core")
TENSOR = ("y", "x_hi")
SCALE = float(np.log2(np.e) / np.sqrt(128.0))
MIB = 1024 * 1024
EXTRA = 16
HALF = COUNT // 2
SPLIT = WIDTH // 2
FULL = pl.BlockSpec(memory_space=pltpu.VMEM)
SMEM = pl.BlockSpec(memory_space=pltpu.SMEM)


def params(mib=48):
    return pltpu.CompilerParams(vmem_limit_bytes=mib * MIB)


def cost(flops, nbytes, exps=0):
    return pl.CostEstimate(flops=flops, bytes_accessed=nbytes, transcendentals=exps)


def head_of(head):
    return slice(head * HEAD, (head + 1) * HEAD)


def qkv_kernel(lat, shift, scale, w, q_gain, k_gain, cosine, sine, q, k, v, normed):
    part = pl.program_id(0)

    @pl.when(part == 0)
    def _():
        x = lat[...].astype(jnp.float32)
        centred = x - jnp.mean(x, axis=-1, keepdims=True)
        spread = jnp.mean(centred * centred, axis=-1, keepdims=True)
        y = centred * lax.rsqrt(spread + 1e-06) * (1.0 + scale[...]) + shift[...]
        normed[...] = y.astype(jnp.bfloat16)

    out = jnp.dot(normed[...], w[0], preferred_element_type=jnp.float32)

    def rotated(gain):
        even = lax.broadcasted_iota(jnp.int32, (COUNT, HEAD), 1) % 2 == 0
        heads = []
        for head in range(LOCAL_HEADS):
            x = out[:, head_of(head)]
            x = x * lax.rsqrt(jnp.mean(x * x, axis=-1, keepdims=True) + 1e-06) * gain[...]
            other = jnp.where(even, pltpu.roll(x, HEAD - 1, 1), pltpu.roll(x, 1, 1))
            heads.append(x * cosine[...] + other * sine[...])
        return heads

    @pl.when(part == 0)
    def _():
        for head, x in enumerate(rotated(q_gain)):
            q[head_of(head), :] = (x * SCALE).T.astype(jnp.bfloat16)

    @pl.when(part == 1)
    def _():
        for head, x in enumerate(rotated(k_gain)):
            k[:, head_of(head)] = x.astype(jnp.bfloat16)

    @pl.when(part == 2)
    def _():
        v[...] = out.astype(jnp.bfloat16)


def whole_spec(shape):
    return pl.BlockSpec(shape, lambda i: (0,) * len(shape))


def at_spec(shape, offset=0):
    return pl.BlockSpec((1, *shape), lambda i: (i + offset, 0, 0))


def qkv_call(latents, shift, scale, w, q_gain, k_gain, cosine, sine):
    shape = lambda *dims: jax.ShapeDtypeStruct(dims, jnp.bfloat16)
    return pl.pallas_call(
        qkv_kernel,
        grid=(3,),
        in_specs=[
            whole_spec((COUNT, MODEL)),
            whole_spec((1, MODEL)),
            whole_spec((1, MODEL)),
            pl.BlockSpec((1, MODEL, WIDTH), lambda i: (i, 0, 0)),
            whole_spec((1, HEAD)),
            whole_spec((1, HEAD)),
            whole_spec((COUNT, HEAD)),
            whole_spec((COUNT, HEAD)),
        ],
        out_specs=[whole_spec((WIDTH, COUNT)), whole_spec((COUNT, WIDTH)), whole_spec((COUNT, WIDTH))],
        out_shape=[shape(WIDTH, COUNT), shape(COUNT, WIDTH), shape(COUNT, WIDTH)],
        scratch_shapes=[pltpu.VMEM((COUNT, MODEL), jnp.bfloat16)],
        compiler_params=params(60),
        cost_estimate=cost(2 * COUNT * MODEL * WIDTH * 3, 10 * MIB),
    )(
        latents,
        shift.reshape(1, MODEL),
        scale.reshape(1, MODEL),
        w,
        q_gain.reshape(1, HEAD),
        k_gain.reshape(1, HEAD),
        cosine,
        sine,
    )


def pick(values, rows):
    at = lax.broadcasted_iota(jnp.int32, (rows, COUNT), 0)
    out = jnp.zeros((rows, COUNT), jnp.float32)
    for n, value in enumerate(values):
        out = jnp.where(at == n, value, out)
    return out


def attend(q, pairs, state):
    scores = [jnp.dot(k, q, preferred_element_type=jnp.float32) for k, _ in pairs]
    top = jnp.max(scores[0], axis=0, keepdims=True)
    for s in scores[1:]:
        top = jnp.maximum(top, jnp.max(s, axis=0, keepdims=True))
    if state is not None:
        top = jnp.maximum(top, state[1])
    num, den = None, None
    for s, (_, v) in zip(scores, pairs):
        p = jnp.exp2(s - top)
        total = jnp.sum(p, axis=0, keepdims=True)
        part = lax.dot_general(
            v, p.astype(jnp.bfloat16), (((0,), (0,)), ((), ())), preferred_element_type=jnp.float32
        )
        num = part if num is None else num + part
        den = total if den is None else den + total
    if state is not None:
        keep = jnp.exp2(state[1] - top)
        num, den = num + keep * state[0], den + keep * state[2]
    return num, top, den


def store_state(num, ml, results):
    for head, result in enumerate(results):
        num[0, head_of(head), :] = result[0]
    ml[0] = pick([r[1] for r in results] + [r[2] for r in results], 8)


def load_state(num, ml):
    return [
        (num[0, head_of(h), :], ml[0, h : h + 1, :], ml[0, LOCAL_HEADS + h : LOCAL_HEADS + h + 1, :])
        for h in range(LOCAL_HEADS)
    ]


def first_kernel(q, k, v, text, own, num, ml):
    def run(pairs_of):
        results = []
        for head in range(LOCAL_HEADS):
            cols = head_of(head)
            results.append(attend(q[0, cols, :], pairs_of(cols), None))
        store_state(num, ml, results)

    @pl.when(pl.program_id(0) == 0)
    def _():
        run(lambda c: [(k[:, c], v[:, c]), (text[0, :, c], text[1, :, c])])

    @pl.when(pl.program_id(0) != 0)
    def _():
        run(lambda c: [(own[0, :, c], own[1, :, c])])


def state_shapes(blocks):
    return [
        jax.ShapeDtypeStruct((blocks, WIDTH, COUNT), jnp.float32),
        jax.ShapeDtypeStruct((blocks, 8, COUNT), jnp.float32),
    ]


def attend_cost(blocks):
    return cost(blocks * COUNT * COUNT * WIDTH * 4, 6 * MIB, blocks * COUNT * COUNT * LOCAL_HEADS)


def first_call(qs, k, v, text, own):
    return pl.pallas_call(
        first_kernel,
        grid=(4,),
        in_specs=[
            at_spec((WIDTH, COUNT)),
            whole_spec((COUNT, WIDTH)),
            whole_spec((COUNT, WIDTH)),
            whole_spec((2, TEXT, WIDTH)),
            whole_spec((2, COUNT, WIDTH)),
        ],
        out_specs=[at_spec((WIDTH, COUNT)), at_spec((8, COUNT))],
        out_shape=state_shapes(4),
        compiler_params=params(),
        cost_estimate=attend_cost(6),
    )(qs, k, v, text, own)


def next_kernel(q, left, right, num_in, ml_in, num, ml):
    states = load_state(num_in, ml_in)
    results = []
    for head in range(LOCAL_HEADS):
        c = head_of(head)
        pairs = [(left[0, :, c], left[1, :, c]), (right[0, :, c], right[1, :, c])]
        results.append(attend(q[0, c, :], pairs, states[head]))
    store_state(num, ml, results)


def next_call(qs, left, right, num, ml):
    return pl.pallas_call(
        next_kernel,
        grid=(4,),
        in_specs=[
            at_spec((WIDTH, COUNT)),
            whole_spec((2, COUNT, WIDTH)),
            whole_spec((2, COUNT, WIDTH)),
            at_spec((WIDTH, COUNT)),
            at_spec((8, COUNT)),
        ],
        out_specs=[at_spec((WIDTH, COUNT)), at_spec((8, COUNT))],
        out_shape=state_shapes(4),
        compiler_params=params(),
        cost_estimate=attend_cost(8),
    )(qs, left, right, num, ml)


def pack_message(message, results):
    logs = []
    for head, (num, top, den) in enumerate(results):
        message[head_of(head), :] = (num * (1.0 / den)).astype(jnp.bfloat16)
        logs.append(top + jnp.log2(den))
    parts = []
    for _ in range(3):
        rounded = [x.astype(jnp.bfloat16).astype(jnp.float32) for x in logs]
        parts += rounded
        logs = [x - r for x, r in zip(logs, rounded)]
    message[WIDTH:, :] = pick(parts, EXTRA).astype(jnp.bfloat16)


def open_message(message):
    stats = message[WIDTH:, :].astype(jnp.float32)
    row = lambda n: stats[n : n + 1, :]
    return [
        (message[head_of(h), :].astype(jnp.float32), row(h) + (row(h + 3) + row(h + 6)), 1.0)
        for h in range(LOCAL_HEADS)
    ]


def merge(states):
    top = states[0][1]
    for s in states[1:]:
        top = jnp.maximum(top, s[1])
    num, den = 0.0, 0.0
    for n, m, d in states:
        keep = jnp.exp2(m - top)
        num, den = num + keep * n, den + keep * d
    return num, top, den


def last_kernel(q, keys, values, num_in, ml_in, num, ml, message):
    states = load_state(num_in, ml_in)
    results = []
    for head in range(LOCAL_HEADS):
        c = head_of(head)
        results.append(attend(q[0, c, :], [(keys[:, c], values[:, c])], states[head]))

    @pl.when(pl.program_id(0) == 0)
    def _():
        pack_message(message, results)

    @pl.when(pl.program_id(0) == 1)
    def _():
        store_state(num, ml, results)


def last_call(qs, keys, values, num, ml, offset):
    back = lambda shape: pl.BlockSpec((1, *shape), lambda i: (offset + 1 - i, 0, 0))
    message = (WIDTH + EXTRA, COUNT)
    return pl.pallas_call(
        last_kernel,
        grid=(2,),
        in_specs=[
            back((WIDTH, COUNT)),
            whole_spec((COUNT, WIDTH)),
            whole_spec((COUNT, WIDTH)),
            back((WIDTH, COUNT)),
            back((8, COUNT)),
        ],
        out_specs=[
            whole_spec((1, WIDTH, COUNT)),
            whole_spec((1, 8, COUNT)),
            whole_spec(message),
        ],
        out_shape=state_shapes(1) + [jax.ShapeDtypeStruct(message, jnp.bfloat16)],
        compiler_params=params(),
        cost_estimate=attend_cost(2),
    )(qs, keys, values, num, ml)


def merge_kernel(num, ml, message, out):
    mine, other = load_state(num, ml), open_message(message)
    pack_message(out, [merge([a, b]) for a, b in zip(mine, other)])


def merge_call(num, ml, message):
    return pl.pallas_call(
        merge_kernel,
        in_specs=[FULL] * 3,
        out_specs=FULL,
        out_shape=jax.ShapeDtypeStruct((WIDTH + EXTRA, COUNT), jnp.bfloat16),
        compiler_params=params(),
        cost_estimate=cost(0, 2 * MIB),
    )(num, ml, message)


def settle_kernel(place, num, ml, near, far, kept, sent, attn):
    triples = zip(load_state(num, ml), open_message(near), open_message(far))
    for head, states in enumerate(triples):
        total, _, den = merge(states)
        attn[:, head_of(head)] = (total * (1.0 / den)).T.astype(jnp.bfloat16)
    x = place[4]
    kept[...] = attn[pl.ds(pl.multiple_of(x * HALF, HALF), HALF), :]
    sent[...] = attn[pl.ds(pl.multiple_of((1 - x) * HALF, HALF), HALF), :]


def settle_call(place, num, ml, near, far):
    return pl.pallas_call(
        settle_kernel,
        in_specs=[SMEM] + [FULL] * 4,
        out_specs=[FULL] * 2,
        out_shape=[jax.ShapeDtypeStruct((HALF, WIDTH), jnp.bfloat16)] * 2,
        scratch_shapes=[pltpu.VMEM((COUNT, WIDTH), jnp.bfloat16)],
        compiler_params=params(),
        cost_estimate=cost(0, 2 * MIB),
    )(place, num, ml, near, far)


def project_kernel(place, attn, other, w, w_x, w_core, own, plus, minus, two, full):
    first = place[5] == 0
    low, high = other[:, :SPLIT].astype(jnp.float32), other[:, SPLIT:].astype(jnp.float32)
    by_x = jnp.where(first, low, high).astype(jnp.bfloat16)
    by_core = jnp.where(first, high, low).astype(jnp.bfloat16)
    for at in range(0, MODEL, 768):
        cols = slice(at, at + 768)
        total = jnp.dot(attn[...], w[:, cols], preferred_element_type=jnp.float32)
        total += jnp.dot(by_x, w_x[:, cols], preferred_element_type=jnp.float32)
        total += jnp.dot(by_core, w_core[:, cols], preferred_element_type=jnp.float32)
        full[:, cols] = total.astype(jnp.bfloat16)
    for n, out in enumerate((own, plus, minus, two)):
        out[...] = full[pl.ds(pl.multiple_of(place[n] * ROWS, ROWS), ROWS), :]


def project_call(place, attn, other, w, w_x, w_core):
    return pl.pallas_call(
        project_kernel,
        in_specs=[SMEM] + [FULL] * 5,
        out_specs=[FULL] * 4,
        out_shape=[jax.ShapeDtypeStruct((ROWS, MODEL), jnp.bfloat16)] * 4,
        scratch_shapes=[pltpu.VMEM((HALF, MODEL), jnp.bfloat16)],
        compiler_params=params(),
        cost_estimate=cost(2 * COUNT * WIDTH * MODEL, 5 * MIB),
    )(place, attn, other, w, w_x, w_core)


def gather_kernel(place, *refs):
    out = refs[8]
    for n in range(8):
        out[pl.ds(pl.multiple_of(place[n] * ROWS, ROWS), ROWS), :] = refs[n][...]


def gather_call(place, pieces):
    return pl.pallas_call(
        gather_kernel,
        in_specs=[SMEM] + [FULL] * 8,
        out_specs=FULL,
        out_shape=jax.ShapeDtypeStruct((COUNT, MODEL), jnp.bfloat16),
        compiler_params=params(),
        cost_estimate=cost(0, 4 * MIB),
    )(place, *pieces)


def ring(value, axis, step):
    size = SIZES[AXES.index(axis)]
    return lax.ppermute(value, axis, [(i, (i + step) % size) for i in range(size)])


def tables(rows):
    row_pos = (rows // WIDTH_TOK).astype(jnp.float32)
    col_pos = (rows % WIDTH_TOK).astype(jnp.float32)
    omega = 10000.0 ** (-2.0 * np.arange(28) / 56.0)
    by_row = np.repeat(np.concatenate([np.zeros(8), omega, np.zeros(28)]), 2).astype(np.float32)
    by_col = np.repeat(np.concatenate([np.zeros(36), omega]), 2).astype(np.float32)
    angles = row_pos[:, None] * by_row[None, :] + col_pos[:, None] * by_col[None, :]
    sign = np.tile(np.array([-1.0, 1.0], np.float32), HEAD // 2)
    return jnp.cos(angles), jnp.sin(angles) * sign[None, :]


def shards(
    latents,
    token_rows,
    mod_shift,
    mod_scale,
    mod_gate,
    w_qkv,
    q_gain,
    k_gain,
    stale_kv,
    text_kv,
    w_out,
    b_out,
):
    after = lax.optimization_barrier
    x, y, core = lax.axis_index("x_hi"), lax.axis_index("y"), lax.axis_index("core")
    own = jnp.transpose(stale_kv, (1, 0, 2))
    r1, l1 = ring(own, "z", 1), ring(own, "z", -1)
    w_x = ring(lax.dynamic_slice_in_dim(w_out, core * SPLIT, SPLIT, 0), "x_hi", 1)

    cosine, sine = tables(token_rows)
    q, k, v = qkv_call(
        latents, mod_shift, mod_scale, jnp.transpose(w_qkv, (1, 0, 2)), q_gain, k_gain, cosine, sine
    )
    q_core = ring(q, "core", 1)
    q_x = ring(q, "x_lo", 1)
    q_both = lax.ppermute(q, ("x_lo", "core"), [(0, 3), (1, 2), (2, 1), (3, 0)])

    r1, l1, q = after((r1, l1, q))
    r2, l2 = ring(r1, "z", 1), ring(l1, "z", -1)
    text = jnp.transpose(text_kv, (1, 0, 2))
    qs = jnp.stack([q, q_core, q_x, q_both])
    num, ml = first_call(qs, k, v, text, own)

    r2, l2, num, w_x = after((r2, l2, num, w_x))
    r3, l3 = ring(r2, "z", 1), ring(l2, "z", -1)
    w_core = ring(w_x, "core", 1)
    num, ml = next_call(qs, r1, l1, num, ml)
    num, ml = next_call(qs, r2, l2, num, ml)

    r3, l3, num = after((r3, l3, num))
    far_k, far_v = ring(r3[0], "z", 1), ring(l3[1], "z", -1)
    num, ml = next_call(qs, r3, l3, num, ml)

    far_k, far_v, num, w_core = after((far_k, far_v, num, w_core))
    x_num, x_ml, x_msg = last_call(qs, far_k, far_v, num, ml, 2)
    x_msg = ring(x_msg, "core", 1)
    o_num, o_ml, o_msg = last_call(qs, far_k, far_v, num, ml, 0)
    o_msg = ring(o_msg, "core", 1)
    x_out = ring(merge_call(x_num, x_ml, x_msg), "x_lo", 1)

    place = jnp.stack([y, (y + 1) % 4, (y + 3) % 4, (y + 2) % 4, x, core]).astype(jnp.int32)
    kept, sent = settle_call(place, o_num, o_ml, o_msg, x_out)
    other = ring(sent, "x_hi", 1)
    mine, plus, minus, two = project_call(place, kept, other, w_out, w_x, w_core)
    parts = [ring(plus, "y", 1), ring(minus, "y", -1), ring(two, "y", 2)]
    rows = lax.dynamic_slice_in_dim(latents, x * HALF + y * ROWS, ROWS, 0).astype(jnp.float32)
    total = mine.astype(jnp.float32)
    for part in parts:
        total = total + part.astype(jnp.float32)
    piece = (rows + mod_gate * (total + b_out)).astype(jnp.bfloat16)

    steps = (1, -1, 2)
    beside = ring(piece, "x_hi", 1)
    pieces = [piece] + [ring(piece, "y", s) for s in steps]
    pieces += [beside] + [ring(beside, "y", s) for s in steps]
    come = [(y - s) % 4 for s in (0, *steps)]
    come = jnp.stack([4 * x + c for c in come] + [4 * (1 - x) + c for c in come]).astype(jnp.int32)
    return (gather_call(come, pieces), jnp.stack([k, v], axis=1))


def solution(mesh):
    fine = Mesh(mesh.devices.reshape(SIZES), AXES)
    return jax.shard_map(
        shards,
        mesh=fine,
        in_specs=(
            P(PATCH, None),
            P(PATCH),
            P(),
            P(),
            P(),
            P(None, None, TENSOR),
            P(),
            P(),
            P(PATCH, None, TENSOR),
            P(None, None, TENSOR),
            P(TENSOR, None),
            P(),
        ),
        out_specs=(P(PATCH, None), P(PATCH, None, TENSOR)),
        check_vma=False,
    )
```

time: 154 us -> 134 us (0.87); the launches traced: 152 us -> 134 us
  waiting for transfers between devices: 53.4 us -> 40 us
  starting transfers between devices: 47.5 us -> 41.9 us
    ppermute x14 -> x0, starting transfers between devices: 28.3 us -> none  [across(): return lax.ppermute(value, TENSOR, pairs)]
    ppermute x14 -> x0, waiting for transfers between devices: 23 us -> none  [across(): return lax.ppermute(value, TENSOR, pairs)]
    ppermute x13 -> x26, starting transfers between devices: 18.3 us -> 40.7 us  [ring(): lax.ppermute(value, axis, [(i, (i + step) % size) for i in range(size)])]
    ppermute x13 -> x26, waiting for transfers between devices: 27.2 us -> 37.5 us  [ring(): lax.ppermute(value, axis, [(i, (i + step) % size) for i in range(size)])]
    pallas_call x7 -> x8, Pallas kernels: 32.8 us -> 34.5 us  [the longest x3 15.3 us: next_call(): pl.pallas_call(next_kernel, grid=(4,), in_specs=[at_spec((WIDTH, COUNT)),...]
    unnamed x21 -> x29, local copies, waits for them, and re-layouts: 7.11 us -> 6.44 us
  transfers between devices with their start and end apart: 28 -> 27, of which waited for: 12 -> 11; matrix products, arithmetic and copies ran while one was open for 2% -> 5% of each run, Pallas kernels for 20% -> 24%
where the time goes in v2:
time: 134 us
  starting transfers between devices  41.9 us (31%)
  waiting for transfers between devices  40 us (30%)
  Pallas kernels  39.5 us (29%)
  local copies, waits for them, and re-layouts  8 us (6%)
  other arithmetic  3.66 us (3%)
    ppermute x26, starting transfers between devices, ring(): lax.ppermute(value, axis, [(i, (i + step) % size) for i in range(size)])  40.7 us
    ppermute x26, waiting for transfers between devices, ring(): lax.ppermute(value, axis, [(i, (i + step) % size) for i in range(size)])  37.5 us
    pallas_call x3, Pallas kernels, next_call(): pl.pallas_call(next_kernel, grid=(4,), in_specs=[at_spec((WIDTH, COUNT)),...  15.3 us
    pallas_call x1, Pallas kernels, qkv_call(): pl.pallas_call(qkv_kernel, grid=(3,), in_specs=[whole_spec((COUNT, MODEL)...  8.5 us
    unnamed x29, local copies, waits for them, and re-layouts  6.44 us
    pallas_call x2, Pallas kernels, last_call(): pl.pallas_call(last_kernel, grid=(2,), in_specs=[back((WIDTH, COUNT)), wh...  4.87 us
    pallas_call x1, Pallas kernels, first_call(): pl.pallas_call(first_kernel, grid=(4,), in_specs=[at_spec((WIDTH, COUNT))...  4.6 us
  transfers between devices with their start and end apart: 27, of which 11 were waited for; matrix products, arithmetic and copies ran while one was open for 5% of the time, Pallas kernels for 24%

profile of v2, /device:TPU:6, one launch (start us, length us, event | category | flops | bytes accessed | tf_op | source)
XLA Modules:
  0.0 134.1 jit_solution(4867736205806407339)
XLA Ops:
  1.7 2.0 %collective-permute-start = (bf16[2,256,384]{2,1,0:T(8,128)(2,1)S(1)}, bf16[2,256,384]{2,1,0:T(8,128)(2,1)S(1)}, u32[]{:S(2)}, u32[]{:S(2)}) collective-permute-start(bf16[2,256,384]{2,1,0:T(8,128)(2,1)S(1)} %bitcast.36), channel_id=1, source_target_pairs={{0,16},{16,32},{32,48},{48,64},{64,80},{80,96},{96,112},{112,0},{1... | collective-permute-start | bytes 1179656 | tf_op jit(solution)/shard_map/ppermute | solution.py:395
  3.7 4.0 %collective-permute-start.1 = (bf16[2,256,384]{2,1,0:T(8,128)(2,1)S(1)}, bf16[2,256,384]{2,1,0:T(8,128)(2,1)S(1)}, u32[]{:S(2)}, u32[]{:S(2)}) collective-permute-start(bf16[2,256,384]{2,1,0:T(8,128)(2,1)S(1)} %bitcast.37), channel_id=1, source_target_pairs={{0,112},{16,0},{32,16},{48,32},{64,48},{80,64},{96,80},{112,96},{1... | collective-permute-start | bytes 1179656 | tf_op jit(solution)/shard_map/ppermute | solution.py:395
  11.9 8.5 %shard_map.158 = (bf16[384,256]{1,0:T(8,128)(2,1)}, bf16[256,384]{1,0:T(8,128)(2,1)}, bf16[256,384]{1,0:T(8,128)(2,1)}) custom-call(bf16[256,3072]{1,0:T(8,128)(2,1)} %lat.1, f32[1,3072]{1,0:T(1,128)} %bitcast.46, f32[1,3072]{1,0:T(1,128)} %bitcast.47, bf16[3,3072,384]{2,1,0:T(8,128)(2,1)} %bitcast.41, f32[1,128]{1,0:T(1,128)} %bitcast.48, ...), custom_call_target="tpu_custom_call" | custom-call | flops 1811939328 | bytes 10485760 | tf_op jit(solution)/shard_map/pallas_call | solution.py:91
  20.7 3.2 %collective-permute-start.6 = (bf16[2,256,384]{2,1,0:T(8,128)(2,1)S(1)}, bf16[2,256,384]{2,1,0:T(8,128)(2,1)S(1)}, u32[]{:S(2)}, u32[]{:S(2)}) collective-permute-start(bf16[2,256,384]{2,1,0:T(8,128)(2,1)S(1)} %collective-permute-done.1.right), channel_id=1, source_target_pairs={{0,112},{16,0},{32,16},{48,32},{64,48},{80,64},{96,80},{112,96},{1... | collective-permute-start | bytes 1179656 | tf_op jit(solution)/shard_map/ppermute | solution.py:395
  26.3 15.3 %collective-permute-done.3 = bf16[384,256]{1,0:T(8,128)(2,1)S(1)} collective-permute-done((bf16[384,256]{1,0:T(8,128)(2,1)}, bf16[384,256]{1,0:T(8,128)(2,1)S(1)}, u32[]{:S(2)}, u32[]{:S(2)}) %collective-permute-start.3) | collective-permute-done | bytes 196640 | tf_op jit(solution)/shard_map/ppermute | solution.py:395
  41.6 2.5 %collective-permute-done.4 = bf16[384,256]{1,0:T(8,128)(2,1)S(1)} collective-permute-done((bf16[384,256]{1,0:T(8,128)(2,1)}, bf16[384,256]{1,0:T(8,128)(2,1)S(1)}, u32[]{:S(2)}, u32[]{:S(2)}) %collective-permute-start.4) | collective-permute-done | bytes 196640 | tf_op jit(solution)/shard_map/ppermute | solution.py:435
  44.2 4.6 %shard_map.159 = (f32[4,384,256]{2,1,0:T(8,128)S(1)}, f32[4,8,256]{2,1,0:T(8,128)S(1)}) custom-call(bf16[4,384,256]{2,1,0:T(8,128)(2,1)S(1)} %pad_maximum_fusion.q, bf16[256,384]{1,0:T(8,128)(2,1)S(1)} %copy-done.3, bf16[256,384]{1,0:T(8,128)(2,1)S(1)} %copy-done.4, bf16[2,512,384]{2,1,0:T(8,128)(2,1)S(1)} %bitcast.35, bf16[2,256,384]{2,1,0:T(8,128)(2,1)S(1)} %bitcast.38), custom_call_target="tpu_custom_call" | custom-call | flops 603979776 | bytes 6291456 | tf_op jit(solution)/shard_map/pallas_call | solution.py:193
  49.2 3.2 %collective-permute-start.9 = (bf16[2,256,384]{2,1,0:T(8,128)(2,1)S(1)}, bf16[2,256,384]{2,1,0:T(8,128)(2,1)S(1)}, u32[]{:S(2)}, u32[]{:S(2)}) collective-permute-start(bf16[2,256,384]{2,1,0:T(8,128)(2,1)S(1)} %collective-permute-done.6.right), channel_id=1, source_target_pairs={{0,112},{16,0},{32,16},{48,32},{64,48},{80,64},{96,80},{112,96},{1... | collective-permute-start | bytes 1179656 | tf_op jit(solution)/shard_map/ppermute | solution.py:395
  52.4 5.1 %shard_map.160 = (f32[4,384,256]{2,1,0:T(8,128)S(1)}, f32[4,8,256]{2,1,0:T(8,128)S(1)}) custom-call(bf16[4,384,256]{2,1,0:T(8,128)(2,1)S(1)} %pad_maximum_fusion.q, bf16[2,256,384]{2,1,0:T(8,128)(2,1)S(1)} %collective-permute-done.left, bf16[2,256,384]{2,1,0:T(8,128)(2,1)S(1)} %collective-permute-done.1.right, f32[4,384,256]{2,1,0:T(8,128)S(1)} %get-tuple-element.48.num_in, ...), custom_call_target="tpu_custom_call" | custom-call | flops 805306368 | bytes 6291456 | tf_op jit(solution)/shard_map/pallas_call | solution.py:221
  57.5 5.1 %shard_map.161 = (f32[4,384,256]{2,1,0:T(8,128)S(1)}, f32[4,8,256]{2,1,0:T(8,128)S(1)}) custom-call(bf16[4,384,256]{2,1,0:T(8,128)(2,1)S(1)} %pad_maximum_fusion.q, bf16[2,256,384]{2,1,0:T(8,128)(2,1)S(1)} %collective-permute-done.5.left, bf16[2,256,384]{2,1,0:T(8,128)(2,1)S(1)} %collective-permute-done.6.right, ...), custom_call_target="tpu_custom_call" | custom-call | flops 805306368 | bytes 6291456 | tf_op jit(solution)/shard_map/pallas_call | solution.py:221
  62.8 3.3 %collective-permute-start.11 = (bf16[256,384]{1,0:T(8,128)(2,1)S(1)}, bf16[256,384]{1,0:T(8,128)(2,1)S(1)}, u32[]{:S(2)}, u32[]{:S(2)}) collective-permute-start(bf16[256,384]{1,0:T(8,128)(2,1)S(1)} %slice_bitcast_fusion), channel_id=1, source_target_pairs={{0,112},{16,0},{32,16},{48,32},{64,48},{80,64},{96,80},{112,96},{1... | collective-permute-start | bytes 589832 | tf_op jit(solution)/shard_map/ppermute | solution.py:395
  66.1 5.1 %shard_map.162 = (f32[4,384,256]{2,1,0:T(8,128)S(1)}, f32[4,8,256]{2,1,0:T(8,128)S(1)}) custom-call(bf16[4,384,256]{2,1,0:T(8,128)(2,1)S(1)} %pad_maximum_fusion.q, bf16[2,256,384]{2,1,0:T(8,128)(2,1)S(1)} %collective-permute-done.8.left, bf16[2,256,384]{2,1,0:T(8,128)(2,1)S(1)} %collective-permute-done.9.right, ...), custom_call_target="tpu_custom_call" | custom-call | flops 805306368 | bytes 6291456 | tf_op jit(solution)/shard_map/pallas_call | solution.py:221
  71.3 2.1 %shard_map.164 = (f32[1,384,256]{2,1,0:T(8,128)S(1)}, f32[1,8,256]{2,1,0:T(8,128)S(1)}, bf16[400,256]{1,0:T(8,128)(2,1)S(1)}) custom-call(bf16[4,384,256]{2,1,0:T(8,128)(2,1)S(1)} %pad_maximum_fusion.q, bf16[256,384]{1,0:T(8,128)(2,1)S(1)} %collective-permute-done.10.keys, bf16[256,384]{1,0:T(8,128)(2,1)S(1)} %collective-permute-done.11.values, ...), custom_call_target="tpu_custom_call" | custom-call | flops 201326592 | bytes 6291456 | tf_op jit(solution)/shard_map/pallas_call | solution.py:290
  73.5 2.8 %shard_map.163 = (f32[1,384,256]{2,1,0:T(8,128)S(1)}, f32[1,8,256]{2,1,0:T(8,128)S(1)}, bf16[400,256]{1,0:T(8,128)(2,1)}) custom-call(bf16[4,384,256]{2,1,0:T(8,128)(2,1)S(1)} %pad_maximum_fusion.q, bf16[256,384]{1,0:T(8,128)(2,1)S(1)} %collective-permute-done.10.keys, bf16[256,384]{1,0:T(8,128)(2,1)S(1)} %collective-permute-done.11.values, ...), custom_call_target="tpu_custom_call" | custom-call | flops 201326592 | bytes 6291456 | tf_op jit(solution)/shard_map/pallas_call | solution.py:290
  77.6 1.9 %collective-permute-start.15 = (bf16[400,256]{1,0:T(8,128)(2,1)}, bf16[400,256]{1,0:T(8,128)(2,1)}, u32[]{:S(2)}, u32[]{:S(2)}) collective-permute-start(bf16[400,256]{1,0:T(8,128)(2,1)} %shard_map.165), channel_id=1, source_target_pairs={{0,128},{128,0},{1,129},{129,1},{2,130},{130,2},{3,131},{131,3},{4... | collective-permute-start | bytes 614408 | tf_op jit(solution)/shard_map/ppermute | solution.py:395
  79.6 5.5 %collective-permute-done.15.far = bf16[400,256]{1,0:T(8,128)(2,1)} collective-permute-done((bf16[400,256]{1,0:T(8,128)(2,1)}, bf16[400,256]{1,0:T(8,128)(2,1)}, u32[]{:S(2)}, u32[]{:S(2)}) %collective-permute-start.15) | collective-permute-done | bytes 204832 | tf_op jit(solution)/shard_map/ppermute | solution.py:395
  87.3 3.4 %collective-permute-start.16 = (bf16[128,384]{1,0:T(8,128)(2,1)S(1)}, bf16[128,384]{1,0:T(8,128)(2,1)S(1)}, u32[]{:S(2)}, u32[]{:S(2)}) collective-permute-start(bf16[128,384]{1,0:T(8,128)(2,1)S(1)} %get-tuple-element.70), channel_id=1, source_target_pairs={{0,1},{1,0},{2,3},{3,2},{4,5},{5,4},{6,7},{7,6},{8,9},{9,8},{10,11... | collective-permute-start | bytes 294920 | tf_op jit(solution)/shard_map/ppermute | solution.py:395
  90.7 2.8 %collective-permute-done.16.other = bf16[128,384]{1,0:T(8,128)(2,1)S(1)} collective-permute-done((bf16[128,384]{1,0:T(8,128)(2,1)S(1)}, bf16[128,384]{1,0:T(8,128)(2,1)S(1)}, u32[]{:S(2)}, u32[]{:S(2)}) %collective-permute-start.16) | collective-permute-done | bytes 98336 | tf_op jit(solution)/shard_map/ppermute | solution.py:395
  94.8 2.4 %shard_map.167 = (bf16[32,3072]{1,0:T(8,128)(2,1)S(1)}, bf16[32,3072]{1,0:T(8,128)(2,1)}, bf16[32,3072]{1,0:T(8,128)(2,1)}, bf16[32,3072]{1,0:T(8,128)(2,1)}) custom-call(s32[6]{0:T(128)S(1)} %stack.87.place, bf16[128,384]{1,0:T(8,128)(2,1)S(1)} %get-tuple-element.69.attn, bf16[128,384]{1,0:T(8,128)(2,1)S(1)} %collective-permute-done.16.other, ...), custom_call_target="tpu_custom_call" | custom-call | flops 603979776 | bytes 5242880 | tf_op jit(solution)/shard_map/pallas_call | solution.py:365
  97.9 1.6 %collective-permute-start.17 = (bf16[32,3072]{1,0:T(8,128)(2,1)}, bf16[32,3072]{1,0:T(8,128)(2,1)S(1)}, u32[]{:S(2)}, u32[]{:S(2)}) collective-permute-start(bf16[32,3072]{1,0:T(8,128)(2,1)} %get-tuple-element.73), channel_id=1, source_target_pairs={{0,2},{2,4},{4,6},{6,0},{1,3},{3,5},{5,7},{7,1},{8,10},{10,12},{12... | collective-permute-start | bytes 589832 | tf_op jit(solution)/shard_map/ppermute | solution.py:395
  99.5 1.7 %collective-permute-start.18 = (bf16[32,3072]{1,0:T(8,128)(2,1)}, bf16[32,3072]{1,0:T(8,128)(2,1)S(1)}, u32[]{:S(2)}, u32[]{:S(2)}) collective-permute-start(bf16[32,3072]{1,0:T(8,128)(2,1)} %get-tuple-element.74), channel_id=1, source_target_pairs={{0,6},{2,0},{4,2},{6,4},{1,7},{3,1},{5,3},{7,5},{8,14},{10,8},{12,... | collective-permute-start | bytes 589832 | tf_op jit(solution)/shard_map/ppermute | solution.py:395
  101.1 2.0 %collective-permute-start.19 = (bf16[32,3072]{1,0:T(8,128)(2,1)}, bf16[32,3072]{1,0:T(8,128)(2,1)S(1)}, u32[]{:S(2)}, u32[]{:S(2)}) collective-permute-start(bf16[32,3072]{1,0:T(8,128)(2,1)} %get-tuple-element.75), channel_id=1, source_target_pairs={{0,4},{2,6},{4,0},{6,2},{1,5},{3,7},{5,1},{7,3},{8,12},{10,14},{12... | collective-permute-start | bytes 589832 | tf_op jit(solution)/shard_map/ppermute | solution.py:395
  103.1 4.0 %collective-permute-done.17 = bf16[32,3072]{1,0:T(8,128)(2,1)S(1)} collective-permute-done((bf16[32,3072]{1,0:T(8,128)(2,1)}, bf16[32,3072]{1,0:T(8,128)(2,1)S(1)}, u32[]{:S(2)}, u32[]{:S(2)}) %collective-permute-start.17) | collective-permute-done | bytes 196640 | tf_op jit(solution)/shard_map/ppermute | solution.py:395
  107.1 2.7 %collective-permute-done.19 = bf16[32,3072]{1,0:T(8,128)(2,1)S(1)} collective-permute-done((bf16[32,3072]{1,0:T(8,128)(2,1)}, bf16[32,3072]{1,0:T(8,128)(2,1)S(1)}, u32[]{:S(2)}, u32[]{:S(2)}) %collective-permute-start.19) | collective-permute-done | bytes 196640 | tf_op jit(solution)/shard_map/ppermute | solution.py:395
  111.0 3.1 %collective-permute-start.23 = (bf16[32,3072]{1,0:T(8,128)(2,1)S(1)}, bf16[32,3072]{1,0:T(8,128)(2,1)S(1)}, u32[]{:S(2)}, u32[]{:S(2)}) collective-permute-start(bf16[32,3072]{1,0:T(8,128)(2,1)S(1)} %add_convert_fusion.refs_0_), channel_id=1, source_target_pairs={{0,1},{1,0},{2,3},{3,2},{4,5},{5,4},{6,7},{7,6},{8,9},{9,8},{10,11... | collective-permute-start | bytes 589832 | tf_op jit(solution)/shard_map/ppermute | solution.py:395
  115.3 2.1 %collective-permute-start.21 = (bf16[32,3072]{1,0:T(8,128)(2,1)S(1)}, bf16[32,3072]{1,0:T(8,128)(2,1)S(1)}, u32[]{:S(2)}, u32[]{:S(2)}) collective-permute-start(bf16[32,3072]{1,0:T(8,128)(2,1)S(1)} %add_convert_fusion.refs_0_), channel_id=1, source_target_pairs={{0,6},{2,0},{4,2},{6,4},{1,7},{3,1},{5,3},{7,5},{8,14},{10,8},{12,... | collective-permute-start | bytes 589832 | tf_op jit(solution)/shard_map/ppermute | solution.py:395
  119.5 2.1 %collective-permute-start.25 = (bf16[32,3072]{1,0:T(8,128)(2,1)S(1)}, bf16[32,3072]{1,0:T(8,128)(2,1)S(1)}, u32[]{:S(2)}, u32[]{:S(2)}) collective-permute-start(bf16[32,3072]{1,0:T(8,128)(2,1)S(1)} %collective-permute-done.23.refs_4_), channel_id=1, source_target_pairs={{0,6},{2,0},{4,2},{6,4},{1,7},{3,1},{5,3},{7,5},{8,14},{10,8},{12,... | collective-permute-start | bytes 589832 | tf_op jit(solution)/shard_map/ppermute | solution.py:395
  121.5 2.9 %collective-permute-done.20.refs_1_ = bf16[32,3072]{1,0:T(8,128)(2,1)S(1)} collective-permute-done((bf16[32,3072]{1,0:T(8,128)(2,1)S(1)}, bf16[32,3072]{1,0:T(8,128)(2,1)S(1)}, u32[]{:S(2)}, u32[]{:S(2)}) %collective-permute-start.20) | collective-permute-done | bytes 196640 | tf_op jit(solution)/shard_map/ppermute | solution.py:395
  124.4 1.8 %collective-permute-start.26 = (bf16[32,3072]{1,0:T(8,128)(2,1)S(1)}, bf16[32,3072]{1,0:T(8,128)(2,1)S(1)}, u32[]{:S(2)}, u32[]{:S(2)}) collective-permute-start(bf16[32,3072]{1,0:T(8,128)(2,1)S(1)} %collective-permute-done.23.refs_4_), channel_id=1, source_target_pairs={{0,4},{2,6},{4,0},{6,2},{1,5},{3,7},{5,1},{7,3},{8,12},{10,14},{12... | collective-permute-start | bytes 589832 | tf_op jit(solution)/shard_map/ppermute | solution.py:395
  128.5 1.7 %collective-permute-done.24.refs_5_ = bf16[32,3072]{1,0:T(8,128)(2,1)S(1)} collective-permute-done((bf16[32,3072]{1,0:T(8,128)(2,1)S(1)}, bf16[32,3072]{1,0:T(8,128)(2,1)S(1)}, u32[]{:S(2)}, u32[]{:S(2)}) %collective-permute-start.24) | collective-permute-done | bytes 196640 | tf_op jit(solution)/shard_map/ppermute | solution.py:395
  130.7 1.6 %collective-permute-done.26.refs_7_ = bf16[32,3072]{1,0:T(8,128)(2,1)S(1)} collective-permute-done((bf16[32,3072]{1,0:T(8,128)(2,1)S(1)}, bf16[32,3072]{1,0:T(8,128)(2,1)S(1)}, u32[]{:S(2)}, u32[]{:S(2)}) %collective-permute-start.26) | collective-permute-done | bytes 196640 | tf_op jit(solution)/shard_map/ppermute | solution.py:395
  132.3 1.8 %shard_map.168 = bf16[256,3072]{1,0:T(8,128)(2,1)} custom-call(s32[8]{0:T(128)S(1)} %stack.80.place, bf16[32,3072]{1,0:T(8,128)(2,1)S(1)} %add_convert_fusion.refs_0_, bf16[32,3072]{1,0:T(8,128)(2,1)S(1)} %collective-permute-done.20.refs_1_, bf16[32,3072]{1,0:T(8,128)(2,1)S(1)} %collective-permute-done.21.refs_2_, ...), custom_call_target="tpu_custom_call" | custom-call | bytes 4194304 | tf_op jit(solution)/shard_map/pallas_call | solution.py:383
  (72 shorter events, 21.4 us)
Async XLA Ops:
  0.6 10.0 %copy-start.10 = (f32[128]{0:T(128)S(1)}, f32[128]{0:T(128)}, u32[]{:S(2)}) copy-start(f32[128]{0:T(128)} %constant.100) | copy-start | bytes 1540
  1.7 18.8 %collective-permute-start = (bf16[2,256,384]{2,1,0:T(8,128)(2,1)S(1)}, bf16[2,256,384]{2,1,0:T(8,128)(2,1)S(1)}, u32[]{:S(2)}, u32[]{:S(2)}) collective-permute-start(bf16[2,256,384]{2,1,0:T(8,128)(2,1)S(1)} %bitcast.36), channel_id=1, source_target_pairs={{0,16},{16,32},{32,48},{48,64},{64,80},{80,96},{96,112},{112,0},{1... | collective-permute-start | bytes 1179656 | tf_op jit(solution)/shard_map/ppermute | solution.py:395
  3.7 16.8 %collective-permute-start.1 = (bf16[2,256,384]{2,1,0:T(8,128)(2,1)S(1)}, bf16[2,256,384]{2,1,0:T(8,128)(2,1)S(1)}, u32[]{:S(2)}, u32[]{:S(2)}) collective-permute-start(bf16[2,256,384]{2,1,0:T(8,128)(2,1)S(1)} %bitcast.37), channel_id=1, source_target_pairs={{0,112},{16,0},{32,16},{48,32},{64,48},{80,64},{96,80},{112,96},{1... | collective-permute-start | bytes 1179656 | tf_op jit(solution)/shard_map/ppermute | solution.py:395
  9.1 39.7 %collective-permute-start.7 = (bf16[192,3072]{1,0:T(8,128)(2,1)S(1)}, bf16[192,3072]{1,0:T(8,128)(2,1)S(1)}, u32[]{:S(2)}, u32[]{:S(2)}) collective-permute-start(bf16[192,3072]{1,0:T(8,128)(2,1)S(1)} %constant_dynamic-slice_fusion), channel_id=1, source_target_pairs={{0,1},{1,0},{2,3},{3,2},{4,5},{5,4},{6,7},{7,6},{8,9},{9,8},{10,11... | collective-permute-start | bytes 3538952 | tf_op jit(solution)/shard_map/ppermute | solution.py:395
  20.4 23.7 %copy-start.8 = (bf16[384,256]{1,0:T(8,128)(2,1)S(1)}, bf16[384,256]{1,0:T(8,128)(2,1)}, u32[]{:S(2)}) copy-start(bf16[384,256]{1,0:T(8,128)(2,1)} %get-tuple-element.40) | copy-start | bytes 589828
  20.4 23.8 %copy-start.3 = (bf16[256,384]{1,0:T(8,128)(2,1)S(1)}, bf16[256,384]{1,0:T(8,128)(2,1)}, u32[]{:S(2)}) copy-start(bf16[256,384]{1,0:T(8,128)(2,1)} %get-tuple-element.43.k) | copy-start | bytes 589828
  20.4 23.8 %copy-start.4 = (bf16[256,384]{1,0:T(8,128)(2,1)S(1)}, bf16[256,384]{1,0:T(8,128)(2,1)}, u32[]{:S(2)}) copy-start(bf16[256,384]{1,0:T(8,128)(2,1)} %get-tuple-element.44.v) | copy-start | bytes 589828
  20.4 3.4 %collective-permute-start.2 = (bf16[384,256]{1,0:T(8,128)(2,1)}, bf16[384,256]{1,0:T(8,128)(2,1)S(1)}, u32[]{:S(2)}, u32[]{:S(2)}) collective-permute-start(bf16[384,256]{1,0:T(8,128)(2,1)} %get-tuple-element.40), channel_id=1, source_target_pairs={{0,8},{8,0},{1,9},{9,1},{2,10},{10,2},{3,11},{11,3},{4,12},{12,4},... | collective-permute-start | bytes 589832 | tf_op jit(solution)/shard_map/ppermute | solution.py:395
  20.6 28.3 %collective-permute-start.5 = (bf16[2,256,384]{2,1,0:T(8,128)(2,1)S(1)}, bf16[2,256,384]{2,1,0:T(8,128)(2,1)S(1)}, u32[]{:S(2)}, u32[]{:S(2)}) collective-permute-start(bf16[2,256,384]{2,1,0:T(8,128)(2,1)S(1)} %collective-permute-done.left), channel_id=1, source_target_pairs={{0,16},{16,32},{32,48},{48,64},{64,80},{80,96},{96,112},{112,0},{1... | collective-permute-start | bytes 1179656 | tf_op jit(solution)/shard_map/ppermute | solution.py:395
  20.7 28.2 %collective-permute-start.6 = (bf16[2,256,384]{2,1,0:T(8,128)(2,1)S(1)}, bf16[2,256,384]{2,1,0:T(8,128)(2,1)S(1)}, u32[]{:S(2)}, u32[]{:S(2)}) collective-permute-start(bf16[2,256,384]{2,1,0:T(8,128)(2,1)S(1)} %collective-permute-done.1.right), channel_id=1, source_target_pairs={{0,112},{16,0},{32,16},{48,32},{64,48},{80,64},{96,80},{112,96},{1... | collective-permute-start | bytes 1179656 | tf_op jit(solution)/shard_map/ppermute | solution.py:395
  23.9 17.7 %collective-permute-start.3 = (bf16[384,256]{1,0:T(8,128)(2,1)}, bf16[384,256]{1,0:T(8,128)(2,1)S(1)}, u32[]{:S(2)}, u32[]{:S(2)}) collective-permute-start(bf16[384,256]{1,0:T(8,128)(2,1)} %get-tuple-element.40), channel_id=1, source_target_pairs={{0,128},{128,0},{1,129},{129,1},{2,130},{130,2},{3,131},{131,3},{4... | collective-permute-start | bytes 589832 | tf_op jit(solution)/shard_map/ppermute | solution.py:395
  23.9 20.2 %collective-permute-start.4 = (bf16[384,256]{1,0:T(8,128)(2,1)}, bf16[384,256]{1,0:T(8,128)(2,1)S(1)}, u32[]{:S(2)}, u32[]{:S(2)}) collective-permute-start(bf16[384,256]{1,0:T(8,128)(2,1)} %get-tuple-element.40), channel_id=1, source_target_pairs={{0,136},{8,128},{128,8},{136,0},{1,137},{9,129},{129,9},{137,1},{2... | collective-permute-start | bytes 589832 | tf_op jit(solution)/shard_map/ppermute | solution.py:435
  48.8 22.4 %collective-permute-start.12 = (bf16[192,3072]{1,0:T(8,128)(2,1)S(1)}, bf16[192,3072]{1,0:T(8,128)(2,1)S(1)}, u32[]{:S(2)}, u32[]{:S(2)}) collective-permute-start(bf16[192,3072]{1,0:T(8,128)(2,1)S(1)} %collective-permute-done.7.w_x), channel_id=1, source_target_pairs={{0,8},{8,0},{1,9},{9,1},{2,10},{10,2},{3,11},{11,3},{4,12},{12,4},... | collective-permute-start | bytes 3538952 | tf_op jit(solution)/shard_map/ppermute | solution.py:395
  49.0 13.6 %collective-permute-start.8 = (bf16[2,256,384]{2,1,0:T(8,128)(2,1)S(1)}, bf16[2,256,384]{2,1,0:T(8,128)(2,1)S(1)}, u32[]{:S(2)}, u32[]{:S(2)}) collective-permute-start(bf16[2,256,384]{2,1,0:T(8,128)(2,1)S(1)} %collective-permute-done.5.left), channel_id=1, source_target_pairs={{0,16},{16,32},{32,48},{48,64},{64,80},{80,96},{96,112},{112,0},{1... | collective-permute-start | bytes 1179656 | tf_op jit(solution)/shard_map/ppermute | solution.py:395
  49.2 13.5 %collective-permute-start.9 = (bf16[2,256,384]{2,1,0:T(8,128)(2,1)S(1)}, bf16[2,256,384]{2,1,0:T(8,128)(2,1)S(1)}, u32[]{:S(2)}, u32[]{:S(2)}) collective-permute-start(bf16[2,256,384]{2,1,0:T(8,128)(2,1)S(1)} %collective-permute-done.6.right), channel_id=1, source_target_pairs={{0,112},{16,0},{32,16},{48,32},{64,48},{80,64},{96,80},{112,96},{1... | collective-permute-start | bytes 1179656 | tf_op jit(solution)/shard_map/ppermute | solution.py:395
  62.7 8.5 %collective-permute-start.10 = (bf16[256,384]{1,0:T(8,128)(2,1)S(1)}, bf16[256,384]{1,0:T(8,128)(2,1)S(1)}, u32[]{:S(2)}, u32[]{:S(2)}) collective-permute-start(bf16[256,384]{1,0:T(8,128)(2,1)S(1)} %slice_bitcast_fusion.1), channel_id=1, source_target_pairs={{0,16},{16,32},{32,48},{48,64},{64,80},{80,96},{96,112},{112,0},{1... | collective-permute-start | bytes 589832 | tf_op jit(solution)/shard_map/ppermute | solution.py:395
  62.8 8.4 %collective-permute-start.11 = (bf16[256,384]{1,0:T(8,128)(2,1)S(1)}, bf16[256,384]{1,0:T(8,128)(2,1)S(1)}, u32[]{:S(2)}, u32[]{:S(2)}) collective-permute-start(bf16[256,384]{1,0:T(8,128)(2,1)S(1)} %slice_bitcast_fusion), channel_id=1, source_target_pairs={{0,112},{16,0},{32,16},{48,32},{64,48},{80,64},{96,80},{112,96},{1... | collective-permute-start | bytes 589832 | tf_op jit(solution)/shard_map/ppermute | solution.py:395
  73.4 20.2 %copy-start = (bf16[384,3072]{1,0:T(8,128)(2,1)S(1)}, bf16[384,3072]{1,0:T(8,128)(2,1)}, u32[]{:S(2)}) copy-start(bf16[384,3072]{1,0:T(8,128)(2,1)} %w.1) | copy-start | bytes 7077892
  73.4 3.4 %collective-permute-start.14 = (bf16[400,256]{1,0:T(8,128)(2,1)S(1)}, bf16[400,256]{1,0:T(8,128)(2,1)S(1)}, u32[]{:S(2)}, u32[]{:S(2)}) collective-permute-start(bf16[400,256]{1,0:T(8,128)(2,1)S(1)} %get-tuple-element.68), channel_id=1, source_target_pairs={{0,8},{8,0},{1,9},{9,1},{2,10},{10,2},{3,11},{11,3},{4,12},{12,4},... | collective-permute-start | bytes 614408 | tf_op jit(solution)/shard_map/ppermute | solution.py:395
  76.3 3.3 %collective-permute-start.13 = (bf16[400,256]{1,0:T(8,128)(2,1)}, bf16[400,256]{1,0:T(8,128)(2,1)}, u32[]{:S(2)}, u32[]{:S(2)}) collective-permute-start(bf16[400,256]{1,0:T(8,128)(2,1)} %get-tuple-element.65), channel_id=1, source_target_pairs={{0,8},{8,0},{1,9},{9,1},{2,10},{10,2},{3,11},{11,3},{4,12},{12,4},... | collective-permute-start | bytes 614408 | tf_op jit(solution)/shard_map/ppermute | solution.py:395
  77.6 7.5 %collective-permute-start.15 = (bf16[400,256]{1,0:T(8,128)(2,1)}, bf16[400,256]{1,0:T(8,128)(2,1)}, u32[]{:S(2)}, u32[]{:S(2)}) collective-permute-start(bf16[400,256]{1,0:T(8,128)(2,1)} %shard_map.165), channel_id=1, source_target_pairs={{0,128},{128,0},{1,129},{129,1},{2,130},{130,2},{3,131},{131,3},{4... | collective-permute-start | bytes 614408 | tf_op jit(solution)/shard_map/ppermute | solution.py:395
  87.3 6.2 %collective-permute-start.16 = (bf16[128,384]{1,0:T(8,128)(2,1)S(1)}, bf16[128,384]{1,0:T(8,128)(2,1)S(1)}, u32[]{:S(2)}, u32[]{:S(2)}) collective-permute-start(bf16[128,384]{1,0:T(8,128)(2,1)S(1)} %get-tuple-element.70), channel_id=1, source_target_pairs={{0,1},{1,0},{2,3},{3,2},{4,5},{5,4},{6,7},{7,6},{8,9},{9,8},{10,11... | collective-permute-start | bytes 294920 | tf_op jit(solution)/shard_map/ppermute | solution.py:395
  97.9 9.2 %collective-permute-start.17 = (bf16[32,3072]{1,0:T(8,128)(2,1)}, bf16[32,3072]{1,0:T(8,128)(2,1)S(1)}, u32[]{:S(2)}, u32[]{:S(2)}) collective-permute-start(bf16[32,3072]{1,0:T(8,128)(2,1)} %get-tuple-element.73), channel_id=1, source_target_pairs={{0,2},{2,4},{4,6},{6,0},{1,3},{3,5},{5,7},{7,1},{8,10},{10,12},{12... | collective-permute-start | bytes 589832 | tf_op jit(solution)/shard_map/ppermute | solution.py:395
  99.5 7.6 %collective-permute-start.18 = (bf16[32,3072]{1,0:T(8,128)(2,1)}, bf16[32,3072]{1,0:T(8,128)(2,1)S(1)}, u32[]{:S(2)}, u32[]{:S(2)}) collective-permute-start(bf16[32,3072]{1,0:T(8,128)(2,1)} %get-tuple-element.74), channel_id=1, source_target_pairs={{0,6},{2,0},{4,2},{6,4},{1,7},{3,1},{5,3},{7,5},{8,14},{10,8},{12,... | collective-permute-start | bytes 589832 | tf_op jit(solution)/shard_map/ppermute | solution.py:395
  101.1 8.7 %collective-permute-start.19 = (bf16[32,3072]{1,0:T(8,128)(2,1)}, bf16[32,3072]{1,0:T(8,128)(2,1)S(1)}, u32[]{:S(2)}, u32[]{:S(2)}) collective-permute-start(bf16[32,3072]{1,0:T(8,128)(2,1)} %get-tuple-element.75), channel_id=1, source_target_pairs={{0,4},{2,6},{4,0},{6,2},{1,5},{3,7},{5,1},{7,3},{8,12},{10,14},{12... | collective-permute-start | bytes 589832 | tf_op jit(solution)/shard_map/ppermute | solution.py:395
  111.0 7.3 %collective-permute-start.23 = (bf16[32,3072]{1,0:T(8,128)(2,1)S(1)}, bf16[32,3072]{1,0:T(8,128)(2,1)S(1)}, u32[]{:S(2)}, u32[]{:S(2)}) collective-permute-start(bf16[32,3072]{1,0:T(8,128)(2,1)S(1)} %add_convert_fusion.refs_0_), channel_id=1, source_target_pairs={{0,1},{1,0},{2,3},{3,2},{4,5},{5,4},{6,7},{7,6},{8,9},{9,8},{10,11... | collective-permute-start | bytes 589832 | tf_op jit(solution)/shard_map/ppermute | solution.py:395
  114.2 10.2 %collective-permute-start.20 = (bf16[32,3072]{1,0:T(8,128)(2,1)S(1)}, bf16[32,3072]{1,0:T(8,128)(2,1)S(1)}, u32[]{:S(2)}, u32[]{:S(2)}) collective-permute-start(bf16[32,3072]{1,0:T(8,128)(2,1)S(1)} %add_convert_fusion.refs_0_), channel_id=1, source_target_pairs={{0,2},{2,4},{4,6},{6,0},{1,3},{3,5},{5,7},{7,1},{8,10},{10,12},{12... | collective-permute-start | bytes 589832 | tf_op jit(solution)/shard_map/ppermute | solution.py:395
  115.3 13.1 %collective-permute-start.21 = (bf16[32,3072]{1,0:T(8,128)(2,1)S(1)}, bf16[32,3072]{1,0:T(8,128)(2,1)S(1)}, u32[]{:S(2)}, u32[]{:S(2)}) collective-permute-start(bf16[32,3072]{1,0:T(8,128)(2,1)S(1)} %add_convert_fusion.refs_0_), channel_id=1, source_target_pairs={{0,6},{2,0},{4,2},{6,4},{1,7},{3,1},{5,3},{7,5},{8,14},{10,8},{12,... | collective-permute-start | bytes 589832 | tf_op jit(solution)/shard_map/ppermute | solution.py:395
  117.4 11.1 %collective-permute-start.22 = (bf16[32,3072]{1,0:T(8,128)(2,1)S(1)}, bf16[32,3072]{1,0:T(8,128)(2,1)S(1)}, u32[]{:S(2)}, u32[]{:S(2)}) collective-permute-start(bf16[32,3072]{1,0:T(8,128)(2,1)S(1)} %add_convert_fusion.refs_0_), channel_id=1, source_target_pairs={{0,4},{2,6},{4,0},{6,2},{1,5},{3,7},{5,1},{7,3},{8,12},{10,14},{12... | collective-permute-start | bytes 589832 | tf_op jit(solution)/shard_map/ppermute | solution.py:395
  118.3 11.8 %collective-permute-start.24 = (bf16[32,3072]{1,0:T(8,128)(2,1)S(1)}, bf16[32,3072]{1,0:T(8,128)(2,1)S(1)}, u32[]{:S(2)}, u32[]{:S(2)}) collective-permute-start(bf16[32,3072]{1,0:T(8,128)(2,1)S(1)} %collective-permute-done.23.refs_4_), channel_id=1, source_target_pairs={{0,2},{2,4},{4,6},{6,0},{1,3},{3,5},{5,7},{7,1},{8,10},{10,12},{12... | collective-permute-start | bytes 589832 | tf_op jit(solution)/shard_map/ppermute | solution.py:395
  119.5 11.2 %collective-permute-start.25 = (bf16[32,3072]{1,0:T(8,128)(2,1)S(1)}, bf16[32,3072]{1,0:T(8,128)(2,1)S(1)}, u32[]{:S(2)}, u32[]{:S(2)}) collective-permute-start(bf16[32,3072]{1,0:T(8,128)(2,1)S(1)} %collective-permute-done.23.refs_4_), channel_id=1, source_target_pairs={{0,6},{2,0},{4,2},{6,4},{1,7},{3,1},{5,3},{7,5},{8,14},{10,8},{12,... | collective-permute-start | bytes 589832 | tf_op jit(solution)/shard_map/ppermute | solution.py:395
  124.4 7.9 %collective-permute-start.26 = (bf16[32,3072]{1,0:T(8,128)(2,1)S(1)}, bf16[32,3072]{1,0:T(8,128)(2,1)S(1)}, u32[]{:S(2)}, u32[]{:S(2)}) collective-permute-start(bf16[32,3072]{1,0:T(8,128)(2,1)S(1)} %collective-permute-done.23.refs_4_), channel_id=1, source_target_pairs={{0,4},{2,6},{4,0},{6,2},{1,5},{3,7},{5,1},{7,3},{8,12},{10,14},{12... | collective-permute-start | bytes 589832 | tf_op jit(solution)/shard_map/ppermute | solution.py:395
  (8 other events, 39.2 us)

commit v3 on v0

v3 whole, which is shorter than its diff:
```python
import functools

import jax
import jax.numpy as jnp
import numpy as np
from jax import lax
from jax.experimental import pallas as pl
from jax.experimental.pallas import tpu as pltpu
from jax.sharding import Mesh
from jax.sharding import PartitionSpec as P

WIDTH_TOK = 256
ROW_POS = 8192 // WIDTH_TOK
HEAD = 128
LOCAL_HEADS = 3
WIDTH = HEAD * LOCAL_HEADS
COUNT = 256
TEXT = 512
MODEL = 3072
ROWS = COUNT // 8
AXES = ("x_lo", "z", "core", "y", "x_hi")
SIZES = (2, 8, 2, 4, 2)
PATCH = ("x_lo", "z", "core")
TENSOR = ("y", "x_hi")
SCALE = float(np.log2(np.e) / np.sqrt(128.0))
MIB = 1024 * 1024
EXTRA = 16
HALF = COUNT // 2
SPLIT = WIDTH // 2
FULL = pl.BlockSpec(memory_space=pltpu.VMEM)
SMEM = pl.BlockSpec(memory_space=pltpu.SMEM)


def params(mib=48):
    return pltpu.CompilerParams(vmem_limit_bytes=mib * MIB)


def cost(flops, nbytes, exps=0):
    del flops, nbytes, exps
    return pl.CostEstimate(flops=1024, bytes_accessed=1024, transcendentals=0)


def head_of(head):
    return slice(head * HEAD, (head + 1) * HEAD)


def whole_spec(shape):
    return pl.BlockSpec(shape, lambda i: (0,) * len(shape))


def trig_parts():
    omega = 10000.0 ** (-2.0 * np.arange(28) / 56.0)
    by_row = np.repeat(np.concatenate([np.zeros(8), omega, np.zeros(28)]), 2).astype(np.float32)
    by_col = np.repeat(np.concatenate([np.zeros(36), omega]), 2).astype(np.float32)
    lanes = np.arange(HEAD)
    sign = np.where(lanes % 2 == 0, -1.0, 1.0)
    blocks = []
    for omegas, count, mine in ((by_row, ROW_POS, lanes < 72), (by_col, WIDTH_TOK, lanes >= 72)):
        angle = (np.arange(count, dtype=np.float32)[:, None] * omegas[None, :]).astype(np.float64)
        blocks.append(np.concatenate([np.cos(angle) * mine, np.sin(angle) * sign * mine], axis=1))
    rest = np.concatenate(blocks).astype(np.float32)
    parts = []
    for _ in range(3):
        parts.append(rest.astype(jnp.bfloat16))
        rest = rest - parts[-1].astype(np.float32)
    return np.concatenate(parts, axis=1)


def qkv_kernel(
    place, lat, w, w_out, rows, trig, shift, scale, q_gain, k_gain, q, k, v, w_half, x_buf, w_buf, half, sems
):
    copies = [pltpu.make_async_copy(lat, x_buf, sems.at[3])]
    copies += [pltpu.make_async_copy(w.at[n], w_buf.at[n], sems.at[n]) for n in range(3)]
    part = pl.ds(pl.multiple_of(place[2] * SPLIT, SPLIT), SPLIT)
    copies.append(pltpu.make_async_copy(w_out.at[part], half, sems.at[4]))
    for copy in copies:
        copy.start()

    at = lax.broadcasted_iota(jnp.int32, (ROW_POS + WIDTH_TOK, COUNT), 0)
    row_pos = lax.shift_right_logical(rows[...], 8)
    col_pos = jnp.bitwise_and(rows[...], WIDTH_TOK - 1) + ROW_POS
    hot = jnp.where((at == row_pos) | (at == col_pos), 1.0, 0.0).astype(jnp.bfloat16)
    table = lax.dot_general(hot, trig[...], (((0,), (0,)), ((), ())), preferred_element_type=jnp.float32)
    table = table[:, : 2 * HEAD] + (table[:, 2 * HEAD : 4 * HEAD] + table[:, 4 * HEAD :])
    cosine, sine = table[:, :HEAD], table[:, HEAD:]

    copies[0].wait()
    x = x_buf[...].astype(jnp.float32)
    centred = x - jnp.mean(x, axis=-1, keepdims=True)
    spread = jnp.mean(centred * centred, axis=-1, keepdims=True)
    y = centred * lax.rsqrt(spread + 1e-06) * (1.0 + scale[...]) + shift[...]
    normed = y.astype(jnp.bfloat16)
    even = lax.broadcasted_iota(jnp.int32, (COUNT, HEAD), 1) % 2 == 0

    def rotated(out, gain, factor):
        heads = []
        for head in range(LOCAL_HEADS):
            x = out[:, head_of(head)]
            x = x * lax.rsqrt(jnp.mean(x * x, axis=-1, keepdims=True) + 1e-06) * gain[...]
            other = jnp.where(even, pltpu.roll(x, HEAD - 1, 1), pltpu.roll(x, 1, 1))
            x = x * cosine + other * sine
            heads.append((x * factor if factor else x).astype(jnp.bfloat16))
        return heads

    for n, (ref, gain, factor) in enumerate(((q, q_gain, SCALE), (k, k_gain, None), (v, None, None))):
        copies[n + 1].wait()
        out = jnp.dot(normed, w_buf[n], preferred_element_type=jnp.float32)
        if gain is None:
            ref[...] = out.astype(jnp.bfloat16)
        else:
            for head, x in enumerate(rotated(out, gain, factor)):
                ref[:, head_of(head)] = x
        if n == 0:
            copies[4].wait()
            back = pltpu.make_async_copy(half, w_half, sems.at[5])
            back.start()
    back.wait()


def qkv_call(place, latents, w, w_out, rows, shift, scale, q_gain, k_gain):
    anywhere = pl.BlockSpec(memory_space=pl.ANY)
    trig = trig_parts()
    return pl.pallas_call(
        qkv_kernel,
        grid=(1,),
        in_specs=[
            SMEM,
            anywhere,
            anywhere,
            anywhere,
            whole_spec((1, COUNT)),
            whole_spec(trig.shape),
            whole_spec((1, MODEL)),
            whole_spec((1, MODEL)),
            whole_spec((1, HEAD)),
            whole_spec((1, HEAD)),
        ],
        out_specs=[whole_spec((COUNT, WIDTH))] * 3 + [anywhere],
        out_shape=[jax.ShapeDtypeStruct((COUNT, WIDTH), jnp.bfloat16)] * 3
        + [jax.ShapeDtypeStruct((SPLIT, MODEL), jnp.bfloat16)],
        scratch_shapes=[
            pltpu.VMEM((COUNT, MODEL), jnp.bfloat16),
            pltpu.VMEM((3, MODEL, WIDTH), jnp.bfloat16),
            pltpu.VMEM((SPLIT, MODEL), jnp.bfloat16),
            pltpu.SemaphoreType.DMA((6,)),
        ],
        compiler_params=params(60),
        cost_estimate=cost(2 * COUNT * MODEL * WIDTH * 3, 10 * MIB),
    )(
        place,
        latents,
        w,
        w_out,
        rows.reshape(1, COUNT),
        jnp.asarray(trig),
        shift.reshape(1, MODEL),
        scale.reshape(1, MODEL),
        q_gain.reshape(1, HEAD),
        k_gain.reshape(1, HEAD),
    )


def attend(q, pairs, state=None):
    scores = []
    for k, _ in pairs:
        s = lax.dot_general(q, k, (((1,), (1,)), ((), ())), preferred_element_type=jnp.float32)
        scores.append([s[:, at : at + HEAD] for at in range(0, s.shape[1], HEAD)])
    top = None
    for piece in sum(scores, []):
        top = piece if top is None else jnp.maximum(top, piece)
    top = jnp.broadcast_to(jnp.max(top, axis=1, keepdims=True), top.shape)
    if state is not None:
        top = jnp.maximum(top, state[1])
    total = None
    for pieces, (_, v) in zip(scores, pairs):
        p = [jnp.exp2(s - top).astype(jnp.bfloat16) for s in pieces]
        wide = jnp.concatenate([v, jnp.ones_like(v)], axis=1)
        part = jnp.dot(jnp.concatenate(p, axis=1), wide, preferred_element_type=jnp.float32)
        total = part if total is None else total + part
    num, den = total[:, :HEAD], total[:, HEAD:]
    if state is not None:
        keep = jnp.exp2(state[1] - top)
        num, den = num + keep * state[0], den + keep * state[2]
    return num, top, den


def store_state(refs, cols, result, rows=slice(None)):
    for ref, value in zip(refs, result):
        ref[rows, cols] = value


def load_state(refs, cols, rows=slice(None)):
    return [ref[rows, cols] for ref in refs]


def both(pair, cols):
    return [(ref[0, :, cols], ref[1, :, cols]) for ref in pair]


HEADS = [head_of(n) for n in range(LOCAL_HEADS)]


def near_kernel(q0, q1, k, v, text, own, right, left, *state):
    for c in HEADS:
        ring_pairs = both((right, left), c)
        first = [(k[:, c], v[:, c]), (text[0, :, c], text[1, :, c])]
        store_state(state, c, attend(q0[:, c], first + ring_pairs), slice(0, COUNT))
        second = both((own,), c) + ring_pairs
        store_state(state, c, attend(q1[:, c], second), slice(COUNT, 2 * COUNT))


def far_kernel(q0, q1, *refs):
    blocks, state = refs[:-3], refs[-3:]
    for c in HEADS:
        q = jnp.concatenate([q0[:, c], q1[:, c]], axis=0)
        store_state(state, c, attend(q, both(blocks, c)))


def next_kernel(q0, q1, *refs):
    blocks, given, state = refs[:-6], refs[-6:-3], refs[-3:]
    for c in HEADS:
        q = jnp.concatenate([q0[:, c], q1[:, c]], axis=0)
        store_state(state, c, attend(q, both(blocks, c), load_state(given, c)))


def state_shapes(rows):
    return [jax.ShapeDtypeStruct((rows, WIDTH), jnp.float32)] * 3


def attend_cost(blocks):
    return cost(blocks * COUNT * COUNT * WIDTH * 4, 6 * MIB, blocks * COUNT * COUNT * LOCAL_HEADS)


def attend_call(kernel, blocks, *args):
    call = pl.pallas_call(
        kernel,
        in_specs=[FULL] * len(args),
        out_specs=[FULL] * 3,
        out_shape=state_shapes(2 * COUNT),
        compiler_params=params(24),
        cost_estimate=attend_cost(blocks),
    )
    return list(call(*args))


def pack(num, top, den):
    log = (top + jnp.log2(den)).T[:EXTRA, :]
    row = lax.broadcasted_iota(jnp.int32, log.shape, 0)
    parts = jnp.zeros_like(log)
    for n in range(3):
        rounded = log.astype(jnp.bfloat16).astype(jnp.float32)
        parts = jnp.where(row == n, rounded, parts)
        log = log - rounded
    return jnp.concatenate([num * (1.0 / den), parts], axis=0).astype(jnp.bfloat16)


def unpack(message):
    value = message[:HALF, :].astype(jnp.float32)
    stats = message[HALF:, :].astype(jnp.float32)
    log = stats[0:1, :] + (stats[1:2, :] + stats[2:3, :])
    return value, jnp.broadcast_to(log, (HALF, HEAD)).T, 1.0


def merge(*states):
    top = states[0][1]
    for s in states[1:]:
        top = jnp.maximum(top, s[1])
    num, den = 0.0, 0.0
    for n, m, d in states:
        keep = jnp.exp2(m - top)
        num, den = num + keep * n, den + keep * d
    return num, top, den


def last_kernel(q0, q1, keys, values, *refs):
    given, state, message = refs[:3], refs[3:6], refs[6]
    for c in HEADS:
        pairs = [(keys[:, c], values[:, c])]
        result = attend(q1[:, c], pairs, load_state(given, c, slice(COUNT, 2 * COUNT)))
        for n in range(2):
            message[n, :, c] = pack(*[a[n * HALF : (n + 1) * HALF] for a in result])
    for c in HEADS:
        pairs = [(keys[:, c], values[:, c])]
        store_state(state, c, attend(q0[:, c], pairs, load_state(given, c, slice(0, COUNT))))


def last_call(q0, q1, keys, values, *state):
    message = jax.ShapeDtypeStruct((2, HALF + EXTRA, WIDTH), jnp.bfloat16)
    *state, message = pl.pallas_call(
        last_kernel,
        in_specs=[FULL] * 7,
        out_specs=[FULL] * 4,
        out_shape=state_shapes(COUNT) + [message],
        compiler_params=params(24),
        cost_estimate=attend_cost(2),
    )(q0, q1, keys, values, *state)
    return state, message


def merge_kernel(place, *refs):
    swap = place[0] == 1
    for block in range(2):
        state, message = refs[4 * block : 4 * block + 3], refs[4 * block + 3]
        mine, other = refs[8 + 2 * block : 10 + 2 * block]
        for c in HEADS:
            halves = []
            for n in range(2):
                part = load_state(state, c, slice(n * HALF, (n + 1) * HALF))
                both_cores = merge(part, unpack(message[n, :, c]))
                halves.append(pack(*both_cores).astype(jnp.float32))
            mine[:, c] = jnp.where(swap, halves[1], halves[0]).astype(jnp.bfloat16)
            other[:, c] = jnp.where(swap, halves[0], halves[1]).astype(jnp.bfloat16)


def merge_call(place, *args):
    return pl.pallas_call(
        merge_kernel,
        in_specs=[SMEM] + [FULL] * 8,
        out_specs=[FULL] * 4,
        out_shape=[jax.ShapeDtypeStruct((HALF + EXTRA, WIDTH), jnp.bfloat16)] * 4,
        compiler_params=params(24),
        cost_estimate=cost(0, 4 * MIB),
    )(place, *args)


def project_kernel(place, *refs):
    messages, (w, w_x, w_core) = refs[:4], refs[4:7]
    own, plus, minus, two, attn, full = refs[7:]
    y, first = place[1], place[2] == 0
    for n in range(2):
        for head in range(LOCAL_HEADS):
            c = head_of(head)
            num, _, den = merge(*[unpack(m[:, c]) for m in messages[2 * n : 2 * n + 2]])
            attn[:, head_of(LOCAL_HEADS * n + head)] = (num * (1.0 / den)).astype(jnp.bfloat16)
    low = attn[:, WIDTH : WIDTH + SPLIT].astype(jnp.float32)
    high = attn[:, WIDTH + SPLIT :].astype(jnp.float32)
    by_x = jnp.where(first, low, high).astype(jnp.bfloat16)
    by_core = jnp.where(first, high, low).astype(jnp.bfloat16)
    for at in range(0, MODEL, 768):
        cols = slice(at, at + 768)
        total = jnp.dot(attn[:, :WIDTH], w[:, cols], preferred_element_type=jnp.float32)
        total += jnp.dot(by_x, w_x[:, cols], preferred_element_type=jnp.float32)
        total += jnp.dot(by_core, w_core[:, cols], preferred_element_type=jnp.float32)
        full[:, cols] = total.astype(jnp.bfloat16)
    for n, out in enumerate((own, plus, minus, two)):
        to = lax.rem(y + (0, 1, 3, 2)[n], 4)
        out[...] = full[pl.ds(pl.multiple_of(to * ROWS, ROWS), ROWS), :]


def project_call(place, messages, weights):
    return pl.pallas_call(
        project_kernel,
        in_specs=[SMEM] + [FULL] * 7,
        out_specs=[FULL] * 4,
        out_shape=[jax.ShapeDtypeStruct((ROWS, MODEL), jnp.bfloat16)] * 4,
        scratch_shapes=[
            pltpu.VMEM((HALF, 2 * WIDTH), jnp.bfloat16),
            pltpu.VMEM((HALF, MODEL), jnp.bfloat16),
        ],
        compiler_params=params(24),
        cost_estimate=cost(2 * COUNT * WIDTH * MODEL, 5 * MIB),
    )(place, *messages, *weights)


def put_kernel(offsets, place, *refs):
    out, sems = refs[-2:]
    x, y = place[0], place[1]
    copies = []
    for n, (flip, step) in enumerate(offsets):
        half = 1 - x if flip else x
        at = half * HALF + lax.rem(y + 4 - step, 4) * ROWS
        rows = pl.ds(pl.multiple_of(at, ROWS), ROWS)
        copies.append(pltpu.make_async_copy(refs[n], out.at[rows], sems.at[n]))
    for copy in copies:
        copy.start()
    for copy in copies:
        copy.wait()


def put_call(place, offsets, pieces, out=None):
    anywhere = pl.BlockSpec(memory_space=pl.ANY)
    count = len(pieces)
    more = [] if out is None else [out]
    return pl.pallas_call(
        functools.partial(put_kernel, offsets),
        in_specs=[SMEM] + [FULL] * count + [anywhere] * len(more),
        out_specs=anywhere,
        out_shape=jax.ShapeDtypeStruct((COUNT, MODEL), jnp.bfloat16),
        input_output_aliases={count + 1: 0} if more else {},
        scratch_shapes=[pltpu.SemaphoreType.DMA((count,))],
        compiler_params=params(24),
        cost_estimate=cost(0, 4 * MIB),
    )(place, *pieces, *more)


def ring(value, axis, step):
    size = SIZES[AXES.index(axis)]
    return lax.ppermute(value, axis, [(i, (i + step) % size) for i in range(size)])


def crossed(value, axes):
    return lax.ppermute(value, axes, [(i, 3 - i) for i in range(4)])


def shards(
    latents,
    token_rows,
    mod_shift,
    mod_scale,
    mod_gate,
    w_qkv,
    q_gain,
    k_gain,
    stale_kv,
    text_kv,
    w_out,
    b_out,
):
    after = lax.optimization_barrier
    x, y, core = lax.axis_index("x_hi"), lax.axis_index("y"), lax.axis_index("core")
    place = jnp.stack([x, y, core]).astype(jnp.int32)
    own = jnp.transpose(stale_kv, (1, 0, 2))
    r1, l1 = ring(own, "z", 1), ring(own, "z", -1)

    w = jnp.transpose(w_qkv, (1, 0, 2))
    q, k, v, w_half = qkv_call(
        place, latents, w, w_out, token_rows, mod_shift, mod_scale, q_gain, k_gain
    )
    q_core, q_x = ring(q, "core", 1), ring(q, "x_lo", 1)
    q_both = ring(q_x, "core", 1)
    w_half, q_x = after((w_half, q_x))
    w_x = ring(w_half, "x_hi", 1)

    r1, l1, q = after((r1, l1, q))
    r2, l2 = ring(r1, "z", 1), ring(l1, "z", -1)
    text = jnp.transpose(text_kv, (1, 0, 2))
    near = attend_call(near_kernel, 8, q, q_core, k, v, text, own, r1, l1)

    r2, l2, near[0], q_both = after((r2, l2, near[0], q_both))
    r3, l3 = ring(r2, "z", 1), ring(l2, "z", -1)
    near = attend_call(next_kernel, 4, q, q_core, r2, l2, *near)
    far = attend_call(far_kernel, 10, q_x, q_both, own, r1, l1, r2, l2)

    r3, l3, near[0], far[0] = after((r3, l3, near[0], far[0]))
    far_k, far_v = ring(r3[0], "z", 1), ring(l3[1], "z", -1)
    far = attend_call(next_kernel, 4, q_x, q_both, r3, l3, *far)
    near = attend_call(next_kernel, 4, q, q_core, r3, l3, *near)

    far_k, far_v, near[0], far[0] = after((far_k, far_v, near[0], far[0]))
    x_state, x_msg = last_call(q_x, q_both, far_k, far_v, *far)
    x_msg = ring(x_msg, "core", 1)
    o_state, o_msg = last_call(q, q_core, far_k, far_v, *near)
    w_x, o_msg = after((w_x, o_msg))
    w_core = ring(w_x, "core", 1)
    o_msg = ring(o_msg, "core", 1)
    x_mine, x_other, o_mine, o_other = merge_call(place, *x_state, x_msg, *o_state, o_msg)
    from_hi = ring(o_other, "x_hi", 1)
    from_x = ring(x_mine, "x_lo", 1)
    from_both = crossed(x_other, ("x_lo", "x_hi"))

    mine, plus, minus, two = project_call(
        place, (o_mine, from_x, from_hi, from_both), (w_out, w_x, w_core)
    )
    parts = [ring(two, "y", 2), ring(plus, "y", 1), ring(minus, "y", -1)]
    rows = lax.dynamic_slice_in_dim(latents, x * HALF + y * ROWS, ROWS, 0).astype(jnp.float32)
    total = mine.astype(jnp.float32)
    for part in parts:
        total = total + part.astype(jnp.float32)
    piece = (rows + mod_gate * (total + b_out)).astype(jnp.bfloat16)

    beside, plus = ring(piece, "x_hi", 1), ring(piece, "y", 1)
    minus, two = ring(piece, "y", -1), ring(piece, "y", 2)
    early = [((0, 0), piece), ((1, 0), beside), ((0, 1), plus), ((0, -1), minus), ((0, 2), two)]
    out = put_call(place, [e[0] for e in early], [e[1] for e in early])
    late = [
        ((1, 1), ring(plus, "x_hi", 1)),
        ((1, -1), ring(minus, "x_hi", 1)),
        ((1, 2), ring(beside, "y", 2)),
    ]
    out = put_call(place, [e[0] for e in late], [e[1] for e in late], out)
    return (out, jnp.stack([k, v], axis=1))


def solution(mesh):
    fine = Mesh(mesh.devices.reshape(SIZES), AXES)
    return jax.shard_map(
        shards,
        mesh=fine,
        in_specs=(
            P(PATCH, None),
            P(PATCH),
            P(),
            P(),
            P(),
            P(None, None, TENSOR),
            P(),
            P(),
            P(PATCH, None, TENSOR),
            P(None, None, TENSOR),
            P(TENSOR, None),
            P(),
        ),
        out_specs=(P(PATCH, None), P(PATCH, None, TENSOR)),
        check_vma=False,
    )
```

time: 251 us -> 113 us (0.45)
  waiting for transfers between devices: 139 us -> 38 us
  starting transfers between devices: 0.08 us -> 42.7 us
  local copies, waits for them, and re-layouts: 35.1 us -> 2.38 us
  other arithmetic: 29.5 us -> 1.78 us
  matrix products: 27 us -> 0 us
  Pallas kernels: 0 us -> 25.5 us
  between operations: 14.3 us -> 1.06 us
    psum x1 -> x0, waiting for transfers between devices: 97.9 us -> none  [shards(): lax.psum(projected.astype(jnp.bfloat16), 'tensor').astype(jnp.float32)]
    ppermute x0 -> x28, starting transfers between devices: none -> 42.7 us  [the longest x27 39.9 us: ring(): lax.ppermute(value, axis, [(i, (i + step) % size) for i in range(size)])]
    all_gather x1 -> x0, waiting for transfers between devices: 41.5 us -> none  [shards(): gathered = lax.all_gather(stale_kv, 'patch', axis=0, tiled=True)]
    ppermute x0 -> x28, waiting for transfers between devices: none -> 38 us  [the longest x27 35.7 us: ring(): lax.ppermute(value, axis, [(i, (i + step) % size) for i in range(size)])]
    dot_general x8 -> x0, matrix products: 27 us -> none  [the longest x3 9.8 us: head_out(): jnp.dot(weights.astype(jnp.bfloat16), head_cols(all_v, head), preferred_e...]
    pallas_call x0 -> x12, Pallas kernels: none -> 25.5 us  [the longest x5 9.55 us: attend_call(): return list(call(*args))]
    unnamed x29 -> x19, local copies, waits for them, and re-layouts: 14.3 us -> 2.33 us
    squeeze x4 -> x2, local copies, waits for them, and re-layouts: 10.2 us -> 0.04 us  [shards(): far_k, far_v = (ring(r3[0], 'z', 1), ring(l3[1], 'z', -1))]
  transfers between devices with their start and end apart: 2 -> 28, of which waited for: 2 -> 18; matrix products, arithmetic and copies ran while one was open for 17% -> 2% of each run, Pallas kernels for 0% -> 20%
where the time goes in v3:
time: 113 us; the launch traced here: 111 us
  starting transfers between devices  42.7 us (38%)
  waiting for transfers between devices  38 us (34%)
  Pallas kernels  25.5 us (23%)
  local copies, waits for them, and re-layouts  2.38 us (2%)
  other arithmetic  1.78 us (2%)
    ppermute x27, starting transfers between devices, ring(): lax.ppermute(value, axis, [(i, (i + step) % size) for i in range(size)])  39.9 us
    ppermute x27, waiting for transfers between devices, ring(): lax.ppermute(value, axis, [(i, (i + step) % size) for i in range(size)])  35.7 us
    pallas_call x5, Pallas kernels, attend_call(): return list(call(*args))  9.55 us
    pallas_call x1, Pallas kernels, qkv_call(): pl.pallas_call(qkv_kernel, grid=(1,), in_specs=[SMEM, anywhere, anywhere,...  8.16 us
    pallas_call x2, Pallas kernels, put_call(): pl.pallas_call(functools.partial(put_kernel, offsets), in_specs=[SMEM] +...  2.91 us
    ppermute x1, starting transfers between devices, crossed(): return lax.ppermute(value, axes, [(i, 3 - i) for i in range(4)])  2.76 us
    unnamed x19, local copies, waits for them, and re-layouts  2.33 us
    ppermute x1, waiting for transfers between devices, crossed(): return lax.ppermute(value, axes, [(i, 3 - i) for i in range(4)])  2.27 us
  transfers between devices with their start and end apart: 28, of which 18 were waited for; matrix products, arithmetic and copies ran while one was open for 2% of the time, Pallas kernels for 20%

profile of v3, /device:TPU:6, one launch (start us, length us, event | category | flops | bytes accessed | tf_op | source)
XLA Modules:
  0.0 111.3 jit_solution(13704500185066525922)
XLA Ops:
  1.7 5.9 %collective-permute-start.2 = (bf16[2,256,384]{2,1,0:T(8,128)(2,1)S(1)}, bf16[2,256,384]{2,1,0:T(8,128)(2,1)S(1)}, u32[]{:S(2)}, u32[]{:S(2)}) collective-permute-start(bf16[2,256,384]{2,1,0:T(8,128)(2,1)S(1)} %bitcast.21), channel_id=1, source_target_pairs={{0,112},{16,0},{32,16},{48,32},{64,48},{80,64},{96,80},{112,96},{1... | collective-permute-start | bytes 1179656 | tf_op jit(solution)/shard_map/ppermute | solution.py:398
  8.3 8.2 %shard_map.140 = (bf16[256,384]{1,0:T(8,128)(2,1)}, bf16[256,384]{1,0:T(8,128)(2,1)}, bf16[256,384]{1,0:T(8,128)(2,1)}, bf16[192,3072]{1,0:T(8,128)(2,1)}) custom-call(s32[3]{0:T(128)} %pad_add_fusion.place, bf16[256,3072]{1,0:T(8,128)(2,1)} %lat.1, bf16[3,3072,384]{2,1,0:T(8,128)(2,1)} %bitcast.28, bf16[384,3072]{1,0:T(8,128)(2,1)} %refs_4_.1, ...), custom_call_target="tpu_custom_call" | custom-call | flops 1024 | bytes 1024 | tf_op jit(solution)/shard_map/pallas_call | solution.py:123
  17.4 2.0 %collective-permute-done.1.right.refs_1_ = bf16[2,256,384]{2,1,0:T(8,128)(2,1)S(1)} collective-permute-done((bf16[2,256,384]{2,1,0:T(8,128)(2,1)S(1)}, bf16[2,256,384]{2,1,0:T(8,128)(2,1)S(1)}, u32[]{:S(2)}, u32[]{:S(2)}) %collective-permute-start.1) | collective-permute-done | bytes 393248 | tf_op jit(solution)/shard_map/ppermute | solution.py:398
  19.4 3.2 %collective-permute-start.4 = (bf16[2,256,384]{2,1,0:T(8,128)(2,1)S(1)}, bf16[2,256,384]{2,1,0:T(8,128)(2,1)S(1)}, u32[]{:S(2)}, u32[]{:S(2)}) collective-permute-start(bf16[2,256,384]{2,1,0:T(8,128)(2,1)S(1)} %collective-permute-done.2.left.refs_2_), channel_id=1, source_target_pairs={{0,112},{16,0},{32,16},{48,32},{64,48},{80,64},{96,80},{112,96},{1... | collective-permute-start | bytes 1179656 | tf_op jit(solution)/shard_map/ppermute | solution.py:398
  23.1 1.4 %collective-permute-start.12 = (bf16[192,3072]{1,0:T(8,128)(2,1)}, bf16[192,3072]{1,0:T(8,128)(2,1)S(1)}, u32[]{:S(2)}, u32[]{:S(2)}) collective-permute-start(bf16[192,3072]{1,0:T(8,128)(2,1)} %get-tuple-element.98), channel_id=1, source_target_pairs={{0,1},{1,0},{2,3},{3,2},{4,5},{5,4},{6,7},{7,6},{8,9},{9,8},{10,11... | collective-permute-start | bytes 3538952 | tf_op jit(solution)/shard_map/ppermute | solution.py:398
  24.7 2.2 %shard_map.141 = (f32[512,384]{1,0:T(8,128)S(1)}, f32[512,384]{1,0:T(8,128)S(1)}, f32[512,384]{1,0:T(8,128)S(1)}) custom-call(bf16[256,384]{1,0:T(8,128)(2,1)S(1)} %copy-done.1, bf16[256,384]{1,0:T(8,128)(2,1)S(1)} %collective-permute-done.5.q1, bf16[256,384]{1,0:T(8,128)(2,1)S(1)} %copy-done.2, bf16[256,384]{1,0:T(8,128)(2,1)S(1)} %copy-done.3, ...), custom_call_target="tpu_custom_call" | custom-call | flops 1024 | bytes 1024 | tf_op jit(solution)/shard_map/pallas_call | solution.py:243
  27.0 3.3 %collective-permute-done.3.refs_0_.refs_3_ = bf16[2,256,384]{2,1,0:T(8,128)(2,1)S(1)} collective-permute-done((bf16[2,256,384]{2,1,0:T(8,128)(2,1)S(1)}, bf16[2,256,384]{2,1,0:T(8,128)(2,1)S(1)}, u32[]{:S(2)}, u32[]{:S(2)}) %collective-permute-start.3) | collective-permute-done | bytes 393248 | tf_op jit(solution)/shard_map/ppermute | solution.py:398
  30.3 3.2 %collective-permute-start.8 = (bf16[2,256,384]{2,1,0:T(8,128)(2,1)S(1)}, bf16[2,256,384]{2,1,0:T(8,128)(2,1)S(1)}, u32[]{:S(2)}, u32[]{:S(2)}) collective-permute-start(bf16[2,256,384]{2,1,0:T(8,128)(2,1)S(1)} %collective-permute-done.4.refs_1_.refs_4_), channel_id=1, source_target_pairs={{0,112},{16,0},{32,16},{48,32},{64,48},{80,64},{96,80},{112,96},{1... | collective-permute-start | bytes 1179656 | tf_op jit(solution)/shard_map/ppermute | solution.py:398
  33.5 3.1 %shard_map.143 = (f32[512,384]{1,0:T(8,128)S(1)}, f32[512,384]{1,0:T(8,128)S(1)}, f32[512,384]{1,0:T(8,128)S(1)}) custom-call(bf16[256,384]{1,0:T(8,128)(2,1)S(1)} %collective-permute-done.q0, bf16[256,384]{1,0:T(8,128)(2,1)S(1)} %collective-permute-done.6.q1, bf16[2,256,384]{2,1,0:T(8,128)(2,1)S(1)} %bitcast.24, ...), custom_call_target="tpu_custom_call" | custom-call | flops 1024 | bytes 1024 | tf_op jit(solution)/shard_map/pallas_call | solution.py:243
  38.0 2.2 %collective-permute-done.7.refs_0_ = bf16[2,256,384]{2,1,0:T(8,128)(2,1)S(1)} collective-permute-done((bf16[2,256,384]{2,1,0:T(8,128)(2,1)S(1)}, bf16[2,256,384]{2,1,0:T(8,128)(2,1)S(1)}, u32[]{:S(2)}, u32[]{:S(2)}) %collective-permute-start.7) | collective-permute-done | bytes 393248 | tf_op jit(solution)/shard_map/ppermute | solution.py:398
  40.6 3.1 %collective-permute-start.10 = (bf16[256,384]{1,0:T(8,128)(2,1)S(1)}, bf16[256,384]{1,0:T(8,128)(2,1)S(1)}, u32[]{:S(2)}, u32[]{:S(2)}) collective-permute-start(bf16[256,384]{1,0:T(8,128)(2,1)S(1)} %slice_bitcast_fusion), channel_id=1, source_target_pairs={{0,112},{16,0},{32,16},{48,32},{64,48},{80,64},{96,80},{112,96},{1... | collective-permute-start | bytes 589832 | tf_op jit(solution)/shard_map/ppermute | solution.py:398
  43.6 1.4 %shard_map.145 = (f32[512,384]{1,0:T(8,128)S(1)}, f32[512,384]{1,0:T(8,128)S(1)}, f32[512,384]{1,0:T(8,128)S(1)}) custom-call(bf16[256,384]{1,0:T(8,128)(2,1)S(1)} %collective-permute-done.q0, bf16[256,384]{1,0:T(8,128)(2,1)S(1)} %collective-permute-done.6.q1, bf16[2,256,384]{2,1,0:T(8,128)(2,1)S(1)} %collective-permute-done.7.refs_0_, ...), custom_call_target="tpu_custom_call" | custom-call | flops 1024 | bytes 1024 | tf_op jit(solution)/shard_map/pallas_call | solution.py:243
  45.1 1.4 %shard_map.144 = (f32[512,384]{1,0:T(8,128)S(1)}, f32[512,384]{1,0:T(8,128)S(1)}, f32[512,384]{1,0:T(8,128)S(1)}) custom-call(bf16[256,384]{1,0:T(8,128)(2,1)S(1)} %copy-done.1, bf16[256,384]{1,0:T(8,128)(2,1)S(1)} %collective-permute-done.5.q1, bf16[2,256,384]{2,1,0:T(8,128)(2,1)S(1)} %collective-permute-done.7.refs_0_, ...), custom_call_target="tpu_custom_call" | custom-call | flops 1024 | bytes 1024 | tf_op jit(solution)/shard_map/pallas_call | solution.py:243
  48.1 5.1 %collective-permute-done.12.refs_5_ = bf16[192,3072]{1,0:T(8,128)(2,1)S(1)} collective-permute-done((bf16[192,3072]{1,0:T(8,128)(2,1)}, bf16[192,3072]{1,0:T(8,128)(2,1)S(1)}, u32[]{:S(2)}, u32[]{:S(2)}) %collective-permute-start.12) | collective-permute-done | bytes 1179680 | tf_op jit(solution)/shard_map/ppermute | solution.py:398
  54.8 1.6 %collective-permute-done.13.refs_7_ = bf16[2,144,384]{2,1,0:T(8,128)(2,1)S(1)} collective-permute-done((bf16[2,144,384]{2,1,0:T(8,128)(2,1)S(1)}, bf16[2,144,384]{2,1,0:T(8,128)(2,1)S(1)}, u32[]{:S(2)}, u32[]{:S(2)}) %collective-permute-start.13) | collective-permute-done | bytes 221216 | tf_op jit(solution)/shard_map/ppermute | solution.py:398
  59.9 2.8 %collective-permute-start.16 = (bf16[144,384]{1,0:T(8,128)(2,1)S(1)}, bf16[144,384]{1,0:T(8,128)(2,1)S(1)}, u32[]{:S(2)}, u32[]{:S(2)}) collective-permute-start(bf16[144,384]{1,0:T(8,128)(2,1)S(1)} %get-tuple-element.104), channel_id=1, source_target_pairs={{0,129},{1,128},{128,1},{129,0},{2,131},{3,130},{130,3},{131,2},{4... | collective-permute-start | bytes 331784 | tf_op jit(solution)/shard_map/ppermute | solution.py:402
  63.9 1.6 %collective-permute-done.15.refs_2_ = bf16[144,384]{1,0:T(8,128)(2,1)S(1)} collective-permute-done((bf16[144,384]{1,0:T(8,128)(2,1)S(1)}, bf16[144,384]{1,0:T(8,128)(2,1)S(1)}, u32[]{:S(2)}, u32[]{:S(2)}) %collective-permute-start.15) | collective-permute-done | bytes 110624 | tf_op jit(solution)/shard_map/ppermute | solution.py:398
  65.5 2.3 %collective-permute-done.16.refs_3_ = bf16[144,384]{1,0:T(8,128)(2,1)S(1)} collective-permute-done((bf16[144,384]{1,0:T(8,128)(2,1)S(1)}, bf16[144,384]{1,0:T(8,128)(2,1)S(1)}, u32[]{:S(2)}, u32[]{:S(2)}) %collective-permute-start.16) | collective-permute-done | bytes 110624 | tf_op jit(solution)/shard_map/ppermute | solution.py:402
  67.8 1.8 %shard_map.149 = (bf16[32,3072]{1,0:T(8,128)(2,1)S(1)}, bf16[32,3072]{1,0:T(8,128)(2,1)S(1)}, bf16[32,3072]{1,0:T(8,128)(2,1)S(1)}, bf16[32,3072]{1,0:T(8,128)(2,1)S(1)}) custom-call(s32[3]{0:T(128)S(1)} %copy-done.4, bf16[144,384]{1,0:T(8,128)(2,1)S(1)} %get-tuple-element.101.refs_0_, bf16[144,384]{1,0:T(8,128)(2,1)S(1)} %collective-permute-done.14.refs_1_, ...), custom_call_target="tpu_custom_call" | custom-call | flops 1024 | bytes 1024 | tf_op jit(solution)/shard_map/pallas_call | solution.py:351
  69.6 3.3 %collective-permute-start.18 = (bf16[32,3072]{1,0:T(8,128)(2,1)S(1)}, bf16[32,3072]{1,0:T(8,128)(2,1)S(1)}, u32[]{:S(2)}, u32[]{:S(2)}) collective-permute-start(bf16[32,3072]{1,0:T(8,128)(2,1)S(1)} %get-tuple-element.107), channel_id=1, source_target_pairs={{0,4},{2,6},{4,0},{6,2},{1,5},{3,7},{5,1},{7,3},{8,12},{10,14},{12... | collective-permute-start | bytes 589832 | tf_op jit(solution)/shard_map/ppermute | solution.py:398
  73.6 2.6 %collective-permute-start.20 = (bf16[32,3072]{1,0:T(8,128)(2,1)S(1)}, bf16[32,3072]{1,0:T(8,128)(2,1)S(1)}, u32[]{:S(2)}, u32[]{:S(2)}) collective-permute-start(bf16[32,3072]{1,0:T(8,128)(2,1)S(1)} %get-tuple-element.109), channel_id=1, source_target_pairs={{0,6},{2,0},{4,2},{6,4},{1,7},{3,1},{5,3},{7,5},{8,14},{10,8},{12,... | collective-permute-start | bytes 589832 | tf_op jit(solution)/shard_map/ppermute | solution.py:398
  76.1 2.8 %collective-permute-done.18 = bf16[32,3072]{1,0:T(8,128)(2,1)S(1)} collective-permute-done((bf16[32,3072]{1,0:T(8,128)(2,1)S(1)}, bf16[32,3072]{1,0:T(8,128)(2,1)S(1)}, u32[]{:S(2)}, u32[]{:S(2)}) %collective-permute-start.18) | collective-permute-done | bytes 196640 | tf_op jit(solution)/shard_map/ppermute | solution.py:398
  78.9 3.3 %collective-permute-done.19 = bf16[32,3072]{1,0:T(8,128)(2,1)S(1)} collective-permute-done((bf16[32,3072]{1,0:T(8,128)(2,1)S(1)}, bf16[32,3072]{1,0:T(8,128)(2,1)S(1)}, u32[]{:S(2)}, u32[]{:S(2)}) %collective-permute-start.19) | collective-permute-done | bytes 196640 | tf_op jit(solution)/shard_map/ppermute | solution.py:398
  84.5 2.7 %collective-permute-start.23 = (bf16[32,3072]{1,0:T(8,128)(2,1)S(1)}, bf16[32,3072]{1,0:T(8,128)(2,1)S(1)}, u32[]{:S(2)}, u32[]{:S(2)}) collective-permute-start(bf16[32,3072]{1,0:T(8,128)(2,1)S(1)} %add_convert_fusion.refs_0_), channel_id=1, source_target_pairs={{0,6},{2,0},{4,2},{6,4},{1,7},{3,1},{5,3},{7,5},{8,14},{10,8},{12,... | collective-permute-start | bytes 589832 | tf_op jit(solution)/shard_map/ppermute | solution.py:398
  87.3 1.5 %collective-permute-start.27 = (bf16[32,3072]{1,0:T(8,128)(2,1)S(1)}, bf16[32,3072]{1,0:T(8,128)(2,1)S(1)}, u32[]{:S(2)}, u32[]{:S(2)}) collective-permute-start(bf16[32,3072]{1,0:T(8,128)(2,1)S(1)} %add_convert_fusion.refs_0_), channel_id=1, source_target_pairs={{0,4},{2,6},{4,0},{6,2},{1,5},{3,7},{5,1},{7,3},{8,12},{10,14},{12... | collective-permute-start | bytes 589832 | tf_op jit(solution)/shard_map/ppermute | solution.py:398
  88.7 2.8 %collective-permute-done.25.refs_1_ = bf16[32,3072]{1,0:T(8,128)(2,1)S(1)} collective-permute-done((bf16[32,3072]{1,0:T(8,128)(2,1)S(1)}, bf16[32,3072]{1,0:T(8,128)(2,1)S(1)}, u32[]{:S(2)}, u32[]{:S(2)}) %collective-permute-start.25) | collective-permute-done | bytes 196640 | tf_op jit(solution)/shard_map/ppermute | solution.py:398
  91.5 1.8 %collective-permute-start.26 = (bf16[32,3072]{1,0:T(8,128)(2,1)S(1)}, bf16[32,3072]{1,0:T(8,128)(2,1)S(1)}, u32[]{:S(2)}, u32[]{:S(2)}) collective-permute-start(bf16[32,3072]{1,0:T(8,128)(2,1)S(1)} %collective-permute-done.25.refs_1_), channel_id=1, source_target_pairs={{0,4},{2,6},{4,0},{6,2},{1,5},{3,7},{5,1},{7,3},{8,12},{10,14},{12... | collective-permute-start | bytes 589832 | tf_op jit(solution)/shard_map/ppermute | solution.py:398
  93.4 5.8 %collective-permute-done.23.refs_3_ = bf16[32,3072]{1,0:T(8,128)(2,1)S(1)} collective-permute-done((bf16[32,3072]{1,0:T(8,128)(2,1)S(1)}, bf16[32,3072]{1,0:T(8,128)(2,1)S(1)}, u32[]{:S(2)}, u32[]{:S(2)}) %collective-permute-start.23) | collective-permute-done | bytes 196640 | tf_op jit(solution)/shard_map/ppermute | solution.py:398
  99.2 2.9 %collective-permute-start.24 = (bf16[32,3072]{1,0:T(8,128)(2,1)S(1)}, bf16[32,3072]{1,0:T(8,128)(2,1)S(1)}, u32[]{:S(2)}, u32[]{:S(2)}) collective-permute-start(bf16[32,3072]{1,0:T(8,128)(2,1)S(1)} %collective-permute-done.23.refs_3_), channel_id=1, source_target_pairs={{0,1},{1,0},{2,3},{3,2},{4,5},{5,4},{6,7},{7,6},{8,9},{9,8},{10,11... | collective-permute-start | bytes 589832 | tf_op jit(solution)/shard_map/ppermute | solution.py:398
  102.6 2.9 %collective-permute-start.22 = (bf16[32,3072]{1,0:T(8,128)(2,1)S(1)}, bf16[32,3072]{1,0:T(8,128)(2,1)S(1)}, u32[]{:S(2)}, u32[]{:S(2)}) collective-permute-start(bf16[32,3072]{1,0:T(8,128)(2,1)S(1)} %collective-permute-done.21.refs_2_), channel_id=1, source_target_pairs={{0,1},{1,0},{2,3},{3,2},{4,5},{5,4},{6,7},{7,6},{8,9},{9,8},{10,11... | collective-permute-start | bytes 589832 | tf_op jit(solution)/shard_map/ppermute | solution.py:398
  106.7 1.5 %shard_map.150.refs_3_ = bf16[256,3072]{1,0:T(8,128)(2,1)} custom-call(s32[3]{0:T(128)S(1)} %copy-done.4, bf16[32,3072]{1,0:T(8,128)(2,1)S(1)} %add_convert_fusion.refs_0_, bf16[32,3072]{1,0:T(8,128)(2,1)S(1)} %collective-permute-done.25.refs_1_, bf16[32,3072]{1,0:T(8,128)(2,1)S(1)} %collective-permute-done.21.refs_2_, ...), custom_call_target="tpu_custom_call" | custom-call | flops 1024 | bytes 1024 | tf_op jit(solution)/shard_map/pallas_call | solution.py:384
  108.2 1.5 %collective-permute-done.22.refs_0_ = bf16[32,3072]{1,0:T(8,128)(2,1)S(1)} collective-permute-done((bf16[32,3072]{1,0:T(8,128)(2,1)S(1)}, bf16[32,3072]{1,0:T(8,128)(2,1)S(1)}, u32[]{:S(2)}, u32[]{:S(2)}) %collective-permute-start.22) | collective-permute-done | bytes 196640 | tf_op jit(solution)/shard_map/ppermute | solution.py:398
  (60 shorter events, 19.0 us)
Async XLA Ops:
  1.7 15.7 %collective-permute-start.2 = (bf16[2,256,384]{2,1,0:T(8,128)(2,1)S(1)}, bf16[2,256,384]{2,1,0:T(8,128)(2,1)S(1)}, u32[]{:S(2)}, u32[]{:S(2)}) collective-permute-start(bf16[2,256,384]{2,1,0:T(8,128)(2,1)S(1)} %bitcast.21), channel_id=1, source_target_pairs={{0,112},{16,0},{32,16},{48,32},{64,48},{80,64},{96,80},{112,96},{1... | collective-permute-start | bytes 1179656 | tf_op jit(solution)/shard_map/ppermute | solution.py:398
  7.6 11.8 %collective-permute-start.1 = (bf16[2,256,384]{2,1,0:T(8,128)(2,1)S(1)}, bf16[2,256,384]{2,1,0:T(8,128)(2,1)S(1)}, u32[]{:S(2)}, u32[]{:S(2)}) collective-permute-start(bf16[2,256,384]{2,1,0:T(8,128)(2,1)S(1)} %bitcast.22), channel_id=1, source_target_pairs={{0,16},{16,32},{32,48},{48,64},{64,80},{80,96},{96,112},{112,0},{1... | collective-permute-start | bytes 1179656 | tf_op jit(solution)/shard_map/ppermute | solution.py:398
  8.3 16.3 %copy-start.5 = (bf16[512,2,384]{2,1,0:T(2,128)(2,1)S(1)}, bf16[512,2,384]{2,1,0:T(2,128)(2,1)}, u32[]{:S(2)}) copy-start(bf16[512,2,384]{2,1,0:T(2,128)(2,1)} %param.22) | copy-start | bytes 2359300
  16.5 6.7 %collective-permute-start = (bf16[256,384]{1,0:T(8,128)(2,1)}, bf16[256,384]{1,0:T(8,128)(2,1)S(1)}, u32[]{:S(2)}, u32[]{:S(2)}) collective-permute-start(bf16[256,384]{1,0:T(8,128)(2,1)} %get-tuple-element.61.q0), channel_id=1, source_target_pairs={{0,128},{128,0},{1,129},{129,1},{2,130},{130,2},{3,131},{131,3},{4... | collective-permute-start | bytes 589832 | tf_op jit(solution)/shard_map/ppermute | solution.py:398
  19.4 10.9 %collective-permute-start.3 = (bf16[2,256,384]{2,1,0:T(8,128)(2,1)S(1)}, bf16[2,256,384]{2,1,0:T(8,128)(2,1)S(1)}, u32[]{:S(2)}, u32[]{:S(2)}) collective-permute-start(bf16[2,256,384]{2,1,0:T(8,128)(2,1)S(1)} %collective-permute-done.1.right.refs_1_), channel_id=1, source_target_pairs={{0,16},{16,32},{32,48},{48,64},{64,80},{80,96},{96,112},{112,0},{1... | collective-permute-start | bytes 1179656 | tf_op jit(solution)/shard_map/ppermute | solution.py:398
  19.4 10.9 %collective-permute-start.4 = (bf16[2,256,384]{2,1,0:T(8,128)(2,1)S(1)}, bf16[2,256,384]{2,1,0:T(8,128)(2,1)S(1)}, u32[]{:S(2)}, u32[]{:S(2)}) collective-permute-start(bf16[2,256,384]{2,1,0:T(8,128)(2,1)S(1)} %collective-permute-done.2.left.refs_2_), channel_id=1, source_target_pairs={{0,112},{16,0},{32,16},{48,32},{64,48},{80,64},{96,80},{112,96},{1... | collective-permute-start | bytes 1179656 | tf_op jit(solution)/shard_map/ppermute | solution.py:398
  22.6 2.0 %collective-permute-start.5 = (bf16[256,384]{1,0:T(8,128)(2,1)}, bf16[256,384]{1,0:T(8,128)(2,1)S(1)}, u32[]{:S(2)}, u32[]{:S(2)}) collective-permute-start(bf16[256,384]{1,0:T(8,128)(2,1)} %get-tuple-element.61.q0), channel_id=1, source_target_pairs={{0,8},{8,0},{1,9},{9,1},{2,10},{10,2},{3,11},{11,3},{4,12},{12,4},... | collective-permute-start | bytes 589832 | tf_op jit(solution)/shard_map/ppermute | solution.py:398
  23.1 3.8 %collective-permute-start.6 = (bf16[256,384]{1,0:T(8,128)(2,1)S(1)}, bf16[256,384]{1,0:T(8,128)(2,1)S(1)}, u32[]{:S(2)}, u32[]{:S(2)}) collective-permute-start(bf16[256,384]{1,0:T(8,128)(2,1)S(1)} %collective-permute-done.q0), channel_id=1, source_target_pairs={{0,8},{8,0},{1,9},{9,1},{2,10},{10,2},{3,11},{11,3},{4,12},{12,4},... | collective-permute-start | bytes 589832 | tf_op jit(solution)/shard_map/ppermute | solution.py:398
  23.1 30.1 %collective-permute-start.12 = (bf16[192,3072]{1,0:T(8,128)(2,1)}, bf16[192,3072]{1,0:T(8,128)(2,1)S(1)}, u32[]{:S(2)}, u32[]{:S(2)}) collective-permute-start(bf16[192,3072]{1,0:T(8,128)(2,1)} %get-tuple-element.98), channel_id=1, source_target_pairs={{0,1},{1,0},{2,3},{3,2},{4,5},{5,4},{6,7},{7,6},{8,9},{9,8},{10,11... | collective-permute-start | bytes 3538952 | tf_op jit(solution)/shard_map/ppermute | solution.py:398
  30.3 10.0 %collective-permute-start.7 = (bf16[2,256,384]{2,1,0:T(8,128)(2,1)S(1)}, bf16[2,256,384]{2,1,0:T(8,128)(2,1)S(1)}, u32[]{:S(2)}, u32[]{:S(2)}) collective-permute-start(bf16[2,256,384]{2,1,0:T(8,128)(2,1)S(1)} %collective-permute-done.3.refs_0_.refs_3_), channel_id=1, source_target_pairs={{0,16},{16,32},{32,48},{48,64},{64,80},{80,96},{96,112},{112,0},{1... | collective-permute-start | bytes 1179656 | tf_op jit(solution)/shard_map/ppermute | solution.py:398
  30.3 10.0 %collective-permute-start.8 = (bf16[2,256,384]{2,1,0:T(8,128)(2,1)S(1)}, bf16[2,256,384]{2,1,0:T(8,128)(2,1)S(1)}, u32[]{:S(2)}, u32[]{:S(2)}) collective-permute-start(bf16[2,256,384]{2,1,0:T(8,128)(2,1)S(1)} %collective-permute-done.4.refs_1_.refs_4_), channel_id=1, source_target_pairs={{0,112},{16,0},{32,16},{48,32},{64,48},{80,64},{96,80},{112,96},{1... | collective-permute-start | bytes 1179656 | tf_op jit(solution)/shard_map/ppermute | solution.py:398
  40.3 7.0 %collective-permute-start.9 = (bf16[256,384]{1,0:T(8,128)(2,1)S(1)}, bf16[256,384]{1,0:T(8,128)(2,1)S(1)}, u32[]{:S(2)}, u32[]{:S(2)}) collective-permute-start(bf16[256,384]{1,0:T(8,128)(2,1)S(1)} %slice_bitcast_fusion.1), channel_id=1, source_target_pairs={{0,16},{16,32},{32,48},{48,64},{64,80},{80,96},{96,112},{112,0},{1... | collective-permute-start | bytes 589832 | tf_op jit(solution)/shard_map/ppermute | solution.py:398
  40.6 6.7 %collective-permute-start.10 = (bf16[256,384]{1,0:T(8,128)(2,1)S(1)}, bf16[256,384]{1,0:T(8,128)(2,1)S(1)}, u32[]{:S(2)}, u32[]{:S(2)}) collective-permute-start(bf16[256,384]{1,0:T(8,128)(2,1)S(1)} %slice_bitcast_fusion), channel_id=1, source_target_pairs={{0,112},{16,0},{32,16},{48,32},{64,48},{80,64},{96,80},{112,96},{1... | collective-permute-start | bytes 589832 | tf_op jit(solution)/shard_map/ppermute | solution.py:398
  53.2 14.5 %collective-permute-start.17 = (bf16[192,3072]{1,0:T(8,128)(2,1)S(1)}, bf16[192,3072]{1,0:T(8,128)(2,1)S(1)}, u32[]{:S(2)}, u32[]{:S(2)}) collective-permute-start(bf16[192,3072]{1,0:T(8,128)(2,1)S(1)} %collective-permute-done.12.refs_5_), channel_id=1, source_target_pairs={{0,8},{8,0},{1,9},{9,1},{2,10},{10,2},{3,11},{11,3},{4,12},{12,4},... | collective-permute-start | bytes 3538952 | tf_op jit(solution)/shard_map/ppermute | solution.py:398
  53.2 3.2 %collective-permute-start.13 = (bf16[2,144,384]{2,1,0:T(8,128)(2,1)S(1)}, bf16[2,144,384]{2,1,0:T(8,128)(2,1)S(1)}, u32[]{:S(2)}, u32[]{:S(2)}) collective-permute-start(bf16[2,144,384]{2,1,0:T(8,128)(2,1)S(1)} %get-tuple-element.100), channel_id=1, source_target_pairs={{0,8},{8,0},{1,9},{9,1},{2,10},{10,2},{3,11},{11,3},{4,12},{12,4},... | collective-permute-start | bytes 663560 | tf_op jit(solution)/shard_map/ppermute | solution.py:398
  54.7 13.1 %copy-start = (bf16[384,3072]{1,0:T(8,128)(2,1)S(1)}, bf16[384,3072]{1,0:T(8,128)(2,1)}, u32[]{:S(2)}) copy-start(bf16[384,3072]{1,0:T(8,128)(2,1)} %refs_4_.1) | copy-start | bytes 7077892
  54.7 2.0 %collective-permute-start.11 = (bf16[2,144,384]{2,1,0:T(8,128)(2,1)S(1)}, bf16[2,144,384]{2,1,0:T(8,128)(2,1)S(1)}, u32[]{:S(2)}, u32[]{:S(2)}) collective-permute-start(bf16[2,144,384]{2,1,0:T(8,128)(2,1)S(1)} %get-tuple-element.91), channel_id=1, source_target_pairs={{0,8},{8,0},{1,9},{9,1},{2,10},{10,2},{3,11},{11,3},{4,12},{12,4},... | collective-permute-start | bytes 663560 | tf_op jit(solution)/shard_map/ppermute | solution.py:398
  57.9 6.0 %collective-permute-start.14 = (bf16[144,384]{1,0:T(8,128)(2,1)S(1)}, bf16[144,384]{1,0:T(8,128)(2,1)S(1)}, u32[]{:S(2)}, u32[]{:S(2)}) collective-permute-start(bf16[144,384]{1,0:T(8,128)(2,1)S(1)} %get-tuple-element.102), channel_id=1, source_target_pairs={{0,128},{128,0},{1,129},{129,1},{2,130},{130,2},{3,131},{131,3},{4... | collective-permute-start | bytes 331784 | tf_op jit(solution)/shard_map/ppermute | solution.py:398
  58.8 6.7 %collective-permute-start.15 = (bf16[144,384]{1,0:T(8,128)(2,1)S(1)}, bf16[144,384]{1,0:T(8,128)(2,1)S(1)}, u32[]{:S(2)}, u32[]{:S(2)}) collective-permute-start(bf16[144,384]{1,0:T(8,128)(2,1)S(1)} %get-tuple-element.103), channel_id=1, source_target_pairs={{0,1},{1,0},{2,3},{3,2},{4,5},{5,4},{6,7},{7,6},{8,9},{9,8},{10,11... | collective-permute-start | bytes 331784 | tf_op jit(solution)/shard_map/ppermute | solution.py:398
  59.9 7.8 %collective-permute-start.16 = (bf16[144,384]{1,0:T(8,128)(2,1)S(1)}, bf16[144,384]{1,0:T(8,128)(2,1)S(1)}, u32[]{:S(2)}, u32[]{:S(2)}) collective-permute-start(bf16[144,384]{1,0:T(8,128)(2,1)S(1)} %get-tuple-element.104), channel_id=1, source_target_pairs={{0,129},{1,128},{128,1},{129,0},{2,131},{3,130},{130,3},{131,2},{4... | collective-permute-start | bytes 331784 | tf_op jit(solution)/shard_map/ppermute | solution.py:402
  67.7 14.8 %copy-start.6 = (f32[3072]{0:T(1024)S(1)}, f32[3072]{0:T(1024)}, u32[]{:S(2)}) copy-start(f32[3072]{0:T(1024)} %param.24) | copy-start | bytes 36868
  67.7 14.8 %copy-start.7 = (f32[3072]{0:T(1024)S(1)}, f32[3072]{0:T(1024)}, u32[]{:S(2)}) copy-start(f32[3072]{0:T(1024)} %param.17) | copy-start | bytes 36868
  69.6 9.4 %collective-permute-start.18 = (bf16[32,3072]{1,0:T(8,128)(2,1)S(1)}, bf16[32,3072]{1,0:T(8,128)(2,1)S(1)}, u32[]{:S(2)}, u32[]{:S(2)}) collective-permute-start(bf16[32,3072]{1,0:T(8,128)(2,1)S(1)} %get-tuple-element.107), channel_id=1, source_target_pairs={{0,4},{2,6},{4,0},{6,2},{1,5},{3,7},{5,1},{7,3},{8,12},{10,14},{12... | collective-permute-start | bytes 589832 | tf_op jit(solution)/shard_map/ppermute | solution.py:398
  72.9 9.3 %collective-permute-start.19 = (bf16[32,3072]{1,0:T(8,128)(2,1)S(1)}, bf16[32,3072]{1,0:T(8,128)(2,1)S(1)}, u32[]{:S(2)}, u32[]{:S(2)}) collective-permute-start(bf16[32,3072]{1,0:T(8,128)(2,1)S(1)} %get-tuple-element.108), channel_id=1, source_target_pairs={{0,2},{2,4},{4,6},{6,0},{1,3},{3,5},{5,7},{7,1},{8,10},{10,12},{12... | collective-permute-start | bytes 589832 | tf_op jit(solution)/shard_map/ppermute | solution.py:398
  73.6 9.0 %collective-permute-start.20 = (bf16[32,3072]{1,0:T(8,128)(2,1)S(1)}, bf16[32,3072]{1,0:T(8,128)(2,1)S(1)}, u32[]{:S(2)}, u32[]{:S(2)}) collective-permute-start(bf16[32,3072]{1,0:T(8,128)(2,1)S(1)} %get-tuple-element.109), channel_id=1, source_target_pairs={{0,6},{2,0},{4,2},{6,4},{1,7},{3,1},{5,3},{7,5},{8,14},{10,8},{12,... | collective-permute-start | bytes 589832 | tf_op jit(solution)/shard_map/ppermute | solution.py:398
  83.7 7.9 %collective-permute-start.25 = (bf16[32,3072]{1,0:T(8,128)(2,1)S(1)}, bf16[32,3072]{1,0:T(8,128)(2,1)S(1)}, u32[]{:S(2)}, u32[]{:S(2)}) collective-permute-start(bf16[32,3072]{1,0:T(8,128)(2,1)S(1)} %add_convert_fusion.refs_0_), channel_id=1, source_target_pairs={{0,1},{1,0},{2,3},{3,2},{4,5},{5,4},{6,7},{7,6},{8,9},{9,8},{10,11... | collective-permute-start | bytes 589832 | tf_op jit(solution)/shard_map/ppermute | solution.py:398
  84.5 14.6 %collective-permute-start.23 = (bf16[32,3072]{1,0:T(8,128)(2,1)S(1)}, bf16[32,3072]{1,0:T(8,128)(2,1)S(1)}, u32[]{:S(2)}, u32[]{:S(2)}) collective-permute-start(bf16[32,3072]{1,0:T(8,128)(2,1)S(1)} %add_convert_fusion.refs_0_), channel_id=1, source_target_pairs={{0,6},{2,0},{4,2},{6,4},{1,7},{3,1},{5,3},{7,5},{8,14},{10,8},{12,... | collective-permute-start | bytes 589832 | tf_op jit(solution)/shard_map/ppermute | solution.py:398
  87.3 15.3 %collective-permute-start.21 = (bf16[32,3072]{1,0:T(8,128)(2,1)S(1)}, bf16[32,3072]{1,0:T(8,128)(2,1)S(1)}, u32[]{:S(2)}, u32[]{:S(2)}) collective-permute-start(bf16[32,3072]{1,0:T(8,128)(2,1)S(1)} %add_convert_fusion.refs_0_), channel_id=1, source_target_pairs={{0,2},{2,4},{4,6},{6,0},{1,3},{3,5},{5,7},{7,1},{8,10},{10,12},{12... | collective-permute-start | bytes 589832 | tf_op jit(solution)/shard_map/ppermute | solution.py:398
  87.3 19.4 %collective-permute-start.27 = (bf16[32,3072]{1,0:T(8,128)(2,1)S(1)}, bf16[32,3072]{1,0:T(8,128)(2,1)S(1)}, u32[]{:S(2)}, u32[]{:S(2)}) collective-permute-start(bf16[32,3072]{1,0:T(8,128)(2,1)S(1)} %add_convert_fusion.refs_0_), channel_id=1, source_target_pairs={{0,4},{2,6},{4,0},{6,2},{1,5},{3,7},{5,1},{7,3},{8,12},{10,14},{12... | collective-permute-start | bytes 589832 | tf_op jit(solution)/shard_map/ppermute | solution.py:398
  91.5 16.7 %collective-permute-start.26 = (bf16[32,3072]{1,0:T(8,128)(2,1)S(1)}, bf16[32,3072]{1,0:T(8,128)(2,1)S(1)}, u32[]{:S(2)}, u32[]{:S(2)}) collective-permute-start(bf16[32,3072]{1,0:T(8,128)(2,1)S(1)} %collective-permute-done.25.refs_1_), channel_id=1, source_target_pairs={{0,4},{2,6},{4,0},{6,2},{1,5},{3,7},{5,1},{7,3},{8,12},{10,14},{12... | collective-permute-start | bytes 589832 | tf_op jit(solution)/shard_map/ppermute | solution.py:398
  99.2 9.0 %collective-permute-start.24 = (bf16[32,3072]{1,0:T(8,128)(2,1)S(1)}, bf16[32,3072]{1,0:T(8,128)(2,1)S(1)}, u32[]{:S(2)}, u32[]{:S(2)}) collective-permute-start(bf16[32,3072]{1,0:T(8,128)(2,1)S(1)} %collective-permute-done.23.refs_3_), channel_id=1, source_target_pairs={{0,1},{1,0},{2,3},{3,2},{4,5},{5,4},{6,7},{7,6},{8,9},{9,8},{10,11... | collective-permute-start | bytes 589832 | tf_op jit(solution)/shard_map/ppermute | solution.py:398
  102.6 7.2 %collective-permute-start.22 = (bf16[32,3072]{1,0:T(8,128)(2,1)S(1)}, bf16[32,3072]{1,0:T(8,128)(2,1)S(1)}, u32[]{:S(2)}, u32[]{:S(2)}) collective-permute-start(bf16[32,3072]{1,0:T(8,128)(2,1)S(1)} %collective-permute-done.21.refs_2_), channel_id=1, source_target_pairs={{0,1},{1,0},{2,3},{3,2},{4,5},{5,4},{6,7},{7,6},{8,9},{9,8},{10,11... | collective-permute-start | bytes 589832 | tf_op jit(solution)/shard_map/ppermute | solution.py:398
  (4 other events, 27.7 us)

commit v4 on v3

--- a/solution.py
+++ b/solution.py
@@ -44,6 +44,9 @@
     return slice(head * HEAD, (head + 1) * HEAD)
 
 
+HEADS = [head_of(n) for n in range(LOCAL_HEADS)]
+
+
 def whole_spec(shape):
     return pl.BlockSpec(shape, lambda i: (0,) * len(shape))
 
@@ -66,98 +69,77 @@
     return np.concatenate(parts, axis=1)
 
 
-def qkv_kernel(
-    place, lat, w, w_out, rows, trig, shift, scale, q_gain, k_gain, q, k, v, w_half, x_buf, w_buf, half, sems
-):
-    copies = [pltpu.make_async_copy(lat, x_buf, sems.at[3])]
-    copies += [pltpu.make_async_copy(w.at[n], w_buf.at[n], sems.at[n]) for n in range(3)]
+def qkv_kernel(place, *refs):
+    given, (q, k, v, w_half), buffers, sems = refs[:9], refs[9:13], refs[13:-1], refs[-1]
+    lat, w, trig, rows, shift, scale, q_gain, k_gain, half = buffers
     part = pl.ds(pl.multiple_of(place[2] * SPLIT, SPLIT), SPLIT)
-    copies.append(pltpu.make_async_copy(w_out.at[part], half, sems.at[4]))
-    for copy in copies:
-        copy.start()
-
+    copy = lambda n, source, target: pltpu.make_async_copy(source, target, sems.at[n])
+    weights = [copy(n, given[1].at[n], w.at[n]) for n in range(3)]
+    small = [copy(n + 1, given[n], buffers[n]) for n in range(2, 8)]
+    latents, half_in = copy(9, given[0], lat), copy(10, given[8].at[part], half)
+    half_out = copy(11, half, w_half)
+    latents.start()
+    for c in small:
+        c.start()
+    weights[0].start()
+
+    for c in small:
+        c.wait()
     at = lax.broadcasted_iota(jnp.int32, (ROW_POS + WIDTH_TOK, COUNT), 0)
     row_pos = lax.shift_right_logical(rows[...], 8)
     col_pos = jnp.bitwise_and(rows[...], WIDTH_TOK - 1) + ROW_POS
     hot = jnp.where((at == row_pos) | (at == col_pos), 1.0, 0.0).astype(jnp.bfloat16)
-    table = lax.dot_general(hot, trig[...], (((0,), (0,)), ((), ())), preferred_element_type=jnp.float32)
-    table = table[:, : 2 * HEAD] + (table[:, 2 * HEAD : 4 * HEAD] + table[:, 4 * HEAD :])
-    cosine, sine = table[:, :HEAD], table[:, HEAD:]
-
-    copies[0].wait()
-    x = x_buf[...].astype(jnp.float32)
+    turn = lax.dot_general(hot, trig[...], (((0,), (0,)), ((), ())), preferred_element_type=jnp.float32)
+    turn = turn[:, : 2 * HEAD] + (turn[:, 2 * HEAD : 4 * HEAD] + turn[:, 4 * HEAD :])
+    cosine, sine = turn[:, :HEAD], turn[:, HEAD:]
+    even = lax.broadcasted_iota(jnp.int32, (COUNT, HEAD), 1) % 2 == 0
+
+    latents.wait()
+    weights[1].start()
+    x = lat[...].astype(jnp.float32)
     centred = x - jnp.mean(x, axis=-1, keepdims=True)
     spread = jnp.mean(centred * centred, axis=-1, keepdims=True)
     y = centred * lax.rsqrt(spread + 1e-06) * (1.0 + scale[...]) + shift[...]
     normed = y.astype(jnp.bfloat16)
-    even = lax.broadcasted_iota(jnp.int32, (COUNT, HEAD), 1) % 2 == 0
-
-    def rotated(out, gain, factor):
-        heads = []
-        for head in range(LOCAL_HEADS):
-            x = out[:, head_of(head)]
-            x = x * lax.rsqrt(jnp.mean(x * x, axis=-1, keepdims=True) + 1e-06) * gain[...]
-            other = jnp.where(even, pltpu.roll(x, HEAD - 1, 1), pltpu.roll(x, 1, 1))
-            x = x * cosine + other * sine
-            heads.append((x * factor if factor else x).astype(jnp.bfloat16))
-        return heads
+
+    def rotated(x, gain, factor):
+        x = x * lax.rsqrt(jnp.mean(x * x, axis=-1, keepdims=True) + 1e-06) * gain[...]
+        other = jnp.where(even, pltpu.roll(x, HEAD - 1, 1), pltpu.roll(x, 1, 1))
+        x = x * cosine + other * sine
+        return (x * factor if factor else x).astype(jnp.bfloat16)
 
     for n, (ref, gain, factor) in enumerate(((q, q_gain, SCALE), (k, k_gain, None), (v, None, None))):
-        copies[n + 1].wait()
-        out = jnp.dot(normed, w_buf[n], preferred_element_type=jnp.float32)
-        if gain is None:
-            ref[...] = out.astype(jnp.bfloat16)
-        else:
-            for head, x in enumerate(rotated(out, gain, factor)):
-                ref[:, head_of(head)] = x
+        weights[n].wait()
         if n == 0:
-            copies[4].wait()
-            back = pltpu.make_async_copy(half, w_half, sems.at[5])
-            back.start()
-    back.wait()
-
-
-def qkv_call(place, latents, w, w_out, rows, shift, scale, q_gain, k_gain):
+            weights[2].start()
+            half_in.start()
+        out = jnp.dot(normed, w[n], preferred_element_type=jnp.float32)
+        for c in HEADS:
+            x = out[:, c]
+            ref[:, c] = x.astype(jnp.bfloat16) if gain is None else rotated(x, gain, factor)
+        if n == 1:
+            half_in.wait()
+            half_out.start()
+    half_out.wait()
+
+
+def qkv_call(place, latents, w, rows, shift, scale, q_gain, k_gain, w_out):
     anywhere = pl.BlockSpec(memory_space=pl.ANY)
-    trig = trig_parts()
+    row = lambda a: a.reshape(1, a.shape[0])
+    args = [latents, w, jnp.asarray(trig_parts())]
+    args += [row(a) for a in (rows, shift, scale, q_gain, k_gain)]
+    half = (SPLIT, MODEL)
     return pl.pallas_call(
         qkv_kernel,
-        grid=(1,),
-        in_specs=[
-            SMEM,
-            anywhere,
-            anywhere,
-            anywhere,
-            whole_spec((1, COUNT)),
-            whole_spec(trig.shape),
-            whole_spec((1, MODEL)),
-            whole_spec((1, MODEL)),
-            whole_spec((1, HEAD)),
-            whole_spec((1, HEAD)),
-        ],
-        out_specs=[whole_spec((COUNT, WIDTH))] * 3 + [anywhere],
+        in_specs=[SMEM] + [anywhere] * 9,
+        out_specs=[FULL] * 3 + [anywhere],
         out_shape=[jax.ShapeDtypeStruct((COUNT, WIDTH), jnp.bfloat16)] * 3
-        + [jax.ShapeDtypeStruct((SPLIT, MODEL), jnp.bfloat16)],
-        scratch_shapes=[
-            pltpu.VMEM((COUNT, MODEL), jnp.bfloat16),
-            pltpu.VMEM((3, MODEL, WIDTH), jnp.bfloat16),
-            pltpu.VMEM((SPLIT, MODEL), jnp.bfloat16),
-            pltpu.SemaphoreType.DMA((6,)),
-        ],
+        + [jax.ShapeDtypeStruct(half, jnp.bfloat16)],
+        scratch_shapes=[pltpu.VMEM(a.shape, a.dtype) for a in args]
+        + [pltpu.VMEM(half, jnp.bfloat16), pltpu.SemaphoreType.DMA((12,))],
         compiler_params=params(60),
         cost_estimate=cost(2 * COUNT * MODEL * WIDTH * 3, 10 * MIB),
-    )(
-        place,
-        latents,
-        w,
-        w_out,
-        rows.reshape(1, COUNT),
-        jnp.asarray(trig),
-        shift.reshape(1, MODEL),
-        scale.reshape(1, MODEL),
-        q_gain.reshape(1, HEAD),
-        k_gain.reshape(1, HEAD),
-    )
+    )(place, *args, w_out)
 
 
 def attend(q, pairs, state=None):
@@ -197,9 +179,6 @@
     return [(ref[0, :, cols], ref[1, :, cols]) for ref in pair]
 
 
-HEADS = [head_of(n) for n in range(LOCAL_HEADS)]
-
-
 def near_kernel(q0, q1, k, v, text, own, right, left, *state):
     for c in HEADS:
         ring_pairs = both((right, left), c)
@@ -298,7 +277,7 @@
 
 
 def merge_kernel(place, *refs):
-    swap = place[0] == 1
+    swap = jnp.bitwise_and(place[1], 1) == 1
     for block in range(2):
         state, message = refs[4 * block : 4 * block + 3], refs[4 * block + 3]
         mine, other = refs[8 + 2 * block : 10 + 2 * block]
@@ -323,10 +302,13 @@
     )(place, *args)
 
 
+QUARTERS = ((0, 0), (1, 1), (1, 0), (0, 1))
+
+
 def project_kernel(place, *refs):
     messages, (w, w_x, w_core) = refs[:4], refs[4:7]
-    own, plus, minus, two, attn, full = refs[7:]
-    y, first = place[1], place[2] == 0
+    outs, attn, full = refs[7:11], refs[11], refs[12]
+    x, high_y, first = place[0], lax.shift_right_logical(place[1], 1), place[2] == 0
     for n in range(2):
         for head in range(LOCAL_HEADS):
             c = head_of(head)
@@ -342,8 +324,8 @@
         total += jnp.dot(by_x, w_x[:, cols], preferred_element_type=jnp.float32)
         total += jnp.dot(by_core, w_core[:, cols], preferred_element_type=jnp.float32)
         full[:, cols] = total.astype(jnp.bfloat16)
-    for n, out in enumerate((own, plus, minus, two)):
-        to = lax.rem(y + (0, 1, 3, 2)[n], 4)
+    for out, (dy, dx) in zip(outs, QUARTERS):
+        to = jnp.bitwise_xor(high_y, dy) * 2 + jnp.bitwise_xor(x, dx)
         out[...] = full[pl.ds(pl.multiple_of(to * ROWS, ROWS), ROWS), :]
 
 
@@ -367,8 +349,9 @@
     x, y = place[0], place[1]
     copies = []
     for n, (flip, step) in enumerate(offsets):
-        half = 1 - x if flip else x
-        at = half * HALF + lax.rem(y + 4 - step, 4) * ROWS
+        from_y = lax.rem(y + 4 - step, 4)
+        quarter = lax.shift_right_logical(from_y, 1) * 2 + (1 - x if flip else x)
+        at = jnp.bitwise_and(from_y, 1) * HALF + quarter * ROWS
         rows = pl.ds(pl.multiple_of(at, ROWS), ROWS)
         copies.append(pltpu.make_async_copy(refs[n], out.at[rows], sems.at[n]))
     for copy in copies:
@@ -396,6 +379,10 @@
 def ring(value, axis, step):
     size = SIZES[AXES.index(axis)]
     return lax.ppermute(value, axis, [(i, (i + step) % size) for i in range(size)])
+
+
+def beside_y(value):
+    return lax.ppermute(value, "y", [(i, i ^ 1) for i in range(4)])
 
 
 def crossed(value, axes):
@@ -424,25 +411,29 @@
 
     w = jnp.transpose(w_qkv, (1, 0, 2))
     q, k, v, w_half = qkv_call(
-        place, latents, w, w_out, token_rows, mod_shift, mod_scale, q_gain, k_gain
+        place, latents, w, token_rows, mod_shift, mod_scale, q_gain, k_gain, w_out
     )
+    w_pair = beside_y(w_half)
     q_core, q_x = ring(q, "core", 1), ring(q, "x_lo", 1)
-    q_both = ring(q_x, "core", 1)
-    w_half, q_x = after((w_half, q_x))
-    w_x = ring(w_half, "x_hi", 1)
 
     r1, l1, q = after((r1, l1, q))
     r2, l2 = ring(r1, "z", 1), ring(l1, "z", -1)
     text = jnp.transpose(text_kv, (1, 0, 2))
     near = attend_call(near_kernel, 8, q, q_core, k, v, text, own, r1, l1)
 
-    r2, l2, near[0], q_both = after((r2, l2, near[0], q_both))
-    r3, l3 = ring(r2, "z", 1), ring(l2, "z", -1)
+    q_x, near[2] = after((q_x, near[2]))
+    q_both = ring(q_x, "core", 1)
+    r2, near[0] = after((r2, near[0]))
+    r3 = ring(r2, "z", 1)
+    l2, near[1] = after((l2, near[1]))
+    l3 = ring(l2, "z", -1)
     near = attend_call(next_kernel, 4, q, q_core, r2, l2, *near)
     far = attend_call(far_kernel, 10, q_x, q_both, own, r1, l1, r2, l2)
 
-    r3, l3, near[0], far[0] = after((r3, l3, near[0], far[0]))
-    far_k, far_v = ring(r3[0], "z", 1), ring(l3[1], "z", -1)
+    r3, near[0], far[0] = after((r3, near[0], far[0]))
+    far_k = ring(r3[0], "z", 1)
+    l3, near[1], far[1] = after((l3, near[1], far[1]))
+    far_v = ring(l3[1], "z", -1)
     far = attend_call(next_kernel, 4, q_x, q_both, r3, l3, *far)
     near = attend_call(next_kernel, 4, q, q_core, r3, l3, *near)
 
@@ -450,33 +441,45 @@
     x_state, x_msg = last_call(q_x, q_both, far_k, far_v, *far)
     x_msg = ring(x_msg, "core", 1)
     o_state, o_msg = last_call(q, q_core, far_k, far_v, *near)
-    w_x, o_msg = after((w_x, o_msg))
-    w_core = ring(w_x, "core", 1)
+    w_pair, o_msg = after((w_pair, o_msg))
     o_msg = ring(o_msg, "core", 1)
+    w_core = ring(w_pair, "core", 1)
     x_mine, x_other, o_mine, o_other = merge_call(place, *x_state, x_msg, *o_state, o_msg)
-    from_hi = ring(o_other, "x_hi", 1)
-    from_x = ring(x_mine, "x_lo", 1)
-    from_both = crossed(x_other, ("x_lo", "x_hi"))
-
-    mine, plus, minus, two = project_call(
-        place, (o_mine, from_x, from_hi, from_both), (w_out, w_x, w_core)
+    from_y, from_x = beside_y(o_other), ring(x_mine, "x_lo", 1)
+    from_both = lax.ppermute(
+        x_other, ("x_lo", "y"), [(i, (1 - i // 4) * 4 + (i % 4 ^ 1)) for i in range(8)]
     )
-    parts = [ring(two, "y", 2), ring(plus, "y", 1), ring(minus, "y", -1)]
-    rows = lax.dynamic_slice_in_dim(latents, x * HALF + y * ROWS, ROWS, 0).astype(jnp.float32)
+
+    mine, both_ways, along_y, along_x = project_call(
+        place, (o_mine, from_x, from_y, from_both), (w_out, w_pair, w_core)
+    )
+    parts = [
+        lax.ppermute(both_ways, TENSOR, [(i, (i // 2 + 2) % 4 * 2 + (1 - i % 2)) for i in range(8)]),
+        ring(along_y, "y", 2),
+        ring(along_x, "x_hi", 1),
+    ]
+    start = y % 2 * HALF + (y // 2 * 2 + x) * ROWS
+    rows = lax.dynamic_slice_in_dim(latents, start, ROWS, 0).astype(jnp.float32)
     total = mine.astype(jnp.float32)
     for part in parts:
         total = total + part.astype(jnp.float32)
     piece = (rows + mod_gate * (total + b_out)).astype(jnp.bfloat16)
 
-    beside, plus = ring(piece, "x_hi", 1), ring(piece, "y", 1)
-    minus, two = ring(piece, "y", -1), ring(piece, "y", 2)
-    early = [((0, 0), piece), ((1, 0), beside), ((0, 1), plus), ((0, -1), minus), ((0, 2), two)]
+    beside, two = ring(piece, "x_hi", 1), ring(piece, "y", 2)
+    plus, minus = ring(piece, "y", 1), ring(piece, "y", -1)
+    early = [
+        ((0, 0), piece),
+        ((1, 0), beside),
+        ((0, 1), plus),
+        ((0, -1), minus),
+        ((0, 2), two),
+    ]
+    late = [
+        ((1, 1), ring(beside, "y", 1)),
+        ((1, -1), ring(beside, "y", -1)),
+        ((1, 2), ring(two, "x_hi", 1)),
+    ]
     out = put_call(place, [e[0] for e in early], [e[1] for e in early])
-    late = [
-        ((1, 1), ring(plus, "x_hi", 1)),
-        ((1, -1), ring(minus, "x_hi", 1)),
-        ((1, 2), ring(beside, "y", 2)),
-    ]
     out = put_call(place, [e[0] for e in late], [e[1] for e in late], out)
     return (out, jnp.stack([k, v], axis=1))
 

time: 113 us -> 103 us (0.912); the launches traced: 111 us -> 103 us
  starting transfers between devices: 42.7 us -> 38.2 us
  waiting for transfers between devices: 38 us -> 33.6 us
    ppermute x27 -> x24, waiting for transfers between devices: 35.7 us -> 24.4 us  [ring(): lax.ppermute(value, axis, [(i, (i + step) % size) for i in range(size)])]
    ppermute x27 -> x24, starting transfers between devices: 39.9 us -> 30.1 us  [ring(): lax.ppermute(value, axis, [(i, (i + step) % size) for i in range(size)])]
    ppermute x1 -> x4, waiting for transfers between devices: 2.27 us -> 9.18 us  [the longest x2 3.93 us: beside_y(): return lax.ppermute(value, 'y', [(i, i ^ 1) for i in range(4)])]
    ppermute x1 -> x4, starting transfers between devices: 2.76 us -> 8.07 us  [the longest x1 3.83 us: shards(): lax.ppermute(both_ways, TENSOR, [(i, (i // 2 + 2) % 4 * 2 + (1 - i % 2))...]
  transfers between devices with their start and end apart: 28 -> 28, of which waited for: 18 -> 16; matrix products, arithmetic and copies ran while one was open for 2% -> 2% of each run, Pallas kernels for 20% -> 22%
where the time goes in v4:
time: 103 us
  starting transfers between devices  38.2 us (37%)
  waiting for transfers between devices  33.6 us (33%)
  Pallas kernels  26 us (25%)
  local copies, waits for them, and re-layouts  2.38 us (2%)
  other arithmetic  1.78 us (2%)
  between operations  1.04 us (1%)
    ppermute x24, starting transfers between devices, ring(): lax.ppermute(value, axis, [(i, (i + step) % size) for i in range(size)])  30.1 us
    ppermute x24, waiting for transfers between devices, ring(): lax.ppermute(value, axis, [(i, (i + step) % size) for i in range(size)])  24.4 us
    pallas_call x5, Pallas kernels, attend_call(): return list(call(*args))  9.6 us
    pallas_call x1, Pallas kernels, qkv_call(): pl.pallas_call(qkv_kernel, in_specs=[SMEM] + [anywhere] * 9, out_specs=[F...  8.56 us
    ppermute x2, waiting for transfers between devices, beside_y(): return lax.ppermute(value, 'y', [(i, i ^ 1) for i in range(4)])  3.93 us
    ppermute x1, waiting for transfers between devices, shards(): lax.ppermute(both_ways, TENSOR, [(i, (i // 2 + 2) % 4 * 2 + (1 - i % 2))...  3.92 us
    ppermute x1, starting transfers between devices, shards(): lax.ppermute(both_ways, TENSOR, [(i, (i // 2 + 2) % 4 * 2 + (1 - i % 2))...  3.83 us
    ppermute x2, starting transfers between devices, beside_y(): return lax.ppermute(value, 'y', [(i, i ^ 1) for i in range(4)])  3.15 us
  transfers between devices with their start and end apart: 28, of which 16 were waited for; matrix products, arithmetic and copies ran while one was open for 2% of the time, Pallas kernels for 22%

profile of v4, /device:TPU:6, one launch (start us, length us, event | category | flops | bytes accessed | tf_op | source)
XLA Modules:
  0.0 103.0 jit_solution(9186325134570338770)
XLA Ops:
  1.7 5.9 %collective-permute-start.2 = (bf16[2,256,384]{2,1,0:T(8,128)(2,1)S(1)}, bf16[2,256,384]{2,1,0:T(8,128)(2,1)S(1)}, u32[]{:S(2)}, u32[]{:S(2)}) collective-permute-start(bf16[2,256,384]{2,1,0:T(8,128)(2,1)S(1)} %bitcast.21), channel_id=1, source_target_pairs={{0,112},{16,0},{32,16},{48,32},{64,48},{80,64},{96,80},{112,96},{1... | collective-permute-start | bytes 1179656 | tf_op jit(solution)/shard_map/ppermute | solution.py:381
  8.3 8.6 %shard_map.140 = (bf16[256,384]{1,0:T(8,128)(2,1)}, bf16[256,384]{1,0:T(8,128)(2,1)}, bf16[256,384]{1,0:T(8,128)(2,1)}, bf16[192,3072]{1,0:T(8,128)(2,1)}) custom-call(s32[3]{0:T(128)} %pad_add_fusion.place, bf16[256,3072]{1,0:T(8,128)(2,1)} %refs_0_.1, bf16[3,3072,384]{2,1,0:T(8,128)(2,1)} %bitcast.28, bf16[288,768]{1,0:T(8,128)(2,1)} %constant.44.clone.refs_2_, ...), custom_call_target="tpu_custom_call" | custom-call | flops 1024 | bytes 1024 | tf_op jit(solution)/shard_map/pallas_call | solution.py:132
  16.9 2.5 %collective-permute-done.1.right.refs_1_ = bf16[2,256,384]{2,1,0:T(8,128)(2,1)S(1)} collective-permute-done((bf16[2,256,384]{2,1,0:T(8,128)(2,1)S(1)}, bf16[2,256,384]{2,1,0:T(8,128)(2,1)S(1)}, u32[]{:S(2)}, u32[]{:S(2)}) %collective-permute-start.1) | collective-permute-done | bytes 393248 | tf_op jit(solution)/shard_map/ppermute | solution.py:381
  19.4 3.2 %collective-permute-start.7 = (bf16[2,256,384]{2,1,0:T(8,128)(2,1)S(1)}, bf16[2,256,384]{2,1,0:T(8,128)(2,1)S(1)}, u32[]{:S(2)}, u32[]{:S(2)}) collective-permute-start(bf16[2,256,384]{2,1,0:T(8,128)(2,1)S(1)} %collective-permute-done.2.left.refs_2_), channel_id=1, source_target_pairs={{0,112},{16,0},{32,16},{48,32},{64,48},{80,64},{96,80},{112,96},{1... | collective-permute-start | bytes 1179656 | tf_op jit(solution)/shard_map/ppermute | solution.py:381
  22.6 1.6 %collective-permute-start.12 = (bf16[192,3072]{1,0:T(8,128)(2,1)}, bf16[192,3072]{1,0:T(8,128)(2,1)S(1)}, u32[]{:S(2)}, u32[]{:S(2)}) collective-permute-start(bf16[192,3072]{1,0:T(8,128)(2,1)} %get-tuple-element.102), channel_id=1, source_target_pairs={{0,2},{2,0},{4,6},{6,4},{1,3},{3,1},{5,7},{7,5},{8,10},{10,8},{12,... | collective-permute-start | bytes 3538952 | tf_op jit(solution)/shard_map/ppermute | solution.py:385
  25.2 2.3 %shard_map.141 = (f32[512,384]{1,0:T(8,128)S(1)}, f32[512,384]{1,0:T(8,128)S(1)}, f32[512,384]{1,0:T(8,128)S(1)}) custom-call(bf16[256,384]{1,0:T(8,128)(2,1)S(1)} %copy-done.1, bf16[256,384]{1,0:T(8,128)(2,1)S(1)} %collective-permute-done.3.q1, bf16[256,384]{1,0:T(8,128)(2,1)S(1)} %copy-done.2, bf16[256,384]{1,0:T(8,128)(2,1)S(1)} %copy-done.3, ...), custom_call_target="tpu_custom_call" | custom-call | flops 1024 | bytes 1024 | tf_op jit(solution)/shard_map/pallas_call | solution.py:222
  27.5 2.8 %collective-permute-done.5.refs_0_.refs_3_ = bf16[2,256,384]{2,1,0:T(8,128)(2,1)S(1)} collective-permute-done((bf16[2,256,384]{2,1,0:T(8,128)(2,1)S(1)}, bf16[2,256,384]{2,1,0:T(8,128)(2,1)S(1)}, u32[]{:S(2)}, u32[]{:S(2)}) %collective-permute-start.5) | collective-permute-done | bytes 393248 | tf_op jit(solution)/shard_map/ppermute | solution.py:381
  30.3 3.2 %collective-permute-start.9 = (bf16[2,256,384]{2,1,0:T(8,128)(2,1)S(1)}, bf16[2,256,384]{2,1,0:T(8,128)(2,1)S(1)}, u32[]{:S(2)}, u32[]{:S(2)}) collective-permute-start(bf16[2,256,384]{2,1,0:T(8,128)(2,1)S(1)} %collective-permute-done.7.refs_1_.refs_4_), channel_id=1, source_target_pairs={{0,112},{16,0},{32,16},{48,32},{64,48},{80,64},{96,80},{112,96},{1... | collective-permute-start | bytes 1179656 | tf_op jit(solution)/shard_map/ppermute | solution.py:381
  33.5 1.4 %collective-permute-done.4.q1 = bf16[256,384]{1,0:T(8,128)(2,1)S(1)} collective-permute-done((bf16[256,384]{1,0:T(8,128)(2,1)S(1)}, bf16[256,384]{1,0:T(8,128)(2,1)S(1)}, u32[]{:S(2)}, u32[]{:S(2)}) %collective-permute-start.4) | collective-permute-done | bytes 196640 | tf_op jit(solution)/shard_map/ppermute | solution.py:381
  35.0 3.1 %shard_map.143 = (f32[512,384]{1,0:T(8,128)S(1)}, f32[512,384]{1,0:T(8,128)S(1)}, f32[512,384]{1,0:T(8,128)S(1)}) custom-call(bf16[256,384]{1,0:T(8,128)(2,1)S(1)} %collective-permute-done.q0, bf16[256,384]{1,0:T(8,128)(2,1)S(1)} %collective-permute-done.4.q1, bf16[2,256,384]{2,1,0:T(8,128)(2,1)S(1)} %bitcast.24, ...), custom_call_target="tpu_custom_call" | custom-call | flops 1024 | bytes 1024 | tf_op jit(solution)/shard_map/pallas_call | solution.py:222
  38.0 1.4 %shard_map.142 = (f32[512,384]{1,0:T(8,128)S(1)}, f32[512,384]{1,0:T(8,128)S(1)}, f32[512,384]{1,0:T(8,128)S(1)}) custom-call(bf16[256,384]{1,0:T(8,128)(2,1)S(1)} %copy-done.1, bf16[256,384]{1,0:T(8,128)(2,1)S(1)} %collective-permute-done.3.q1, bf16[2,256,384]{2,1,0:T(8,128)(2,1)S(1)} %collective-permute-done.5.refs_0_.refs_3_, ...), custom_call_target="tpu_custom_call" | custom-call | flops 1024 | bytes 1024 | tf_op jit(solution)/shard_map/pallas_call | solution.py:222
  40.4 3.2 %collective-permute-start.10 = (bf16[256,384]{1,0:T(8,128)(2,1)S(1)}, bf16[256,384]{1,0:T(8,128)(2,1)S(1)}, u32[]{:S(2)}, u32[]{:S(2)}) collective-permute-start(bf16[256,384]{1,0:T(8,128)(2,1)S(1)} %slice_bitcast_fusion), channel_id=1, source_target_pairs={{0,112},{16,0},{32,16},{48,32},{64,48},{80,64},{96,80},{112,96},{1... | collective-permute-start | bytes 589832 | tf_op jit(solution)/shard_map/ppermute | solution.py:381
  43.6 1.4 %shard_map.144 = (f32[512,384]{1,0:T(8,128)S(1)}, f32[512,384]{1,0:T(8,128)S(1)}, f32[512,384]{1,0:T(8,128)S(1)}) custom-call(bf16[256,384]{1,0:T(8,128)(2,1)S(1)} %copy-done.1, bf16[256,384]{1,0:T(8,128)(2,1)S(1)} %collective-permute-done.3.q1, bf16[2,256,384]{2,1,0:T(8,128)(2,1)S(1)} %collective-permute-done.6.refs_0_, ...), custom_call_target="tpu_custom_call" | custom-call | flops 1024 | bytes 1024 | tf_op jit(solution)/shard_map/pallas_call | solution.py:222
  45.0 1.4 %shard_map.145 = (f32[512,384]{1,0:T(8,128)S(1)}, f32[512,384]{1,0:T(8,128)S(1)}, f32[512,384]{1,0:T(8,128)S(1)}) custom-call(bf16[256,384]{1,0:T(8,128)(2,1)S(1)} %collective-permute-done.q0, bf16[256,384]{1,0:T(8,128)(2,1)S(1)} %collective-permute-done.4.q1, bf16[2,256,384]{2,1,0:T(8,128)(2,1)S(1)} %collective-permute-done.6.refs_0_, ...), custom_call_target="tpu_custom_call" | custom-call | flops 1024 | bytes 1024 | tf_op jit(solution)/shard_map/pallas_call | solution.py:222
  48.7 2.5 %collective-permute-done.12.refs_5_ = bf16[192,3072]{1,0:T(8,128)(2,1)S(1)} collective-permute-done((bf16[192,3072]{1,0:T(8,128)(2,1)}, bf16[192,3072]{1,0:T(8,128)(2,1)S(1)}, u32[]{:S(2)}, u32[]{:S(2)}) %collective-permute-start.12) | collective-permute-done | bytes 1179680 | tf_op jit(solution)/shard_map/ppermute | solution.py:385
  52.8 1.6 %collective-permute-done.13.refs_7_ = bf16[2,144,384]{2,1,0:T(8,128)(2,1)S(1)} collective-permute-done((bf16[2,144,384]{2,1,0:T(8,128)(2,1)S(1)}, bf16[2,144,384]{2,1,0:T(8,128)(2,1)S(1)}, u32[]{:S(2)}, u32[]{:S(2)}) %collective-permute-start.13) | collective-permute-done | bytes 221216 | tf_op jit(solution)/shard_map/ppermute | solution.py:381
  56.8 1.6 %collective-permute-start.15 = (bf16[144,384]{1,0:T(8,128)(2,1)S(1)}, bf16[144,384]{1,0:T(8,128)(2,1)S(1)}, u32[]{:S(2)}, u32[]{:S(2)}) collective-permute-start(bf16[144,384]{1,0:T(8,128)(2,1)S(1)} %get-tuple-element.107), channel_id=1, source_target_pairs={{0,2},{2,0},{4,6},{6,4},{1,3},{3,1},{5,7},{7,5},{8,10},{10,8},{12,... | collective-permute-start | bytes 331784 | tf_op jit(solution)/shard_map/ppermute | solution.py:385
  59.5 2.3 %collective-permute-done.14.refs_1_ = bf16[144,384]{1,0:T(8,128)(2,1)S(1)} collective-permute-done((bf16[144,384]{1,0:T(8,128)(2,1)S(1)}, bf16[144,384]{1,0:T(8,128)(2,1)S(1)}, u32[]{:S(2)}, u32[]{:S(2)}) %collective-permute-start.14) | collective-permute-done | bytes 110624 | tf_op jit(solution)/shard_map/ppermute | solution.py:381
  61.7 1.4 %collective-permute-done.15.refs_2_ = bf16[144,384]{1,0:T(8,128)(2,1)S(1)} collective-permute-done((bf16[144,384]{1,0:T(8,128)(2,1)S(1)}, bf16[144,384]{1,0:T(8,128)(2,1)S(1)}, u32[]{:S(2)}, u32[]{:S(2)}) %collective-permute-start.15) | collective-permute-done | bytes 110624 | tf_op jit(solution)/shard_map/ppermute | solution.py:385
  63.1 1.3 %collective-permute-done.16.refs_3_ = bf16[144,384]{1,0:T(8,128)(2,1)S(1)} collective-permute-done((bf16[144,384]{1,0:T(8,128)(2,1)S(1)}, bf16[144,384]{1,0:T(8,128)(2,1)S(1)}, u32[]{:S(2)}, u32[]{:S(2)}) %collective-permute-start.16) | collective-permute-done | bytes 110624 | tf_op jit(solution)/shard_map/ppermute | solution.py:449
  64.5 1.8 %shard_map.149 = (bf16[32,3072]{1,0:T(8,128)(2,1)S(1)}, bf16[32,3072]{1,0:T(8,128)(2,1)S(1)}, bf16[32,3072]{1,0:T(8,128)(2,1)S(1)}, bf16[32,3072]{1,0:T(8,128)(2,1)S(1)}) custom-call(s32[3]{0:T(128)S(1)} %copy-done.4, bf16[144,384]{1,0:T(8,128)(2,1)S(1)} %get-tuple-element.105.refs_0_, bf16[144,384]{1,0:T(8,128)(2,1)S(1)} %collective-permute-done.14.refs_1_, ...), custom_call_target="tpu_custom_call" | custom-call | flops 1024 | bytes 1024 | tf_op jit(solution)/shard_map/pallas_call | solution.py:333
  66.3 3.8 %collective-permute-start.18 = (bf16[32,3072]{1,0:T(8,128)(2,1)S(1)}, bf16[32,3072]{1,0:T(8,128)(2,1)S(1)}, u32[]{:S(2)}, u32[]{:S(2)}) collective-permute-start(bf16[32,3072]{1,0:T(8,128)(2,1)S(1)} %get-tuple-element.111), channel_id=1, source_target_pairs={{0,5},{1,4},{2,7},{3,6},{4,1},{5,0},{6,3},{7,2},{8,13},{9,12},{10,... | collective-permute-start | bytes 589832 | tf_op jit(solution)/shard_map/ppermute | solution.py:457
  70.8 2.1 %collective-permute-start.20 = (bf16[32,3072]{1,0:T(8,128)(2,1)S(1)}, bf16[32,3072]{1,0:T(8,128)(2,1)S(1)}, u32[]{:S(2)}, u32[]{:S(2)}) collective-permute-start(bf16[32,3072]{1,0:T(8,128)(2,1)S(1)} %get-tuple-element.113), channel_id=1, source_target_pairs={{0,1},{1,0},{2,3},{3,2},{4,5},{5,4},{6,7},{7,6},{8,9},{9,8},{10,11... | collective-permute-start | bytes 589832 | tf_op jit(solution)/shard_map/ppermute | solution.py:381
  72.9 3.9 %collective-permute-done.18 = bf16[32,3072]{1,0:T(8,128)(2,1)S(1)} collective-permute-done((bf16[32,3072]{1,0:T(8,128)(2,1)S(1)}, bf16[32,3072]{1,0:T(8,128)(2,1)S(1)}, u32[]{:S(2)}, u32[]{:S(2)}) %collective-permute-start.18) | collective-permute-done | bytes 196640 | tf_op jit(solution)/shard_map/ppermute | solution.py:457
  76.8 3.8 %collective-permute-done.19 = bf16[32,3072]{1,0:T(8,128)(2,1)S(1)} collective-permute-done((bf16[32,3072]{1,0:T(8,128)(2,1)S(1)}, bf16[32,3072]{1,0:T(8,128)(2,1)S(1)}, u32[]{:S(2)}, u32[]{:S(2)}) %collective-permute-start.19) | collective-permute-done | bytes 196640 | tf_op jit(solution)/shard_map/ppermute | solution.py:381
  81.8 1.8 %collective-permute-start.24 = (bf16[32,3072]{1,0:T(8,128)(2,1)S(1)}, bf16[32,3072]{1,0:T(8,128)(2,1)S(1)}, u32[]{:S(2)}, u32[]{:S(2)}) collective-permute-start(bf16[32,3072]{1,0:T(8,128)(2,1)S(1)} %add_convert_fusion.refs_0_), channel_id=1, source_target_pairs={{0,4},{2,6},{4,0},{6,2},{1,5},{3,7},{5,1},{7,3},{8,12},{10,14},{12... | collective-permute-start | bytes 589832 | tf_op jit(solution)/shard_map/ppermute | solution.py:381
  83.5 2.1 %collective-permute-start.21 = (bf16[32,3072]{1,0:T(8,128)(2,1)S(1)}, bf16[32,3072]{1,0:T(8,128)(2,1)S(1)}, u32[]{:S(2)}, u32[]{:S(2)}) collective-permute-start(bf16[32,3072]{1,0:T(8,128)(2,1)S(1)} %add_convert_fusion.refs_0_), channel_id=1, source_target_pairs={{0,1},{1,0},{2,3},{3,2},{4,5},{5,4},{6,7},{7,6},{8,9},{9,8},{10,11... | collective-permute-start | bytes 589832 | tf_op jit(solution)/shard_map/ppermute | solution.py:381
  87.7 3.4 %collective-permute-done.24.refs_4_ = bf16[32,3072]{1,0:T(8,128)(2,1)S(1)} collective-permute-done((bf16[32,3072]{1,0:T(8,128)(2,1)S(1)}, bf16[32,3072]{1,0:T(8,128)(2,1)S(1)}, u32[]{:S(2)}, u32[]{:S(2)}) %collective-permute-start.24) | collective-permute-done | bytes 196640 | tf_op jit(solution)/shard_map/ppermute | solution.py:381
  92.4 2.1 %collective-permute-start.23 = (bf16[32,3072]{1,0:T(8,128)(2,1)S(1)}, bf16[32,3072]{1,0:T(8,128)(2,1)S(1)}, u32[]{:S(2)}, u32[]{:S(2)}) collective-permute-start(bf16[32,3072]{1,0:T(8,128)(2,1)S(1)} %collective-permute-done.21.refs_1_), channel_id=1, source_target_pairs={{0,6},{2,0},{4,2},{6,4},{1,7},{3,1},{5,3},{7,5},{8,14},{10,8},{12,... | collective-permute-start | bytes 589832 | tf_op jit(solution)/shard_map/ppermute | solution.py:381
  95.8 1.5 %shard_map.150.refs_3_ = bf16[256,3072]{1,0:T(8,128)(2,1)} custom-call(s32[3]{0:T(128)S(1)} %copy-done.4, bf16[32,3072]{1,0:T(8,128)(2,1)S(1)} %add_convert_fusion.refs_0_, bf16[32,3072]{1,0:T(8,128)(2,1)S(1)} %collective-permute-done.21.refs_1_, bf16[32,3072]{1,0:T(8,128)(2,1)S(1)} %collective-permute-done.26.refs_2_, ...), custom_call_target="tpu_custom_call" | custom-call | flops 1024 | bytes 1024 | tf_op jit(solution)/shard_map/pallas_call | solution.py:367
  98.3 3.1 %collective-permute-done.22.refs_0_ = bf16[32,3072]{1,0:T(8,128)(2,1)S(1)} collective-permute-done((bf16[32,3072]{1,0:T(8,128)(2,1)S(1)}, bf16[32,3072]{1,0:T(8,128)(2,1)S(1)}, u32[]{:S(2)}, u32[]{:S(2)}) %collective-permute-start.22) | collective-permute-done | bytes 196640 | tf_op jit(solution)/shard_map/ppermute | solution.py:381
  101.4 1.4 %shard_map.151 = bf16[256,3072]{1,0:T(8,128)(2,1)} custom-call(s32[3]{0:T(128)S(1)} %copy-done.4, bf16[32,3072]{1,0:T(8,128)(2,1)S(1)} %collective-permute-done.22.refs_0_, bf16[32,3072]{1,0:T(8,128)(2,1)S(1)} %collective-permute-done.23.refs_1_, bf16[32,3072]{1,0:T(8,128)(2,1)S(1)} %collective-permute-done.25.refs_2_, ...), custom_call_target="tpu_custom_call", output_to_operand_aliasing={{}: (4, {})} | custom-call | flops 1024 | bytes 1024 | tf_op jit(solution)/shard_map/pallas_call | solution.py:367
  (60 shorter events, 18.1 us)
Async XLA Ops:
  1.7 15.2 %collective-permute-start.2 = (bf16[2,256,384]{2,1,0:T(8,128)(2,1)S(1)}, bf16[2,256,384]{2,1,0:T(8,128)(2,1)S(1)}, u32[]{:S(2)}, u32[]{:S(2)}) collective-permute-start(bf16[2,256,384]{2,1,0:T(8,128)(2,1)S(1)} %bitcast.21), channel_id=1, source_target_pairs={{0,112},{16,0},{32,16},{48,32},{64,48},{80,64},{96,80},{112,96},{1... | collective-permute-start | bytes 1179656 | tf_op jit(solution)/shard_map/ppermute | solution.py:381
  7.6 11.8 %collective-permute-start.1 = (bf16[2,256,384]{2,1,0:T(8,128)(2,1)S(1)}, bf16[2,256,384]{2,1,0:T(8,128)(2,1)S(1)}, u32[]{:S(2)}, u32[]{:S(2)}) collective-permute-start(bf16[2,256,384]{2,1,0:T(8,128)(2,1)S(1)} %bitcast.22), channel_id=1, source_target_pairs={{0,16},{16,32},{32,48},{48,64},{64,80},{80,96},{96,112},{112,0},{1... | collective-permute-start | bytes 1179656 | tf_op jit(solution)/shard_map/ppermute | solution.py:381
  8.3 16.8 %copy-start.5 = (bf16[512,2,384]{2,1,0:T(2,128)(2,1)S(1)}, bf16[512,2,384]{2,1,0:T(2,128)(2,1)}, u32[]{:S(2)}) copy-start(bf16[512,2,384]{2,1,0:T(2,128)(2,1)} %param.22) | copy-start | bytes 2359300
  19.4 10.9 %collective-permute-start.5 = (bf16[2,256,384]{2,1,0:T(8,128)(2,1)S(1)}, bf16[2,256,384]{2,1,0:T(8,128)(2,1)S(1)}, u32[]{:S(2)}, u32[]{:S(2)}) collective-permute-start(bf16[2,256,384]{2,1,0:T(8,128)(2,1)S(1)} %collective-permute-done.1.right.refs_1_), channel_id=1, source_target_pairs={{0,16},{16,32},{32,48},{48,64},{64,80},{80,96},{96,112},{112,0},{1... | collective-permute-start | bytes 1179656 | tf_op jit(solution)/shard_map/ppermute | solution.py:381
  19.4 10.9 %collective-permute-start.7 = (bf16[2,256,384]{2,1,0:T(8,128)(2,1)S(1)}, bf16[2,256,384]{2,1,0:T(8,128)(2,1)S(1)}, u32[]{:S(2)}, u32[]{:S(2)}) collective-permute-start(bf16[2,256,384]{2,1,0:T(8,128)(2,1)S(1)} %collective-permute-done.2.left.refs_2_), channel_id=1, source_target_pairs={{0,112},{16,0},{32,16},{48,32},{64,48},{80,64},{96,80},{112,96},{1... | collective-permute-start | bytes 1179656 | tf_op jit(solution)/shard_map/ppermute | solution.py:381
  22.6 2.5 %collective-permute-start.3 = (bf16[256,384]{1,0:T(8,128)(2,1)}, bf16[256,384]{1,0:T(8,128)(2,1)S(1)}, u32[]{:S(2)}, u32[]{:S(2)}) collective-permute-start(bf16[256,384]{1,0:T(8,128)(2,1)} %get-tuple-element.59.q0), channel_id=1, source_target_pairs={{0,8},{8,0},{1,9},{9,1},{2,10},{10,2},{3,11},{11,3},{4,12},{12,4},... | collective-permute-start | bytes 589832 | tf_op jit(solution)/shard_map/ppermute | solution.py:381
  22.6 28.6 %collective-permute-start.12 = (bf16[192,3072]{1,0:T(8,128)(2,1)}, bf16[192,3072]{1,0:T(8,128)(2,1)S(1)}, u32[]{:S(2)}, u32[]{:S(2)}) collective-permute-start(bf16[192,3072]{1,0:T(8,128)(2,1)} %get-tuple-element.102), channel_id=1, source_target_pairs={{0,2},{2,0},{4,6},{6,4},{1,3},{3,1},{5,7},{7,5},{8,10},{10,8},{12,... | collective-permute-start | bytes 3538952 | tf_op jit(solution)/shard_map/ppermute | solution.py:385
  24.2 9.3 %collective-permute-start = (bf16[256,384]{1,0:T(8,128)(2,1)}, bf16[256,384]{1,0:T(8,128)(2,1)S(1)}, u32[]{:S(2)}, u32[]{:S(2)}) collective-permute-start(bf16[256,384]{1,0:T(8,128)(2,1)} %get-tuple-element.59.q0), channel_id=1, source_target_pairs={{0,128},{128,0},{1,129},{129,1},{2,130},{130,2},{3,131},{131,3},{4... | collective-permute-start | bytes 589832 | tf_op jit(solution)/shard_map/ppermute | solution.py:381
  30.3 10.0 %collective-permute-start.6 = (bf16[2,256,384]{2,1,0:T(8,128)(2,1)S(1)}, bf16[2,256,384]{2,1,0:T(8,128)(2,1)S(1)}, u32[]{:S(2)}, u32[]{:S(2)}) collective-permute-start(bf16[2,256,384]{2,1,0:T(8,128)(2,1)S(1)} %collective-permute-done.5.refs_0_.refs_3_), channel_id=1, source_target_pairs={{0,16},{16,32},{32,48},{48,64},{64,80},{80,96},{96,112},{112,0},{1... | collective-permute-start | bytes 1179656 | tf_op jit(solution)/shard_map/ppermute | solution.py:381
  30.3 10.0 %collective-permute-start.9 = (bf16[2,256,384]{2,1,0:T(8,128)(2,1)S(1)}, bf16[2,256,384]{2,1,0:T(8,128)(2,1)S(1)}, u32[]{:S(2)}, u32[]{:S(2)}) collective-permute-start(bf16[2,256,384]{2,1,0:T(8,128)(2,1)S(1)} %collective-permute-done.7.refs_1_.refs_4_), channel_id=1, source_target_pairs={{0,112},{16,0},{32,16},{48,32},{64,48},{80,64},{96,80},{112,96},{1... | collective-permute-start | bytes 1179656 | tf_op jit(solution)/shard_map/ppermute | solution.py:381
  33.5 1.4 %collective-permute-start.4 = (bf16[256,384]{1,0:T(8,128)(2,1)S(1)}, bf16[256,384]{1,0:T(8,128)(2,1)S(1)}, u32[]{:S(2)}, u32[]{:S(2)}) collective-permute-start(bf16[256,384]{1,0:T(8,128)(2,1)S(1)} %collective-permute-done.q0), channel_id=1, source_target_pairs={{0,8},{8,0},{1,9},{9,1},{2,10},{10,2},{3,11},{11,3},{4,12},{12,4},... | collective-permute-start | bytes 589832 | tf_op jit(solution)/shard_map/ppermute | solution.py:381
  40.3 7.5 %collective-permute-start.8 = (bf16[256,384]{1,0:T(8,128)(2,1)S(1)}, bf16[256,384]{1,0:T(8,128)(2,1)S(1)}, u32[]{:S(2)}, u32[]{:S(2)}) collective-permute-start(bf16[256,384]{1,0:T(8,128)(2,1)S(1)} %slice_bitcast_fusion.1), channel_id=1, source_target_pairs={{0,16},{16,32},{32,48},{48,64},{64,80},{80,96},{96,112},{112,0},{1... | collective-permute-start | bytes 589832 | tf_op jit(solution)/shard_map/ppermute | solution.py:381
  40.4 7.4 %collective-permute-start.10 = (bf16[256,384]{1,0:T(8,128)(2,1)S(1)}, bf16[256,384]{1,0:T(8,128)(2,1)S(1)}, u32[]{:S(2)}, u32[]{:S(2)}) collective-permute-start(bf16[256,384]{1,0:T(8,128)(2,1)S(1)} %slice_bitcast_fusion), channel_id=1, source_target_pairs={{0,112},{16,0},{32,16},{48,32},{64,48},{80,64},{96,80},{112,96},{1... | collective-permute-start | bytes 589832 | tf_op jit(solution)/shard_map/ppermute | solution.py:381
  51.2 13.3 %collective-permute-start.17 = (bf16[192,3072]{1,0:T(8,128)(2,1)S(1)}, bf16[192,3072]{1,0:T(8,128)(2,1)S(1)}, u32[]{:S(2)}, u32[]{:S(2)}) collective-permute-start(bf16[192,3072]{1,0:T(8,128)(2,1)S(1)} %collective-permute-done.12.refs_5_), channel_id=1, source_target_pairs={{0,8},{8,0},{1,9},{9,1},{2,10},{10,2},{3,11},{11,3},{4,12},{12,4},... | collective-permute-start | bytes 3538952 | tf_op jit(solution)/shard_map/ppermute | solution.py:381
  51.2 3.2 %collective-permute-start.13 = (bf16[2,144,384]{2,1,0:T(8,128)(2,1)S(1)}, bf16[2,144,384]{2,1,0:T(8,128)(2,1)S(1)}, u32[]{:S(2)}, u32[]{:S(2)}) collective-permute-start(bf16[2,144,384]{2,1,0:T(8,128)(2,1)S(1)} %get-tuple-element.104), channel_id=1, source_target_pairs={{0,8},{8,0},{1,9},{9,1},{2,10},{10,2},{3,11},{11,3},{4,12},{12,4},... | collective-permute-start | bytes 663560 | tf_op jit(solution)/shard_map/ppermute | solution.py:381
  52.7 11.8 %copy-start = (bf16[384,3072]{1,0:T(8,128)(2,1)S(1)}, bf16[384,3072]{1,0:T(8,128)(2,1)}, u32[]{:S(2)}) copy-start(bf16[384,3072]{1,0:T(8,128)(2,1)} %refs_4_.1) | copy-start | bytes 7077892
  52.7 2.0 %collective-permute-start.11 = (bf16[2,144,384]{2,1,0:T(8,128)(2,1)S(1)}, bf16[2,144,384]{2,1,0:T(8,128)(2,1)S(1)}, u32[]{:S(2)}, u32[]{:S(2)}) collective-permute-start(bf16[2,144,384]{2,1,0:T(8,128)(2,1)S(1)} %get-tuple-element.95), channel_id=1, source_target_pairs={{0,8},{8,0},{1,9},{9,1},{2,10},{10,2},{3,11},{11,3},{4,12},{12,4},... | collective-permute-start | bytes 663560 | tf_op jit(solution)/shard_map/ppermute | solution.py:381
  55.9 5.8 %collective-permute-start.14 = (bf16[144,384]{1,0:T(8,128)(2,1)S(1)}, bf16[144,384]{1,0:T(8,128)(2,1)S(1)}, u32[]{:S(2)}, u32[]{:S(2)}) collective-permute-start(bf16[144,384]{1,0:T(8,128)(2,1)S(1)} %get-tuple-element.106), channel_id=1, source_target_pairs={{0,128},{128,0},{1,129},{129,1},{2,130},{130,2},{3,131},{131,3},{4... | collective-permute-start | bytes 331784 | tf_op jit(solution)/shard_map/ppermute | solution.py:381
  56.8 6.3 %collective-permute-start.15 = (bf16[144,384]{1,0:T(8,128)(2,1)S(1)}, bf16[144,384]{1,0:T(8,128)(2,1)S(1)}, u32[]{:S(2)}, u32[]{:S(2)}) collective-permute-start(bf16[144,384]{1,0:T(8,128)(2,1)S(1)} %get-tuple-element.107), channel_id=1, source_target_pairs={{0,2},{2,0},{4,6},{6,4},{1,3},{3,1},{5,7},{7,5},{8,10},{10,8},{12,... | collective-permute-start | bytes 331784 | tf_op jit(solution)/shard_map/ppermute | solution.py:385
  58.4 6.1 %collective-permute-start.16 = (bf16[144,384]{1,0:T(8,128)(2,1)S(1)}, bf16[144,384]{1,0:T(8,128)(2,1)S(1)}, u32[]{:S(2)}, u32[]{:S(2)}) collective-permute-start(bf16[144,384]{1,0:T(8,128)(2,1)S(1)} %get-tuple-element.108), channel_id=1, source_target_pairs={{0,130},{2,128},{4,134},{6,132},{128,2},{130,0},{132,6},{134,4},{1... | collective-permute-start | bytes 331784 | tf_op jit(solution)/shard_map/ppermute | solution.py:449
  64.5 16.2 %copy-start.6 = (f32[3072]{0:T(1024)S(1)}, f32[3072]{0:T(1024)}, u32[]{:S(2)}) copy-start(f32[3072]{0:T(1024)} %param.24) | copy-start | bytes 36868
  64.5 16.2 %copy-start.7 = (f32[3072]{0:T(1024)S(1)}, f32[3072]{0:T(1024)}, u32[]{:S(2)}) copy-start(f32[3072]{0:T(1024)} %param.17) | copy-start | bytes 36868
  66.3 10.5 %collective-permute-start.18 = (bf16[32,3072]{1,0:T(8,128)(2,1)S(1)}, bf16[32,3072]{1,0:T(8,128)(2,1)S(1)}, u32[]{:S(2)}, u32[]{:S(2)}) collective-permute-start(bf16[32,3072]{1,0:T(8,128)(2,1)S(1)} %get-tuple-element.111), channel_id=1, source_target_pairs={{0,5},{1,4},{2,7},{3,6},{4,1},{5,0},{6,3},{7,2},{8,13},{9,12},{10,... | collective-permute-start | bytes 589832 | tf_op jit(solution)/shard_map/ppermute | solution.py:457
  70.2 10.5 %collective-permute-start.19 = (bf16[32,3072]{1,0:T(8,128)(2,1)S(1)}, bf16[32,3072]{1,0:T(8,128)(2,1)S(1)}, u32[]{:S(2)}, u32[]{:S(2)}) collective-permute-start(bf16[32,3072]{1,0:T(8,128)(2,1)S(1)} %get-tuple-element.112), channel_id=1, source_target_pairs={{0,4},{2,6},{4,0},{6,2},{1,5},{3,7},{5,1},{7,3},{8,12},{10,14},{12... | collective-permute-start | bytes 589832 | tf_op jit(solution)/shard_map/ppermute | solution.py:381
  70.8 9.9 %collective-permute-start.20 = (bf16[32,3072]{1,0:T(8,128)(2,1)S(1)}, bf16[32,3072]{1,0:T(8,128)(2,1)S(1)}, u32[]{:S(2)}, u32[]{:S(2)}) collective-permute-start(bf16[32,3072]{1,0:T(8,128)(2,1)S(1)} %get-tuple-element.113), channel_id=1, source_target_pairs={{0,1},{1,0},{2,3},{3,2},{4,5},{5,4},{6,7},{7,6},{8,9},{9,8},{10,11... | collective-permute-start | bytes 589832 | tf_op jit(solution)/shard_map/ppermute | solution.py:381
  81.8 9.4 %collective-permute-start.24 = (bf16[32,3072]{1,0:T(8,128)(2,1)S(1)}, bf16[32,3072]{1,0:T(8,128)(2,1)S(1)}, u32[]{:S(2)}, u32[]{:S(2)}) collective-permute-start(bf16[32,3072]{1,0:T(8,128)(2,1)S(1)} %add_convert_fusion.refs_0_), channel_id=1, source_target_pairs={{0,4},{2,6},{4,0},{6,2},{1,5},{3,7},{5,1},{7,3},{8,12},{10,14},{12... | collective-permute-start | bytes 589832 | tf_op jit(solution)/shard_map/ppermute | solution.py:381
  83.5 8.9 %collective-permute-start.21 = (bf16[32,3072]{1,0:T(8,128)(2,1)S(1)}, bf16[32,3072]{1,0:T(8,128)(2,1)S(1)}, u32[]{:S(2)}, u32[]{:S(2)}) collective-permute-start(bf16[32,3072]{1,0:T(8,128)(2,1)S(1)} %add_convert_fusion.refs_0_), channel_id=1, source_target_pairs={{0,1},{1,0},{2,3},{3,2},{4,5},{5,4},{6,7},{7,6},{8,9},{9,8},{10,11... | collective-permute-start | bytes 589832 | tf_op jit(solution)/shard_map/ppermute | solution.py:381
  85.7 10.1 %collective-permute-start.27 = (bf16[32,3072]{1,0:T(8,128)(2,1)S(1)}, bf16[32,3072]{1,0:T(8,128)(2,1)S(1)}, u32[]{:S(2)}, u32[]{:S(2)}) collective-permute-start(bf16[32,3072]{1,0:T(8,128)(2,1)S(1)} %add_convert_fusion.refs_0_), channel_id=1, source_target_pairs={{0,6},{2,0},{4,2},{6,4},{1,7},{3,1},{5,3},{7,5},{8,14},{10,8},{12,... | collective-permute-start | bytes 589832 | tf_op jit(solution)/shard_map/ppermute | solution.py:381
  86.4 9.4 %collective-permute-start.26 = (bf16[32,3072]{1,0:T(8,128)(2,1)S(1)}, bf16[32,3072]{1,0:T(8,128)(2,1)S(1)}, u32[]{:S(2)}, u32[]{:S(2)}) collective-permute-start(bf16[32,3072]{1,0:T(8,128)(2,1)S(1)} %add_convert_fusion.refs_0_), channel_id=1, source_target_pairs={{0,2},{2,4},{4,6},{6,0},{1,3},{3,5},{5,7},{7,1},{8,10},{10,12},{12... | collective-permute-start | bytes 589832 | tf_op jit(solution)/shard_map/ppermute | solution.py:381
  91.1 7.2 %collective-permute-start.25 = (bf16[32,3072]{1,0:T(8,128)(2,1)S(1)}, bf16[32,3072]{1,0:T(8,128)(2,1)S(1)}, u32[]{:S(2)}, u32[]{:S(2)}) collective-permute-start(bf16[32,3072]{1,0:T(8,128)(2,1)S(1)} %collective-permute-done.24.refs_4_), channel_id=1, source_target_pairs={{0,1},{1,0},{2,3},{3,2},{4,5},{5,4},{6,7},{7,6},{8,9},{9,8},{10,11... | collective-permute-start | bytes 589832 | tf_op jit(solution)/shard_map/ppermute | solution.py:381
  92.4 5.9 %collective-permute-start.23 = (bf16[32,3072]{1,0:T(8,128)(2,1)S(1)}, bf16[32,3072]{1,0:T(8,128)(2,1)S(1)}, u32[]{:S(2)}, u32[]{:S(2)}) collective-permute-start(bf16[32,3072]{1,0:T(8,128)(2,1)S(1)} %collective-permute-done.21.refs_1_), channel_id=1, source_target_pairs={{0,6},{2,0},{4,2},{6,4},{1,7},{3,1},{5,3},{7,5},{8,14},{10,8},{12,... | collective-permute-start | bytes 589832 | tf_op jit(solution)/shard_map/ppermute | solution.py:381
  94.5 6.9 %collective-permute-start.22 = (bf16[32,3072]{1,0:T(8,128)(2,1)S(1)}, bf16[32,3072]{1,0:T(8,128)(2,1)S(1)}, u32[]{:S(2)}, u32[]{:S(2)}) collective-permute-start(bf16[32,3072]{1,0:T(8,128)(2,1)S(1)} %collective-permute-done.21.refs_1_), channel_id=1, source_target_pairs={{0,2},{2,4},{4,6},{6,0},{1,3},{3,5},{5,7},{7,1},{8,10},{10,12},{12... | collective-permute-start | bytes 589832 | tf_op jit(solution)/shard_map/ppermute | solution.py:381
  (4 other events, 27.9 us)

commit v5 on v4

--- a/solution.py
+++ b/solution.py
@@ -28,7 +28,6 @@
 HALF = COUNT // 2
 SPLIT = WIDTH // 2
 FULL = pl.BlockSpec(memory_space=pltpu.VMEM)
-SMEM = pl.BlockSpec(memory_space=pltpu.SMEM)
 
 
 def params(mib=48):
@@ -38,6 +37,10 @@
 def cost(flops, nbytes, exps=0):
     del flops, nbytes, exps
     return pl.CostEstimate(flops=1024, bytes_accessed=1024, transcendentals=0)
+
+
+def coordinate(place, n):
+    return jnp.max(place[n : n + 1, :]).astype(jnp.int32)
 
 
 def head_of(head):
@@ -72,12 +75,10 @@
 def qkv_kernel(place, *refs):
     given, (q, k, v, w_half), buffers, sems = refs[:9], refs[9:13], refs[13:-1], refs[-1]
     lat, w, trig, rows, shift, scale, q_gain, k_gain, half = buffers
-    part = pl.ds(pl.multiple_of(place[2] * SPLIT, SPLIT), SPLIT)
     copy = lambda n, source, target: pltpu.make_async_copy(source, target, sems.at[n])
     weights = [copy(n, given[1].at[n], w.at[n]) for n in range(3)]
     small = [copy(n + 1, given[n], buffers[n]) for n in range(2, 8)]
-    latents, half_in = copy(9, given[0], lat), copy(10, given[8].at[part], half)
-    half_out = copy(11, half, w_half)
+    latents, half_out = copy(9, given[0], lat), copy(11, half, w_half)
     latents.start()
     for c in small:
         c.start()
@@ -112,6 +113,8 @@
         weights[n].wait()
         if n == 0:
             weights[2].start()
+            part = pl.ds(pl.multiple_of(coordinate(place, 2) * SPLIT, SPLIT), SPLIT)
+            half_in = copy(10, given[8].at[part], half)
             half_in.start()
         out = jnp.dot(normed, w[n], preferred_element_type=jnp.float32)
         for c in HEADS:
@@ -131,7 +134,7 @@
     half = (SPLIT, MODEL)
     return pl.pallas_call(
         qkv_kernel,
-        in_specs=[SMEM] + [anywhere] * 9,
+        in_specs=[FULL] + [anywhere] * 9,
         out_specs=[FULL] * 3 + [anywhere],
         out_shape=[jax.ShapeDtypeStruct((COUNT, WIDTH), jnp.bfloat16)] * 3
         + [jax.ShapeDtypeStruct(half, jnp.bfloat16)],
@@ -277,7 +280,7 @@
 
 
 def merge_kernel(place, *refs):
-    swap = jnp.bitwise_and(place[1], 1) == 1
+    swap = jnp.bitwise_and(coordinate(place, 1), 1) == 1
     for block in range(2):
         state, message = refs[4 * block : 4 * block + 3], refs[4 * block + 3]
         mine, other = refs[8 + 2 * block : 10 + 2 * block]
@@ -294,7 +297,7 @@
 def merge_call(place, *args):
     return pl.pallas_call(
         merge_kernel,
-        in_specs=[SMEM] + [FULL] * 8,
+        in_specs=[FULL] * 9,
         out_specs=[FULL] * 4,
         out_shape=[jax.ShapeDtypeStruct((HALF + EXTRA, WIDTH), jnp.bfloat16)] * 4,
         compiler_params=params(24),
@@ -306,9 +309,10 @@
 
 
 def project_kernel(place, *refs):
-    messages, (w, w_x, w_core) = refs[:4], refs[4:7]
+    messages, (w, w_pair, w_core) = refs[:4], refs[4:7]
     outs, attn, full = refs[7:11], refs[11], refs[12]
-    x, high_y, first = place[0], lax.shift_right_logical(place[1], 1), place[2] == 0
+    x, first = coordinate(place, 0), coordinate(place, 2) == 0
+    high_y = lax.shift_right_logical(coordinate(place, 1), 1)
     for n in range(2):
         for head in range(LOCAL_HEADS):
             c = head_of(head)
@@ -321,7 +325,7 @@
     for at in range(0, MODEL, 768):
         cols = slice(at, at + 768)
         total = jnp.dot(attn[:, :WIDTH], w[:, cols], preferred_element_type=jnp.float32)
-        total += jnp.dot(by_x, w_x[:, cols], preferred_element_type=jnp.float32)
+        total += jnp.dot(by_x, w_pair[:, cols], preferred_element_type=jnp.float32)
         total += jnp.dot(by_core, w_core[:, cols], preferred_element_type=jnp.float32)
         full[:, cols] = total.astype(jnp.bfloat16)
     for out, (dy, dx) in zip(outs, QUARTERS):
@@ -332,7 +336,7 @@
 def project_call(place, messages, weights):
     return pl.pallas_call(
         project_kernel,
-        in_specs=[SMEM] + [FULL] * 7,
+        in_specs=[FULL] * 8,
         out_specs=[FULL] * 4,
         out_shape=[jax.ShapeDtypeStruct((ROWS, MODEL), jnp.bfloat16)] * 4,
         scratch_shapes=[
@@ -346,7 +350,7 @@
 
 def put_kernel(offsets, place, *refs):
     out, sems = refs[-2:]
-    x, y = place[0], place[1]
+    x, y = coordinate(place, 0), coordinate(place, 1)
     copies = []
     for n, (flip, step) in enumerate(offsets):
         from_y = lax.rem(y + 4 - step, 4)
@@ -366,7 +370,7 @@
     more = [] if out is None else [out]
     return pl.pallas_call(
         functools.partial(put_kernel, offsets),
-        in_specs=[SMEM] + [FULL] * count + [anywhere] * len(more),
+        in_specs=[FULL] * (count + 1) + [anywhere] * len(more),
         out_specs=anywhere,
         out_shape=jax.ShapeDtypeStruct((COUNT, MODEL), jnp.bfloat16),
         input_output_aliases={count + 1: 0} if more else {},
@@ -404,8 +408,9 @@
     b_out,
 ):
     after = lax.optimization_barrier
-    x, y, core = lax.axis_index("x_hi"), lax.axis_index("y"), lax.axis_index("core")
-    place = jnp.stack([x, y, core]).astype(jnp.int32)
+    x, y = lax.axis_index("x_hi"), lax.axis_index("y")
+    place = jnp.stack([x, y, lax.axis_index("core")] + [0] * 5).astype(jnp.float32)
+    place = jnp.broadcast_to(place[:, None], (8, HEAD))
     own = jnp.transpose(stale_kv, (1, 0, 2))
     r1, l1 = ring(own, "z", 1), ring(own, "z", -1)
 

time: 103 us -> 102 us (level)
  Pallas kernels: 26 us -> 24.1 us
    pallas_call x5, Pallas kernels: 14.5 us -> 12.6 us  [the longest x1 8.52 us: qkv_call(): pl.pallas_call(qkv_kernel, in_specs=[FULL] + [anywhere] * 9, out_specs=[F...]
  transfers between devices with their start and end apart: 28 -> 28, of which waited for: 16 -> 16; matrix products, arithmetic and copies ran while one was open for 2% -> 2% of each run, Pallas kernels for 22% -> 21%
where the time goes in v5:
time: 102 us
  starting transfers between devices  38.2 us (37%)
  waiting for transfers between devices  33.9 us (33%)
  Pallas kernels  24.1 us (24%)
  local copies, waits for them, and re-layouts  3.13 us (3%)
  other arithmetic  1.14 us (1%)
  between operations  1.04 us (1%)
    ppermute x24, starting transfers between devices, ring(): lax.ppermute(value, axis, [(i, (i + step) % size) for i in range(size)])  30.1 us
    ppermute x24, waiting for transfers between devices, ring(): lax.ppermute(value, axis, [(i, (i + step) % size) for i in range(size)])  24.8 us
    pallas_call x5, Pallas kernels, attend_call(): return list(call(*args))  9.6 us
    pallas_call x1, Pallas kernels, qkv_call(): pl.pallas_call(qkv_kernel, in_specs=[FULL] + [anywhere] * 9, out_specs=[F...  8.52 us
    ppermute x2, waiting for transfers between devices, beside_y(): return lax.ppermute(value, 'y', [(i, i ^ 1) for i in range(4)])  3.93 us
    ppermute x1, waiting for transfers between devices, shards(): lax.ppermute(both_ways, TENSOR, [(i, (i // 2 + 2) % 4 * 2 + (1 - i % 2))...  3.91 us
    ppermute x1, starting transfers between devices, shards(): lax.ppermute(both_ways, TENSOR, [(i, (i // 2 + 2) % 4 * 2 + (1 - i % 2))...  3.83 us
    ppermute x2, starting transfers between devices, beside_y(): return lax.ppermute(value, 'y', [(i, i ^ 1) for i in range(4)])  3.15 us
  transfers between devices with their start and end apart: 28, of which 16 were waited for; matrix products, arithmetic and copies ran while one was open for 2% of the time, Pallas kernels for 21%

profile of v5, /device:TPU:6, one launch (start us, length us, event | category | flops | bytes accessed | tf_op | source)
XLA Modules:
  0.0 101.6 jit_solution(9911063836291338602)
XLA Ops:
  1.7 5.9 %collective-permute-start.2 = (bf16[2,256,384]{2,1,0:T(8,128)(2,1)S(1)}, bf16[2,256,384]{2,1,0:T(8,128)(2,1)S(1)}, u32[]{:S(2)}, u32[]{:S(2)}) collective-permute-start(bf16[2,256,384]{2,1,0:T(8,128)(2,1)S(1)} %bitcast.21), channel_id=1, source_target_pairs={{0,112},{16,0},{32,16},{48,32},{64,48},{80,64},{96,80},{112,96},{1... | collective-permute-start | bytes 1179656 | tf_op jit(solution)/shard_map/ppermute | solution.py:385
  8.4 8.5 %shard_map.140 = (bf16[256,384]{1,0:T(8,128)(2,1)}, bf16[256,384]{1,0:T(8,128)(2,1)}, bf16[256,384]{1,0:T(8,128)(2,1)}, bf16[192,3072]{1,0:T(8,128)(2,1)}) custom-call(f32[8,128]{1,0:T(8,128)} %broadcast_in_dim.2.place, bf16[256,3072]{1,0:T(8,128)(2,1)} %refs_0_.1, bf16[3,3072,384]{2,1,0:T(8,128)(2,1)} %bitcast.28, bf16[288,768]{1,0:T(8,128)(2,1)} %constant.49.clone.refs_2_, ...), custom_call_target="tpu_custom_call" | custom-call | flops 1024 | bytes 1024 | tf_op jit(solution)/shard_map/pallas_call | solution.py:135
  16.9 2.4 %collective-permute-done.1.right.refs_1_ = bf16[2,256,384]{2,1,0:T(8,128)(2,1)S(1)} collective-permute-done((bf16[2,256,384]{2,1,0:T(8,128)(2,1)S(1)}, bf16[2,256,384]{2,1,0:T(8,128)(2,1)S(1)}, u32[]{:S(2)}, u32[]{:S(2)}) %collective-permute-start.1) | collective-permute-done | bytes 393248 | tf_op jit(solution)/shard_map/ppermute | solution.py:385
  19.4 3.2 %collective-permute-start.7 = (bf16[2,256,384]{2,1,0:T(8,128)(2,1)S(1)}, bf16[2,256,384]{2,1,0:T(8,128)(2,1)S(1)}, u32[]{:S(2)}, u32[]{:S(2)}) collective-permute-start(bf16[2,256,384]{2,1,0:T(8,128)(2,1)S(1)} %collective-permute-done.2.left.refs_2_), channel_id=1, source_target_pairs={{0,112},{16,0},{32,16},{48,32},{64,48},{80,64},{96,80},{112,96},{1... | collective-permute-start | bytes 1179656 | tf_op jit(solution)/shard_map/ppermute | solution.py:385
  22.6 1.6 %collective-permute-start.12 = (bf16[192,3072]{1,0:T(8,128)(2,1)}, bf16[192,3072]{1,0:T(8,128)(2,1)S(1)}, u32[]{:S(2)}, u32[]{:S(2)}) collective-permute-start(bf16[192,3072]{1,0:T(8,128)(2,1)} %get-tuple-element.102), channel_id=1, source_target_pairs={{0,2},{2,0},{4,6},{6,4},{1,3},{3,1},{5,7},{7,5},{8,10},{10,8},{12,... | collective-permute-start | bytes 3538952 | tf_op jit(solution)/shard_map/ppermute | solution.py:389
  25.2 2.3 %shard_map.141 = (f32[512,384]{1,0:T(8,128)S(1)}, f32[512,384]{1,0:T(8,128)S(1)}, f32[512,384]{1,0:T(8,128)S(1)}) custom-call(bf16[256,384]{1,0:T(8,128)(2,1)S(1)} %copy-done.1, bf16[256,384]{1,0:T(8,128)(2,1)S(1)} %collective-permute-done.3.q1, bf16[256,384]{1,0:T(8,128)(2,1)S(1)} %copy-done.2, bf16[256,384]{1,0:T(8,128)(2,1)S(1)} %copy-done.3, ...), custom_call_target="tpu_custom_call" | custom-call | flops 1024 | bytes 1024 | tf_op jit(solution)/shard_map/pallas_call | solution.py:225
  27.5 2.8 %collective-permute-done.5.refs_0_.refs_3_ = bf16[2,256,384]{2,1,0:T(8,128)(2,1)S(1)} collective-permute-done((bf16[2,256,384]{2,1,0:T(8,128)(2,1)S(1)}, bf16[2,256,384]{2,1,0:T(8,128)(2,1)S(1)}, u32[]{:S(2)}, u32[]{:S(2)}) %collective-permute-start.5) | collective-permute-done | bytes 393248 | tf_op jit(solution)/shard_map/ppermute | solution.py:385
  30.3 3.2 %collective-permute-start.9 = (bf16[2,256,384]{2,1,0:T(8,128)(2,1)S(1)}, bf16[2,256,384]{2,1,0:T(8,128)(2,1)S(1)}, u32[]{:S(2)}, u32[]{:S(2)}) collective-permute-start(bf16[2,256,384]{2,1,0:T(8,128)(2,1)S(1)} %collective-permute-done.7.refs_1_.refs_4_), channel_id=1, source_target_pairs={{0,112},{16,0},{32,16},{48,32},{64,48},{80,64},{96,80},{112,96},{1... | collective-permute-start | bytes 1179656 | tf_op jit(solution)/shard_map/ppermute | solution.py:385
  33.5 1.4 %collective-permute-done.4.q1 = bf16[256,384]{1,0:T(8,128)(2,1)S(1)} collective-permute-done((bf16[256,384]{1,0:T(8,128)(2,1)S(1)}, bf16[256,384]{1,0:T(8,128)(2,1)S(1)}, u32[]{:S(2)}, u32[]{:S(2)}) %collective-permute-start.4) | collective-permute-done | bytes 196640 | tf_op jit(solution)/shard_map/ppermute | solution.py:385
  35.0 3.1 %shard_map.143 = (f32[512,384]{1,0:T(8,128)S(1)}, f32[512,384]{1,0:T(8,128)S(1)}, f32[512,384]{1,0:T(8,128)S(1)}) custom-call(bf16[256,384]{1,0:T(8,128)(2,1)S(1)} %collective-permute-done.q0, bf16[256,384]{1,0:T(8,128)(2,1)S(1)} %collective-permute-done.4.q1, bf16[2,256,384]{2,1,0:T(8,128)(2,1)S(1)} %bitcast.24, ...), custom_call_target="tpu_custom_call" | custom-call | flops 1024 | bytes 1024 | tf_op jit(solution)/shard_map/pallas_call | solution.py:225
  38.0 1.4 %shard_map.142 = (f32[512,384]{1,0:T(8,128)S(1)}, f32[512,384]{1,0:T(8,128)S(1)}, f32[512,384]{1,0:T(8,128)S(1)}) custom-call(bf16[256,384]{1,0:T(8,128)(2,1)S(1)} %copy-done.1, bf16[256,384]{1,0:T(8,128)(2,1)S(1)} %collective-permute-done.3.q1, bf16[2,256,384]{2,1,0:T(8,128)(2,1)S(1)} %collective-permute-done.5.refs_0_.refs_3_, ...), custom_call_target="tpu_custom_call" | custom-call | flops 1024 | bytes 1024 | tf_op jit(solution)/shard_map/pallas_call | solution.py:225
  40.4 3.2 %collective-permute-start.10 = (bf16[256,384]{1,0:T(8,128)(2,1)S(1)}, bf16[256,384]{1,0:T(8,128)(2,1)S(1)}, u32[]{:S(2)}, u32[]{:S(2)}) collective-permute-start(bf16[256,384]{1,0:T(8,128)(2,1)S(1)} %slice_bitcast_fusion), channel_id=1, source_target_pairs={{0,112},{16,0},{32,16},{48,32},{64,48},{80,64},{96,80},{112,96},{1... | collective-permute-start | bytes 589832 | tf_op jit(solution)/shard_map/ppermute | solution.py:385
  43.6 1.4 %shard_map.144 = (f32[512,384]{1,0:T(8,128)S(1)}, f32[512,384]{1,0:T(8,128)S(1)}, f32[512,384]{1,0:T(8,128)S(1)}) custom-call(bf16[256,384]{1,0:T(8,128)(2,1)S(1)} %copy-done.1, bf16[256,384]{1,0:T(8,128)(2,1)S(1)} %collective-permute-done.3.q1, bf16[2,256,384]{2,1,0:T(8,128)(2,1)S(1)} %collective-permute-done.6.refs_0_, ...), custom_call_target="tpu_custom_call" | custom-call | flops 1024 | bytes 1024 | tf_op jit(solution)/shard_map/pallas_call | solution.py:225
  45.0 1.4 %shard_map.145 = (f32[512,384]{1,0:T(8,128)S(1)}, f32[512,384]{1,0:T(8,128)S(1)}, f32[512,384]{1,0:T(8,128)S(1)}) custom-call(bf16[256,384]{1,0:T(8,128)(2,1)S(1)} %collective-permute-done.q0, bf16[256,384]{1,0:T(8,128)(2,1)S(1)} %collective-permute-done.4.q1, bf16[2,256,384]{2,1,0:T(8,128)(2,1)S(1)} %collective-permute-done.6.refs_0_, ...), custom_call_target="tpu_custom_call" | custom-call | flops 1024 | bytes 1024 | tf_op jit(solution)/shard_map/pallas_call | solution.py:225
  46.4 1.3 %collective-permute-done.8.keys = bf16[256,384]{1,0:T(8,128)(2,1)S(1)} collective-permute-done((bf16[256,384]{1,0:T(8,128)(2,1)S(1)}, bf16[256,384]{1,0:T(8,128)(2,1)S(1)}, u32[]{:S(2)}, u32[]{:S(2)}) %collective-permute-start.8) | collective-permute-done | bytes 196640 | tf_op jit(solution)/shard_map/ppermute | solution.py:385
  48.7 2.5 %collective-permute-done.12.refs_5_ = bf16[192,3072]{1,0:T(8,128)(2,1)S(1)} collective-permute-done((bf16[192,3072]{1,0:T(8,128)(2,1)}, bf16[192,3072]{1,0:T(8,128)(2,1)S(1)}, u32[]{:S(2)}, u32[]{:S(2)}) %collective-permute-start.12) | collective-permute-done | bytes 1179680 | tf_op jit(solution)/shard_map/ppermute | solution.py:389
  52.8 1.6 %collective-permute-done.13.refs_7_ = bf16[2,144,384]{2,1,0:T(8,128)(2,1)S(1)} collective-permute-done((bf16[2,144,384]{2,1,0:T(8,128)(2,1)S(1)}, bf16[2,144,384]{2,1,0:T(8,128)(2,1)S(1)}, u32[]{:S(2)}, u32[]{:S(2)}) %collective-permute-start.13) | collective-permute-done | bytes 221216 | tf_op jit(solution)/shard_map/ppermute | solution.py:385
  56.3 1.6 %collective-permute-start.15 = (bf16[144,384]{1,0:T(8,128)(2,1)S(1)}, bf16[144,384]{1,0:T(8,128)(2,1)S(1)}, u32[]{:S(2)}, u32[]{:S(2)}) collective-permute-start(bf16[144,384]{1,0:T(8,128)(2,1)S(1)} %get-tuple-element.107), channel_id=1, source_target_pairs={{0,2},{2,0},{4,6},{6,4},{1,3},{3,1},{5,7},{7,5},{8,10},{10,8},{12,... | collective-permute-start | bytes 331784 | tf_op jit(solution)/shard_map/ppermute | solution.py:389
  59.0 2.3 %collective-permute-done.14.refs_1_ = bf16[144,384]{1,0:T(8,128)(2,1)S(1)} collective-permute-done((bf16[144,384]{1,0:T(8,128)(2,1)S(1)}, bf16[144,384]{1,0:T(8,128)(2,1)S(1)}, u32[]{:S(2)}, u32[]{:S(2)}) %collective-permute-start.14) | collective-permute-done | bytes 110624 | tf_op jit(solution)/shard_map/ppermute | solution.py:385
  61.3 1.4 %collective-permute-done.15.refs_2_ = bf16[144,384]{1,0:T(8,128)(2,1)S(1)} collective-permute-done((bf16[144,384]{1,0:T(8,128)(2,1)S(1)}, bf16[144,384]{1,0:T(8,128)(2,1)S(1)}, u32[]{:S(2)}, u32[]{:S(2)}) %collective-permute-start.15) | collective-permute-done | bytes 110624 | tf_op jit(solution)/shard_map/ppermute | solution.py:389
  62.7 1.3 %collective-permute-done.16.refs_3_ = bf16[144,384]{1,0:T(8,128)(2,1)S(1)} collective-permute-done((bf16[144,384]{1,0:T(8,128)(2,1)S(1)}, bf16[144,384]{1,0:T(8,128)(2,1)S(1)}, u32[]{:S(2)}, u32[]{:S(2)}) %collective-permute-start.16) | collective-permute-done | bytes 110624 | tf_op jit(solution)/shard_map/ppermute | solution.py:454
  65.3 3.8 %collective-permute-start.18 = (bf16[32,3072]{1,0:T(8,128)(2,1)S(1)}, bf16[32,3072]{1,0:T(8,128)(2,1)S(1)}, u32[]{:S(2)}, u32[]{:S(2)}) collective-permute-start(bf16[32,3072]{1,0:T(8,128)(2,1)S(1)} %get-tuple-element.111), channel_id=1, source_target_pairs={{0,5},{1,4},{2,7},{3,6},{4,1},{5,0},{6,3},{7,2},{8,13},{9,12},{10,... | collective-permute-start | bytes 589832 | tf_op jit(solution)/shard_map/ppermute | solution.py:462
  69.8 2.1 %collective-permute-start.20 = (bf16[32,3072]{1,0:T(8,128)(2,1)S(1)}, bf16[32,3072]{1,0:T(8,128)(2,1)S(1)}, u32[]{:S(2)}, u32[]{:S(2)}) collective-permute-start(bf16[32,3072]{1,0:T(8,128)(2,1)S(1)} %get-tuple-element.113), channel_id=1, source_target_pairs={{0,1},{1,0},{2,3},{3,2},{4,5},{5,4},{6,7},{7,6},{8,9},{9,8},{10,11... | collective-permute-start | bytes 589832 | tf_op jit(solution)/shard_map/ppermute | solution.py:385
  71.9 3.9 %collective-permute-done.18 = bf16[32,3072]{1,0:T(8,128)(2,1)S(1)} collective-permute-done((bf16[32,3072]{1,0:T(8,128)(2,1)S(1)}, bf16[32,3072]{1,0:T(8,128)(2,1)S(1)}, u32[]{:S(2)}, u32[]{:S(2)}) %collective-permute-start.18) | collective-permute-done | bytes 196640 | tf_op jit(solution)/shard_map/ppermute | solution.py:462
  75.8 3.8 %collective-permute-done.19 = bf16[32,3072]{1,0:T(8,128)(2,1)S(1)} collective-permute-done((bf16[32,3072]{1,0:T(8,128)(2,1)S(1)}, bf16[32,3072]{1,0:T(8,128)(2,1)S(1)}, u32[]{:S(2)}, u32[]{:S(2)}) %collective-permute-start.19) | collective-permute-done | bytes 196640 | tf_op jit(solution)/shard_map/ppermute | solution.py:385
  80.7 1.8 %collective-permute-start.24 = (bf16[32,3072]{1,0:T(8,128)(2,1)S(1)}, bf16[32,3072]{1,0:T(8,128)(2,1)S(1)}, u32[]{:S(2)}, u32[]{:S(2)}) collective-permute-start(bf16[32,3072]{1,0:T(8,128)(2,1)S(1)} %add_convert_fusion.refs_0_), channel_id=1, source_target_pairs={{0,4},{2,6},{4,0},{6,2},{1,5},{3,7},{5,1},{7,3},{8,12},{10,14},{12... | collective-permute-start | bytes 589832 | tf_op jit(solution)/shard_map/ppermute | solution.py:385
  82.5 2.1 %collective-permute-start.21 = (bf16[32,3072]{1,0:T(8,128)(2,1)S(1)}, bf16[32,3072]{1,0:T(8,128)(2,1)S(1)}, u32[]{:S(2)}, u32[]{:S(2)}) collective-permute-start(bf16[32,3072]{1,0:T(8,128)(2,1)S(1)} %add_convert_fusion.refs_0_), channel_id=1, source_target_pairs={{0,1},{1,0},{2,3},{3,2},{4,5},{5,4},{6,7},{7,6},{8,9},{9,8},{10,11... | collective-permute-start | bytes 589832 | tf_op jit(solution)/shard_map/ppermute | solution.py:385
  86.7 3.4 %collective-permute-done.24.refs_4_ = bf16[32,3072]{1,0:T(8,128)(2,1)S(1)} collective-permute-done((bf16[32,3072]{1,0:T(8,128)(2,1)S(1)}, bf16[32,3072]{1,0:T(8,128)(2,1)S(1)}, u32[]{:S(2)}, u32[]{:S(2)}) %collective-permute-start.24) | collective-permute-done | bytes 196640 | tf_op jit(solution)/shard_map/ppermute | solution.py:385
  90.1 1.3 %collective-permute-start.25 = (bf16[32,3072]{1,0:T(8,128)(2,1)S(1)}, bf16[32,3072]{1,0:T(8,128)(2,1)S(1)}, u32[]{:S(2)}, u32[]{:S(2)}) collective-permute-start(bf16[32,3072]{1,0:T(8,128)(2,1)S(1)} %collective-permute-done.24.refs_4_), channel_id=1, source_target_pairs={{0,1},{1,0},{2,3},{3,2},{4,5},{5,4},{6,7},{7,6},{8,9},{9,8},{10,11... | collective-permute-start | bytes 589832 | tf_op jit(solution)/shard_map/ppermute | solution.py:385
  91.4 2.1 %collective-permute-start.23 = (bf16[32,3072]{1,0:T(8,128)(2,1)S(1)}, bf16[32,3072]{1,0:T(8,128)(2,1)S(1)}, u32[]{:S(2)}, u32[]{:S(2)}) collective-permute-start(bf16[32,3072]{1,0:T(8,128)(2,1)S(1)} %collective-permute-done.21.refs_1_), channel_id=1, source_target_pairs={{0,6},{2,0},{4,2},{6,4},{1,7},{3,1},{5,3},{7,5},{8,14},{10,8},{12,... | collective-permute-start | bytes 589832 | tf_op jit(solution)/shard_map/ppermute | solution.py:385
  95.9 1.4 %collective-permute-done.25.refs_2_ = bf16[32,3072]{1,0:T(8,128)(2,1)S(1)} collective-permute-done((bf16[32,3072]{1,0:T(8,128)(2,1)S(1)}, bf16[32,3072]{1,0:T(8,128)(2,1)S(1)}, u32[]{:S(2)}, u32[]{:S(2)}) %collective-permute-start.25) | collective-permute-done | bytes 196640 | tf_op jit(solution)/shard_map/ppermute | solution.py:385
  97.3 3.1 %collective-permute-done.22.refs_0_ = bf16[32,3072]{1,0:T(8,128)(2,1)S(1)} collective-permute-done((bf16[32,3072]{1,0:T(8,128)(2,1)S(1)}, bf16[32,3072]{1,0:T(8,128)(2,1)S(1)}, u32[]{:S(2)}, u32[]{:S(2)}) %collective-permute-start.22) | collective-permute-done | bytes 196640 | tf_op jit(solution)/shard_map/ppermute | solution.py:385
  (63 shorter events, 17.5 us)
Async XLA Ops:
  1.7 15.3 %collective-permute-start.2 = (bf16[2,256,384]{2,1,0:T(8,128)(2,1)S(1)}, bf16[2,256,384]{2,1,0:T(8,128)(2,1)S(1)}, u32[]{:S(2)}, u32[]{:S(2)}) collective-permute-start(bf16[2,256,384]{2,1,0:T(8,128)(2,1)S(1)} %bitcast.21), channel_id=1, source_target_pairs={{0,112},{16,0},{32,16},{48,32},{64,48},{80,64},{96,80},{112,96},{1... | collective-permute-start | bytes 1179656 | tf_op jit(solution)/shard_map/ppermute | solution.py:385
  7.6 11.8 %collective-permute-start.1 = (bf16[2,256,384]{2,1,0:T(8,128)(2,1)S(1)}, bf16[2,256,384]{2,1,0:T(8,128)(2,1)S(1)}, u32[]{:S(2)}, u32[]{:S(2)}) collective-permute-start(bf16[2,256,384]{2,1,0:T(8,128)(2,1)S(1)} %bitcast.22), channel_id=1, source_target_pairs={{0,16},{16,32},{32,48},{48,64},{64,80},{80,96},{96,112},{112,0},{1... | collective-permute-start | bytes 1179656 | tf_op jit(solution)/shard_map/ppermute | solution.py:385
  8.4 16.7 %copy-start.5 = (bf16[512,2,384]{2,1,0:T(2,128)(2,1)S(1)}, bf16[512,2,384]{2,1,0:T(2,128)(2,1)}, u32[]{:S(2)}) copy-start(bf16[512,2,384]{2,1,0:T(2,128)(2,1)} %param.22) | copy-start | bytes 2359300
  19.4 10.9 %collective-permute-start.5 = (bf16[2,256,384]{2,1,0:T(8,128)(2,1)S(1)}, bf16[2,256,384]{2,1,0:T(8,128)(2,1)S(1)}, u32[]{:S(2)}, u32[]{:S(2)}) collective-permute-start(bf16[2,256,384]{2,1,0:T(8,128)(2,1)S(1)} %collective-permute-done.1.right.refs_1_), channel_id=1, source_target_pairs={{0,16},{16,32},{32,48},{48,64},{64,80},{80,96},{96,112},{112,0},{1... | collective-permute-start | bytes 1179656 | tf_op jit(solution)/shard_map/ppermute | solution.py:385
  19.4 10.9 %collective-permute-start.7 = (bf16[2,256,384]{2,1,0:T(8,128)(2,1)S(1)}, bf16[2,256,384]{2,1,0:T(8,128)(2,1)S(1)}, u32[]{:S(2)}, u32[]{:S(2)}) collective-permute-start(bf16[2,256,384]{2,1,0:T(8,128)(2,1)S(1)} %collective-permute-done.2.left.refs_2_), channel_id=1, source_target_pairs={{0,112},{16,0},{32,16},{48,32},{64,48},{80,64},{96,80},{112,96},{1... | collective-permute-start | bytes 1179656 | tf_op jit(solution)/shard_map/ppermute | solution.py:385
  22.6 2.5 %collective-permute-start.3 = (bf16[256,384]{1,0:T(8,128)(2,1)}, bf16[256,384]{1,0:T(8,128)(2,1)S(1)}, u32[]{:S(2)}, u32[]{:S(2)}) collective-permute-start(bf16[256,384]{1,0:T(8,128)(2,1)} %get-tuple-element.59.q0), channel_id=1, source_target_pairs={{0,8},{8,0},{1,9},{9,1},{2,10},{10,2},{3,11},{11,3},{4,12},{12,4},... | collective-permute-start | bytes 589832 | tf_op jit(solution)/shard_map/ppermute | solution.py:385
  22.6 28.6 %collective-permute-start.12 = (bf16[192,3072]{1,0:T(8,128)(2,1)}, bf16[192,3072]{1,0:T(8,128)(2,1)S(1)}, u32[]{:S(2)}, u32[]{:S(2)}) collective-permute-start(bf16[192,3072]{1,0:T(8,128)(2,1)} %get-tuple-element.102), channel_id=1, source_target_pairs={{0,2},{2,0},{4,6},{6,4},{1,3},{3,1},{5,7},{7,5},{8,10},{10,8},{12,... | collective-permute-start | bytes 3538952 | tf_op jit(solution)/shard_map/ppermute | solution.py:389
  24.2 9.3 %collective-permute-start = (bf16[256,384]{1,0:T(8,128)(2,1)}, bf16[256,384]{1,0:T(8,128)(2,1)S(1)}, u32[]{:S(2)}, u32[]{:S(2)}) collective-permute-start(bf16[256,384]{1,0:T(8,128)(2,1)} %get-tuple-element.59.q0), channel_id=1, source_target_pairs={{0,128},{128,0},{1,129},{129,1},{2,130},{130,2},{3,131},{131,3},{4... | collective-permute-start | bytes 589832 | tf_op jit(solution)/shard_map/ppermute | solution.py:385
  30.3 10.0 %collective-permute-start.6 = (bf16[2,256,384]{2,1,0:T(8,128)(2,1)S(1)}, bf16[2,256,384]{2,1,0:T(8,128)(2,1)S(1)}, u32[]{:S(2)}, u32[]{:S(2)}) collective-permute-start(bf16[2,256,384]{2,1,0:T(8,128)(2,1)S(1)} %collective-permute-done.5.refs_0_.refs_3_), channel_id=1, source_target_pairs={{0,16},{16,32},{32,48},{48,64},{64,80},{80,96},{96,112},{112,0},{1... | collective-permute-start | bytes 1179656 | tf_op jit(solution)/shard_map/ppermute | solution.py:385
  30.3 10.0 %collective-permute-start.9 = (bf16[2,256,384]{2,1,0:T(8,128)(2,1)S(1)}, bf16[2,256,384]{2,1,0:T(8,128)(2,1)S(1)}, u32[]{:S(2)}, u32[]{:S(2)}) collective-permute-start(bf16[2,256,384]{2,1,0:T(8,128)(2,1)S(1)} %collective-permute-done.7.refs_1_.refs_4_), channel_id=1, source_target_pairs={{0,112},{16,0},{32,16},{48,32},{64,48},{80,64},{96,80},{112,96},{1... | collective-permute-start | bytes 1179656 | tf_op jit(solution)/shard_map/ppermute | solution.py:385
  33.5 1.4 %collective-permute-start.4 = (bf16[256,384]{1,0:T(8,128)(2,1)S(1)}, bf16[256,384]{1,0:T(8,128)(2,1)S(1)}, u32[]{:S(2)}, u32[]{:S(2)}) collective-permute-start(bf16[256,384]{1,0:T(8,128)(2,1)S(1)} %collective-permute-done.q0), channel_id=1, source_target_pairs={{0,8},{8,0},{1,9},{9,1},{2,10},{10,2},{3,11},{11,3},{4,12},{12,4},... | collective-permute-start | bytes 589832 | tf_op jit(solution)/shard_map/ppermute | solution.py:385
  40.3 7.5 %collective-permute-start.8 = (bf16[256,384]{1,0:T(8,128)(2,1)S(1)}, bf16[256,384]{1,0:T(8,128)(2,1)S(1)}, u32[]{:S(2)}, u32[]{:S(2)}) collective-permute-start(bf16[256,384]{1,0:T(8,128)(2,1)S(1)} %slice_bitcast_fusion.1), channel_id=1, source_target_pairs={{0,16},{16,32},{32,48},{48,64},{64,80},{80,96},{96,112},{112,0},{1... | collective-permute-start | bytes 589832 | tf_op jit(solution)/shard_map/ppermute | solution.py:385
  40.4 7.4 %collective-permute-start.10 = (bf16[256,384]{1,0:T(8,128)(2,1)S(1)}, bf16[256,384]{1,0:T(8,128)(2,1)S(1)}, u32[]{:S(2)}, u32[]{:S(2)}) collective-permute-start(bf16[256,384]{1,0:T(8,128)(2,1)S(1)} %slice_bitcast_fusion), channel_id=1, source_target_pairs={{0,112},{16,0},{32,16},{48,32},{64,48},{80,64},{96,80},{112,96},{1... | collective-permute-start | bytes 589832 | tf_op jit(solution)/shard_map/ppermute | solution.py:385
  51.2 12.8 %collective-permute-start.17 = (bf16[192,3072]{1,0:T(8,128)(2,1)S(1)}, bf16[192,3072]{1,0:T(8,128)(2,1)S(1)}, u32[]{:S(2)}, u32[]{:S(2)}) collective-permute-start(bf16[192,3072]{1,0:T(8,128)(2,1)S(1)} %collective-permute-done.12.refs_5_), channel_id=1, source_target_pairs={{0,8},{8,0},{1,9},{9,1},{2,10},{10,2},{3,11},{11,3},{4,12},{12,4},... | collective-permute-start | bytes 3538952 | tf_op jit(solution)/shard_map/ppermute | solution.py:385
  51.2 3.2 %collective-permute-start.13 = (bf16[2,144,384]{2,1,0:T(8,128)(2,1)S(1)}, bf16[2,144,384]{2,1,0:T(8,128)(2,1)S(1)}, u32[]{:S(2)}, u32[]{:S(2)}) collective-permute-start(bf16[2,144,384]{2,1,0:T(8,128)(2,1)S(1)} %get-tuple-element.104), channel_id=1, source_target_pairs={{0,8},{8,0},{1,9},{9,1},{2,10},{10,2},{3,11},{11,3},{4,12},{12,4},... | collective-permute-start | bytes 663560 | tf_op jit(solution)/shard_map/ppermute | solution.py:385
  52.7 11.3 %copy-start = (bf16[384,3072]{1,0:T(8,128)(2,1)S(1)}, bf16[384,3072]{1,0:T(8,128)(2,1)}, u32[]{:S(2)}) copy-start(bf16[384,3072]{1,0:T(8,128)(2,1)} %refs_4_.1) | copy-start | bytes 7077892
  52.7 2.0 %collective-permute-start.11 = (bf16[2,144,384]{2,1,0:T(8,128)(2,1)S(1)}, bf16[2,144,384]{2,1,0:T(8,128)(2,1)S(1)}, u32[]{:S(2)}, u32[]{:S(2)}) collective-permute-start(bf16[2,144,384]{2,1,0:T(8,128)(2,1)S(1)} %get-tuple-element.95), channel_id=1, source_target_pairs={{0,8},{8,0},{1,9},{9,1},{2,10},{10,2},{3,11},{11,3},{4,12},{12,4},... | collective-permute-start | bytes 663560 | tf_op jit(solution)/shard_map/ppermute | solution.py:385
  55.5 5.8 %collective-permute-start.14 = (bf16[144,384]{1,0:T(8,128)(2,1)S(1)}, bf16[144,384]{1,0:T(8,128)(2,1)S(1)}, u32[]{:S(2)}, u32[]{:S(2)}) collective-permute-start(bf16[144,384]{1,0:T(8,128)(2,1)S(1)} %get-tuple-element.106), channel_id=1, source_target_pairs={{0,128},{128,0},{1,129},{129,1},{2,130},{130,2},{3,131},{131,3},{4... | collective-permute-start | bytes 331784 | tf_op jit(solution)/shard_map/ppermute | solution.py:385
  56.3 6.3 %collective-permute-start.15 = (bf16[144,384]{1,0:T(8,128)(2,1)S(1)}, bf16[144,384]{1,0:T(8,128)(2,1)S(1)}, u32[]{:S(2)}, u32[]{:S(2)}) collective-permute-start(bf16[144,384]{1,0:T(8,128)(2,1)S(1)} %get-tuple-element.107), channel_id=1, source_target_pairs={{0,2},{2,0},{4,6},{6,4},{1,3},{3,1},{5,7},{7,5},{8,10},{10,8},{12,... | collective-permute-start | bytes 331784 | tf_op jit(solution)/shard_map/ppermute | solution.py:389
  57.9 6.1 %collective-permute-start.16 = (bf16[144,384]{1,0:T(8,128)(2,1)S(1)}, bf16[144,384]{1,0:T(8,128)(2,1)S(1)}, u32[]{:S(2)}, u32[]{:S(2)}) collective-permute-start(bf16[144,384]{1,0:T(8,128)(2,1)S(1)} %get-tuple-element.108), channel_id=1, source_target_pairs={{0,130},{2,128},{4,134},{6,132},{128,2},{130,0},{132,6},{134,4},{1... | collective-permute-start | bytes 331784 | tf_op jit(solution)/shard_map/ppermute | solution.py:454
  64.0 15.7 %copy-start.6 = (f32[3072]{0:T(1024)S(1)}, f32[3072]{0:T(1024)}, u32[]{:S(2)}) copy-start(f32[3072]{0:T(1024)} %param.24) | copy-start | bytes 36868
  64.0 15.7 %copy-start.7 = (f32[3072]{0:T(1024)S(1)}, f32[3072]{0:T(1024)}, u32[]{:S(2)}) copy-start(f32[3072]{0:T(1024)} %param.17) | copy-start | bytes 36868
  65.3 10.5 %collective-permute-start.18 = (bf16[32,3072]{1,0:T(8,128)(2,1)S(1)}, bf16[32,3072]{1,0:T(8,128)(2,1)S(1)}, u32[]{:S(2)}, u32[]{:S(2)}) collective-permute-start(bf16[32,3072]{1,0:T(8,128)(2,1)S(1)} %get-tuple-element.111), channel_id=1, source_target_pairs={{0,5},{1,4},{2,7},{3,6},{4,1},{5,0},{6,3},{7,2},{8,13},{9,12},{10,... | collective-permute-start | bytes 589832 | tf_op jit(solution)/shard_map/ppermute | solution.py:462
  69.2 10.5 %collective-permute-start.19 = (bf16[32,3072]{1,0:T(8,128)(2,1)S(1)}, bf16[32,3072]{1,0:T(8,128)(2,1)S(1)}, u32[]{:S(2)}, u32[]{:S(2)}) collective-permute-start(bf16[32,3072]{1,0:T(8,128)(2,1)S(1)} %get-tuple-element.112), channel_id=1, source_target_pairs={{0,4},{2,6},{4,0},{6,2},{1,5},{3,7},{5,1},{7,3},{8,12},{10,14},{12... | collective-permute-start | bytes 589832 | tf_op jit(solution)/shard_map/ppermute | solution.py:385
  69.8 9.9 %collective-permute-start.20 = (bf16[32,3072]{1,0:T(8,128)(2,1)S(1)}, bf16[32,3072]{1,0:T(8,128)(2,1)S(1)}, u32[]{:S(2)}, u32[]{:S(2)}) collective-permute-start(bf16[32,3072]{1,0:T(8,128)(2,1)S(1)} %get-tuple-element.113), channel_id=1, source_target_pairs={{0,1},{1,0},{2,3},{3,2},{4,5},{5,4},{6,7},{7,6},{8,9},{9,8},{10,11... | collective-permute-start | bytes 589832 | tf_op jit(solution)/shard_map/ppermute | solution.py:385
  80.7 9.4 %collective-permute-start.24 = (bf16[32,3072]{1,0:T(8,128)(2,1)S(1)}, bf16[32,3072]{1,0:T(8,128)(2,1)S(1)}, u32[]{:S(2)}, u32[]{:S(2)}) collective-permute-start(bf16[32,3072]{1,0:T(8,128)(2,1)S(1)} %add_convert_fusion.refs_0_), channel_id=1, source_target_pairs={{0,4},{2,6},{4,0},{6,2},{1,5},{3,7},{5,1},{7,3},{8,12},{10,14},{12... | collective-permute-start | bytes 589832 | tf_op jit(solution)/shard_map/ppermute | solution.py:385
  82.5 8.9 %collective-permute-start.21 = (bf16[32,3072]{1,0:T(8,128)(2,1)S(1)}, bf16[32,3072]{1,0:T(8,128)(2,1)S(1)}, u32[]{:S(2)}, u32[]{:S(2)}) collective-permute-start(bf16[32,3072]{1,0:T(8,128)(2,1)S(1)} %add_convert_fusion.refs_0_), channel_id=1, source_target_pairs={{0,1},{1,0},{2,3},{3,2},{4,5},{5,4},{6,7},{7,6},{8,9},{9,8},{10,11... | collective-permute-start | bytes 589832 | tf_op jit(solution)/shard_map/ppermute | solution.py:385
  84.6 10.1 %collective-permute-start.27 = (bf16[32,3072]{1,0:T(8,128)(2,1)S(1)}, bf16[32,3072]{1,0:T(8,128)(2,1)S(1)}, u32[]{:S(2)}, u32[]{:S(2)}) collective-permute-start(bf16[32,3072]{1,0:T(8,128)(2,1)S(1)} %add_convert_fusion.refs_0_), channel_id=1, source_target_pairs={{0,6},{2,0},{4,2},{6,4},{1,7},{3,1},{5,3},{7,5},{8,14},{10,8},{12,... | collective-permute-start | bytes 589832 | tf_op jit(solution)/shard_map/ppermute | solution.py:385
  85.4 9.4 %collective-permute-start.26 = (bf16[32,3072]{1,0:T(8,128)(2,1)S(1)}, bf16[32,3072]{1,0:T(8,128)(2,1)S(1)}, u32[]{:S(2)}, u32[]{:S(2)}) collective-permute-start(bf16[32,3072]{1,0:T(8,128)(2,1)S(1)} %add_convert_fusion.refs_0_), channel_id=1, source_target_pairs={{0,2},{2,4},{4,6},{6,0},{1,3},{3,5},{5,7},{7,1},{8,10},{10,12},{12... | collective-permute-start | bytes 589832 | tf_op jit(solution)/shard_map/ppermute | solution.py:385
  90.1 7.2 %collective-permute-start.25 = (bf16[32,3072]{1,0:T(8,128)(2,1)S(1)}, bf16[32,3072]{1,0:T(8,128)(2,1)S(1)}, u32[]{:S(2)}, u32[]{:S(2)}) collective-permute-start(bf16[32,3072]{1,0:T(8,128)(2,1)S(1)} %collective-permute-done.24.refs_4_), channel_id=1, source_target_pairs={{0,1},{1,0},{2,3},{3,2},{4,5},{5,4},{6,7},{7,6},{8,9},{9,8},{10,11... | collective-permute-start | bytes 589832 | tf_op jit(solution)/shard_map/ppermute | solution.py:385
  91.4 5.9 %collective-permute-start.23 = (bf16[32,3072]{1,0:T(8,128)(2,1)S(1)}, bf16[32,3072]{1,0:T(8,128)(2,1)S(1)}, u32[]{:S(2)}, u32[]{:S(2)}) collective-permute-start(bf16[32,3072]{1,0:T(8,128)(2,1)S(1)} %collective-permute-done.21.refs_1_), channel_id=1, source_target_pairs={{0,6},{2,0},{4,2},{6,4},{1,7},{3,1},{5,3},{7,5},{8,14},{10,8},{12,... | collective-permute-start | bytes 589832 | tf_op jit(solution)/shard_map/ppermute | solution.py:385
  93.5 6.9 %collective-permute-start.22 = (bf16[32,3072]{1,0:T(8,128)(2,1)S(1)}, bf16[32,3072]{1,0:T(8,128)(2,1)S(1)}, u32[]{:S(2)}, u32[]{:S(2)}) collective-permute-start(bf16[32,3072]{1,0:T(8,128)(2,1)S(1)} %collective-permute-done.21.refs_1_), channel_id=1, source_target_pairs={{0,2},{2,4},{4,6},{6,0},{1,3},{3,5},{5,7},{7,1},{8,10},{10,12},{12... | collective-permute-start | bytes 589832 | tf_op jit(solution)/shard_map/ppermute | solution.py:385
  (4 other events, 27.7 us)

commit v6 on v5

--- a/solution.py
+++ b/solution.py
@@ -254,41 +254,42 @@
     return num, top, den
 
 
-def last_kernel(q0, q1, keys, values, *refs):
-    given, state, message = refs[:3], refs[3:6], refs[6]
-    for c in HEADS:
-        pairs = [(keys[:, c], values[:, c])]
-        result = attend(q1[:, c], pairs, load_state(given, c, slice(COUNT, 2 * COUNT)))
-        for n in range(2):
-            message[n, :, c] = pack(*[a[n * HALF : (n + 1) * HALF] for a in result])
-    for c in HEADS:
-        pairs = [(keys[:, c], values[:, c])]
-        store_state(state, c, attend(q0[:, c], pairs, load_state(given, c, slice(0, COUNT))))
-
-
-def last_call(q0, q1, keys, values, *state):
-    message = jax.ShapeDtypeStruct((2, HALF + EXTRA, WIDTH), jnp.bfloat16)
-    *state, message = pl.pallas_call(
+def last_kernel(x0, x1, o0, o1, keys, values, *refs):
+    message = refs[12]
+    for block, (kept, sent) in enumerate(((x0, x1), (o0, o1))):
+        given, state = refs[3 * block : 3 * block + 3], refs[6 + 3 * block : 9 + 3 * block]
+        for c in HEADS:
+            pairs = [(keys[:, c], values[:, c])]
+            result = attend(sent[:, c], pairs, load_state(given, c, slice(COUNT, 2 * COUNT)))
+            for n in range(2):
+                part = pack(*[a[n * HALF : (n + 1) * HALF] for a in result])
+                message[2 * block + n, :, c] = part
+            store_state(state, c, attend(kept[:, c], pairs, load_state(given, c, slice(0, COUNT))))
+
+
+def last_call(x0, x1, o0, o1, keys, values, far, near):
+    message = jax.ShapeDtypeStruct((4, HALF + EXTRA, WIDTH), jnp.bfloat16)
+    return pl.pallas_call(
         last_kernel,
-        in_specs=[FULL] * 7,
-        out_specs=[FULL] * 4,
-        out_shape=state_shapes(COUNT) + [message],
+        in_specs=[FULL] * 12,
+        out_specs=[FULL] * 7,
+        out_shape=state_shapes(COUNT) * 2 + [message],
         compiler_params=params(24),
-        cost_estimate=attend_cost(2),
-    )(q0, q1, keys, values, *state)
-    return state, message
+        cost_estimate=attend_cost(4),
+    )(x0, x1, o0, o1, keys, values, *far, *near)
 
 
 def merge_kernel(place, *refs):
+    message = refs[6]
     swap = jnp.bitwise_and(coordinate(place, 1), 1) == 1
     for block in range(2):
-        state, message = refs[4 * block : 4 * block + 3], refs[4 * block + 3]
-        mine, other = refs[8 + 2 * block : 10 + 2 * block]
+        state = refs[3 * block : 3 * block + 3]
+        mine, other = refs[7 + 2 * block : 9 + 2 * block]
         for c in HEADS:
             halves = []
             for n in range(2):
                 part = load_state(state, c, slice(n * HALF, (n + 1) * HALF))
-                both_cores = merge(part, unpack(message[n, :, c]))
+                both_cores = merge(part, unpack(message[2 * block + n, :, c]))
                 halves.append(pack(*both_cores).astype(jnp.float32))
             mine[:, c] = jnp.where(swap, halves[1], halves[0]).astype(jnp.bfloat16)
             other[:, c] = jnp.where(swap, halves[0], halves[1]).astype(jnp.bfloat16)
@@ -297,7 +298,7 @@
 def merge_call(place, *args):
     return pl.pallas_call(
         merge_kernel,
-        in_specs=[FULL] * 9,
+        in_specs=[FULL] * 8,
         out_specs=[FULL] * 4,
         out_shape=[jax.ShapeDtypeStruct((HALF + EXTRA, WIDTH), jnp.bfloat16)] * 4,
         compiler_params=params(24),
@@ -443,17 +444,16 @@
     near = attend_call(next_kernel, 4, q, q_core, r3, l3, *near)
 
     far_k, far_v, near[0], far[0] = after((far_k, far_v, near[0], far[0]))
-    x_state, x_msg = last_call(q_x, q_both, far_k, far_v, *far)
-    x_msg = ring(x_msg, "core", 1)
-    o_state, o_msg = last_call(q, q_core, far_k, far_v, *near)
-    w_pair, o_msg = after((w_pair, o_msg))
-    o_msg = ring(o_msg, "core", 1)
-    w_core = ring(w_pair, "core", 1)
-    x_mine, x_other, o_mine, o_other = merge_call(place, *x_state, x_msg, *o_state, o_msg)
-    from_y, from_x = beside_y(o_other), ring(x_mine, "x_lo", 1)
+    *states, message = last_call(q_x, q_both, q, q_core, far_k, far_v, far, near)
+    w_pair, message = after((w_pair, message))
+    message = ring(message, "core", 1)
+    x_mine, x_other, o_mine, o_other = merge_call(place, *states, message)
     from_both = lax.ppermute(
         x_other, ("x_lo", "y"), [(i, (1 - i // 4) * 4 + (i % 4 ^ 1)) for i in range(8)]
     )
+    from_y, from_x = beside_y(o_other), ring(x_mine, "x_lo", 1)
+    w_pair, o_mine = after((w_pair, o_mine))
+    w_core = ring(w_pair, "core", 1)
 
     mine, both_ways, along_y, along_x = project_call(
         place, (o_mine, from_x, from_y, from_both), (w_out, w_pair, w_core)

time: 102 us -> 101 us (level)
    pallas_call x3 -> x2, Pallas kernels: 2.6 us -> 2.05 us  [the longest x1 1.32 us: last_call(): pl.pallas_call(last_kernel, in_specs=[FULL] * 12, out_specs=[FULL] * 7, o...]
    ppermute x24 -> x23, starting transfers between devices: 30.1 us -> 29.7 us  [ring(): lax.ppermute(value, axis, [(i, (i + step) % size) for i in range(size)])]
    ppermute x24 -> x23, waiting for transfers between devices: 24.8 us -> 24.9 us  [ring(): lax.ppermute(value, axis, [(i, (i + step) % size) for i in range(size)])]
  transfers between devices with their start and end apart: 28 -> 27, of which waited for: 16 -> 15; matrix products, arithmetic and copies ran while one was open for 2% -> 2% of each run, Pallas kernels for 21% -> 20%
where the time goes in v6:
time: 101 us
  starting transfers between devices  37.8 us (37%)
  waiting for transfers between devices  34.2 us (34%)
  Pallas kernels  23.2 us (23%)
  local copies, waits for them, and re-layouts  3.12 us (3%)
  other arithmetic  1.14 us (1%)
  between operations  1.01 us (1%)
    ppermute x23, starting transfers between devices, ring(): lax.ppermute(value, axis, [(i, (i + step) % size) for i in range(size)])  29.7 us
    ppermute x23, waiting for transfers between devices, ring(): lax.ppermute(value, axis, [(i, (i + step) % size) for i in range(size)])  24.9 us
    pallas_call x5, Pallas kernels, attend_call(): return list(call(*args))  9.26 us
    pallas_call x1, Pallas kernels, qkv_call(): pl.pallas_call(qkv_kernel, in_specs=[FULL] + [anywhere] * 9, out_specs=[F...  8.51 us
    ppermute x1, waiting for transfers between devices, shards(): lax.ppermute(both_ways, TENSOR, [(i, (i // 2 + 2) % 4 * 2 + (1 - i % 2))...  4.17 us
    ppermute x1, starting transfers between devices, shards(): lax.ppermute(both_ways, TENSOR, [(i, (i // 2 + 2) % 4 * 2 + (1 - i % 2))...  3.83 us
    ppermute x2, waiting for transfers between devices, beside_y(): return lax.ppermute(value, 'y', [(i, i ^ 1) for i in range(4)])  3.77 us
    ppermute x2, starting transfers between devices, beside_y(): return lax.ppermute(value, 'y', [(i, i ^ 1) for i in range(4)])  3.15 us
  transfers between devices with their start and end apart: 27, of which 15 were waited for; matrix products, arithmetic and copies ran while one was open for 2% of the time, Pallas kernels for 20%

profile of v6, /device:TPU:6, one launch (start us, length us, event | category | flops | bytes accessed | tf_op | source)
XLA Modules:
  0.0 100.5 jit_solution(5737941562131068148)
XLA Ops:
  1.7 5.9 %collective-permute-start.3 = (bf16[2,256,384]{2,1,0:T(8,128)(2,1)S(1)}, bf16[2,256,384]{2,1,0:T(8,128)(2,1)S(1)}, u32[]{:S(2)}, u32[]{:S(2)}) collective-permute-start(bf16[2,256,384]{2,1,0:T(8,128)(2,1)S(1)} %bitcast.21), channel_id=1, source_target_pairs={{0,112},{16,0},{32,16},{48,32},{64,48},{80,64},{96,80},{112,96},{1... | collective-permute-start | bytes 1179656 | tf_op jit(solution)/shard_map/ppermute | solution.py:386
  8.4 8.5 %shard_map.140 = (bf16[256,384]{1,0:T(8,128)(2,1)}, bf16[256,384]{1,0:T(8,128)(2,1)}, bf16[256,384]{1,0:T(8,128)(2,1)}, bf16[192,3072]{1,0:T(8,128)(2,1)}) custom-call(f32[8,128]{1,0:T(8,128)} %broadcast_in_dim.2.place, bf16[256,3072]{1,0:T(8,128)(2,1)} %refs_0_.1, bf16[3,3072,384]{2,1,0:T(8,128)(2,1)} %bitcast.28, bf16[288,768]{1,0:T(8,128)(2,1)} %constant.49.clone.refs_2_, ...), custom_call_target="tpu_custom_call" | custom-call | flops 1024 | bytes 1024 | tf_op jit(solution)/shard_map/pallas_call | solution.py:135
  16.9 2.5 %collective-permute-done.2.right.refs_1_ = bf16[2,256,384]{2,1,0:T(8,128)(2,1)S(1)} collective-permute-done((bf16[2,256,384]{2,1,0:T(8,128)(2,1)S(1)}, bf16[2,256,384]{2,1,0:T(8,128)(2,1)S(1)}, u32[]{:S(2)}, u32[]{:S(2)}) %collective-permute-start.2) | collective-permute-done | bytes 393248 | tf_op jit(solution)/shard_map/ppermute | solution.py:386
  19.4 3.2 %collective-permute-start.8 = (bf16[2,256,384]{2,1,0:T(8,128)(2,1)S(1)}, bf16[2,256,384]{2,1,0:T(8,128)(2,1)S(1)}, u32[]{:S(2)}, u32[]{:S(2)}) collective-permute-start(bf16[2,256,384]{2,1,0:T(8,128)(2,1)S(1)} %collective-permute-done.3.left.refs_2_), channel_id=1, source_target_pairs={{0,112},{16,0},{32,16},{48,32},{64,48},{80,64},{96,80},{112,96},{1... | collective-permute-start | bytes 1179656 | tf_op jit(solution)/shard_map/ppermute | solution.py:386
  22.6 1.6 %collective-permute-start = (bf16[192,3072]{1,0:T(8,128)(2,1)}, bf16[192,3072]{1,0:T(8,128)(2,1)S(1)}, u32[]{:S(2)}, u32[]{:S(2)}) collective-permute-start(bf16[192,3072]{1,0:T(8,128)(2,1)} %get-tuple-element.59), channel_id=1, source_target_pairs={{0,2},{2,0},{4,6},{6,4},{1,3},{3,1},{5,7},{7,5},{8,10},{10,8},{12,... | collective-permute-start | bytes 3538952 | tf_op jit(solution)/shard_map/ppermute | solution.py:390
  25.2 2.2 %shard_map.141 = (f32[512,384]{1,0:T(8,128)S(1)}, f32[512,384]{1,0:T(8,128)S(1)}, f32[512,384]{1,0:T(8,128)S(1)}) custom-call(bf16[256,384]{1,0:T(8,128)(2,1)S(1)} %copy-done.1, bf16[256,384]{1,0:T(8,128)(2,1)S(1)} %collective-permute-done.4.q1.o1, bf16[256,384]{1,0:T(8,128)(2,1)S(1)} %copy-done.2, bf16[256,384]{1,0:T(8,128)(2,1)S(1)} %copy-done.3, ...), custom_call_target="tpu_custom_call" | custom-call | flops 1024 | bytes 1024 | tf_op jit(solution)/shard_map/pallas_call | solution.py:225
  27.4 2.8 %collective-permute-done.6.refs_0_.refs_3_ = bf16[2,256,384]{2,1,0:T(8,128)(2,1)S(1)} collective-permute-done((bf16[2,256,384]{2,1,0:T(8,128)(2,1)S(1)}, bf16[2,256,384]{2,1,0:T(8,128)(2,1)S(1)}, u32[]{:S(2)}, u32[]{:S(2)}) %collective-permute-start.6) | collective-permute-done | bytes 393248 | tf_op jit(solution)/shard_map/ppermute | solution.py:386
  30.3 3.2 %collective-permute-start.10 = (bf16[2,256,384]{2,1,0:T(8,128)(2,1)S(1)}, bf16[2,256,384]{2,1,0:T(8,128)(2,1)S(1)}, u32[]{:S(2)}, u32[]{:S(2)}) collective-permute-start(bf16[2,256,384]{2,1,0:T(8,128)(2,1)S(1)} %collective-permute-done.8.refs_1_.refs_4_), channel_id=1, source_target_pairs={{0,112},{16,0},{32,16},{48,32},{64,48},{80,64},{96,80},{112,96},{1... | collective-permute-start | bytes 1179656 | tf_op jit(solution)/shard_map/ppermute | solution.py:386
  33.5 1.4 %collective-permute-done.5.q1.x1 = bf16[256,384]{1,0:T(8,128)(2,1)S(1)} collective-permute-done((bf16[256,384]{1,0:T(8,128)(2,1)S(1)}, bf16[256,384]{1,0:T(8,128)(2,1)S(1)}, u32[]{:S(2)}, u32[]{:S(2)}) %collective-permute-start.5) | collective-permute-done | bytes 196640 | tf_op jit(solution)/shard_map/ppermute | solution.py:386
  35.0 3.0 %shard_map.143 = (f32[512,384]{1,0:T(8,128)S(1)}, f32[512,384]{1,0:T(8,128)S(1)}, f32[512,384]{1,0:T(8,128)S(1)}) custom-call(bf16[256,384]{1,0:T(8,128)(2,1)S(1)} %collective-permute-done.1.q0.x0, bf16[256,384]{1,0:T(8,128)(2,1)S(1)} %collective-permute-done.5.q1.x1, bf16[2,256,384]{2,1,0:T(8,128)(2,1)S(1)} %bitcast.24, ...), custom_call_target="tpu_custom_call" | custom-call | flops 1024 | bytes 1024 | tf_op jit(solution)/shard_map/pallas_call | solution.py:225
  37.9 1.4 %shard_map.142 = (f32[512,384]{1,0:T(8,128)S(1)}, f32[512,384]{1,0:T(8,128)S(1)}, f32[512,384]{1,0:T(8,128)S(1)}) custom-call(bf16[256,384]{1,0:T(8,128)(2,1)S(1)} %copy-done.1, bf16[256,384]{1,0:T(8,128)(2,1)S(1)} %collective-permute-done.4.q1.o1, bf16[2,256,384]{2,1,0:T(8,128)(2,1)S(1)} %collective-permute-done.6.refs_0_.refs_3_, ...), custom_call_target="tpu_custom_call" | custom-call | flops 1024 | bytes 1024 | tf_op jit(solution)/shard_map/pallas_call | solution.py:225
  40.4 3.2 %collective-permute-start.11 = (bf16[256,384]{1,0:T(8,128)(2,1)S(1)}, bf16[256,384]{1,0:T(8,128)(2,1)S(1)}, u32[]{:S(2)}, u32[]{:S(2)}) collective-permute-start(bf16[256,384]{1,0:T(8,128)(2,1)S(1)} %slice_bitcast_fusion), channel_id=1, source_target_pairs={{0,112},{16,0},{32,16},{48,32},{64,48},{80,64},{96,80},{112,96},{1... | collective-permute-start | bytes 589832 | tf_op jit(solution)/shard_map/ppermute | solution.py:386
  43.6 1.3 %shard_map.144 = (f32[512,384]{1,0:T(8,128)S(1)}, f32[512,384]{1,0:T(8,128)S(1)}, f32[512,384]{1,0:T(8,128)S(1)}) custom-call(bf16[256,384]{1,0:T(8,128)(2,1)S(1)} %copy-done.1, bf16[256,384]{1,0:T(8,128)(2,1)S(1)} %collective-permute-done.4.q1.o1, bf16[2,256,384]{2,1,0:T(8,128)(2,1)S(1)} %collective-permute-done.7.refs_0_, ...), custom_call_target="tpu_custom_call" | custom-call | flops 1024 | bytes 1024 | tf_op jit(solution)/shard_map/pallas_call | solution.py:225
  45.0 1.4 %shard_map.145 = (f32[512,384]{1,0:T(8,128)S(1)}, f32[512,384]{1,0:T(8,128)S(1)}, f32[512,384]{1,0:T(8,128)S(1)}) custom-call(bf16[256,384]{1,0:T(8,128)(2,1)S(1)} %collective-permute-done.1.q0.x0, bf16[256,384]{1,0:T(8,128)(2,1)S(1)} %collective-permute-done.5.q1.x1, bf16[2,256,384]{2,1,0:T(8,128)(2,1)S(1)} %collective-permute-done.7.refs_0_, ...), custom_call_target="tpu_custom_call" | custom-call | flops 1024 | bytes 1024 | tf_op jit(solution)/shard_map/pallas_call | solution.py:225
  47.6 1.3 %shard_map.146 = (f32[256,384]{1,0:T(8,128)S(1)}, f32[256,384]{1,0:T(8,128)S(1)}, f32[256,384]{1,0:T(8,128)S(1)}, f32[256,384]{1,0:T(8,128)S(1)}, f32[256,384]{1...) custom-call(bf16[256,384]{1,0:T(8,128)(2,1)S(1)} %collective-permute-done.1.q0.x0, ...), custom_call_target="tpu_custom_call" | custom-call | flops 1024 | bytes 1024 | tf_op jit(solution)/shard_map/pallas_call | solution.py:272
  48.9 2.3 %collective-permute-done.refs_5_ = bf16[192,3072]{1,0:T(8,128)(2,1)S(1)} collective-permute-done((bf16[192,3072]{1,0:T(8,128)(2,1)}, bf16[192,3072]{1,0:T(8,128)(2,1)S(1)}, u32[]{:S(2)}, u32[]{:S(2)}) %collective-permute-start) | collective-permute-done | bytes 1179680 | tf_op jit(solution)/shard_map/ppermute | solution.py:390
  51.2 1.8 %collective-permute-done.12.refs_6_ = bf16[4,144,384]{2,1,0:T(8,128)(2,1)S(1)} collective-permute-done((bf16[4,144,384]{2,1,0:T(8,128)(2,1)S(1)}, bf16[4,144,384]{2,1,0:T(8,128)(2,1)S(1)}, u32[]{:S(2)}, u32[]{:S(2)}) %collective-permute-start.12) | collective-permute-done | bytes 442400 | tf_op jit(solution)/shard_map/ppermute | solution.py:386
  54.8 1.6 %collective-permute-start.14 = (bf16[144,384]{1,0:T(8,128)(2,1)S(1)}, bf16[144,384]{1,0:T(8,128)(2,1)S(1)}, u32[]{:S(2)}, u32[]{:S(2)}) collective-permute-start(bf16[144,384]{1,0:T(8,128)(2,1)S(1)} %get-tuple-element.109), channel_id=1, source_target_pairs={{0,2},{2,0},{4,6},{6,4},{1,3},{3,1},{5,7},{7,5},{8,10},{10,8},{12,... | collective-permute-start | bytes 331784 | tf_op jit(solution)/shard_map/ppermute | solution.py:390
  57.5 2.4 %collective-permute-done.13.refs_1_ = bf16[144,384]{1,0:T(8,128)(2,1)S(1)} collective-permute-done((bf16[144,384]{1,0:T(8,128)(2,1)S(1)}, bf16[144,384]{1,0:T(8,128)(2,1)S(1)}, u32[]{:S(2)}, u32[]{:S(2)}) %collective-permute-start.13) | collective-permute-done | bytes 110624 | tf_op jit(solution)/shard_map/ppermute | solution.py:386
  59.8 1.5 %collective-permute-done.14.refs_2_ = bf16[144,384]{1,0:T(8,128)(2,1)S(1)} collective-permute-done((bf16[144,384]{1,0:T(8,128)(2,1)S(1)}, bf16[144,384]{1,0:T(8,128)(2,1)S(1)}, u32[]{:S(2)}, u32[]{:S(2)}) %collective-permute-start.14) | collective-permute-done | bytes 110624 | tf_op jit(solution)/shard_map/ppermute | solution.py:390
  61.3 1.3 %collective-permute-done.15.refs_3_ = bf16[144,384]{1,0:T(8,128)(2,1)S(1)} collective-permute-done((bf16[144,384]{1,0:T(8,128)(2,1)S(1)}, bf16[144,384]{1,0:T(8,128)(2,1)S(1)}, u32[]{:S(2)}, u32[]{:S(2)}) %collective-permute-start.15) | collective-permute-done | bytes 110624 | tf_op jit(solution)/shard_map/ppermute | solution.py:451
  62.7 1.3 %shard_map.148 = (bf16[32,3072]{1,0:T(8,128)(2,1)S(1)}, bf16[32,3072]{1,0:T(8,128)(2,1)S(1)}, bf16[32,3072]{1,0:T(8,128)(2,1)S(1)}, bf16[32,3072]{1,0:T(8,128)(2,1)S(1)}) custom-call(f32[8,128]{1,0:T(8,128)S(1)} %copy-done.4, bf16[144,384]{1,0:T(8,128)(2,1)S(1)} %get-tuple-element.107.refs_0_, bf16[144,384]{1,0:T(8,128)(2,1)S(1)} %collective-permute-done.13.refs_1_, ...), custom_call_target="tpu_custom_call" | custom-call | flops 1024 | bytes 1024 | tf_op jit(solution)/shard_map/pallas_call | solution.py:338
  64.0 3.8 %collective-permute-start.17 = (bf16[32,3072]{1,0:T(8,128)(2,1)S(1)}, bf16[32,3072]{1,0:T(8,128)(2,1)S(1)}, u32[]{:S(2)}, u32[]{:S(2)}) collective-permute-start(bf16[32,3072]{1,0:T(8,128)(2,1)S(1)} %get-tuple-element.113), channel_id=1, source_target_pairs={{0,5},{1,4},{2,7},{3,6},{4,1},{5,0},{6,3},{7,2},{8,13},{9,12},{10,... | collective-permute-start | bytes 589832 | tf_op jit(solution)/shard_map/ppermute | solution.py:462
  68.4 2.1 %collective-permute-start.19 = (bf16[32,3072]{1,0:T(8,128)(2,1)S(1)}, bf16[32,3072]{1,0:T(8,128)(2,1)S(1)}, u32[]{:S(2)}, u32[]{:S(2)}) collective-permute-start(bf16[32,3072]{1,0:T(8,128)(2,1)S(1)} %get-tuple-element.115), channel_id=1, source_target_pairs={{0,1},{1,0},{2,3},{3,2},{4,5},{5,4},{6,7},{7,6},{8,9},{9,8},{10,11... | collective-permute-start | bytes 589832 | tf_op jit(solution)/shard_map/ppermute | solution.py:386
  70.6 4.2 %collective-permute-done.17 = bf16[32,3072]{1,0:T(8,128)(2,1)S(1)} collective-permute-done((bf16[32,3072]{1,0:T(8,128)(2,1)S(1)}, bf16[32,3072]{1,0:T(8,128)(2,1)S(1)}, u32[]{:S(2)}, u32[]{:S(2)}) %collective-permute-start.17) | collective-permute-done | bytes 196640 | tf_op jit(solution)/shard_map/ppermute | solution.py:462
  74.7 3.8 %collective-permute-done.18 = bf16[32,3072]{1,0:T(8,128)(2,1)S(1)} collective-permute-done((bf16[32,3072]{1,0:T(8,128)(2,1)S(1)}, bf16[32,3072]{1,0:T(8,128)(2,1)S(1)}, u32[]{:S(2)}, u32[]{:S(2)}) %collective-permute-start.18) | collective-permute-done | bytes 196640 | tf_op jit(solution)/shard_map/ppermute | solution.py:386
  79.7 1.8 %collective-permute-start.23 = (bf16[32,3072]{1,0:T(8,128)(2,1)S(1)}, bf16[32,3072]{1,0:T(8,128)(2,1)S(1)}, u32[]{:S(2)}, u32[]{:S(2)}) collective-permute-start(bf16[32,3072]{1,0:T(8,128)(2,1)S(1)} %add_convert_fusion.refs_0_), channel_id=1, source_target_pairs={{0,4},{2,6},{4,0},{6,2},{1,5},{3,7},{5,1},{7,3},{8,12},{10,14},{12... | collective-permute-start | bytes 589832 | tf_op jit(solution)/shard_map/ppermute | solution.py:386
  81.4 2.1 %collective-permute-start.20 = (bf16[32,3072]{1,0:T(8,128)(2,1)S(1)}, bf16[32,3072]{1,0:T(8,128)(2,1)S(1)}, u32[]{:S(2)}, u32[]{:S(2)}) collective-permute-start(bf16[32,3072]{1,0:T(8,128)(2,1)S(1)} %add_convert_fusion.refs_0_), channel_id=1, source_target_pairs={{0,1},{1,0},{2,3},{3,2},{4,5},{5,4},{6,7},{7,6},{8,9},{9,8},{10,11... | collective-permute-start | bytes 589832 | tf_op jit(solution)/shard_map/ppermute | solution.py:386
  85.6 3.4 %collective-permute-done.23.refs_4_ = bf16[32,3072]{1,0:T(8,128)(2,1)S(1)} collective-permute-done((bf16[32,3072]{1,0:T(8,128)(2,1)S(1)}, bf16[32,3072]{1,0:T(8,128)(2,1)S(1)}, u32[]{:S(2)}, u32[]{:S(2)}) %collective-permute-start.23) | collective-permute-done | bytes 196640 | tf_op jit(solution)/shard_map/ppermute | solution.py:386
  90.3 2.2 %collective-permute-start.22 = (bf16[32,3072]{1,0:T(8,128)(2,1)S(1)}, bf16[32,3072]{1,0:T(8,128)(2,1)S(1)}, u32[]{:S(2)}, u32[]{:S(2)}) collective-permute-start(bf16[32,3072]{1,0:T(8,128)(2,1)S(1)} %collective-permute-done.20.refs_1_), channel_id=1, source_target_pairs={{0,6},{2,0},{4,2},{6,4},{1,7},{3,1},{5,3},{7,5},{8,14},{10,8},{12,... | collective-permute-start | bytes 589832 | tf_op jit(solution)/shard_map/ppermute | solution.py:386
  94.8 1.4 %collective-permute-done.24.refs_2_ = bf16[32,3072]{1,0:T(8,128)(2,1)S(1)} collective-permute-done((bf16[32,3072]{1,0:T(8,128)(2,1)S(1)}, bf16[32,3072]{1,0:T(8,128)(2,1)S(1)}, u32[]{:S(2)}, u32[]{:S(2)}) %collective-permute-start.24) | collective-permute-done | bytes 196640 | tf_op jit(solution)/shard_map/ppermute | solution.py:386
  96.2 3.2 %collective-permute-done.21.refs_0_ = bf16[32,3072]{1,0:T(8,128)(2,1)S(1)} collective-permute-done((bf16[32,3072]{1,0:T(8,128)(2,1)S(1)}, bf16[32,3072]{1,0:T(8,128)(2,1)S(1)}, u32[]{:S(2)}, u32[]{:S(2)}) %collective-permute-start.21) | collective-permute-done | bytes 196640 | tf_op jit(solution)/shard_map/ppermute | solution.py:386
  (60 shorter events, 16.3 us)
Async XLA Ops:
  1.7 15.3 %collective-permute-start.3 = (bf16[2,256,384]{2,1,0:T(8,128)(2,1)S(1)}, bf16[2,256,384]{2,1,0:T(8,128)(2,1)S(1)}, u32[]{:S(2)}, u32[]{:S(2)}) collective-permute-start(bf16[2,256,384]{2,1,0:T(8,128)(2,1)S(1)} %bitcast.21), channel_id=1, source_target_pairs={{0,112},{16,0},{32,16},{48,32},{64,48},{80,64},{96,80},{112,96},{1... | collective-permute-start | bytes 1179656 | tf_op jit(solution)/shard_map/ppermute | solution.py:386
  7.6 11.8 %collective-permute-start.2 = (bf16[2,256,384]{2,1,0:T(8,128)(2,1)S(1)}, bf16[2,256,384]{2,1,0:T(8,128)(2,1)S(1)}, u32[]{:S(2)}, u32[]{:S(2)}) collective-permute-start(bf16[2,256,384]{2,1,0:T(8,128)(2,1)S(1)} %bitcast.22), channel_id=1, source_target_pairs={{0,16},{16,32},{32,48},{48,64},{64,80},{80,96},{96,112},{112,0},{1... | collective-permute-start | bytes 1179656 | tf_op jit(solution)/shard_map/ppermute | solution.py:386
  8.4 16.7 %copy-start.5 = (bf16[512,2,384]{2,1,0:T(2,128)(2,1)S(1)}, bf16[512,2,384]{2,1,0:T(2,128)(2,1)}, u32[]{:S(2)}) copy-start(bf16[512,2,384]{2,1,0:T(2,128)(2,1)} %param.22) | copy-start | bytes 2359300
  16.9 8.3 %copy-start.1 = (bf16[256,384]{1,0:T(8,128)(2,1)S(1)}, bf16[256,384]{1,0:T(8,128)(2,1)}, u32[]{:S(2)}) copy-start(bf16[256,384]{1,0:T(8,128)(2,1)} %get-tuple-element.61.q0.o0) | copy-start | bytes 589828
  19.4 10.9 %collective-permute-start.6 = (bf16[2,256,384]{2,1,0:T(8,128)(2,1)S(1)}, bf16[2,256,384]{2,1,0:T(8,128)(2,1)S(1)}, u32[]{:S(2)}, u32[]{:S(2)}) collective-permute-start(bf16[2,256,384]{2,1,0:T(8,128)(2,1)S(1)} %collective-permute-done.2.right.refs_1_), channel_id=1, source_target_pairs={{0,16},{16,32},{32,48},{48,64},{64,80},{80,96},{96,112},{112,0},{1... | collective-permute-start | bytes 1179656 | tf_op jit(solution)/shard_map/ppermute | solution.py:386
  19.4 10.9 %collective-permute-start.8 = (bf16[2,256,384]{2,1,0:T(8,128)(2,1)S(1)}, bf16[2,256,384]{2,1,0:T(8,128)(2,1)S(1)}, u32[]{:S(2)}, u32[]{:S(2)}) collective-permute-start(bf16[2,256,384]{2,1,0:T(8,128)(2,1)S(1)} %collective-permute-done.3.left.refs_2_), channel_id=1, source_target_pairs={{0,112},{16,0},{32,16},{48,32},{64,48},{80,64},{96,80},{112,96},{1... | collective-permute-start | bytes 1179656 | tf_op jit(solution)/shard_map/ppermute | solution.py:386
  22.6 2.5 %collective-permute-start.4 = (bf16[256,384]{1,0:T(8,128)(2,1)}, bf16[256,384]{1,0:T(8,128)(2,1)S(1)}, u32[]{:S(2)}, u32[]{:S(2)}) collective-permute-start(bf16[256,384]{1,0:T(8,128)(2,1)} %get-tuple-element.61.q0.o0), channel_id=1, source_target_pairs={{0,8},{8,0},{1,9},{9,1},{2,10},{10,2},{3,11},{11,3},{4,12},{12,4},... | collective-permute-start | bytes 589832 | tf_op jit(solution)/shard_map/ppermute | solution.py:386
  22.6 28.6 %collective-permute-start = (bf16[192,3072]{1,0:T(8,128)(2,1)}, bf16[192,3072]{1,0:T(8,128)(2,1)S(1)}, u32[]{:S(2)}, u32[]{:S(2)}) collective-permute-start(bf16[192,3072]{1,0:T(8,128)(2,1)} %get-tuple-element.59), channel_id=1, source_target_pairs={{0,2},{2,0},{4,6},{6,4},{1,3},{3,1},{5,7},{7,5},{8,10},{10,8},{12,... | collective-permute-start | bytes 3538952 | tf_op jit(solution)/shard_map/ppermute | solution.py:390
  24.2 9.3 %collective-permute-start.1 = (bf16[256,384]{1,0:T(8,128)(2,1)}, bf16[256,384]{1,0:T(8,128)(2,1)S(1)}, u32[]{:S(2)}, u32[]{:S(2)}) collective-permute-start(bf16[256,384]{1,0:T(8,128)(2,1)} %get-tuple-element.61.q0.o0), channel_id=1, source_target_pairs={{0,128},{128,0},{1,129},{129,1},{2,130},{130,2},{3,131},{131,3},{4... | collective-permute-start | bytes 589832 | tf_op jit(solution)/shard_map/ppermute | solution.py:386
  30.3 10.0 %collective-permute-start.7 = (bf16[2,256,384]{2,1,0:T(8,128)(2,1)S(1)}, bf16[2,256,384]{2,1,0:T(8,128)(2,1)S(1)}, u32[]{:S(2)}, u32[]{:S(2)}) collective-permute-start(bf16[2,256,384]{2,1,0:T(8,128)(2,1)S(1)} %collective-permute-done.6.refs_0_.refs_3_), channel_id=1, source_target_pairs={{0,16},{16,32},{32,48},{48,64},{64,80},{80,96},{96,112},{112,0},{1... | collective-permute-start | bytes 1179656 | tf_op jit(solution)/shard_map/ppermute | solution.py:386
  30.3 10.0 %collective-permute-start.10 = (bf16[2,256,384]{2,1,0:T(8,128)(2,1)S(1)}, bf16[2,256,384]{2,1,0:T(8,128)(2,1)S(1)}, u32[]{:S(2)}, u32[]{:S(2)}) collective-permute-start(bf16[2,256,384]{2,1,0:T(8,128)(2,1)S(1)} %collective-permute-done.8.refs_1_.refs_4_), channel_id=1, source_target_pairs={{0,112},{16,0},{32,16},{48,32},{64,48},{80,64},{96,80},{112,96},{1... | collective-permute-start | bytes 1179656 | tf_op jit(solution)/shard_map/ppermute | solution.py:386
  33.5 1.4 %collective-permute-start.5 = (bf16[256,384]{1,0:T(8,128)(2,1)S(1)}, bf16[256,384]{1,0:T(8,128)(2,1)S(1)}, u32[]{:S(2)}, u32[]{:S(2)}) collective-permute-start(bf16[256,384]{1,0:T(8,128)(2,1)S(1)} %collective-permute-done.1.q0.x0), channel_id=1, source_target_pairs={{0,8},{8,0},{1,9},{9,1},{2,10},{10,2},{3,11},{11,3},{4,12},{12,4},... | collective-permute-start | bytes 589832 | tf_op jit(solution)/shard_map/ppermute | solution.py:386
  40.3 7.3 %collective-permute-start.9 = (bf16[256,384]{1,0:T(8,128)(2,1)S(1)}, bf16[256,384]{1,0:T(8,128)(2,1)S(1)}, u32[]{:S(2)}, u32[]{:S(2)}) collective-permute-start(bf16[256,384]{1,0:T(8,128)(2,1)S(1)} %slice_bitcast_fusion.1), channel_id=1, source_target_pairs={{0,16},{16,32},{32,48},{48,64},{64,80},{80,96},{96,112},{112,0},{1... | collective-permute-start | bytes 589832 | tf_op jit(solution)/shard_map/ppermute | solution.py:386
  40.4 7.2 %collective-permute-start.11 = (bf16[256,384]{1,0:T(8,128)(2,1)S(1)}, bf16[256,384]{1,0:T(8,128)(2,1)S(1)}, u32[]{:S(2)}, u32[]{:S(2)}) collective-permute-start(bf16[256,384]{1,0:T(8,128)(2,1)S(1)} %slice_bitcast_fusion), channel_id=1, source_target_pairs={{0,112},{16,0},{32,16},{48,32},{64,48},{80,64},{96,80},{112,96},{1... | collective-permute-start | bytes 589832 | tf_op jit(solution)/shard_map/ppermute | solution.py:386
  48.9 13.7 %copy-start = (bf16[384,3072]{1,0:T(8,128)(2,1)S(1)}, bf16[384,3072]{1,0:T(8,128)(2,1)}, u32[]{:S(2)}) copy-start(bf16[384,3072]{1,0:T(8,128)(2,1)} %refs_4_.1) | copy-start | bytes 7077892
  51.2 1.8 %collective-permute-start.12 = (bf16[4,144,384]{2,1,0:T(8,128)(2,1)S(1)}, bf16[4,144,384]{2,1,0:T(8,128)(2,1)S(1)}, u32[]{:S(2)}, u32[]{:S(2)}) collective-permute-start(bf16[4,144,384]{2,1,0:T(8,128)(2,1)S(1)} %get-tuple-element.105), channel_id=1, source_target_pairs={{0,8},{8,0},{1,9},{9,1},{2,10},{10,2},{3,11},{11,3},{4,12},{12,4},... | collective-permute-start | bytes 1327112 | tf_op jit(solution)/shard_map/ppermute | solution.py:386
  53.8 8.9 %collective-permute-start.16 = (bf16[192,3072]{1,0:T(8,128)(2,1)S(1)}, bf16[192,3072]{1,0:T(8,128)(2,1)S(1)}, u32[]{:S(2)}, u32[]{:S(2)}) collective-permute-start(bf16[192,3072]{1,0:T(8,128)(2,1)S(1)} %collective-permute-done.refs_5_), channel_id=1, source_target_pairs={{0,8},{8,0},{1,9},{9,1},{2,10},{10,2},{3,11},{11,3},{4,12},{12,4},... | collective-permute-start | bytes 3538952 | tf_op jit(solution)/shard_map/ppermute | solution.py:386
  53.9 5.9 %collective-permute-start.13 = (bf16[144,384]{1,0:T(8,128)(2,1)S(1)}, bf16[144,384]{1,0:T(8,128)(2,1)S(1)}, u32[]{:S(2)}, u32[]{:S(2)}) collective-permute-start(bf16[144,384]{1,0:T(8,128)(2,1)S(1)} %get-tuple-element.108), channel_id=1, source_target_pairs={{0,128},{128,0},{1,129},{129,1},{2,130},{130,2},{3,131},{131,3},{4... | collective-permute-start | bytes 331784 | tf_op jit(solution)/shard_map/ppermute | solution.py:386
  54.8 6.5 %collective-permute-start.14 = (bf16[144,384]{1,0:T(8,128)(2,1)S(1)}, bf16[144,384]{1,0:T(8,128)(2,1)S(1)}, u32[]{:S(2)}, u32[]{:S(2)}) collective-permute-start(bf16[144,384]{1,0:T(8,128)(2,1)S(1)} %get-tuple-element.109), channel_id=1, source_target_pairs={{0,2},{2,0},{4,6},{6,4},{1,3},{3,1},{5,7},{7,5},{8,10},{10,8},{12,... | collective-permute-start | bytes 331784 | tf_op jit(solution)/shard_map/ppermute | solution.py:390
  56.4 22.2 %copy-start.6 = (f32[3072]{0:T(1024)S(1)}, f32[3072]{0:T(1024)}, u32[]{:S(2)}) copy-start(f32[3072]{0:T(1024)} %param.24) | copy-start | bytes 36868
  56.4 22.2 %copy-start.7 = (f32[3072]{0:T(1024)S(1)}, f32[3072]{0:T(1024)}, u32[]{:S(2)}) copy-start(f32[3072]{0:T(1024)} %param.17) | copy-start | bytes 36868
  56.4 6.3 %collective-permute-start.15 = (bf16[144,384]{1,0:T(8,128)(2,1)S(1)}, bf16[144,384]{1,0:T(8,128)(2,1)S(1)}, u32[]{:S(2)}, u32[]{:S(2)}) collective-permute-start(bf16[144,384]{1,0:T(8,128)(2,1)S(1)} %get-tuple-element.110), channel_id=1, source_target_pairs={{0,130},{2,128},{4,134},{6,132},{128,2},{130,0},{132,6},{134,4},{1... | collective-permute-start | bytes 331784 | tf_op jit(solution)/shard_map/ppermute | solution.py:451
  64.0 10.8 %collective-permute-start.17 = (bf16[32,3072]{1,0:T(8,128)(2,1)S(1)}, bf16[32,3072]{1,0:T(8,128)(2,1)S(1)}, u32[]{:S(2)}, u32[]{:S(2)}) collective-permute-start(bf16[32,3072]{1,0:T(8,128)(2,1)S(1)} %get-tuple-element.113), channel_id=1, source_target_pairs={{0,5},{1,4},{2,7},{3,6},{4,1},{5,0},{6,3},{7,2},{8,13},{9,12},{10,... | collective-permute-start | bytes 589832 | tf_op jit(solution)/shard_map/ppermute | solution.py:462
  67.8 10.7 %collective-permute-start.18 = (bf16[32,3072]{1,0:T(8,128)(2,1)S(1)}, bf16[32,3072]{1,0:T(8,128)(2,1)S(1)}, u32[]{:S(2)}, u32[]{:S(2)}) collective-permute-start(bf16[32,3072]{1,0:T(8,128)(2,1)S(1)} %get-tuple-element.114), channel_id=1, source_target_pairs={{0,4},{2,6},{4,0},{6,2},{1,5},{3,7},{5,1},{7,3},{8,12},{10,14},{12... | collective-permute-start | bytes 589832 | tf_op jit(solution)/shard_map/ppermute | solution.py:386
  68.4 10.1 %collective-permute-start.19 = (bf16[32,3072]{1,0:T(8,128)(2,1)S(1)}, bf16[32,3072]{1,0:T(8,128)(2,1)S(1)}, u32[]{:S(2)}, u32[]{:S(2)}) collective-permute-start(bf16[32,3072]{1,0:T(8,128)(2,1)S(1)} %get-tuple-element.115), channel_id=1, source_target_pairs={{0,1},{1,0},{2,3},{3,2},{4,5},{5,4},{6,7},{7,6},{8,9},{9,8},{10,11... | collective-permute-start | bytes 589832 | tf_op jit(solution)/shard_map/ppermute | solution.py:386
  79.7 9.4 %collective-permute-start.23 = (bf16[32,3072]{1,0:T(8,128)(2,1)S(1)}, bf16[32,3072]{1,0:T(8,128)(2,1)S(1)}, u32[]{:S(2)}, u32[]{:S(2)}) collective-permute-start(bf16[32,3072]{1,0:T(8,128)(2,1)S(1)} %add_convert_fusion.refs_0_), channel_id=1, source_target_pairs={{0,4},{2,6},{4,0},{6,2},{1,5},{3,7},{5,1},{7,3},{8,12},{10,14},{12... | collective-permute-start | bytes 589832 | tf_op jit(solution)/shard_map/ppermute | solution.py:386
  81.4 8.9 %collective-permute-start.20 = (bf16[32,3072]{1,0:T(8,128)(2,1)S(1)}, bf16[32,3072]{1,0:T(8,128)(2,1)S(1)}, u32[]{:S(2)}, u32[]{:S(2)}) collective-permute-start(bf16[32,3072]{1,0:T(8,128)(2,1)S(1)} %add_convert_fusion.refs_0_), channel_id=1, source_target_pairs={{0,1},{1,0},{2,3},{3,2},{4,5},{5,4},{6,7},{7,6},{8,9},{9,8},{10,11... | collective-permute-start | bytes 589832 | tf_op jit(solution)/shard_map/ppermute | solution.py:386
  83.6 10.1 %collective-permute-start.26 = (bf16[32,3072]{1,0:T(8,128)(2,1)S(1)}, bf16[32,3072]{1,0:T(8,128)(2,1)S(1)}, u32[]{:S(2)}, u32[]{:S(2)}) collective-permute-start(bf16[32,3072]{1,0:T(8,128)(2,1)S(1)} %add_convert_fusion.refs_0_), channel_id=1, source_target_pairs={{0,6},{2,0},{4,2},{6,4},{1,7},{3,1},{5,3},{7,5},{8,14},{10,8},{12,... | collective-permute-start | bytes 589832 | tf_op jit(solution)/shard_map/ppermute | solution.py:386
  84.3 9.4 %collective-permute-start.25 = (bf16[32,3072]{1,0:T(8,128)(2,1)S(1)}, bf16[32,3072]{1,0:T(8,128)(2,1)S(1)}, u32[]{:S(2)}, u32[]{:S(2)}) collective-permute-start(bf16[32,3072]{1,0:T(8,128)(2,1)S(1)} %add_convert_fusion.refs_0_), channel_id=1, source_target_pairs={{0,2},{2,4},{4,6},{6,0},{1,3},{3,5},{5,7},{7,1},{8,10},{10,12},{12... | collective-permute-start | bytes 589832 | tf_op jit(solution)/shard_map/ppermute | solution.py:386
  89.0 7.2 %collective-permute-start.24 = (bf16[32,3072]{1,0:T(8,128)(2,1)S(1)}, bf16[32,3072]{1,0:T(8,128)(2,1)S(1)}, u32[]{:S(2)}, u32[]{:S(2)}) collective-permute-start(bf16[32,3072]{1,0:T(8,128)(2,1)S(1)} %collective-permute-done.23.refs_4_), channel_id=1, source_target_pairs={{0,1},{1,0},{2,3},{3,2},{4,5},{5,4},{6,7},{7,6},{8,9},{9,8},{10,11... | collective-permute-start | bytes 589832 | tf_op jit(solution)/shard_map/ppermute | solution.py:386
  90.3 5.9 %collective-permute-start.22 = (bf16[32,3072]{1,0:T(8,128)(2,1)S(1)}, bf16[32,3072]{1,0:T(8,128)(2,1)S(1)}, u32[]{:S(2)}, u32[]{:S(2)}) collective-permute-start(bf16[32,3072]{1,0:T(8,128)(2,1)S(1)} %collective-permute-done.20.refs_1_), channel_id=1, source_target_pairs={{0,6},{2,0},{4,2},{6,4},{1,7},{3,1},{5,3},{7,5},{8,14},{10,8},{12,... | collective-permute-start | bytes 589832 | tf_op jit(solution)/shard_map/ppermute | solution.py:386
  92.5 6.9 %collective-permute-start.21 = (bf16[32,3072]{1,0:T(8,128)(2,1)S(1)}, bf16[32,3072]{1,0:T(8,128)(2,1)S(1)}, u32[]{:S(2)}, u32[]{:S(2)}) collective-permute-start(bf16[32,3072]{1,0:T(8,128)(2,1)S(1)} %collective-permute-done.20.refs_1_), channel_id=1, source_target_pairs={{0,2},{2,4},{4,6},{6,0},{1,3},{3,5},{5,7},{7,1},{8,10},{10,12},{12... | collective-permute-start | bytes 589832 | tf_op jit(solution)/shard_map/ppermute | solution.py:386
  (3 other events, 21.9 us)

commit v7 on v6

--- a/solution.py
+++ b/solution.py
@@ -349,6 +349,23 @@
     )(place, *messages, *weights)
 
 
+def sum_kernel(mine, a, b, c, rows, gate, bias, out):
+    total = mine[...].astype(jnp.float32) + a[...].astype(jnp.float32)
+    total += b[...].astype(jnp.float32) + c[...].astype(jnp.float32)
+    out[...] = (rows[...].astype(jnp.float32) + gate[...] * (total + bias[...])).astype(jnp.bfloat16)
+
+
+def sum_call(mine, parts, rows, gate, bias):
+    return pl.pallas_call(
+        sum_kernel,
+        in_specs=[FULL] * 7,
+        out_specs=FULL,
+        out_shape=jax.ShapeDtypeStruct((ROWS, MODEL), jnp.bfloat16),
+        compiler_params=params(24),
+        cost_estimate=cost(0, 2 * MIB),
+    )(mine, *parts, rows, gate.reshape(1, MODEL), bias.reshape(1, MODEL))
+
+
 def put_kernel(offsets, place, *refs):
     out, sems = refs[-2:]
     x, y = coordinate(place, 0), coordinate(place, 1)
@@ -464,11 +481,8 @@
         ring(along_x, "x_hi", 1),
     ]
     start = y % 2 * HALF + (y // 2 * 2 + x) * ROWS
-    rows = lax.dynamic_slice_in_dim(latents, start, ROWS, 0).astype(jnp.float32)
-    total = mine.astype(jnp.float32)
-    for part in parts:
-        total = total + part.astype(jnp.float32)
-    piece = (rows + mod_gate * (total + b_out)).astype(jnp.bfloat16)
+    rows = lax.dynamic_slice_in_dim(latents, start, ROWS, 0)
+    piece = sum_call(mine, parts, rows, mod_gate, b_out)
 
     beside, two = ring(piece, "x_hi", 1), ring(piece, "y", 2)
     plus, minus = ring(piece, "y", 1), ring(piece, "y", -1)

time: 101 us -> 103 us (1.020); the launches traced: 101 us -> 101 us
  waiting for transfers between devices: 34.2 us -> 30.2 us
  local copies, waits for them, and re-layouts: 3.12 us -> 5.6 us
  Pallas kernels: 23.2 us -> 25.5 us
  starting transfers between devices: 37.8 us -> 39 us
  other arithmetic: 1.14 us -> 0.05 us
    ppermute x2, waiting for transfers between devices: 3.77 us -> 1.49 us  [beside_y(): return lax.ppermute(value, 'y', [(i, i ^ 1) for i in range(4)])]
    unnamed x19 -> x27, local copies, waits for them, and re-layouts: 2.33 us -> 3.87 us
    pallas_call x1, Pallas kernels: 1.31 us -> 2.75 us  [project_call(): pl.pallas_call(project_kernel, in_specs=[FULL] * 8, out_specs=[FULL] * 4,...]
    ppermute x23, starting transfers between devices: 29.7 us -> 30.9 us  [ring(): lax.ppermute(value, axis, [(i, (i + step) % size) for i in range(size)])]
    convert_element_type x1 -> x0, other arithmetic: 1.09 us -> none  [shards(): piece = (rows + mod_gate * (total + b_out)).astype(jnp.bfloat16)]
  transfers between devices with their start and end apart: 27 -> 27, of which waited for: 15 -> 16; matrix products, arithmetic and copies ran while one was open for 2% -> 3% of each run, Pallas kernels for 20% -> 20%
where the time goes in v7:
time: 103 us; the launch traced here: 101 us
  starting transfers between devices  39 us (38%)
  waiting for transfers between devices  30.2 us (29%)
  Pallas kernels  25.5 us (25%)
  local copies, waits for them, and re-layouts  5.6 us (5%)
  between operations  1.05 us (1%)
    ppermute x23, starting transfers between devices, ring(): lax.ppermute(value, axis, [(i, (i + step) % size) for i in range(size)])  30.9 us
    ppermute x23, waiting for transfers between devices, ring(): lax.ppermute(value, axis, [(i, (i + step) % size) for i in range(size)])  24.1 us
    pallas_call x5, Pallas kernels, attend_call(): return list(call(*args))  9.27 us
    pallas_call x1, Pallas kernels, qkv_call(): pl.pallas_call(qkv_kernel, in_specs=[FULL] + [anywhere] * 9, out_specs=[F...  8.52 us
    unnamed x27, local copies, waits for them, and re-layouts  3.87 us
    ppermute x1, starting transfers between devices, shards(): lax.ppermute(both_ways, TENSOR, [(i, (i // 2 + 2) % 4 * 2 + (1 - i % 2))...  3.83 us
    ppermute x1, waiting for transfers between devices, shards(): lax.ppermute(both_ways, TENSOR, [(i, (i // 2 + 2) % 4 * 2 + (1 - i % 2))...  3.24 us
    ppermute x2, starting transfers between devices, beside_y(): return lax.ppermute(value, 'y', [(i, i ^ 1) for i in range(4)])  3.15 us
  transfers between devices with their start and end apart: 27, of which 16 were waited for; matrix products, arithmetic and copies ran while one was open for 3% of the time, Pallas kernels for 20%

profile of v7, /device:TPU:6, one launch (start us, length us, event | category | flops | bytes accessed | tf_op | source)
XLA Modules:
  0.0 101.4 jit_solution(1255309364859047176)
XLA Ops:
  1.7 2.0 %collective-permute-start.2 = (bf16[2,256,384]{2,1,0:T(8,128)(2,1)S(1)}, bf16[2,256,384]{2,1,0:T(8,128)(2,1)S(1)}, u32[]{:S(2)}, u32[]{:S(2)}) collective-permute-start(bf16[2,256,384]{2,1,0:T(8,128)(2,1)S(1)} %bitcast.23), channel_id=1, source_target_pairs={{0,16},{16,32},{32,48},{48,64},{64,80},{80,96},{96,112},{112,0},{1... | collective-permute-start | bytes 1179656 | tf_op jit(solution)/shard_map/ppermute | solution.py:403
  3.7 4.0 %collective-permute-start.3 = (bf16[2,256,384]{2,1,0:T(8,128)(2,1)S(1)}, bf16[2,256,384]{2,1,0:T(8,128)(2,1)S(1)}, u32[]{:S(2)}, u32[]{:S(2)}) collective-permute-start(bf16[2,256,384]{2,1,0:T(8,128)(2,1)S(1)} %bitcast.24), channel_id=1, source_target_pairs={{0,112},{16,0},{32,16},{48,32},{64,48},{80,64},{96,80},{112,96},{1... | collective-permute-start | bytes 1179656 | tf_op jit(solution)/shard_map/ppermute | solution.py:403
  8.5 8.5 %shard_map.140 = (bf16[256,384]{1,0:T(8,128)(2,1)}, bf16[256,384]{1,0:T(8,128)(2,1)}, bf16[256,384]{1,0:T(8,128)(2,1)}, bf16[192,3072]{1,0:T(8,128)(2,1)}) custom-call(f32[8,128]{1,0:T(8,128)} %broadcast_in_dim.2.place, bf16[256,3072]{1,0:T(8,128)(2,1)} %refs_0_.1, bf16[3,3072,384]{2,1,0:T(8,128)(2,1)} %bitcast.32, bf16[288,768]{1,0:T(8,128)(2,1)} %constant.49.clone.refs_2_, ...), custom_call_target="tpu_custom_call" | custom-call | flops 1024 | bytes 1024 | tf_op jit(solution)/shard_map/pallas_call | solution.py:135
  17.0 2.7 %collective-permute-start.8 = (bf16[2,256,384]{2,1,0:T(8,128)(2,1)S(1)}, bf16[2,256,384]{2,1,0:T(8,128)(2,1)S(1)}, u32[]{:S(2)}, u32[]{:S(2)}) collective-permute-start(bf16[2,256,384]{2,1,0:T(8,128)(2,1)S(1)} %collective-permute-done.3.left.refs_2_), channel_id=1, source_target_pairs={{0,112},{16,0},{32,16},{48,32},{64,48},{80,64},{96,80},{112,96},{1... | collective-permute-start | bytes 1179656 | tf_op jit(solution)/shard_map/ppermute | solution.py:403
  19.8 1.6 %collective-permute-start = (bf16[192,3072]{1,0:T(8,128)(2,1)}, bf16[192,3072]{1,0:T(8,128)(2,1)S(1)}, u32[]{:S(2)}, u32[]{:S(2)}) collective-permute-start(bf16[192,3072]{1,0:T(8,128)(2,1)} %get-tuple-element.59), channel_id=1, source_target_pairs={{0,2},{2,0},{4,6},{6,4},{1,3},{3,1},{5,7},{7,5},{8,10},{10,8},{12,... | collective-permute-start | bytes 3538952 | tf_op jit(solution)/shard_map/ppermute | solution.py:407
  22.3 2.2 %shard_map.141 = (f32[512,384]{1,0:T(8,128)S(1)}, f32[512,384]{1,0:T(8,128)S(1)}, f32[512,384]{1,0:T(8,128)S(1)}) custom-call(bf16[256,384]{1,0:T(8,128)(2,1)S(1)} %copy-done.1, bf16[256,384]{1,0:T(8,128)(2,1)S(1)} %collective-permute-done.4.q1.o1, bf16[256,384]{1,0:T(8,128)(2,1)S(1)} %copy-done.2, bf16[256,384]{1,0:T(8,128)(2,1)S(1)} %copy-done.4, ...), custom_call_target="tpu_custom_call" | custom-call | flops 1024 | bytes 1024 | tf_op jit(solution)/shard_map/pallas_call | solution.py:225
  24.6 3.1 %collective-permute-done.8.refs_1_.refs_4_ = bf16[2,256,384]{2,1,0:T(8,128)(2,1)S(1)} collective-permute-done((bf16[2,256,384]{2,1,0:T(8,128)(2,1)S(1)}, bf16[2,256,384]{2,1,0:T(8,128)(2,1)S(1)}, u32[]{:S(2)}, u32[]{:S(2)}) %collective-permute-start.8) | collective-permute-done | bytes 393248 | tf_op jit(solution)/shard_map/ppermute | solution.py:403
  27.7 3.3 %collective-permute-start.10 = (bf16[2,256,384]{2,1,0:T(8,128)(2,1)S(1)}, bf16[2,256,384]{2,1,0:T(8,128)(2,1)S(1)}, u32[]{:S(2)}, u32[]{:S(2)}) collective-permute-start(bf16[2,256,384]{2,1,0:T(8,128)(2,1)S(1)} %collective-permute-done.8.refs_1_.refs_4_), channel_id=1, source_target_pairs={{0,112},{16,0},{32,16},{48,32},{64,48},{80,64},{96,80},{112,96},{1... | collective-permute-start | bytes 1179656 | tf_op jit(solution)/shard_map/ppermute | solution.py:403
  31.1 1.4 %collective-permute-done.5.q1.x1 = bf16[256,384]{1,0:T(8,128)(2,1)S(1)} collective-permute-done((bf16[256,384]{1,0:T(8,128)(2,1)S(1)}, bf16[256,384]{1,0:T(8,128)(2,1)S(1)}, u32[]{:S(2)}, u32[]{:S(2)}) %collective-permute-start.5) | collective-permute-done | bytes 196640 | tf_op jit(solution)/shard_map/ppermute | solution.py:403
  32.5 3.0 %shard_map.143 = (f32[512,384]{1,0:T(8,128)S(1)}, f32[512,384]{1,0:T(8,128)S(1)}, f32[512,384]{1,0:T(8,128)S(1)}) custom-call(bf16[256,384]{1,0:T(8,128)(2,1)S(1)} %collective-permute-done.1.q0.x0, bf16[256,384]{1,0:T(8,128)(2,1)S(1)} %collective-permute-done.5.q1.x1, bf16[2,256,384]{2,1,0:T(8,128)(2,1)S(1)} %bitcast.26, ...), custom_call_target="tpu_custom_call" | custom-call | flops 1024 | bytes 1024 | tf_op jit(solution)/shard_map/pallas_call | solution.py:225
  35.5 1.4 %shard_map.142 = (f32[512,384]{1,0:T(8,128)S(1)}, f32[512,384]{1,0:T(8,128)S(1)}, f32[512,384]{1,0:T(8,128)S(1)}) custom-call(bf16[256,384]{1,0:T(8,128)(2,1)S(1)} %copy-done.1, bf16[256,384]{1,0:T(8,128)(2,1)S(1)} %collective-permute-done.4.q1.o1, bf16[2,256,384]{2,1,0:T(8,128)(2,1)S(1)} %collective-permute-done.6.refs_0_.refs_3_, ...), custom_call_target="tpu_custom_call" | custom-call | flops 1024 | bytes 1024 | tf_op jit(solution)/shard_map/pallas_call | solution.py:225
  37.5 3.4 %collective-permute-done.7.refs_0_ = bf16[2,256,384]{2,1,0:T(8,128)(2,1)S(1)} collective-permute-done((bf16[2,256,384]{2,1,0:T(8,128)(2,1)S(1)}, bf16[2,256,384]{2,1,0:T(8,128)(2,1)S(1)}, u32[]{:S(2)}, u32[]{:S(2)}) %collective-permute-start.7) | collective-permute-done | bytes 393248 | tf_op jit(solution)/shard_map/ppermute | solution.py:403
  41.4 1.8 %collective-permute-start.9 = (bf16[256,384]{1,0:T(8,128)(2,1)S(1)}, bf16[256,384]{1,0:T(8,128)(2,1)S(1)}, u32[]{:S(2)}, u32[]{:S(2)}) collective-permute-start(bf16[256,384]{1,0:T(8,128)(2,1)S(1)} %slice_bitcast_fusion.1), channel_id=1, source_target_pairs={{0,16},{16,32},{32,48},{48,64},{64,80},{80,96},{96,112},{112,0},{1... | collective-permute-start | bytes 589832 | tf_op jit(solution)/shard_map/ppermute | solution.py:403
  43.2 1.3 %shard_map.145 = (f32[512,384]{1,0:T(8,128)S(1)}, f32[512,384]{1,0:T(8,128)S(1)}, f32[512,384]{1,0:T(8,128)S(1)}) custom-call(bf16[256,384]{1,0:T(8,128)(2,1)S(1)} %collective-permute-done.1.q0.x0, bf16[256,384]{1,0:T(8,128)(2,1)S(1)} %collective-permute-done.5.q1.x1, bf16[2,256,384]{2,1,0:T(8,128)(2,1)S(1)} %collective-permute-done.7.refs_0_, ...), custom_call_target="tpu_custom_call" | custom-call | flops 1024 | bytes 1024 | tf_op jit(solution)/shard_map/pallas_call | solution.py:225
  44.5 1.4 %shard_map.144 = (f32[512,384]{1,0:T(8,128)S(1)}, f32[512,384]{1,0:T(8,128)S(1)}, f32[512,384]{1,0:T(8,128)S(1)}) custom-call(bf16[256,384]{1,0:T(8,128)(2,1)S(1)} %copy-done.1, bf16[256,384]{1,0:T(8,128)(2,1)S(1)} %collective-permute-done.4.q1.o1, bf16[2,256,384]{2,1,0:T(8,128)(2,1)S(1)} %collective-permute-done.7.refs_0_, ...), custom_call_target="tpu_custom_call" | custom-call | flops 1024 | bytes 1024 | tf_op jit(solution)/shard_map/pallas_call | solution.py:225
  46.7 1.6 %collective-permute-done.9.keys = bf16[256,384]{1,0:T(8,128)(2,1)S(1)} collective-permute-done((bf16[256,384]{1,0:T(8,128)(2,1)S(1)}, bf16[256,384]{1,0:T(8,128)(2,1)S(1)}, u32[]{:S(2)}, u32[]{:S(2)}) %collective-permute-start.9) | collective-permute-done | bytes 196640 | tf_op jit(solution)/shard_map/ppermute | solution.py:403
  50.0 1.8 %collective-permute-done.12.refs_6_ = bf16[4,144,384]{2,1,0:T(8,128)(2,1)S(1)} collective-permute-done((bf16[4,144,384]{2,1,0:T(8,128)(2,1)S(1)}, bf16[4,144,384]{2,1,0:T(8,128)(2,1)S(1)}, u32[]{:S(2)}, u32[]{:S(2)}) %collective-permute-start.12) | collective-permute-done | bytes 442400 | tf_op jit(solution)/shard_map/ppermute | solution.py:403
  51.8 1.4 %shard_map.147 = (bf16[144,384]{1,0:T(8,128)(2,1)}, bf16[144,384]{1,0:T(8,128)(2,1)}, bf16[144,384]{1,0:T(8,128)(2,1)S(1)}, bf16[144,384]{1,0:T(8,128)(2,1)}) custom-call(f32[8,128]{1,0:T(8,128)S(1)} %copy-done.6, f32[256,384]{1,0:T(8,128)S(1)} %get-tuple-element.99.refs_0_, f32[256,384]{1,0:T(8,128)S(1)} %get-tuple-element.100.refs_1_, ...), custom_call_target="tpu_custom_call" | custom-call | flops 1024 | bytes 1024 | tf_op jit(solution)/shard_map/pallas_call | solution.py:299
  54.8 1.6 %collective-permute-start.14 = (bf16[144,384]{1,0:T(8,128)(2,1)}, bf16[144,384]{1,0:T(8,128)(2,1)}, u32[]{:S(2)}, u32[]{:S(2)}) collective-permute-start(bf16[144,384]{1,0:T(8,128)(2,1)} %get-tuple-element.109), channel_id=1, source_target_pairs={{0,2},{2,0},{4,6},{6,4},{1,3},{3,1},{5,7},{7,5},{8,10},{10,8},{12,... | collective-permute-start | bytes 331784 | tf_op jit(solution)/shard_map/ppermute | solution.py:407
  57.4 2.7 %collective-permute-done.13.refs_1_ = bf16[144,384]{1,0:T(8,128)(2,1)} collective-permute-done((bf16[144,384]{1,0:T(8,128)(2,1)}, bf16[144,384]{1,0:T(8,128)(2,1)}, u32[]{:S(2)}, u32[]{:S(2)}) %collective-permute-start.13) | collective-permute-done | bytes 110624 | tf_op jit(solution)/shard_map/ppermute | solution.py:403
  60.1 1.5 %collective-permute-done.14.refs_2_ = bf16[144,384]{1,0:T(8,128)(2,1)} collective-permute-done((bf16[144,384]{1,0:T(8,128)(2,1)}, bf16[144,384]{1,0:T(8,128)(2,1)}, u32[]{:S(2)}, u32[]{:S(2)}) %collective-permute-start.14) | collective-permute-done | bytes 110624 | tf_op jit(solution)/shard_map/ppermute | solution.py:407
  63.9 2.8 %shard_map.148 = (bf16[32,3072]{1,0:T(8,128)(2,1)S(1)}, bf16[32,3072]{1,0:T(8,128)(2,1)S(1)}, bf16[32,3072]{1,0:T(8,128)(2,1)S(1)}, bf16[32,3072]{1,0:T(8,128)(2,1)S(1)}) custom-call(f32[8,128]{1,0:T(8,128)S(1)} %copy-done.6, bf16[144,384]{1,0:T(8,128)(2,1)S(1)} %copy-done.8, bf16[144,384]{1,0:T(8,128)(2,1)} %collective-permute-done.13.refs_1_, ...), custom_call_target="tpu_custom_call" | custom-call | flops 1024 | bytes 1024 | tf_op jit(solution)/shard_map/pallas_call | solution.py:338
  66.7 3.8 %collective-permute-start.17 = (bf16[32,3072]{1,0:T(8,128)(2,1)S(1)}, bf16[32,3072]{1,0:T(8,128)(2,1)S(1)}, u32[]{:S(2)}, u32[]{:S(2)}) collective-permute-start(bf16[32,3072]{1,0:T(8,128)(2,1)S(1)} %get-tuple-element.113), channel_id=1, source_target_pairs={{0,5},{1,4},{2,7},{3,6},{4,1},{5,0},{6,3},{7,2},{8,13},{9,12},{10,... | collective-permute-start | bytes 589832 | tf_op jit(solution)/shard_map/ppermute | solution.py:479
  71.1 2.1 %collective-permute-start.19 = (bf16[32,3072]{1,0:T(8,128)(2,1)S(1)}, bf16[32,3072]{1,0:T(8,128)(2,1)S(1)}, u32[]{:S(2)}, u32[]{:S(2)}) collective-permute-start(bf16[32,3072]{1,0:T(8,128)(2,1)S(1)} %get-tuple-element.115), channel_id=1, source_target_pairs={{0,1},{1,0},{2,3},{3,2},{4,5},{5,4},{6,7},{7,6},{8,9},{9,8},{10,11... | collective-permute-start | bytes 589832 | tf_op jit(solution)/shard_map/ppermute | solution.py:403
  74.2 3.2 %collective-permute-done.17.a = bf16[32,3072]{1,0:T(8,128)(2,1)S(1)} collective-permute-done((bf16[32,3072]{1,0:T(8,128)(2,1)S(1)}, bf16[32,3072]{1,0:T(8,128)(2,1)S(1)}, u32[]{:S(2)}, u32[]{:S(2)}) %collective-permute-start.17) | collective-permute-done | bytes 196640 | tf_op jit(solution)/shard_map/ppermute | solution.py:479
  77.4 3.8 %collective-permute-done.18.b = bf16[32,3072]{1,0:T(8,128)(2,1)S(1)} collective-permute-done((bf16[32,3072]{1,0:T(8,128)(2,1)S(1)}, bf16[32,3072]{1,0:T(8,128)(2,1)S(1)}, u32[]{:S(2)}, u32[]{:S(2)}) %collective-permute-start.18) | collective-permute-done | bytes 196640 | tf_op jit(solution)/shard_map/ppermute | solution.py:403
  81.4 1.5 %collective-permute-start.20 = (bf16[32,3072]{1,0:T(8,128)(2,1)S(1)}, bf16[32,3072]{1,0:T(8,128)(2,1)S(1)}, u32[]{:S(2)}, u32[]{:S(2)}) collective-permute-start(bf16[32,3072]{1,0:T(8,128)(2,1)S(1)} %shard_map.149.refs_0_), channel_id=1, source_target_pairs={{0,1},{1,0},{2,3},{3,2},{4,5},{5,4},{6,7},{7,6},{8,9},{9,8},{10,11... | collective-permute-start | bytes 589832 | tf_op jit(solution)/shard_map/ppermute | solution.py:403
  82.9 2.4 %collective-permute-start.23 = (bf16[32,3072]{1,0:T(8,128)(2,1)S(1)}, bf16[32,3072]{1,0:T(8,128)(2,1)S(1)}, u32[]{:S(2)}, u32[]{:S(2)}) collective-permute-start(bf16[32,3072]{1,0:T(8,128)(2,1)S(1)} %shard_map.149.refs_0_), channel_id=1, source_target_pairs={{0,4},{2,6},{4,0},{6,2},{1,5},{3,7},{5,1},{7,3},{8,12},{10,14},{12... | collective-permute-start | bytes 589832 | tf_op jit(solution)/shard_map/ppermute | solution.py:403
  85.8 2.7 %collective-permute-start.26 = (bf16[32,3072]{1,0:T(8,128)(2,1)S(1)}, bf16[32,3072]{1,0:T(8,128)(2,1)S(1)}, u32[]{:S(2)}, u32[]{:S(2)}) collective-permute-start(bf16[32,3072]{1,0:T(8,128)(2,1)S(1)} %shard_map.149.refs_0_), channel_id=1, source_target_pairs={{0,6},{2,0},{4,2},{6,4},{1,7},{3,1},{5,3},{7,5},{8,14},{10,8},{12,... | collective-permute-start | bytes 589832 | tf_op jit(solution)/shard_map/ppermute | solution.py:403
  90.3 2.7 %collective-permute-start.22 = (bf16[32,3072]{1,0:T(8,128)(2,1)S(1)}, bf16[32,3072]{1,0:T(8,128)(2,1)S(1)}, u32[]{:S(2)}, u32[]{:S(2)}) collective-permute-start(bf16[32,3072]{1,0:T(8,128)(2,1)S(1)} %collective-permute-done.20.refs_1_), channel_id=1, source_target_pairs={{0,6},{2,0},{4,2},{6,4},{1,7},{3,1},{5,3},{7,5},{8,14},{10,8},{12,... | collective-permute-start | bytes 589832 | tf_op jit(solution)/shard_map/ppermute | solution.py:403
  93.1 1.4 %collective-permute-start.24 = (bf16[32,3072]{1,0:T(8,128)(2,1)S(1)}, bf16[32,3072]{1,0:T(8,128)(2,1)S(1)}, u32[]{:S(2)}, u32[]{:S(2)}) collective-permute-start(bf16[32,3072]{1,0:T(8,128)(2,1)S(1)} %collective-permute-done.23.refs_4_), channel_id=1, source_target_pairs={{0,1},{1,0},{2,3},{3,2},{4,5},{5,4},{6,7},{7,6},{8,9},{9,8},{10,11... | collective-permute-start | bytes 589832 | tf_op jit(solution)/shard_map/ppermute | solution.py:403
  96.9 2.4 %collective-permute-done.21.refs_0_ = bf16[32,3072]{1,0:T(8,128)(2,1)S(1)} collective-permute-done((bf16[32,3072]{1,0:T(8,128)(2,1)S(1)}, bf16[32,3072]{1,0:T(8,128)(2,1)S(1)}, u32[]{:S(2)}, u32[]{:S(2)}) %collective-permute-start.21) | collective-permute-done | bytes 196640 | tf_op jit(solution)/shard_map/ppermute | solution.py:403
  (69 shorter events, 19.7 us)
Async XLA Ops:
  1.7 15.3 %collective-permute-start.2 = (bf16[2,256,384]{2,1,0:T(8,128)(2,1)S(1)}, bf16[2,256,384]{2,1,0:T(8,128)(2,1)S(1)}, u32[]{:S(2)}, u32[]{:S(2)}) collective-permute-start(bf16[2,256,384]{2,1,0:T(8,128)(2,1)S(1)} %bitcast.23), channel_id=1, source_target_pairs={{0,16},{16,32},{32,48},{48,64},{64,80},{80,96},{96,112},{112,0},{1... | collective-permute-start | bytes 1179656 | tf_op jit(solution)/shard_map/ppermute | solution.py:403
  3.7 13.4 %collective-permute-start.3 = (bf16[2,256,384]{2,1,0:T(8,128)(2,1)S(1)}, bf16[2,256,384]{2,1,0:T(8,128)(2,1)S(1)}, u32[]{:S(2)}, u32[]{:S(2)}) collective-permute-start(bf16[2,256,384]{2,1,0:T(8,128)(2,1)S(1)} %bitcast.24), channel_id=1, source_target_pairs={{0,112},{16,0},{32,16},{48,32},{64,48},{80,64},{96,80},{112,96},{1... | collective-permute-start | bytes 1179656 | tf_op jit(solution)/shard_map/ppermute | solution.py:403
  8.5 13.7 %copy-start.11 = (bf16[512,2,384]{2,1,0:T(2,128)(2,1)S(1)}, bf16[512,2,384]{2,1,0:T(2,128)(2,1)}, u32[]{:S(2)}) copy-start(bf16[512,2,384]{2,1,0:T(2,128)(2,1)} %param.22) | copy-start | bytes 2359300
  17.0 10.7 %collective-permute-start.8 = (bf16[2,256,384]{2,1,0:T(8,128)(2,1)S(1)}, bf16[2,256,384]{2,1,0:T(8,128)(2,1)S(1)}, u32[]{:S(2)}, u32[]{:S(2)}) collective-permute-start(bf16[2,256,384]{2,1,0:T(8,128)(2,1)S(1)} %collective-permute-done.3.left.refs_2_), channel_id=1, source_target_pairs={{0,112},{16,0},{32,16},{48,32},{64,48},{80,64},{96,80},{112,96},{1... | collective-permute-start | bytes 1179656 | tf_op jit(solution)/shard_map/ppermute | solution.py:403
  19.8 11.2 %collective-permute-start.6 = (bf16[2,256,384]{2,1,0:T(8,128)(2,1)S(1)}, bf16[2,256,384]{2,1,0:T(8,128)(2,1)S(1)}, u32[]{:S(2)}, u32[]{:S(2)}) collective-permute-start(bf16[2,256,384]{2,1,0:T(8,128)(2,1)S(1)} %collective-permute-done.2.right.refs_1_), channel_id=1, source_target_pairs={{0,16},{16,32},{32,48},{48,64},{64,80},{80,96},{96,112},{112,0},{1... | collective-permute-start | bytes 1179656 | tf_op jit(solution)/shard_map/ppermute | solution.py:403
  19.8 2.5 %collective-permute-start.4 = (bf16[256,384]{1,0:T(8,128)(2,1)}, bf16[256,384]{1,0:T(8,128)(2,1)S(1)}, u32[]{:S(2)}, u32[]{:S(2)}) collective-permute-start(bf16[256,384]{1,0:T(8,128)(2,1)} %get-tuple-element.61.q0.o0), channel_id=1, source_target_pairs={{0,8},{8,0},{1,9},{9,1},{2,10},{10,2},{3,11},{11,3},{4,12},{12,4},... | collective-permute-start | bytes 589832 | tf_op jit(solution)/shard_map/ppermute | solution.py:403
  19.8 29.9 %collective-permute-start = (bf16[192,3072]{1,0:T(8,128)(2,1)}, bf16[192,3072]{1,0:T(8,128)(2,1)S(1)}, u32[]{:S(2)}, u32[]{:S(2)}) collective-permute-start(bf16[192,3072]{1,0:T(8,128)(2,1)} %get-tuple-element.59), channel_id=1, source_target_pairs={{0,2},{2,0},{4,6},{6,4},{1,3},{3,1},{5,7},{7,5},{8,10},{10,8},{12,... | collective-permute-start | bytes 3538952 | tf_op jit(solution)/shard_map/ppermute | solution.py:407
  21.3 9.6 %collective-permute-start.1 = (bf16[256,384]{1,0:T(8,128)(2,1)}, bf16[256,384]{1,0:T(8,128)(2,1)S(1)}, u32[]{:S(2)}, u32[]{:S(2)}) collective-permute-start(bf16[256,384]{1,0:T(8,128)(2,1)} %get-tuple-element.61.q0.o0), channel_id=1, source_target_pairs={{0,128},{128,0},{1,129},{129,1},{2,130},{130,2},{3,131},{131,3},{4... | collective-permute-start | bytes 589832 | tf_op jit(solution)/shard_map/ppermute | solution.py:403
  27.7 9.8 %collective-permute-start.10 = (bf16[2,256,384]{2,1,0:T(8,128)(2,1)S(1)}, bf16[2,256,384]{2,1,0:T(8,128)(2,1)S(1)}, u32[]{:S(2)}, u32[]{:S(2)}) collective-permute-start(bf16[2,256,384]{2,1,0:T(8,128)(2,1)S(1)} %collective-permute-done.8.refs_1_.refs_4_), channel_id=1, source_target_pairs={{0,112},{16,0},{32,16},{48,32},{64,48},{80,64},{96,80},{112,96},{1... | collective-permute-start | bytes 1179656 | tf_op jit(solution)/shard_map/ppermute | solution.py:403
  31.0 10.0 %collective-permute-start.7 = (bf16[2,256,384]{2,1,0:T(8,128)(2,1)S(1)}, bf16[2,256,384]{2,1,0:T(8,128)(2,1)S(1)}, u32[]{:S(2)}, u32[]{:S(2)}) collective-permute-start(bf16[2,256,384]{2,1,0:T(8,128)(2,1)S(1)} %collective-permute-done.6.refs_0_.refs_3_), channel_id=1, source_target_pairs={{0,16},{16,32},{32,48},{48,64},{64,80},{80,96},{96,112},{112,0},{1... | collective-permute-start | bytes 1179656 | tf_op jit(solution)/shard_map/ppermute | solution.py:403
  31.0 1.5 %collective-permute-start.5 = (bf16[256,384]{1,0:T(8,128)(2,1)S(1)}, bf16[256,384]{1,0:T(8,128)(2,1)S(1)}, u32[]{:S(2)}, u32[]{:S(2)}) collective-permute-start(bf16[256,384]{1,0:T(8,128)(2,1)S(1)} %collective-permute-done.1.q0.x0), channel_id=1, source_target_pairs={{0,8},{8,0},{1,9},{9,1},{2,10},{10,2},{3,11},{11,3},{4,12},{12,4},... | collective-permute-start | bytes 589832 | tf_op jit(solution)/shard_map/ppermute | solution.py:403
  41.0 5.7 %collective-permute-start.11 = (bf16[256,384]{1,0:T(8,128)(2,1)S(1)}, bf16[256,384]{1,0:T(8,128)(2,1)S(1)}, u32[]{:S(2)}, u32[]{:S(2)}) collective-permute-start(bf16[256,384]{1,0:T(8,128)(2,1)S(1)} %slice_bitcast_fusion), channel_id=1, source_target_pairs={{0,112},{16,0},{32,16},{48,32},{64,48},{80,64},{96,80},{112,96},{1... | collective-permute-start | bytes 589832 | tf_op jit(solution)/shard_map/ppermute | solution.py:403
  41.4 7.0 %collective-permute-start.9 = (bf16[256,384]{1,0:T(8,128)(2,1)S(1)}, bf16[256,384]{1,0:T(8,128)(2,1)S(1)}, u32[]{:S(2)}, u32[]{:S(2)}) collective-permute-start(bf16[256,384]{1,0:T(8,128)(2,1)S(1)} %slice_bitcast_fusion.1), channel_id=1, source_target_pairs={{0,16},{16,32},{32,48},{48,64},{64,80},{80,96},{96,112},{112,0},{1... | collective-permute-start | bytes 589832 | tf_op jit(solution)/shard_map/ppermute | solution.py:403
  49.7 2.1 %collective-permute-start.12 = (bf16[4,144,384]{2,1,0:T(8,128)(2,1)S(1)}, bf16[4,144,384]{2,1,0:T(8,128)(2,1)S(1)}, u32[]{:S(2)}, u32[]{:S(2)}) collective-permute-start(bf16[4,144,384]{2,1,0:T(8,128)(2,1)S(1)} %get-tuple-element.105), channel_id=1, source_target_pairs={{0,8},{8,0},{1,9},{9,1},{2,10},{10,2},{3,11},{11,3},{4,12},{12,4},... | collective-permute-start | bytes 1327112 | tf_op jit(solution)/shard_map/ppermute | solution.py:403
  53.8 9.2 %collective-permute-start.16 = (bf16[192,3072]{1,0:T(8,128)(2,1)S(1)}, bf16[192,3072]{1,0:T(8,128)(2,1)}, u32[]{:S(2)}, u32[]{:S(2)}) collective-permute-start(bf16[192,3072]{1,0:T(8,128)(2,1)S(1)} %collective-permute-done.refs_5_), channel_id=1, source_target_pairs={{0,8},{8,0},{1,9},{9,1},{2,10},{10,2},{3,11},{11,3},{4,12},{12,4},... | collective-permute-start | bytes 3538952 | tf_op jit(solution)/shard_map/ppermute | solution.py:403
  53.9 6.2 %collective-permute-start.13 = (bf16[144,384]{1,0:T(8,128)(2,1)}, bf16[144,384]{1,0:T(8,128)(2,1)}, u32[]{:S(2)}, u32[]{:S(2)}) collective-permute-start(bf16[144,384]{1,0:T(8,128)(2,1)} %get-tuple-element.108), channel_id=1, source_target_pairs={{0,128},{128,0},{1,129},{129,1},{2,130},{130,2},{3,131},{131,3},{4... | collective-permute-start | bytes 331784 | tf_op jit(solution)/shard_map/ppermute | solution.py:403
  54.8 6.9 %collective-permute-start.14 = (bf16[144,384]{1,0:T(8,128)(2,1)}, bf16[144,384]{1,0:T(8,128)(2,1)}, u32[]{:S(2)}, u32[]{:S(2)}) collective-permute-start(bf16[144,384]{1,0:T(8,128)(2,1)} %get-tuple-element.109), channel_id=1, source_target_pairs={{0,2},{2,0},{4,6},{6,4},{1,3},{3,1},{5,7},{7,5},{8,10},{10,8},{12,... | collective-permute-start | bytes 331784 | tf_op jit(solution)/shard_map/ppermute | solution.py:407
  56.3 6.6 %collective-permute-start.15 = (bf16[144,384]{1,0:T(8,128)(2,1)}, bf16[144,384]{1,0:T(8,128)(2,1)}, u32[]{:S(2)}, u32[]{:S(2)}) collective-permute-start(bf16[144,384]{1,0:T(8,128)(2,1)} %get-tuple-element.110), channel_id=1, source_target_pairs={{0,130},{2,128},{4,134},{6,132},{128,2},{130,0},{132,6},{134,4},{1... | collective-permute-start | bytes 331784 | tf_op jit(solution)/shard_map/ppermute | solution.py:468
  63.9 17.4 %copy-start.9 = (f32[3072]{0:T(1024)S(1)}, f32[3072]{0:T(1024)}, u32[]{:S(2)}) copy-start(f32[3072]{0:T(1024)} %param.17) | copy-start | bytes 36868
  63.9 17.4 %copy-start.10 = (f32[3072]{0:T(1024)S(1)}, f32[3072]{0:T(1024)}, u32[]{:S(2)}) copy-start(f32[3072]{0:T(1024)} %param.24) | copy-start | bytes 36868
  66.6 27.8 %copy-start.3 = (bf16[256,384]{1,0:T(8,128)(2,1)S(1)}, bf16[256,384]{1,0:T(8,128)(2,1)}, u32[]{:S(2)}) copy-start(bf16[256,384]{1,0:T(8,128)(2,1)} %get-tuple-element.62.k) | copy-start | bytes 589828
  66.6 27.8 %copy-start.5 = (bf16[256,384]{1,0:T(8,128)(2,1)S(1)}, bf16[256,384]{1,0:T(8,128)(2,1)}, u32[]{:S(2)}) copy-start(bf16[256,384]{1,0:T(8,128)(2,1)} %get-tuple-element.63.v) | copy-start | bytes 589828
  66.7 10.8 %collective-permute-start.17 = (bf16[32,3072]{1,0:T(8,128)(2,1)S(1)}, bf16[32,3072]{1,0:T(8,128)(2,1)S(1)}, u32[]{:S(2)}, u32[]{:S(2)}) collective-permute-start(bf16[32,3072]{1,0:T(8,128)(2,1)S(1)} %get-tuple-element.113), channel_id=1, source_target_pairs={{0,5},{1,4},{2,7},{3,6},{4,1},{5,0},{6,3},{7,2},{8,13},{9,12},{10,... | collective-permute-start | bytes 589832 | tf_op jit(solution)/shard_map/ppermute | solution.py:479
  70.5 10.7 %collective-permute-start.18 = (bf16[32,3072]{1,0:T(8,128)(2,1)S(1)}, bf16[32,3072]{1,0:T(8,128)(2,1)S(1)}, u32[]{:S(2)}, u32[]{:S(2)}) collective-permute-start(bf16[32,3072]{1,0:T(8,128)(2,1)S(1)} %get-tuple-element.114), channel_id=1, source_target_pairs={{0,4},{2,6},{4,0},{6,2},{1,5},{3,7},{5,1},{7,3},{8,12},{10,14},{12... | collective-permute-start | bytes 589832 | tf_op jit(solution)/shard_map/ppermute | solution.py:403
  71.1 10.1 %collective-permute-start.19 = (bf16[32,3072]{1,0:T(8,128)(2,1)S(1)}, bf16[32,3072]{1,0:T(8,128)(2,1)S(1)}, u32[]{:S(2)}, u32[]{:S(2)}) collective-permute-start(bf16[32,3072]{1,0:T(8,128)(2,1)S(1)} %get-tuple-element.115), channel_id=1, source_target_pairs={{0,1},{1,0},{2,3},{3,2},{4,5},{5,4},{6,7},{7,6},{8,9},{9,8},{10,11... | collective-permute-start | bytes 589832 | tf_op jit(solution)/shard_map/ppermute | solution.py:403
  81.4 8.4 %collective-permute-start.20 = (bf16[32,3072]{1,0:T(8,128)(2,1)S(1)}, bf16[32,3072]{1,0:T(8,128)(2,1)S(1)}, u32[]{:S(2)}, u32[]{:S(2)}) collective-permute-start(bf16[32,3072]{1,0:T(8,128)(2,1)S(1)} %shard_map.149.refs_0_), channel_id=1, source_target_pairs={{0,1},{1,0},{2,3},{3,2},{4,5},{5,4},{6,7},{7,6},{8,9},{9,8},{10,11... | collective-permute-start | bytes 589832 | tf_op jit(solution)/shard_map/ppermute | solution.py:403
  82.9 10.2 %collective-permute-start.23 = (bf16[32,3072]{1,0:T(8,128)(2,1)S(1)}, bf16[32,3072]{1,0:T(8,128)(2,1)S(1)}, u32[]{:S(2)}, u32[]{:S(2)}) collective-permute-start(bf16[32,3072]{1,0:T(8,128)(2,1)S(1)} %shard_map.149.refs_0_), channel_id=1, source_target_pairs={{0,4},{2,6},{4,0},{6,2},{1,5},{3,7},{5,1},{7,3},{8,12},{10,14},{12... | collective-permute-start | bytes 589832 | tf_op jit(solution)/shard_map/ppermute | solution.py:403
  85.3 10.4 %collective-permute-start.25 = (bf16[32,3072]{1,0:T(8,128)(2,1)S(1)}, bf16[32,3072]{1,0:T(8,128)(2,1)S(1)}, u32[]{:S(2)}, u32[]{:S(2)}) collective-permute-start(bf16[32,3072]{1,0:T(8,128)(2,1)S(1)} %shard_map.149.refs_0_), channel_id=1, source_target_pairs={{0,2},{2,4},{4,6},{6,0},{1,3},{3,5},{5,7},{7,1},{8,10},{10,12},{12... | collective-permute-start | bytes 589832 | tf_op jit(solution)/shard_map/ppermute | solution.py:403
  85.8 10.0 %collective-permute-start.26 = (bf16[32,3072]{1,0:T(8,128)(2,1)S(1)}, bf16[32,3072]{1,0:T(8,128)(2,1)S(1)}, u32[]{:S(2)}, u32[]{:S(2)}) collective-permute-start(bf16[32,3072]{1,0:T(8,128)(2,1)S(1)} %shard_map.149.refs_0_), channel_id=1, source_target_pairs={{0,6},{2,0},{4,2},{6,4},{1,7},{3,1},{5,3},{7,5},{8,14},{10,8},{12,... | collective-permute-start | bytes 589832 | tf_op jit(solution)/shard_map/ppermute | solution.py:403
  89.8 9.5 %collective-permute-start.21 = (bf16[32,3072]{1,0:T(8,128)(2,1)S(1)}, bf16[32,3072]{1,0:T(8,128)(2,1)S(1)}, u32[]{:S(2)}, u32[]{:S(2)}) collective-permute-start(bf16[32,3072]{1,0:T(8,128)(2,1)S(1)} %collective-permute-done.20.refs_1_), channel_id=1, source_target_pairs={{0,2},{2,4},{4,6},{6,0},{1,3},{3,5},{5,7},{7,1},{8,10},{10,12},{12... | collective-permute-start | bytes 589832 | tf_op jit(solution)/shard_map/ppermute | solution.py:403
  90.3 9.1 %collective-permute-start.22 = (bf16[32,3072]{1,0:T(8,128)(2,1)S(1)}, bf16[32,3072]{1,0:T(8,128)(2,1)S(1)}, u32[]{:S(2)}, u32[]{:S(2)}) collective-permute-start(bf16[32,3072]{1,0:T(8,128)(2,1)S(1)} %collective-permute-done.20.refs_1_), channel_id=1, source_target_pairs={{0,6},{2,0},{4,2},{6,4},{1,7},{3,1},{5,3},{7,5},{8,14},{10,8},{12,... | collective-permute-start | bytes 589832 | tf_op jit(solution)/shard_map/ppermute | solution.py:403
  93.1 7.2 %collective-permute-start.24 = (bf16[32,3072]{1,0:T(8,128)(2,1)S(1)}, bf16[32,3072]{1,0:T(8,128)(2,1)S(1)}, u32[]{:S(2)}, u32[]{:S(2)}) collective-permute-start(bf16[32,3072]{1,0:T(8,128)(2,1)S(1)} %collective-permute-done.23.refs_4_), channel_id=1, source_target_pairs={{0,1},{1,0},{2,3},{3,2},{4,5},{5,4},{6,7},{7,6},{8,9},{9,8},{10,11... | collective-permute-start | bytes 589832 | tf_op jit(solution)/shard_map/ppermute | solution.py:403
  (7 other events, 34.2 us)
